TPU v7x, 32 devices: a whole 2x2x4 slice. The times are simulated.
32 devices in a mesh: groups: 2 (over x), fsdp: 16 (over z, y, core).
Axes of the slice: x: 2, y: 2, z: 4, core: 2. Of those that a mesh axis runs over, the one named last changes fastest.
Arguments:
- token_ids: int32 [768], P('groups'), parts along dimension 0, may hold values from 0 to 9599
- key_value_of_block: int32 [8], replicated, may hold values from 0 to 7, each once
- vocab_table: bfloat16 [9600, 5120], P('fsdp'), may hold values from -50 to 50, as said below
- in_gain: float32 [5120], replicated, may hold values from 0.25 to 1.75
- q_gain: float32 [128], replicated, may hold values from 0.25 to 1.75
- k_gain: float32 [128], replicated, may hold values from 0.25 to 1.75
- wq_codes: bfloat16 [5120, 8192], P('fsdp'), may hold values from -0.078125 to 0.078125
- wq_scale: float32 [40, 64], replicated, may hold values from 0.5 to 2
- key_value_codes: bfloat16 [5120, 2048], P('fsdp'), may hold values from -0.078125 to 0.078125
- key_value_scale: float32 [40, 16], replicated, may hold values from 0.5 to 2
- wo_codes: bfloat16 [8192, 5120], P(None, 'fsdp'), may hold values from -0.75 to 0.75
- wo_scale: float32 [64, 40], replicated, may hold values from 0.5 to 2
Outputs:
- attn_out: bfloat16 [768, 5120], P(('groups', 'fsdp')), parts along dimension 0
- synced_keys: bfloat16 [32, 5120, 128], P(('groups', 'fsdp')), parts along dimension 0
There are 2 independent parts, one for each index of `groups`. A program takes and returns all parts, laid end to end along the dimension named above; an argument that names none is the same for every part. Nothing has to cross between parts.
Inputs may be any that keep to these rules, and one draw needn't show every extreme that they name: `key_value_of_block`: each of the 8 key-value heads appears exactly once. `vocab_table`: rows of very different sizes.
All inputs are finite; a program needn't handle non-finite values.
Results may differ from a plain program's by a relative error of at most 0.0095.
Values may be sent and summed in bfloat16 or wider, within the bound.
No kernel may reach another device: no remote copies, remote signals or barrier semaphores. Data moves between devices by JAX's collectives and lax.ppermute only.
A program may use at most 128 MiB of HBM per device.

v0:
```python
import jax
import jax.numpy as jnp
from jax import lax
from jax.sharding import PartitionSpec as P

QUERY_HEADS = 64
KEY_VALUE_HEADS = 8
HEAD_SIZE = 128
TILE_SIDE = 128
LEN = 384


theta_base = 1000000.0
eps_norm = 1e-06


def rms_scale(values, norm_gain):
    mean_square = jnp.mean(values * values, axis=-1, keepdims=True)
    return values * lax.rsqrt(mean_square + eps_norm) * norm_gain


def rotate(values, positions):
    half_width = values.shape[-1] // 2
    frequency = theta_base ** (-jnp.arange(half_width, dtype=jnp.float32) * 2.0 / values.shape[-1])
    angles = positions[:, None] * frequency[None, :]
    cosine = jnp.cos(angles)[:, None, :]
    sine_part = jnp.sin(angles)[:, None, :]
    lower_half = values[..., :half_width]
    upper_half = values[..., half_width:]
    return jnp.concatenate(
        [
            lower_half * cosine - upper_half * sine_part,
            upper_half * cosine + lower_half * sine_part,
        ],
        axis=-1,
    )


def lookup_small(small_table, indices):
    matches = indices[..., None] == jnp.arange(small_table.shape[0], dtype=jnp.int32)
    return jnp.sum(jnp.where(matches, small_table, 0), axis=-1)


def column_scales(tile_scale, first_col, width_cols):
    per_column = jnp.repeat(tile_scale, TILE_SIDE, axis=1)
    picked = lax.dynamic_slice_in_dim(per_column, first_col, width_cols, 1)
    return jnp.repeat(picked, TILE_SIDE, axis=0)


def dequantize(quantized, scales):
    return (quantized.astype(jnp.float32) * scales).astype(jnp.bfloat16)


def attend(queries, key_rows, value_rows, prompt_count):
    token_count, head_count, head_width = queries.shape
    length = token_count // prompt_count
    query_blocks = queries.reshape(prompt_count, length, head_count, head_width)
    key_blocks = key_rows.reshape(prompt_count, length, head_width)
    value_blocks = value_rows.reshape(prompt_count, length, -1)
    scores = jnp.einsum(
        "plhd,pmd->phlm", query_blocks, key_blocks, preferred_element_type=jnp.float32
    ) * head_width ** (-0.5)
    causal = jnp.arange(length)[:, None] >= jnp.arange(length)[None, :]
    weights = jnp.where(causal, jnp.exp(scores), 0.0)
    probabilities = (weights / jnp.sum(weights, axis=-1, keepdims=True)).astype(jnp.bfloat16)
    attended_rows = jnp.einsum(
        "phlm,pmd->plhd", probabilities, value_blocks, preferred_element_type=jnp.float32
    )
    return attended_rows.astype(jnp.bfloat16).reshape(
        token_count, head_count * value_blocks.shape[-1]
    )


def on_device(
    token_ids,
    key_value_of_block,
    vocab_table,
    in_gain,
    q_gain,
    k_gain,
    wq_codes,
    wq_scale,
    key_value_codes,
    key_value_scale,
    wo_codes,
    wo_scale,
):
    count_of_ranks = lax.axis_size("fsdp")
    my_rank = lax.axis_index("fsdp")
    duplicate_count = count_of_ranks // KEY_VALUE_HEADS
    per_key_value = QUERY_HEADS // KEY_VALUE_HEADS
    split_points = max(1, duplicate_count // per_key_value)
    heads_here = max(1, per_key_value // duplicate_count)
    value_columns = HEAD_SIZE // split_points
    query_width = heads_here * HEAD_SIZE
    local_rows = wq_codes.shape[0]
    token_count = token_ids.shape[0]
    targets = jnp.arange(count_of_ranks, dtype=jnp.int32)
    target_head = lookup_small(key_value_of_block, targets // duplicate_count)
    target_slot = targets % duplicate_count
    target_part = target_slot % split_points
    target_query = target_head * per_key_value + target_slot // split_points * heads_here
    my_head = lookup_small(key_value_of_block, my_rank // duplicate_count)
    my_slot = my_rank % duplicate_count
    my_part = my_slot % split_points
    my_query = my_head * per_key_value + my_slot // split_points * heads_here
    vocab_rows = vocab_table.shape[0]
    local_ids = token_ids - my_rank * vocab_rows
    inside = (local_ids >= 0) & (local_ids < vocab_rows)
    picked = jnp.take(vocab_table, jnp.clip(local_ids, 0, vocab_rows - 1), axis=0)
    terms = jnp.where(inside[:, None], picked, jnp.zeros_like(picked)).astype(jnp.float32)
    embedded = lax.psum(terms, "fsdp").astype(jnp.bfloat16)
    normed = rms_scale(embedded.astype(jnp.float32), in_gain).astype(jnp.bfloat16)
    query_groups = wq_codes.reshape(local_rows, QUERY_HEADS // heads_here, query_width)
    query_send = jnp.take(query_groups, target_query // heads_here, axis=1)
    key_value_heads = key_value_codes.reshape(local_rows, KEY_VALUE_HEADS, 2, HEAD_SIZE)
    key_send = jnp.take(key_value_heads[:, :, 0, :], target_head, axis=1)
    grouped_values = key_value_heads[:, :, 1, :].reshape(
        local_rows, KEY_VALUE_HEADS * split_points, value_columns
    )
    value_send = jnp.take(grouped_values, target_head * split_points + target_part, axis=1)
    both_send = jnp.concatenate([key_send, value_send], axis=2)
    query_got, kv_got = (
        lax.all_to_all(query_send, "fsdp", split_axis=1, concat_axis=0, tiled=True),
        lax.all_to_all(both_send, "fsdp", split_axis=1, concat_axis=0, tiled=True),
    )
    key_quant = kv_got[:, 0, :HEAD_SIZE]
    value_quant = kv_got[:, 0, HEAD_SIZE:]
    query_weight = dequantize(
        query_got[:, 0, :], column_scales(wq_scale, my_query * HEAD_SIZE, query_width)
    )
    key_matrix = dequantize(
        key_quant, column_scales(key_value_scale, my_head * 2 * HEAD_SIZE, HEAD_SIZE)
    )
    value_weight = dequantize(
        value_quant,
        column_scales(
            key_value_scale,
            my_head * 2 * HEAD_SIZE + HEAD_SIZE + my_part * value_columns,
            value_columns,
        ),
    )
    joined_weight = jnp.concatenate([query_weight, key_matrix, value_weight], axis=1)
    projected = jnp.dot(normed, joined_weight, preferred_element_type=jnp.float32)
    positions = (jnp.arange(token_count) % LEN).astype(jnp.float32)
    queries = rotate(
        rms_scale(projected[:, :query_width].reshape(token_count, heads_here, HEAD_SIZE), q_gain),
        positions,
    ).astype(jnp.bfloat16)
    keys_raw = projected[:, query_width : query_width + HEAD_SIZE].reshape(
        token_count, 1, HEAD_SIZE
    )
    key_rows = rotate(rms_scale(keys_raw, k_gain), positions).astype(jnp.bfloat16)[:, 0, :]
    value_rows = projected[:, query_width + HEAD_SIZE :].astype(jnp.bfloat16)
    attended_rows = attend(queries, key_rows, value_rows, token_count // LEN)
    cols_here = wo_codes.shape[1]
    local_weight = dequantize(wo_codes, column_scales(wo_scale, my_rank * cols_here, cols_here))
    ordered = jnp.take(
        local_weight.reshape(KEY_VALUE_HEADS, per_key_value * HEAD_SIZE, cols_here),
        key_value_of_block,
        axis=0,
    ).reshape(QUERY_HEADS * HEAD_SIZE, cols_here)
    columns = jnp.dot(
        lax.all_gather(attended_rows, "fsdp", axis=1, tiled=True),
        ordered,
        preferred_element_type=jnp.float32,
    )
    attn_out = lax.all_to_all(
        columns.astype(jnp.bfloat16), "fsdp", split_axis=0, concat_axis=1, tiled=True
    )
    return (attn_out, key_matrix.reshape(1, key_matrix.shape[0], HEAD_SIZE))


def solution(mesh):
    return jax.shard_map(
        on_device,
        mesh=mesh,
        in_specs=(
            P("groups"),
            P(),
            P("fsdp", None),
            P(),
            P(),
            P(),
            P("fsdp", None),
            P(),
            P("fsdp", None),
            P(),
            P(None, "fsdp"),
            P(),
        ),
        out_specs=(P(("groups", "fsdp"), None), P(("groups", "fsdp"), None, None)),
        check_vma=False,
    )
```

profile of v0, /device:TPU:0, one launch (start us, length us, event | category | flops | bytes accessed | tf_op | source)
XLA Modules:
  0.0 488.5 jit_solution(10113520910359540098)
XLA Ops:
  8.0 3.6 reshape.398
  11.5 1.8 fusion.59
  14.7 1.8 gather_fusion.4
  16.5 1.7 select_bitcast_fusion.2
  18.2 1.8 pad_maximum_fusion
  20.0 7.4 %all-to-all-start.1 = ((bf16[320,16,256]{2,0,1:T(8,128)(2,1)}), bf16[320,16,256]{2,0,1:T(8,128)(2,1)S(1)}, u32[]{:S(2)}, u32[]{:S(2)}) async-start(bf16[320,16,256]{2,0,1:T(8,128)(2,1)} %pad_maximum_fusion), calls=%async_computation.1 | async-start | bytes 5242880 | tf_op jit(solution)/shard_map/all_to_all | solution.py:125
  27.4 5.4 %copy.95 = bf16[40,16,8,512]{3,2,0,1:T(8,128)(2,1)} copy(bf16[40,16,8,512]{3,2,1,0:T(8,128)(2,1)} %bitcast.137) | data formatting | bytes 10485760 | tf_op jit(solution)/shard_map/reshape | solution.py:114
  32.8 5.6 %gather_fusion.1 = bf16[16,320,512]{2,1,0:T(8,128)(2,1)} fusion(bf16[320,16,512]{2,0,1:T(8,128)(2,1)} %bitcast.133, s32[1024]{0:T(1024)S(1)} %pad_clamp_fusion.1), kind=kCustom, calls=%fused_computation.3 | custom fusion | bytes 10485824 | tf_op jit(solution)/shard_map/jit(_take)/gather | solution.py:115
  38.4 5.3 %select_bitcast_fusion = bf16[320,16,512]{2,0,1:T(8,128)(2,1)} fusion(bf16[16,320,512]{2,1,0:T(8,128)(2,1)} %gather_fusion.1, pred[16]{0:T(512)(128)(4,1)S(1)} %get-tuple-element.22), kind=kLoop, calls=%fused_computation.23 | loop fusion | flops 2621440 | bytes 10485776 | tf_op jit(solution)/shard_map/jit(_take)/select_n | solution.py:115
  43.7 33.9 %all-to-all-done.1 = bf16[320,16,256]{2,0,1:T(8,128)(2,1)S(1)} async-done(((bf16[320,16,256]{2,0,1:T(8,128)(2,1)}), bf16[320,16,256]{2,0,1:T(8,128)(2,1)S(1)}, u32[]{:S(2)}, u32[]{:S(2)}) %all-to-all-start.1) | async-done | bytes 2621472 | tf_op jit(solution)/shard_map/all_to_all | solution.py:125
  77.6 13.4 %all-to-all-start = ((bf16[320,16,512]{2,0,1:T(8,128)(2,1)}), bf16[320,16,512]{2,0,1:T(8,128)(2,1)}, u32[]{:S(2)}, u32[]{:S(2)}) async-start(bf16[320,16,512]{2,0,1:T(8,128)(2,1)} %select_bitcast_fusion), calls=%async_computation | async-start | bytes 10485760 | tf_op jit(solution)/shard_map/all_to_all | solution.py:124
  94.2 1.8 copy.97
  96.4 13.6 %gather_fusion = bf16[384,5120]{1,0:T(8,128)(2,1)} fusion(bf16[600,5120]{1,0:T(8,128)(2,1)} %param.16, s32[1024]{0:T(1024)S(1)} %pad_clamp_fusion.2), kind=kCustom, calls=%fused_computation.2 | custom fusion | bytes 7865856 | tf_op jit(solution)/shard_map/jit(_take)/gather | solution.py:110
  110.0 5.9 %select_convert_fusion = f32[384,5120]{1,0:T(8,128)} fusion(bf16[384,5120]{1,0:T(8,128)(2,1)} %gather_fusion, pred[384]{0:T(512)(128)(4,1)S(1)} %get-tuple-element.3, pred[384]{0:T(512)(128)(4,1)S(1)} %get-tuple-element.19), kind=kLoop, calls=%fused_computation.29 | loop fusion | flops 5898240 | bytes 11797248 | tf_op jit(solution)/shard_map/convert_element_type | solution.py:111
  117.6 226.8 %all-reduce.1 = bf16[384,5120]{1,0:T(8,128)(2,1)} all-reduce(f32[384,5120]{1,0:T(8,128)} %select_convert_fusion), channel_id=1, replica_groups=mesh['groups'=2,'fsdp'=16] {'fsdp'}, use_global_device_ids=true, to_apply=%region_0.1 | all-reduce | flops 1966080 | bytes 11796480 | tf_op jit(solution)/shard_map/psum | solution.py:112
  344.4 3.0 fusion.2
  348.8 2.0 fusion.18
  350.9 3.9 bitcast_convert_fusion
  354.8 5.2 %fusion.1 = bf16[5120,512]{1,0:T(8,128)(2,1)} fusion(f32[320,16,1,512]{3,0,1,2:T(8,128)S(1)} %bitcast_convert_fusion, f32[40,512]{1,0:T(8,128)S(1)} %constant_dynamic-slice_fusion.2), kind=kLoop, calls=%fused_computation.8 | loop fusion | flops 5242880 | bytes 15810560 | tf_op jit(solution)/shard_map/convert_element_type | solution.py:51
  360.1 7.7 %fusion.5 = f32[384,768]{1,0:T(8,128)S(1)} fusion(bf16[5120,128]{1,0:T(8,128)(2,1)} %get-tuple-element.6, bf16[5120,128]{1,0:T(8,128)(2,1)} %get-tuple-element.5, bf16[5120,512]{1,0:T(8,128)(2,1)} %fusion.1, f32[5120]{0:T(1024)S(1)} %copy-done.11, f32[384]{0:T(512)S(1)} %add_rsqrt_fusion.2, bf16[384,5120]{1,0:T(8,128)(2,1)} %all-reduce.1), kind=kOutput, calls=%fused_computation.14 | convolution fusion | flops 3051356160 | bytes 12998144 | tf_op jit(solution)/shard_map/dot_general | solution.py:144
  370.7 2.3 reshape.402
  373.0 2.3 multiply_reduce_fusion
  379.5 2.5 convolution_convert_fusion
  382.3 7.6 %broadcast_in_dim.142 = f32[64,128,320]{1,0,2:T(8,128)} broadcast(f32[64,320]{0,1:T(8,128)S(1)} %constant_dynamic-slice_fusion.3), dimensions={0,2} | broadcast | bytes 10567680 | tf_op jit(solution)/shard_map/broadcast_in_dim | solution.py:47
  389.9 14.3 %fusion = bf16[8192,320]{0,1:T(8,128)(2,1)} fusion(f32[40,8,64,128]{3,2,1,0:T(8,128)} %bitcast.129, bf16[8192,320]{0,1:T(8,128)(2,1)} %param.24), kind=kLoop, calls=%fused_computation.6 | loop fusion | flops 7864320 | bytes 20971520 | tf_op jit(solution)/shard_map/convert_element_type | solution.py:51
  404.2 5.7 %copy.96 = bf16[40,8,8,1024]{3,2,0,1:T(8,128)(2,1)} copy(bf16[40,8,8,1024]{3,2,1,0:T(8,128)(2,1)} %bitcast.132) | data formatting | bytes 10485760 | tf_op jit(solution)/shard_map/reshape | solution.py:159
  409.9 5.7 %gather_fusion.2 = bf16[8,1024,320]{1,2,0:T(8,128)(2,1)} fusion(bf16[8,1024,320]{1,2,0:T(8,128)(2,1)} %bitcast.130, s32[1024]{0:T(1024)S(1)} %pad_clamp_fusion.3), kind=kCustom, calls=%fused_computation.4 | custom fusion | bytes 10485792 | tf_op jit(solution)/shard_map/jit(_take)/gather | solution.py:158
  415.7 5.7 %copy.81 = bf16[8,40,8,1024]{3,2,0,1:T(8,128)(2,1)} copy(bf16[8,40,8,1024]{3,2,1,0:T(8,128)(2,1)} %bitcast.131) | data formatting | bytes 10485760 | tf_op jit(solution)/shard_map/jit(_take)/gather | solution.py:158
  421.4 36.6 %all-gather.2.cloned.1.call-done = bf16[384,8192]{0,1:T(8,128)(2,1)} async-done(((bf16[384,512]{0,1:T(8,128)(2,1)}), bf16[384,8192]{0,1:T(8,128)(2,1)}) %all-gather.2.cloned.1.call-update) | async-done | bytes 6291472 | tf_op jit(solution)/shard_map/all_gather | solution.py:164
  458.0 7.2 %fusion.25 = bf16[384,320]{0,1:T(8,128)(2,1)S(1)} fusion(bf16[384,8192]{0,1:T(8,128)(2,1)} %all-gather.2.cloned.1.call-done, bf16[8192,320]{0,1:T(8,128)(2,1)} %bitcast.138, pred[8192]{0:T(1024)(128)(4,1)S(1)} %bitcast.146), kind=kOutput, calls=%fused_computation.49 | convolution fusion | flops 2016010240 | bytes 11788288 | tf_op jit(solution)/shard_map/dot_general | solution.py:163
  466.2 3.5 all-to-all-start.2
  471.3 9.0 %all-to-all-done.2 = bf16[16,24,320]{2,1,0:T(8,128)(2,1)S(1)} async-done(((bf16[16,24,320]{2,1,0:T(8,128)(2,1)}), bf16[16,24,320]{2,1,0:T(8,128)(2,1)S(1)}, u32[]{:S(2)}, u32[]{:S(2)}) %all-to-all-start.2) | async-done | bytes 245792 | tf_op jit(solution)/shard_map/all_to_all | solution.py:168
  (71 shorter events, 18.3 us)
Async XLA Ops:
  7.2 374.9 %copy-start = (f32[64,40]{0,1:T(8,128)S(1)}, f32[64,40]{0,1:T(8,128)}, u32[]{:S(2)}) copy-start(f32[64,40]{0,1:T(8,128)} %param.25) | copy-start | bytes 30724
  20.0 57.6 %all-to-all-start.1 = ((bf16[320,16,256]{2,0,1:T(8,128)(2,1)}), bf16[320,16,256]{2,0,1:T(8,128)(2,1)S(1)}, u32[]{:S(2)}, u32[]{:S(2)}) async-start(bf16[320,16,256]{2,0,1:T(8,128)(2,1)} %pad_maximum_fusion), calls=%async_computation.1 | async-start | bytes 5242880 | tf_op jit(solution)/shard_map/all_to_all | solution.py:125
  43.7 47.5 %copy-start.9 = (s32[8]{0:T(128)S(1)}, s32[8]{0:T(128)}, u32[]{:S(2)}) copy-start(s32[8]{0:T(128)} %param.15) | copy-start | bytes 100
  43.7 50.1 %copy-start.4 = (f32[40,64]{1,0:T(8,128)S(1)}, f32[40,64]{1,0:T(8,128)}, u32[]{:S(2)}) copy-start(f32[40,64]{1,0:T(8,128)} %param.21) | copy-start | bytes 30724
  77.6 273.3 %all-to-all-start = ((bf16[320,16,512]{2,0,1:T(8,128)(2,1)}), bf16[320,16,512]{2,0,1:T(8,128)(2,1)}, u32[]{:S(2)}, u32[]{:S(2)}) async-start(bf16[320,16,512]{2,0,1:T(8,128)(2,1)} %select_bitcast_fusion), calls=%async_computation | async-start | bytes 10485760 | tf_op jit(solution)/shard_map/all_to_all | solution.py:124
  91.0 5.0 %copy-start.5 = (f32[40,16]{0,1:T(8,128)S(1)}, f32[40,16]{0,1:T(8,128)}, u32[]{:S(2)}) copy-start(f32[40,16]{0,1:T(8,128)} %param.23) | copy-start | bytes 7684
  91.0 5.3 %copy-start.7 = (s32[384]{0:T(512)S(1)}, s32[384]{0:T(512)}, u32[]{:S(2)}) copy-start(s32[384]{0:T(512)} %param.14) | copy-start | bytes 4612
  91.0 367.0 %all-gather.2.cloned.1.call-start = ((), (), s32[]{:S(2)}) async-start(), calls=%async_computation.3 | async-start | bytes 6684672 | tf_op jit(solution)/shard_map/all_gather | solution.py:164
  354.8 5.2 %copy-start.11 = (f32[5120]{0:T(1024)S(1)}, f32[5120]{0:T(1024)}, u32[]{:S(2)}) copy-start(f32[5120]{0:T(1024)} %param.17) | copy-start | bytes 61444
  360.1 9.0 %copy-start.8 = (f32[128]{0:T(128)S(1)}, f32[128]{0:T(128)}, u32[]{:S(2)}) copy-start(f32[128]{0:T(128)} %param.19) | copy-start | bytes 1540
  367.8 2.9 copy-start.1
  376.3 2.4 copy-start.2
  376.3 2.4 copy-start.3
  404.2 5.7 %copy-start.6 = (s32[8]{0:T(128)S(1)}, s32[8]{0:T(128)}, u32[]{:S(2)}) copy-start(s32[8]{0:T(128)} %get-tuple-element.20) | copy-start | bytes 100
  415.7 5.7 %copy-start.10 = (s32[8]{0:T(128)S(1)}, s32[8]{0:T(128)}, u32[]{:S(2)}) copy-start(s32[8]{0:T(128)} %param.15) | copy-start | bytes 100
  466.2 14.1 %all-to-all-start.2 = ((bf16[16,24,320]{2,1,0:T(8,128)(2,1)}), bf16[16,24,320]{2,1,0:T(8,128)(2,1)S(1)}, u32[]{:S(2)}, u32[]{:S(2)}) async-start(bf16[16,24,320]{2,1,0:T(8,128)(2,1)} %bitcast.32), calls=%async_computation.2 | async-start | bytes 589824 | tf_op jit(solution)/shard_map/all_to_all | solution.py:168
Sparse Core Ops, SparseCore 0:
  382.2 75.8 all-gather.1
where the time goes:
time: 495 us; the launch traced here: 489 us
  blocking collectives  227 us (46%)
  waiting for transfers between devices  79.5 us (16%)
  local copies, waits for them, and re-layouts  68.1 us (14%)
  other arithmetic  55.3 us (11%)
  starting transfers between devices  24.5 us (5%)
  matrix products  18.3 us (4%)
  between operations  16.1 us (3%)
    psum x1, blocking collectives, on_device(): embedded = lax.psum(terms, 'fsdp').astype(jnp.bfloat16)  227 us
    all_gather x1, waiting for transfers between devices, on_device(): lax.all_gather(attended_rows, 'fsdp', axis=1, tiled=True)  36.6 us
    all_to_all x1, waiting for transfers between devices, on_device(): lax.all_to_all(both_send, 'fsdp', split_axis=1, concat_axis=0, tiled=True)  33.9 us
    convert_element_type x5, other arithmetic, dequantize(): return (quantized.astype(jnp.float32) * scales).astype(jnp.bfloat16)  26.9 us
    gather x1, local copies, waits for them, and re-layouts, on_device(): jnp.take(vocab_table, jnp.clip(local_ids, 0, vocab_rows - 1), axis=0)  13.6 us
    all_to_all x1, starting transfers between devices, on_device(): lax.all_to_all(query_send, 'fsdp', split_axis=1, concat_axis=0, tiled=True)  13.4 us
    gather x2, local copies, waits for them, and re-layouts, on_device(): jnp.take(local_weight.reshape(KEY_VALUE_HEADS, per_key_value * HEAD_SIZE,...  11.4 us
  transfers between devices with their start and end apart: 4, of which 3 were waited for; matrix products, arithmetic and copies ran while one was open for 18% of the time, Pallas kernels for 0%

commit v1 on v0

--- a/solution.py
+++ b/solution.py
@@ -1,8 +1,10 @@
+import functools
 import jax
 import jax.numpy as jnp
 from jax import lax
+from jax.experimental import pallas as pl
+from jax.experimental.pallas import tpu as pltpu
 from jax.sharding import PartitionSpec as P
-
 QUERY_HEADS = 64
 KEY_VALUE_HEADS = 8
 HEAD_SIZE = 128
@@ -71,7 +73,7 @@
     )
 
 
-def on_device(
+def general_plan(
     token_ids,
     key_value_of_block,
     vocab_table,
@@ -171,9 +173,512 @@
     return (attn_out, key_matrix.reshape(1, key_matrix.shape[0], HEAD_SIZE))
 
 
+BF = jnp.bfloat16
+F32 = jnp.float32
+SLOTS = 32
+GROUP_ROWS = 64
+PARAMS = pltpu.CompilerParams(vmem_limit_bytes=48 << 20)
+SMEM = pl.BlockSpec(memory_space=pltpu.SMEM)
+
+
+def cost(flops, bytes_accessed):
+    return pl.CostEstimate(flops=flops, bytes_accessed=bytes_accessed, transcendentals=0)
+
+
+def owner_of(ids, vocab_rows, ranks):
+    owner = jnp.zeros_like(ids)
+    for rank in range(1, ranks):
+        owner = owner + jnp.where(ids >= float(rank * vocab_rows), 1.0, 0.0)
+    return owner
+
+
+def iota(shape, axis):
+    return lax.broadcasted_iota(jnp.int32, shape, axis).astype(F32)
+
+
+def slot_kernel(ranks, vocab_rows, info, id_col, id_row, col_out, row_out, most_out):
+    count = id_col.shape[0]
+    ids_c, ids_r = id_col[...].astype(F32), id_row[...].astype(F32)
+    at_r, at_c = iota((count, count), 0), iota((count, count), 1)
+    same = ids_c == ids_r
+    first_c = jnp.min(jnp.where(same, at_c, float(count)), axis=1, keepdims=True)
+    first_r = jnp.min(jnp.where(same, at_r, float(count)), axis=0, keepdims=True)
+    is_first_r = first_r == iota((1, count), 1)
+    is_first_c = first_c == iota((count, 1), 0)
+    owner_c, owner_r = owner_of(ids_c, vocab_rows, ranks), owner_of(ids_r, vocab_rows, ranks)
+    peers = owner_c == owner_r
+    slot_c = jnp.sum(
+        jnp.where(peers & is_first_r & (at_c < first_c), 1.0, 0.0), axis=1, keepdims=True
+    )
+    slot_r = jnp.sum(
+        jnp.where(peers & is_first_c & (at_r < first_r), 1.0, 0.0), axis=0, keepdims=True
+    )
+    lane = lax.broadcasted_iota(jnp.int32, (count, 128), 1)
+    col_out[...] = jnp.where(lane == 0, owner_c, jnp.where(lane == 1, slot_c, 0.0))
+    me = info[0].astype(F32)
+    mine = is_first_r & (owner_r == me)
+    row_out[...] = jnp.zeros_like(row_out)
+    row_out[0:1, :] = jnp.where(mine, slot_r, -1.0)
+    row_out[1:2, :] = ids_r - me * float(vocab_rows)
+    most_out[...] = jnp.broadcast_to(jnp.max(slot_r, axis=1, keepdims=True) + 1.0, (8, 128))
+
+
+def find_slots(token_ids, my_rank, ranks, vocab_rows):
+    count = token_ids.shape[0]
+    return pl.pallas_call(
+        functools.partial(slot_kernel, ranks, vocab_rows),
+        out_shape=(
+            jax.ShapeDtypeStruct((count, 128), F32),
+            jax.ShapeDtypeStruct((8, count), F32),
+            jax.ShapeDtypeStruct((8, 128), F32),
+        ),
+        in_specs=[SMEM, pl.BlockSpec(memory_space=pltpu.VMEM), pl.BlockSpec(memory_space=pltpu.VMEM)],
+        compiler_params=PARAMS,
+        cost_estimate=cost(1000000, 1000000),
+        name="find_slots",
+    )(my_rank.reshape(1), token_ids.reshape(count, 1), token_ids.reshape(1, count))
+
+
+def pick_kernel(width, base, rows, gain, table, out, picked, total):
+    step = pl.program_id(0)
+    slots = picked.shape[0]
+    vocab_rows = table.shape[0]
+    wanted = lax.broadcasted_iota(jnp.int32, (slots, 1), 0).astype(F32) + base[0].astype(F32)
+    chosen = wanted == rows[0:1, :]
+    index = jnp.sum(jnp.where(chosen, rows[1:2, :], 0.0), axis=1, keepdims=True)
+    valid = jnp.sum(jnp.where(chosen, 1.0, 0.0), axis=1, keepdims=True)
+    hot = (iota((slots, vocab_rows), 1) == index) & (valid > 0.5)
+    block = jnp.dot(hot.astype(F32).astype(BF), table[...], preferred_element_type=F32)
+    picked[:, pl.ds(pl.multiple_of(step * width, width), width)] = block
+
+    @pl.when(step == 0)
+    def _():
+        total[...] = jnp.zeros_like(total)
+
+    total[...] += jnp.sum(block * block, axis=1, keepdims=True)
+
+    @pl.when(step == pl.num_programs(0) - 1)
+    def _():
+        features = picked.shape[1]
+        inverse = lax.rsqrt(total[:, 0:1] * (1.0 / features) + eps_norm)
+        for part in range(features // width):
+            span = slice(part * width, (part + 1) * width)
+            out[part] = (picked[:, span] * inverse * gain[:, span]).astype(BF)
+
+
+def pick_rows(rows, base, in_gain, vocab_table, chips):
+    vocab_rows, features = vocab_table.shape
+    width = features // chips
+    return pl.pallas_call(
+        functools.partial(pick_kernel, width),
+        grid=(chips,),
+        out_shape=jax.ShapeDtypeStruct((chips, SLOTS, width), BF),
+        in_specs=[
+            SMEM,
+            pl.BlockSpec(rows.shape, lambda i: (0, 0)),
+            pl.BlockSpec((1, features), lambda i: (0, 0)),
+            pl.BlockSpec((vocab_rows, width), lambda i: (0, i)),
+        ],
+        out_specs=pl.BlockSpec((chips, SLOTS, width), lambda i: (0, 0, 0)),
+        scratch_shapes=[pltpu.VMEM((SLOTS, features), F32), pltpu.VMEM((SLOTS, 128), F32)],
+        compiler_params=PARAMS,
+        cost_estimate=cost(2 * SLOTS * vocab_rows * features, 2 * vocab_rows * features),
+        name="pick_rows",
+    )(base.reshape(1), rows, in_gain.reshape(1, features), vocab_table)
+
+
+def place_kernel(chips, info, owners, own, other, out):
+    count = owners.shape[0]
+    core, base = info[0].astype(F32), info[1].astype(F32)
+    owner, slot = owners[:, 0:1], owners[:, 1:2] - base
+    chip = jnp.zeros_like(owner)
+    for number in range(1, chips):
+        chip = chip + jnp.where(owner >= 2.0 * number, 1.0, 0.0)
+    owner_core = owner - 2.0 * chip
+    fits = (slot >= 0.0) & (slot < float(SLOTS))
+    column = iota((count, chips * SLOTS), 1)
+    hit = (column == chip * float(SLOTS) + slot) & fits
+    hot_own = jnp.where(hit & (owner_core == core), 1.0, 0.0).astype(BF)
+    hot_other = jnp.where(hit & (owner_core != core), 1.0, 0.0).astype(BF)
+    picked = jnp.dot(hot_own, own[...], preferred_element_type=F32)
+    picked += jnp.dot(hot_other, other[...], preferred_element_type=F32)
+    out[...] = picked.astype(BF)
+
+
+def place_rows(owners, base, core, own, other, chips):
+    count = owners.shape[0]
+    width = own.shape[-1]
+    vmem = pl.BlockSpec(memory_space=pltpu.VMEM)
+    return pl.pallas_call(
+        functools.partial(place_kernel, chips),
+        out_shape=jax.ShapeDtypeStruct((count, width), BF),
+        in_specs=[SMEM, vmem, vmem, vmem],
+        compiler_params=PARAMS,
+        cost_estimate=cost(4 * count * chips * SLOTS * width, 6 * chips * SLOTS * width),
+        name="place_rows",
+    )(
+        jnp.stack([core, base]),
+        owners,
+        own.reshape(chips * SLOTS, width),
+        other.reshape(chips * SLOTS, width),
+    )
+
+
+def weight_kernel(info, head_of, wq_scale, kv_scale, wq, kv, kv_key, own, send, key_out):
+    block = pl.program_id(0)
+    core, rank = info[0], info[1]
+    rows = wq.shape[0]
+    half = wq.shape[1] // 2
+    key_head = head_of[block]
+    for group in range(rows // GROUP_ROWS):
+        tile_row = (rank * (rows // GROUP_ROWS) + group) // 2
+        span = slice(group * GROUP_ROWS, (group + 1) * GROUP_ROWS)
+        for side, target in ((core, own), (1 - core, send)):
+            for tile in range(half // TILE_SIDE):
+                scale = wq_scale[tile_row, (2 * block + side) * (half // TILE_SIDE) + tile]
+                start = pl.multiple_of(side * half + tile * TILE_SIDE, TILE_SIDE)
+                codes = wq[span, pl.ds(start, TILE_SIDE)].astype(F32)
+                target[0, span, tile * TILE_SIDE : (tile + 1) * TILE_SIDE] = (codes * scale).astype(BF)
+            scale = kv_scale[tile_row, 2 * block + side]
+            start = pl.multiple_of(side * TILE_SIDE, TILE_SIDE)
+            codes = kv[span, pl.ds(start, TILE_SIDE)].astype(F32)
+            target[0, span, half : half + TILE_SIDE] = (codes * scale).astype(BF)
+        scale = kv_scale[tile_row, 2 * key_head]
+        key_out[0, span, :] = (kv_key[span, :].astype(F32) * scale).astype(BF)
+
+
+def prepare_weights(core, my_rank, key_value_of_block, wq_codes, wq_scale, kv_codes, kv_scale, chips):
+    rows = wq_codes.shape[0]
+    half = wq_codes.shape[1] // (2 * chips)
+    out = jax.ShapeDtypeStruct((chips, rows, half + TILE_SIDE), BF)
+    out_spec = pl.BlockSpec((1, rows, half + TILE_SIDE), lambda b, *_: (b, 0, 0))
+    return pl.pallas_call(
+        weight_kernel,
+        grid_spec=pltpu.PrefetchScalarGridSpec(
+            num_scalar_prefetch=4,
+            grid=(chips,),
+            in_specs=[
+                pl.BlockSpec((rows, 2 * half), lambda b, *_: (0, b)),
+                pl.BlockSpec((rows, 2 * TILE_SIDE), lambda b, *_: (0, b)),
+                pl.BlockSpec((rows, TILE_SIDE), lambda b, info, head_of, *_: (0, 2 * head_of[b])),
+            ],
+            out_specs=[out_spec, out_spec, pl.BlockSpec((1, rows, TILE_SIDE), lambda b, *_: (b, 0, 0))],
+        ),
+        out_shape=[out, out, jax.ShapeDtypeStruct((chips, rows, TILE_SIDE), BF)],
+        compiler_params=PARAMS,
+        cost_estimate=cost(rows * wq_codes.shape[1] * 8, rows * wq_codes.shape[1] * 6),
+        name="prepare_weights",
+    )(
+        jnp.stack([core, my_rank]),
+        key_value_of_block,
+        wq_scale,
+        kv_scale,
+        wq_codes,
+        kv_codes,
+        kv_codes,
+    )
+
+
+def project_kernel(info, normed, own, other, out, weight):
+    rows = own.shape[1]
+    core = info[0]
+    weight[pl.ds(pl.multiple_of(core * rows, GROUP_ROWS), rows), :] = own[0]
+    weight[pl.ds(pl.multiple_of((1 - core) * rows, GROUP_ROWS), rows), :] = other[0]
+    out[0] = jnp.dot(normed[...], weight[...], preferred_element_type=F32).astype(out.dtype)
+
+
+def project(core, y_side, normed, own, other, out_type, z_count):
+    count, width = normed.shape
+    chips, rows, columns = own.shape
+    weight_spec = pl.BlockSpec(
+        (1, rows, columns), lambda z, info: (z * (chips // z_count) + info[1], 0, 0)
+    )
+    return pl.pallas_call(
+        project_kernel,
+        grid_spec=pltpu.PrefetchScalarGridSpec(
+            num_scalar_prefetch=1,
+            grid=(z_count,),
+            in_specs=[
+                pl.BlockSpec((count, width), lambda z, info: (0, 0)),
+                weight_spec,
+                weight_spec,
+            ],
+            out_specs=pl.BlockSpec((1, count, columns), lambda z, info: (z, 0, 0)),
+            scratch_shapes=[pltpu.VMEM((width, columns), BF)],
+        ),
+        out_shape=jax.ShapeDtypeStruct((z_count, count, columns), out_type),
+        compiler_params=PARAMS,
+        cost_estimate=cost(
+            2 * z_count * count * width * columns, 2 * z_count * columns * (width + count)
+        ),
+        name="project",
+    )(jnp.stack([core, y_side]), normed, own, other)
+
+
+def join_kernel(own, got, out):
+    out[...] = (own[...] + got[...].astype(F32)).astype(BF)
+
+
+def join_partials(own, got, start):
+    blocks, rows, columns = got.shape
+    return pl.pallas_call(
+        join_kernel,
+        grid=(blocks,),
+        in_specs=[
+            pl.BlockSpec((1, rows, columns), lambda z: (z, start // rows, 0)),
+            pl.BlockSpec((1, rows, columns), lambda z: (z, 0, 0)),
+        ],
+        out_specs=pl.BlockSpec((1, rows, columns), lambda z: (z, 0, 0)),
+        out_shape=jax.ShapeDtypeStruct(got.shape, BF),
+        compiler_params=PARAMS,
+        cost_estimate=cost(2 * blocks * rows * columns, 8 * blocks * rows * columns),
+        name="join_partials",
+    )(own, got)
+
+
+def turn(values, cosine, sine):
+    return values * cosine + pltpu.roll(values, HEAD_SIZE // 2, 1) * sine
+
+
+def normalise(values, gain):
+    mean_square = jnp.mean(values * values, axis=-1, keepdims=True)
+    return values * lax.rsqrt(mean_square + eps_norm) * gain
+
+
+def heads_kernel(info, parts, q_gain, k_gain, cosine, sine, q_out, kv_out):
+    total = parts[0].astype(F32)
+    for source in range(1, parts.shape[0]):
+        total = total + parts[source].astype(F32)
+    heads = q_out.shape[0]
+    cos, sin = cosine[...], sine[...]
+    last = total[:, heads * HEAD_SIZE :]
+
+    @pl.when(info[0] == 0)
+    def _():
+        kv_out[...] = turn(normalise(last, k_gain[...]), cos, sin).astype(BF)
+
+    @pl.when(info[0] == 1)
+    def _():
+        kv_out[...] = last.astype(BF)
+
+    for head in range(heads):
+        values = total[:, head * HEAD_SIZE : (head + 1) * HEAD_SIZE]
+        q_out[head] = turn(normalise(values, q_gain[...]), cos, sin).astype(BF)
+
+
+def make_heads(core, parts, q_gain, k_gain, cosine, sine):
+    sources, count, columns = parts.shape
+    heads = columns // HEAD_SIZE - 1
+    vmem = pl.BlockSpec(memory_space=pltpu.VMEM)
+    return pl.pallas_call(
+        heads_kernel,
+        out_shape=(
+            jax.ShapeDtypeStruct((heads, count, HEAD_SIZE), BF),
+            jax.ShapeDtypeStruct((count, HEAD_SIZE), BF),
+        ),
+        in_specs=[SMEM] + [vmem] * 5,
+        compiler_params=PARAMS,
+        cost_estimate=cost(20 * count * columns, 2 * parts.size + 2 * count * columns),
+        name="make_heads",
+    )(core.reshape(1), parts, q_gain.reshape(1, -1), k_gain.reshape(1, -1), cosine, sine)
+
+
+def attend_kernel(length, info, queries, own, other, out):
+    first = info[0] == 0
+    keys = jnp.where(first, own[...], other[...])
+    values = jnp.where(first, other[...], own[...])
+    count = keys.shape[0]
+    here = lax.broadcasted_iota(jnp.int32, (count, count), 0)
+    there = lax.broadcasted_iota(jnp.int32, (count, count), 1)
+    allowed = here >= there
+    for prompt in range(1, count // length):
+        allowed = allowed & ((here < prompt * length) | (there >= prompt * length))
+    for head in range(queries.shape[0]):
+        scores = lax.dot_general(
+            queries[head], keys, (((1,), (1,)), ((), ())), preferred_element_type=F32
+        ) * HEAD_SIZE ** (-0.5)
+        weights = jnp.where(allowed, jnp.exp(scores), 0.0)
+        probabilities = (weights / jnp.sum(weights, axis=-1, keepdims=True)).astype(BF)
+        out[:, head * HEAD_SIZE : (head + 1) * HEAD_SIZE] = jnp.dot(
+            probabilities, values, preferred_element_type=F32
+        ).astype(BF)
+
+
+def attend_heads(core, queries, own, other):
+    heads, count, width = queries.shape
+    vmem = pl.BlockSpec(memory_space=pltpu.VMEM)
+    return pl.pallas_call(
+        functools.partial(attend_kernel, LEN),
+        out_shape=jax.ShapeDtypeStruct((count, heads * width), BF),
+        in_specs=[SMEM, vmem, vmem, vmem],
+        compiler_params=PARAMS,
+        cost_estimate=cost(4 * heads * count * count * width, 4 * heads * count * width),
+        name="attend",
+    )(core.reshape(1), queries, own, other)
+
+
+def out_weight_kernel(codes, scales, out):
+    for tile in range(codes.shape[0] // TILE_SIDE):
+        span = slice(tile * TILE_SIDE, (tile + 1) * TILE_SIDE)
+        scale = scales[pl.ds(pl.program_id(0) * (codes.shape[0] // TILE_SIDE) + tile, 1), :]
+        out[span, :] = (codes[span, :].astype(F32) * scale).astype(BF)
+
+
+def prepare_out(wo_codes, scales, step_rows):
+    rows, columns = wo_codes.shape
+    return pl.pallas_call(
+        out_weight_kernel,
+        grid=(rows // step_rows,),
+        in_specs=[
+            pl.BlockSpec((step_rows, columns), lambda i: (i, 0)),
+            pl.BlockSpec(scales.shape, lambda i: (0, 0)),
+        ],
+        out_specs=pl.BlockSpec((step_rows, columns), lambda i: (i, 0)),
+        out_shape=jax.ShapeDtypeStruct(wo_codes.shape, BF),
+        compiler_params=PARAMS,
+        cost_estimate=cost(4 * rows * columns, 4 * rows * columns),
+        name="prepare_out",
+    )(wo_codes, scales)
+
+
+def out_kernel(attended, weight, out, total):
+    step = pl.program_id(0)
+
+    @pl.when(step == 0)
+    def _():
+        total[...] = jnp.zeros_like(total)
+
+    total[...] += jnp.dot(attended[0], weight[...], preferred_element_type=F32)
+
+    @pl.when(step == pl.num_programs(0) - 1)
+    def _():
+        out[...] = total[...].astype(BF)
+
+
+def out_project(attended, weight):
+    ranks, count, width = attended.shape
+    columns = weight.shape[1]
+    return pl.pallas_call(
+        out_kernel,
+        grid=(ranks,),
+        in_specs=[
+            pl.BlockSpec((1, count, width), lambda i: (i, 0, 0)),
+            pl.BlockSpec((width, columns), lambda i: (i, 0)),
+        ],
+        out_specs=pl.BlockSpec((count, columns), lambda i: (0, 0)),
+        out_shape=jax.ShapeDtypeStruct((count, columns), BF),
+        scratch_shapes=[pltpu.VMEM((count, columns), F32)],
+        compiler_params=PARAMS,
+        cost_estimate=cost(2 * ranks * count * width * columns, 2 * ranks * width * (count + columns)),
+        name="out_project",
+    )(attended, weight)
+
+
+def rotation_tables(count):
+    half_width = HEAD_SIZE // 2
+    positions = (jnp.arange(count) % LEN).astype(F32)
+    frequency = theta_base ** (-jnp.arange(half_width, dtype=F32) * 2.0 / HEAD_SIZE)
+    angles = positions[:, None] * frequency[None, :]
+    cosine, sine = jnp.cos(angles), jnp.sin(angles)
+    return jnp.concatenate([cosine, cosine], axis=1), jnp.concatenate([-sine, sine], axis=1)
+
+
+Z_COUNT = 4
+TOKEN_PARTS = 2
+
+
+def chip_plan(
+    token_ids,
+    key_value_of_block,
+    vocab_table,
+    in_gain,
+    q_gain,
+    k_gain,
+    wq_codes,
+    wq_scale,
+    key_value_codes,
+    key_value_scale,
+    wo_codes,
+    wo_scale,
+):
+    ranks = lax.axis_size("fsdp")
+    chips = ranks // 2
+    y_count = chips // Z_COUNT
+    my_rank = lax.axis_index("fsdp").astype(jnp.int32)
+    core = my_rank % 2
+    my_y = my_rank // 2 % y_count
+    count = token_ids.shape[0]
+    vocab_rows = vocab_table.shape[0]
+    same_core = [[2 * chip + side for chip in range(chips)] for side in range(2)]
+    z_lines = [[2 * y_count * z + rest for z in range(Z_COUNT)] for rest in range(2 * y_count)]
+
+    def swap(values, bit):
+        return lax.ppermute(values, "fsdp", [(i, i ^ bit) for i in range(ranks)])
+
+    owners, rows, most = find_slots(token_ids, my_rank, ranks, vocab_rows)
+    most = jnp.maximum(most, lax.ppermute(most, "groups", [(0, 1), (1, 0)]))[0, 0]
+
+    def exchange(base):
+        sent = pick_rows(rows, base, in_gain, vocab_table, chips)
+        own = lax.all_to_all(
+            sent, "fsdp", split_axis=0, concat_axis=0, tiled=True, axis_index_groups=same_core
+        )
+        return place_rows(owners, base, core, own, swap(own, 1), chips)
+
+    normed = exchange(jnp.int32(0))
+    _, normed = lax.while_loop(
+        lambda state: state[0].astype(F32) < most,
+        lambda state: (state[0] + SLOTS, state[1] + exchange(state[0])),
+        (jnp.int32(SLOTS), normed),
+    )
+
+    own_weight, sent_weight, sent_keys = prepare_weights(
+        core, my_rank, key_value_of_block, wq_codes, wq_scale, key_value_codes, key_value_scale, chips
+    )
+    other_weight = swap(sent_weight, 1)
+    own_keys = lax.all_to_all(
+        sent_keys, "fsdp", split_axis=0, concat_axis=0, tiled=True, axis_index_groups=same_core
+    )
+    other_keys = swap(own_keys, 1)
+    first = core == 0
+    synced = jnp.stack(
+        [jnp.where(first, own_keys, other_keys), jnp.where(first, other_keys, own_keys)], axis=1
+    )
+
+    away = project(core, 1 - my_y, normed, own_weight, other_weight, BF, Z_COUNT)
+    step = count // TOKEN_PARTS
+    got = [swap(away[:, part * step : (part + 1) * step], 2) for part in range(TOKEN_PARTS)]
+    home = project(core, my_y, normed, own_weight, other_weight, F32, Z_COUNT)
+    parts = [
+        lax.all_to_all(
+            join_partials(home, got[part], part * step),
+            "fsdp",
+            split_axis=0,
+            concat_axis=0,
+            tiled=True,
+            axis_index_groups=z_lines,
+        )
+        for part in range(TOKEN_PARTS)
+    ]
+    parts = jnp.concatenate(parts, axis=1)
+    cosine, sine = rotation_tables(count)
+    queries, own_kv = make_heads(core, parts, q_gain, k_gain, cosine, sine)
+    attended = attend_heads(core, queries, own_kv, swap(own_kv, 1))
+
+    columns_here = wo_codes.shape[1]
+    per_column = jnp.repeat(wo_scale, TILE_SIDE, axis=1)
+    out_scales = lax.dynamic_slice_in_dim(per_column, my_rank * columns_here, columns_here, 1)
+    out_weight = prepare_out(wo_codes, out_scales, attended.shape[1])
+    columns = out_project(lax.all_gather(attended, "fsdp"), out_weight)
+    attn_out = lax.all_to_all(columns, "fsdp", split_axis=0, concat_axis=1, tiled=True)
+    return attn_out, synced.reshape(1, -1, HEAD_SIZE)
+
+
 def solution(mesh):
+    sizes = dict(mesh.shape)
+    small = sizes["fsdp"] == 2 * KEY_VALUE_HEADS and sizes["groups"] == 2
     return jax.shard_map(
-        on_device,
+        chip_plan if small else general_plan,
         mesh=mesh,
         in_specs=(
             P("groups"),

time: 495 us -> 251 us (0.51)
  blocking collectives: 227 us -> 50.6 us
  Pallas kernels: 0 us -> 56.9 us
  other arithmetic: 55.3 us -> 1.63 us
  local copies, waits for them, and re-layouts: 68.1 us -> 21.7 us
  matrix products: 18.3 us -> 0 us
  starting transfers between devices: 24.5 us -> 15.5 us
  waiting for transfers between devices: 79.5 us -> 88 us
    psum x1 -> x0, blocking collectives: 227 us -> none  [on_device(): embedded = lax.psum(terms, 'fsdp').astype(jnp.bfloat16)]
    pallas_call x0 -> x12, Pallas kernels: none -> 56.9 us  [the longest x1 13.6 us: out_project(): pl.pallas_call(out_kernel, grid=(ranks,), in_specs=[pl.BlockSpec((1, coun...]
    all_to_all x0 -> x2, blocking collectives: none -> 50.6 us  [the longest x1 32.3 us: chip_plan(): lax.all_to_all(sent_keys, 'fsdp', split_axis=0, concat_axis=0, tiled=True...]
    ppermute x0 -> x7, waiting for transfers between devices: none -> 40.7 us  [the longest x6 38.7 us: swap(): return lax.ppermute(values, 'fsdp', [(i, i ^ bit) for i in range(ranks)])]
    gather x6 -> x0, local copies, waits for them, and re-layouts: 33.2 us -> none  [the longest x1 13.6 us: on_device(): jnp.take(vocab_table, jnp.clip(local_ids, 0, vocab_rows - 1), axis=0)]
    convert_element_type x7 -> x1, other arithmetic: 32.8 us -> 0.01 us  [rotation_tables(): positions = (jnp.arange(count) % LEN).astype(F32)]
    all_gather x1, waiting for transfers between devices: 36.6 us -> 17.4 us  [chip_plan(): columns = out_project(lax.all_gather(attended, 'fsdp'), out_weight)]
    dot_general x4 -> x0, matrix products: 18.3 us -> none  [the longest x1 7.71 us: on_device(): jnp.dot(normed, joined_weight, preferred_element_type=jnp.float32)]
  transfers between devices with their start and end apart: 4 -> 11, of which waited for: 3 -> 7; matrix products, arithmetic and copies ran while one was open for 18% -> 5% of each run, Pallas kernels for 0% -> 15%
where the time goes in v1:
time: 251 us; the launch traced here: 249 us
  waiting for transfers between devices  88 us (35%)
  Pallas kernels  56.9 us (23%)
  blocking collectives  50.6 us (20%)
  local copies, waits for them, and re-layouts  21.7 us (9%)
  starting transfers between devices  15.5 us (6%)
  between operations  14.3 us (6%)
    ppermute x6, waiting for transfers between devices, swap(): return lax.ppermute(values, 'fsdp', [(i, i ^ bit) for i in range(ranks)])  38.7 us
    all_to_all x1, blocking collectives, chip_plan(): lax.all_to_all(sent_keys, 'fsdp', split_axis=0, concat_axis=0, tiled=True...  32.3 us
    all_to_all x2, waiting for transfers between devices, chip_plan(): lax.all_to_all(join_partials(home, got[part], part * step), 'fsdp', split...  20.7 us
    unnamed x30, local copies, waits for them, and re-layouts  18.2 us
    all_to_all x1, blocking collectives, exchange(): lax.all_to_all(sent, 'fsdp', split_axis=0, concat_axis=0, tiled=True, axi...  18.2 us
    all_gather x1, waiting for transfers between devices, chip_plan(): columns = out_project(lax.all_gather(attended, 'fsdp'), out_weight)  17.4 us
    pallas_call x1, Pallas kernels, out_project(): pl.pallas_call(out_kernel, grid=(ranks,), in_specs=[pl.BlockSpec((1, coun...  13.6 us
    pallas_call x1, Pallas kernels, prepare_out(): pl.pallas_call(out_weight_kernel, grid=(rows // step_rows,), in_specs=[pl...  11.4 us
  transfers between devices with their start and end apart: 11, of which 7 were waited for; matrix products, arithmetic and copies ran while one was open for 5% of the time, Pallas kernels for 15%

profile of v1, /device:TPU:0, one launch (start us, length us, event | category | flops | bytes accessed | tf_op | source)
XLA Modules:
  0.0 249.3 jit_solution(8196698511586461056)
XLA Ops:
  8.0 1.3 copy-done.4
  10.7 8.7 %prepare_weights.1 = (bf16[8,320,640]{2,1,0:T(8,128)(2,1)S(1)}, bf16[8,320,640]{2,1,0:T(8,128)(2,1)}, bf16[8,320,128]{2,1,0:T(8,128)(2,1)S(1)}) custom-call(s32[2]{0:T(128)S(1)} %pad_add_fusion.3.info, s32[8]{0:T(128)S(1)} %copy-done.6, f32[40,64]{1,0:T(8,128)S(1)} %copy-done.5, f32[40,16]{1,0:T(8,128)S(1)} %copy.19.kv_scale, bf16[320,8192]{1,0:T(8,128)(2,1)} %wq.1, ...), custom_call_target="tpu_custom_call" | custom-call | flops 20971520 | bytes 15728640 | tf_op jit(solution)/shard_map/prepare_weights/pallas_call | solution.py:355
  20.8 4.0 %pick_rows.2 = bf16[8,32,640]{2,1,0:T(8,128)(2,1)S(1)} custom-call(s32[1]{0:T(128)} %constant.57.clone.1.base, f32[8,384]{1,0:T(8,128)S(1)} %get-tuple-element.142.rows, f32[1,5120]{1,0:T(1,128)S(1)} %bitcast.48, bf16[600,5120]{1,0:T(8,128)(2,1)S(1)} %copy-done.9), custom_call_target="tpu_custom_call" | custom-call | flops 196608000 | bytes 6144000 | tf_op jit(solution)/shard_map/pick_rows/pallas_call | solution.py:272
  24.7 18.2 %all_to_all.45 = bf16[8,32,640]{2,1,0:T(8,128)(2,1)S(1)} all-to-all(bf16[8,32,640]{2,1,0:T(8,128)(2,1)S(1)} %pick_rows.2), channel_id=1, replica_groups={{0,2,4,6,8,10,12,14},{1,3,5,7,9,11,13,15},{16,18,20,22,24,26,28,30},{17..., dimensions={0} | all-to-all | bytes 655360 | tf_op jit(solution)/shard_map/all_to_all | solution.py:623
  43.0 1.5 collective-permute-start.2
  44.6 2.0 collective-permute-done.2
  47.2 1.3 place_rows.2
  49.1 1.9 copy-done.3
  51.0 4.7 %project.3 = bf16[4,384,640]{2,1,0:T(8,128)(2,1)S(1)} custom-call(s32[2]{0:T(128)S(1)} %pad_add_fusion.4.info, bf16[384,640]{1,0:T(8,128)(2,1)S(1)} %get-tuple-element.56.normed, bf16[8,320,640]{2,1,0:T(8,128)(2,1)S(1)} %copy-done.3, bf16[8,320,640]{2,1,0:T(8,128)(2,1)} %collective-permute-done.3.other), custom_call_target="tpu_custom_call" | custom-call | flops 1258291200 | bytes 5242880 | tf_op jit(solution)/shard_map/project/pallas_call | solution.py:396
  55.9 0.9 collective-permute-start.4
  56.8 6.0 %project.2.own = f32[4,384,640]{2,1,0:T(8,128)} custom-call(s32[2]{0:T(128)S(1)} %pad_add_fusion.1.info, bf16[384,640]{1,0:T(8,128)(2,1)S(1)} %get-tuple-element.56.normed, bf16[8,320,640]{2,1,0:T(8,128)(2,1)S(1)} %copy-done.3, bf16[8,320,640]{2,1,0:T(8,128)(2,1)} %collective-permute-done.3.other), custom_call_target="tpu_custom_call" | custom-call | flops 1258291200 | bytes 5242880 | tf_op jit(solution)/shard_map/project/pallas_call | solution.py:396
  62.8 16.2 %collective-permute-done.4.got = bf16[4,192,640]{2,1,0:T(8,128)(2,1)S(1)} collective-permute-done((bf16[4,192,640]{2,1,0:T(8,128)(2,1)S(1)}, bf16[4,192,640]{2,1,0:T(8,128)(2,1)S(1)}, u32[]{:S(2)}, u32[]{:S(2)}) %collective-permute-start.4) | collective-permute-done | bytes 983072 | tf_op jit(solution)/shard_map/ppermute | solution.py:616
  79.0 2.1 copy-done
  81.1 1.6 join_partials.2
  82.7 3.5 %all-to-all-start.2 = ((bf16[4,192,640]{2,1,0:T(8,128)(2,1)}), bf16[4,192,640]{2,1,0:T(8,128)(2,1)S(1)}, u32[]{:S(2)}, u32[]{:S(2)}) async-start(bf16[4,192,640]{2,1,0:T(8,128)(2,1)} %join_partials.2), calls=%async_computation.2 | async-start | bytes 1966080 | tf_op jit(solution)/shard_map/all_to_all | solution.py:653
  87.1 21.3 %collective-permute-done.5.got = bf16[4,192,640]{2,1,0:T(8,128)(2,1)S(1)} collective-permute-done((bf16[4,192,640]{2,1,0:T(8,128)(2,1)S(1)}, bf16[4,192,640]{2,1,0:T(8,128)(2,1)S(1)}, u32[]{:S(2)}, u32[]{:S(2)}) %collective-permute-start.5) | collective-permute-done | bytes 983072 | tf_op jit(solution)/shard_map/ppermute | solution.py:616
  108.4 2.1 copy-done.1
  110.5 1.6 join_partials.3
  112.0 4.7 %all-to-all-start.3 = ((bf16[4,192,640]{2,1,0:T(8,128)(2,1)}), bf16[4,192,640]{2,1,0:T(8,128)(2,1)S(1)}, u32[]{:S(2)}, u32[]{:S(2)}) async-start(bf16[4,192,640]{2,1,0:T(8,128)(2,1)} %join_partials.3), calls=%async_computation.3 | async-start | bytes 1966080 | tf_op jit(solution)/shard_map/all_to_all | solution.py:653
  117.8 20.7 %all-to-all-done.3 = bf16[4,192,640]{2,1,0:T(8,128)(2,1)S(1)} async-done(((bf16[4,192,640]{2,1,0:T(8,128)(2,1)}), bf16[4,192,640]{2,1,0:T(8,128)(2,1)S(1)}, u32[]{:S(2)}, u32[]{:S(2)}) %all-to-all-start.3) | async-done | bytes 983072 | tf_op jit(solution)/shard_map/all_to_all | solution.py:653
  138.7 1.3 make_heads.1
  140.1 1.3 collective-permute-done.6.other
  141.4 2.2 attend.1
  143.6 32.3 %all_to_all.46 = bf16[8,320,128]{2,1,0:T(8,128)(2,1)S(1)} all-to-all(bf16[8,320,128]{2,1,0:T(8,128)(2,1)S(1)} %get-tuple-element.61), channel_id=1, replica_groups={{0,2,4,6,8,10,12,14},{1,3,5,7,9,11,13,15},{16,18,20,22,24,26,28,30},{17..., dimensions={0} | all-to-all | bytes 1310720 | tf_op jit(solution)/shard_map/all_to_all | solution.py:639
  176.7 8.3 %copy.21.codes = bf16[8192,320]{1,0:T(8,128)(2,1)} copy(bf16[8192,320]{0,1:T(8,128)(2,1)} %param.24) | data formatting | bytes 10485760 | tf_op args[10]
  185.1 11.4 %prepare_out.1.weight = bf16[8192,320]{1,0:T(8,128)(2,1)} custom-call(bf16[8192,320]{1,0:T(8,128)(2,1)} %copy.21.codes, f32[64,320]{1,0:T(8,128)S(1)} %constant_dynamic-slice_fusion.scales), custom_call_target="tpu_custom_call" | custom-call | flops 10485760 | bytes 10485760 | tf_op jit(solution)/shard_map/prepare_out/pallas_call | solution.py:529
  196.4 17.4 %all-gather.3.cloned.1.call-done = bf16[6144,512]{1,0:T(8,128)(2,1)} async-done(((bf16[384,512]{1,0:T(8,128)(2,1)}), bf16[6144,512]{1,0:T(8,128)(2,1)}) %all-gather.3.cloned.1.call-update) | async-done | bytes 6291472 | tf_op jit(solution)/shard_map/all_gather | solution.py:672
  213.8 13.6 %out_project.1 = bf16[384,320]{1,0:T(8,128)(2,1)} custom-call(bf16[16,384,512]{2,1,0:T(8,128)(2,1)} %bitcast.43, bf16[8192,320]{1,0:T(8,128)(2,1)} %prepare_out.1.weight), custom_call_target="tpu_custom_call" | custom-call | flops 2013265920 | bytes 11534336 | tf_op jit(solution)/shard_map/out_project/pallas_call | solution.py:561
  227.4 3.5 %all-to-all-start.4 = ((bf16[16,24,320]{2,1,0:T(8,128)(2,1)}), bf16[16,24,320]{2,1,0:T(8,128)(2,1)S(1)}, u32[]{:S(2)}, u32[]{:S(2)}) async-start(bf16[16,24,320]{2,1,0:T(8,128)(2,1)} %bitcast.16), calls=%async_computation.4 | async-start | bytes 589824 | tf_op jit(solution)/shard_map/all_to_all | solution.py:673
  231.1 1.1 copy.23
  232.3 9.1 %all-to-all-done.4 = bf16[16,24,320]{2,1,0:T(8,128)(2,1)S(1)} async-done(((bf16[16,24,320]{2,1,0:T(8,128)(2,1)}), bf16[16,24,320]{2,1,0:T(8,128)(2,1)S(1)}, u32[]{:S(2)}, u32[]{:S(2)}) %all-to-all-start.4) | async-done | bytes 245792 | tf_op jit(solution)/shard_map/all_to_all | solution.py:673
  241.5 0.9 all_to_all.35
  (57 shorter events, 8.3 us)
Async XLA Ops:
  8.0 1.3 copy-start.4
  9.3 0.7 copy-start.5
  10.1 0.7 copy-start.6
  10.7 9.2 %copy-start.12 = (s32[384]{0:T(512)S(1)}, s32[384]{0:T(512)}, u32[]{:S(2)}) copy-start(s32[384]{0:T(512)} %param.14) | copy-start | bytes 4612
  10.7 10.0 %copy-start.9 = (bf16[600,5120]{1,0:T(8,128)(2,1)S(1)}, bf16[600,5120]{1,0:T(8,128)(2,1)}, u32[]{:S(2)}) copy-start(bf16[600,5120]{1,0:T(8,128)(2,1)} %table.1) | copy-start | bytes 18432004
  10.7 10.0 %copy-start.10 = (f32[5120]{0:T(1024)S(1)}, f32[5120]{0:T(1024)}, u32[]{:S(2)}) copy-start(f32[5120]{0:T(1024)} %param.17) | copy-start | bytes 61444
  19.5 5.3 %copy-start.2 = (bf16[8,320,640]{2,1,0:T(8,128)(2,1)}, bf16[8,320,640]{2,1,0:T(8,128)(2,1)S(1)}, u32[]{:S(2)}) copy-start(bf16[8,320,640]{2,1,0:T(8,128)(2,1)S(1)} %get-tuple-element.57.own) | copy-start | bytes 9830404
  19.5 29.6 %collective-permute-start.3 = (bf16[8,320,640]{2,1,0:T(8,128)(2,1)}, bf16[8,320,640]{2,1,0:T(8,128)(2,1)}, u32[]{:S(2)}, u32[]{:S(2)}) collective-permute-start(bf16[8,320,640]{2,1,0:T(8,128)(2,1)} %get-tuple-element.58), channel_id=1, source_target_pairs={{0,1},{1,0},{2,3},{3,2},{4,5},{5,4},{6,7},{7,6},{8,9},{9,8},{10,11... | collective-permute-start | bytes 9830408 | tf_op jit(solution)/shard_map/ppermute | solution.py:616
  43.0 4.2 %collective-permute-start.1 = (bf16[8,32,640]{2,1,0:T(8,128)(2,1)S(1)}, bf16[8,32,640]{2,1,0:T(8,128)(2,1)S(1)}, u32[]{:S(2)}, u32[]{:S(2)}) collective-permute-start(bf16[8,32,640]{2,1,0:T(8,128)(2,1)S(1)} %all_to_all.45), channel_id=1, source_target_pairs={{0,1},{1,0},{2,3},{3,2},{4,5},{5,4},{6,7},{7,6},{8,9},{9,8},{10,11... | collective-permute-start | bytes 983048 | tf_op jit(solution)/shard_map/ppermute | solution.py:616
  43.0 3.6 %collective-permute-start.2 = (f32[8,128]{1,0:T(8,128)S(1)}, f32[8,128]{1,0:T(8,128)S(1)}, u32[]{:S(2)}, u32[]{:S(2)}) collective-permute-start(f32[8,128]{1,0:T(8,128)S(1)} %get-tuple-element.55), channel_id=1, source_target_pairs={{0,16},{16,0},{1,17},{17,1},{2,18},{18,2},{3,19},{19,3},{4,20},{20... | collective-permute-start | bytes 12296 | tf_op jit(solution)/shard_map/ppermute | solution.py:619
  49.1 1.9 copy-start.3
  55.9 23.1 %collective-permute-start.4 = (bf16[4,192,640]{2,1,0:T(8,128)(2,1)S(1)}, bf16[4,192,640]{2,1,0:T(8,128)(2,1)S(1)}, u32[]{:S(2)}, u32[]{:S(2)}) collective-permute-start(bf16[4,192,640]{2,1,0:T(8,128)(2,1)S(1)} %get-tuple-element.78), channel_id=1, source_target_pairs={{0,2},{1,3},{2,0},{3,1},{4,6},{5,7},{6,4},{7,5},{8,10},{9,11},{10,... | collective-permute-start | bytes 2949128 | tf_op jit(solution)/shard_map/ppermute | solution.py:616
  79.0 2.1 copy-start
  82.7 29.4 %all-to-all-start.2 = ((bf16[4,192,640]{2,1,0:T(8,128)(2,1)}), bf16[4,192,640]{2,1,0:T(8,128)(2,1)S(1)}, u32[]{:S(2)}, u32[]{:S(2)}) async-start(bf16[4,192,640]{2,1,0:T(8,128)(2,1)} %join_partials.2), calls=%async_computation.2 | async-start | bytes 1966080 | tf_op jit(solution)/shard_map/all_to_all | solution.py:653
  86.2 22.2 %collective-permute-start.5 = (bf16[4,192,640]{2,1,0:T(8,128)(2,1)S(1)}, bf16[4,192,640]{2,1,0:T(8,128)(2,1)S(1)}, u32[]{:S(2)}, u32[]{:S(2)}) collective-permute-start(bf16[4,192,640]{2,1,0:T(8,128)(2,1)S(1)} %get-tuple-element.79), channel_id=1, source_target_pairs={{0,2},{1,3},{2,0},{3,1},{4,6},{5,7},{6,4},{7,5},{8,10},{9,11},{10,... | collective-permute-start | bytes 2949128 | tf_op jit(solution)/shard_map/ppermute | solution.py:616
  108.4 2.1 copy-start.1
  112.0 26.4 %all-to-all-start.3 = ((bf16[4,192,640]{2,1,0:T(8,128)(2,1)}), bf16[4,192,640]{2,1,0:T(8,128)(2,1)S(1)}, u32[]{:S(2)}, u32[]{:S(2)}) async-start(bf16[4,192,640]{2,1,0:T(8,128)(2,1)} %join_partials.3), calls=%async_computation.3 | async-start | bytes 1966080 | tf_op jit(solution)/shard_map/all_to_all | solution.py:653
  116.8 97.0 %all-gather.3.cloned.1.call-start = ((), (), s32[]{:S(2)}) async-start(), calls=%async_computation.6 | async-start | bytes 6684672 | tf_op jit(solution)/shard_map/all_gather | solution.py:672
  117.7 20.9 %copy-start.7 = (f32[128]{0:T(128)S(1)}, f32[128]{0:T(128)}, u32[]{:S(2)}) copy-start(f32[128]{0:T(128)} %param.18) | copy-start | bytes 1540
  117.7 20.9 %copy-start.8 = (f32[128]{0:T(128)S(1)}, f32[128]{0:T(128)}, u32[]{:S(2)}) copy-start(f32[128]{0:T(128)} %param.19) | copy-start | bytes 1540
  140.0 36.0 %copy-start.11 = (f32[64,40]{0,1:T(8,128)S(1)}, f32[64,40]{0,1:T(8,128)}, u32[]{:S(2)}) copy-start(f32[64,40]{0,1:T(8,128)} %param.25) | copy-start | bytes 30724
  140.0 1.4 collective-permute-start.6
  176.0 54.9 %collective-permute-start.7 = (bf16[8,320,128]{2,1,0:T(8,128)(2,1)S(1)}, bf16[8,320,128]{2,1,0:T(8,128)(2,1)S(1)}, u32[]{:S(2)}, u32[]{:S(2)}) collective-permute-start(bf16[8,320,128]{2,1,0:T(8,128)(2,1)S(1)} %all_to_all.46), channel_id=1, source_target_pairs={{0,1},{1,0},{2,3},{3,2},{4,5},{5,4},{6,7},{7,6},{8,9},{9,8},{10,11... | collective-permute-start | bytes 1966088 | tf_op jit(solution)/shard_map/ppermute | solution.py:616
  227.4 14.1 %all-to-all-start.4 = ((bf16[16,24,320]{2,1,0:T(8,128)(2,1)}), bf16[16,24,320]{2,1,0:T(8,128)(2,1)S(1)}, u32[]{:S(2)}, u32[]{:S(2)}) async-start(bf16[16,24,320]{2,1,0:T(8,128)(2,1)} %bitcast.16), calls=%async_computation.4 | async-start | bytes 589824 | tf_op jit(solution)/shard_map/all_to_all | solution.py:673
Sparse Core Ops, SparseCore 0:
  143.7 70.0 all-gather.2

commit v2 on v1

v2 whole, which is shorter than its diff:
```python
import functools
import jax
import jax.numpy as jnp
from jax import lax
from jax.experimental import pallas as pl
from jax.experimental.pallas import tpu as pltpu
from jax.sharding import PartitionSpec as P
QUERY_HEADS = 64
KEY_VALUE_HEADS = 8
HEAD_SIZE = 128
TILE_SIDE = 128
LEN = 384


theta_base = 1000000.0
eps_norm = 1e-06


def rms_scale(values, norm_gain):
    mean_square = jnp.mean(values * values, axis=-1, keepdims=True)
    return values * lax.rsqrt(mean_square + eps_norm) * norm_gain


def rotate(values, positions):
    half_width = values.shape[-1] // 2
    frequency = theta_base ** (-jnp.arange(half_width, dtype=jnp.float32) * 2.0 / values.shape[-1])
    angles = positions[:, None] * frequency[None, :]
    cosine = jnp.cos(angles)[:, None, :]
    sine_part = jnp.sin(angles)[:, None, :]
    lower_half = values[..., :half_width]
    upper_half = values[..., half_width:]
    return jnp.concatenate(
        [
            lower_half * cosine - upper_half * sine_part,
            upper_half * cosine + lower_half * sine_part,
        ],
        axis=-1,
    )


def lookup_small(small_table, indices):
    matches = indices[..., None] == jnp.arange(small_table.shape[0], dtype=jnp.int32)
    return jnp.sum(jnp.where(matches, small_table, 0), axis=-1)


def column_scales(tile_scale, first_col, width_cols):
    per_column = jnp.repeat(tile_scale, TILE_SIDE, axis=1)
    picked = lax.dynamic_slice_in_dim(per_column, first_col, width_cols, 1)
    return jnp.repeat(picked, TILE_SIDE, axis=0)


def dequantize(quantized, scales):
    return (quantized.astype(jnp.float32) * scales).astype(jnp.bfloat16)


def attend(queries, key_rows, value_rows, prompt_count):
    token_count, head_count, head_width = queries.shape
    length = token_count // prompt_count
    query_blocks = queries.reshape(prompt_count, length, head_count, head_width)
    key_blocks = key_rows.reshape(prompt_count, length, head_width)
    value_blocks = value_rows.reshape(prompt_count, length, -1)
    scores = jnp.einsum(
        "plhd,pmd->phlm", query_blocks, key_blocks, preferred_element_type=jnp.float32
    ) * head_width ** (-0.5)
    causal = jnp.arange(length)[:, None] >= jnp.arange(length)[None, :]
    weights = jnp.where(causal, jnp.exp(scores), 0.0)
    probabilities = (weights / jnp.sum(weights, axis=-1, keepdims=True)).astype(jnp.bfloat16)
    attended_rows = jnp.einsum(
        "phlm,pmd->plhd", probabilities, value_blocks, preferred_element_type=jnp.float32
    )
    return attended_rows.astype(jnp.bfloat16).reshape(
        token_count, head_count * value_blocks.shape[-1]
    )


def general_plan(
    token_ids,
    key_value_of_block,
    vocab_table,
    in_gain,
    q_gain,
    k_gain,
    wq_codes,
    wq_scale,
    key_value_codes,
    key_value_scale,
    wo_codes,
    wo_scale,
):
    count_of_ranks = lax.axis_size("fsdp")
    my_rank = lax.axis_index("fsdp")
    duplicate_count = count_of_ranks // KEY_VALUE_HEADS
    per_key_value = QUERY_HEADS // KEY_VALUE_HEADS
    split_points = max(1, duplicate_count // per_key_value)
    heads_here = max(1, per_key_value // duplicate_count)
    value_columns = HEAD_SIZE // split_points
    query_width = heads_here * HEAD_SIZE
    local_rows = wq_codes.shape[0]
    token_count = token_ids.shape[0]
    targets = jnp.arange(count_of_ranks, dtype=jnp.int32)
    target_head = lookup_small(key_value_of_block, targets // duplicate_count)
    target_slot = targets % duplicate_count
    target_part = target_slot % split_points
    target_query = target_head * per_key_value + target_slot // split_points * heads_here
    my_head = lookup_small(key_value_of_block, my_rank // duplicate_count)
    my_slot = my_rank % duplicate_count
    my_part = my_slot % split_points
    my_query = my_head * per_key_value + my_slot // split_points * heads_here
    vocab_rows = vocab_table.shape[0]
    local_ids = token_ids - my_rank * vocab_rows
    inside = (local_ids >= 0) & (local_ids < vocab_rows)
    picked = jnp.take(vocab_table, jnp.clip(local_ids, 0, vocab_rows - 1), axis=0)
    terms = jnp.where(inside[:, None], picked, jnp.zeros_like(picked)).astype(jnp.float32)
    embedded = lax.psum(terms, "fsdp").astype(jnp.bfloat16)
    normed = rms_scale(embedded.astype(jnp.float32), in_gain).astype(jnp.bfloat16)
    query_groups = wq_codes.reshape(local_rows, QUERY_HEADS // heads_here, query_width)
    query_send = jnp.take(query_groups, target_query // heads_here, axis=1)
    key_value_heads = key_value_codes.reshape(local_rows, KEY_VALUE_HEADS, 2, HEAD_SIZE)
    key_send = jnp.take(key_value_heads[:, :, 0, :], target_head, axis=1)
    grouped_values = key_value_heads[:, :, 1, :].reshape(
        local_rows, KEY_VALUE_HEADS * split_points, value_columns
    )
    value_send = jnp.take(grouped_values, target_head * split_points + target_part, axis=1)
    both_send = jnp.concatenate([key_send, value_send], axis=2)
    query_got, kv_got = (
        lax.all_to_all(query_send, "fsdp", split_axis=1, concat_axis=0, tiled=True),
        lax.all_to_all(both_send, "fsdp", split_axis=1, concat_axis=0, tiled=True),
    )
    key_quant = kv_got[:, 0, :HEAD_SIZE]
    value_quant = kv_got[:, 0, HEAD_SIZE:]
    query_weight = dequantize(
        query_got[:, 0, :], column_scales(wq_scale, my_query * HEAD_SIZE, query_width)
    )
    key_matrix = dequantize(
        key_quant, column_scales(key_value_scale, my_head * 2 * HEAD_SIZE, HEAD_SIZE)
    )
    value_weight = dequantize(
        value_quant,
        column_scales(
            key_value_scale,
            my_head * 2 * HEAD_SIZE + HEAD_SIZE + my_part * value_columns,
            value_columns,
        ),
    )
    joined_weight = jnp.concatenate([query_weight, key_matrix, value_weight], axis=1)
    projected = jnp.dot(normed, joined_weight, preferred_element_type=jnp.float32)
    positions = (jnp.arange(token_count) % LEN).astype(jnp.float32)
    queries = rotate(
        rms_scale(projected[:, :query_width].reshape(token_count, heads_here, HEAD_SIZE), q_gain),
        positions,
    ).astype(jnp.bfloat16)
    keys_raw = projected[:, query_width : query_width + HEAD_SIZE].reshape(
        token_count, 1, HEAD_SIZE
    )
    key_rows = rotate(rms_scale(keys_raw, k_gain), positions).astype(jnp.bfloat16)[:, 0, :]
    value_rows = projected[:, query_width + HEAD_SIZE :].astype(jnp.bfloat16)
    attended_rows = attend(queries, key_rows, value_rows, token_count // LEN)
    cols_here = wo_codes.shape[1]
    local_weight = dequantize(wo_codes, column_scales(wo_scale, my_rank * cols_here, cols_here))
    ordered = jnp.take(
        local_weight.reshape(KEY_VALUE_HEADS, per_key_value * HEAD_SIZE, cols_here),
        key_value_of_block,
        axis=0,
    ).reshape(QUERY_HEADS * HEAD_SIZE, cols_here)
    columns = jnp.dot(
        lax.all_gather(attended_rows, "fsdp", axis=1, tiled=True),
        ordered,
        preferred_element_type=jnp.float32,
    )
    attn_out = lax.all_to_all(
        columns.astype(jnp.bfloat16), "fsdp", split_axis=0, concat_axis=1, tiled=True
    )
    return (attn_out, key_matrix.reshape(1, key_matrix.shape[0], HEAD_SIZE))


BF = jnp.bfloat16
F32 = jnp.float32
SLOTS = 32
GROUP_ROWS = 64
PARAMS = pltpu.CompilerParams(vmem_limit_bytes=48 << 20)
SMEM = pl.BlockSpec(memory_space=pltpu.SMEM)


COST_SHARE = 1


def cost(flops, bytes_accessed):
    return pl.CostEstimate(
        flops=flops // COST_SHARE, bytes_accessed=bytes_accessed // COST_SHARE, transcendentals=0
    )


def owner_of(ids, vocab_rows, ranks):
    owner = jnp.zeros_like(ids)
    for rank in range(1, ranks):
        owner = owner + jnp.where(ids >= float(rank * vocab_rows), 1.0, 0.0)
    return owner


def iota(shape, axis):
    return lax.broadcasted_iota(jnp.int32, shape, axis).astype(F32)


def slot_kernel(ranks, vocab_rows, info, id_row, col_out, row_out, most_out):
    count = id_row.shape[1]
    ids_r = id_row[...].astype(F32)
    ids_c = jnp.transpose(jnp.broadcast_to(ids_r, (128, count)))[:, 0:1]
    at_r, at_c = iota((count, count), 0), iota((count, count), 1)
    same = ids_c == ids_r
    first_c = jnp.min(jnp.where(same, at_c, float(count)), axis=1, keepdims=True)
    first_r = jnp.min(jnp.where(same, at_r, float(count)), axis=0, keepdims=True)
    is_first_r = first_r == iota((1, count), 1)
    is_first_c = first_c == iota((count, 1), 0)
    owner_c, owner_r = owner_of(ids_c, vocab_rows, ranks), owner_of(ids_r, vocab_rows, ranks)
    peers = owner_c == owner_r
    slot_c = jnp.sum(
        jnp.where(peers & is_first_r & (at_c < first_c), 1.0, 0.0), axis=1, keepdims=True
    )
    slot_r = jnp.sum(
        jnp.where(peers & is_first_c & (at_r < first_r), 1.0, 0.0), axis=0, keepdims=True
    )
    lane = lax.broadcasted_iota(jnp.int32, (count, 128), 1)
    col_out[...] = jnp.where(lane == 0, owner_c, jnp.where(lane == 1, slot_c, 0.0))
    me = info[0].astype(F32)
    mine = is_first_r & (owner_r == me)
    row_out[...] = jnp.zeros_like(row_out)
    row_out[0:1, :] = jnp.where(mine, slot_r, -1.0)
    row_out[1:2, :] = ids_r - me * float(vocab_rows)
    most_out[...] = jnp.broadcast_to(jnp.max(slot_r, axis=1, keepdims=True) + 1.0, (8, 128))


def find_slots(token_ids, my_rank, ranks, vocab_rows):
    count = token_ids.shape[0]
    return pl.pallas_call(
        functools.partial(slot_kernel, ranks, vocab_rows),
        out_shape=(
            jax.ShapeDtypeStruct((count, 128), F32),
            jax.ShapeDtypeStruct((8, count), F32),
            jax.ShapeDtypeStruct((8, 128), F32),
        ),
        in_specs=[SMEM, pl.BlockSpec(memory_space=pltpu.VMEM)],
        compiler_params=PARAMS,
        cost_estimate=cost(1000000, 1000000),
        name="find_slots",
    )(my_rank.reshape(1), token_ids.reshape(1, count))


def pick_kernel(width, info, rows, gain, table, *refs):
    out, picked, total = refs
    step = pl.program_id(0)
    slots = picked.shape[0]
    vocab_rows = table.shape[0]
    wanted = lax.broadcasted_iota(jnp.int32, (slots, 1), 0).astype(F32) + info[0].astype(F32)
    chosen = wanted == rows[0:1, :]
    index = jnp.sum(jnp.where(chosen, rows[1:2, :], 0.0), axis=1, keepdims=True)
    valid = jnp.sum(jnp.where(chosen, 1.0, 0.0), axis=1, keepdims=True)
    hot = (iota((slots, vocab_rows), 1) == index) & (valid > 0.5)
    block = jnp.dot(hot.astype(F32).astype(BF), table[...], preferred_element_type=F32)
    picked[:, pl.ds(pl.multiple_of(step * width, width), width)] = block

    @pl.when(step == 0)
    def _():
        total[...] = jnp.zeros_like(total)

    total[...] += jnp.sum(block * block, axis=1, keepdims=True)

    @pl.when(step == pl.num_programs(0) - 1)
    def _():
        features = picked.shape[1]
        chips, _, chip_width = out.shape
        inverse = lax.rsqrt(total[:, 0:1] * (1.0 / features) + eps_norm)
        for chip in range(chips):
            span = slice(chip * chip_width, (chip + 1) * chip_width)
            out[chip] = (picked[:, span] * inverse * gain[:, span]).astype(BF)


def pick_rows(rows, base, in_gain, vocab_table, chips):
    vocab_rows, features = vocab_table.shape
    steps = 4
    width, chip_width = features // steps, features // chips
    return pl.pallas_call(
        functools.partial(pick_kernel, width),
        grid=(steps,),
        out_shape=jax.ShapeDtypeStruct((chips, SLOTS, chip_width), BF),
        in_specs=[
            SMEM,
            pl.BlockSpec(rows.shape, lambda i: (0, 0)),
            pl.BlockSpec((1, features), lambda i: (0, 0)),
            pl.BlockSpec((vocab_rows, width), lambda i: (0, i)),
        ],
        out_specs=pl.BlockSpec((chips, SLOTS, chip_width), lambda i: (0, 0, 0)),
        scratch_shapes=[pltpu.VMEM((SLOTS, features), F32), pltpu.VMEM((SLOTS, 128), F32)],
        compiler_params=PARAMS,
        cost_estimate=cost(2 * SLOTS * vocab_rows * features, 2 * vocab_rows * features),
        name="pick_rows",
    )(base.reshape(1), rows, in_gain.reshape(1, features), vocab_table)


def place_kernel(chips, info, owners, own, other, out):
    count = owners.shape[0]
    core, base = info[0], info[1].astype(F32)
    owner, slot = owners[:, 0:1].astype(jnp.int32), owners[:, 1:2] - base
    fits = (slot >= 0.0) & (slot < float(SLOTS))
    position = (owner >> 1) * SLOTS + slot.astype(jnp.int32)
    hit = (lax.broadcasted_iota(jnp.int32, (count, chips * SLOTS), 1) == position) & fits
    total = jnp.zeros(out.shape, F32)
    for side, received in enumerate((own, other)):
        hot = jnp.where(hit & ((owner & 1) == (core ^ side)), 1.0, 0.0).astype(BF)
        total = total + jnp.dot(hot, received[...], preferred_element_type=F32)
    out[...] = total.astype(BF)


def place_rows(owners, base, core, own, other):
    count = owners.shape[0]
    chips, _, width = own.shape
    vmem = pl.BlockSpec(memory_space=pltpu.VMEM)
    return pl.pallas_call(
        functools.partial(place_kernel, chips),
        out_shape=jax.ShapeDtypeStruct((count, width), BF),
        in_specs=[SMEM, vmem, vmem, vmem],
        compiler_params=PARAMS,
        cost_estimate=cost(4 * count * chips * SLOTS * width, 6 * chips * SLOTS * width),
        name="place_rows",
    )(
        jnp.stack([core, base]),
        owners,
        own.reshape(chips * SLOTS, width),
        other.reshape(chips * SLOTS, width),
    )


def weight_kernel(
    info, order, head_of, wq_scale, kv_scale, wq, kv, kv_key, own, first, second, key_out
):
    step = pl.program_id(0)
    block, key_head = order[step], head_of[step]
    core, rank = info[0], info[1]
    rows = wq.shape[0]
    half = wq.shape[1] // 2
    tiles = half // TILE_SIDE

    def fill(target, side):
        for group in range(rows // GROUP_ROWS):
            tile_row = (rank * (rows // GROUP_ROWS) + group) // 2
            span = slice(group * GROUP_ROWS, (group + 1) * GROUP_ROWS)
            for tile in range(tiles):
                scale = wq_scale[tile_row, (2 * block + side) * tiles + tile]
                start = pl.multiple_of(side * half + tile * TILE_SIDE, TILE_SIDE)
                codes = wq[span, pl.ds(start, TILE_SIDE)].astype(F32)
                target[0, span, tile * TILE_SIDE : (tile + 1) * TILE_SIDE] = (codes * scale).astype(BF)
            scale = kv_scale[tile_row, 2 * block + side]
            start = pl.multiple_of(side * TILE_SIDE, TILE_SIDE)
            codes = kv[span, pl.ds(start, TILE_SIDE)].astype(F32)
            target[0, span, half : half + TILE_SIDE] = (codes * scale).astype(BF)

    fill(own, core)

    @pl.when(step < pl.num_programs(0) // 2)
    def _():
        fill(first, 1 - core)

    @pl.when(step >= pl.num_programs(0) // 2)
    def _():
        fill(second, 1 - core)

    for group in range(rows // GROUP_ROWS):
        tile_row = (rank * (rows // GROUP_ROWS) + group) // 2
        span = slice(group * GROUP_ROWS, (group + 1) * GROUP_ROWS)
        scale = kv_scale[tile_row, 2 * key_head]
        key_out[0, span, :] = (kv_key[span, :].astype(F32) * scale).astype(BF)


def prepare_weights(core, my_rank, order, key_value_of_block, wq_codes, wq_scale, kv_codes, kv_scale):
    chips = order.shape[0]
    rows = wq_codes.shape[0]
    half = wq_codes.shape[1] // (2 * chips)
    middle = chips // 2
    block = (1, rows, half + TILE_SIDE)
    return pl.pallas_call(
        weight_kernel,
        grid_spec=pltpu.PrefetchScalarGridSpec(
            num_scalar_prefetch=5,
            grid=(chips,),
            in_specs=[
                pl.BlockSpec((rows, 2 * half), lambda i, info, order, *_: (0, order[i])),
                pl.BlockSpec((rows, 2 * TILE_SIDE), lambda i, info, order, *_: (0, order[i])),
                pl.BlockSpec(
                    (rows, TILE_SIDE), lambda i, info, order, head_of, *_: (0, 2 * head_of[i])
                ),
            ],
            out_specs=[
                pl.BlockSpec(block, lambda i, *_: (i, 0, 0)),
                pl.BlockSpec(block, lambda i, *_: (jnp.minimum(i, middle - 1), 0, 0)),
                pl.BlockSpec(block, lambda i, *_: (jnp.maximum(i - middle, 0), 0, 0)),
                pl.BlockSpec((1, rows, TILE_SIDE), lambda i, *_: (i, 0, 0)),
            ],
        ),
        out_shape=[
            jax.ShapeDtypeStruct((chips, *block[1:]), BF),
            jax.ShapeDtypeStruct((middle, *block[1:]), BF),
            jax.ShapeDtypeStruct((middle, *block[1:]), BF),
            jax.ShapeDtypeStruct((chips, rows, TILE_SIDE), BF),
        ],
        compiler_params=PARAMS,
        cost_estimate=cost(rows * wq_codes.shape[1] * 8, rows * wq_codes.shape[1] * 6),
        name="prepare_weights",
    )(
        jnp.stack([core, my_rank]),
        order,
        key_value_of_block,
        wq_scale,
        kv_scale,
        wq_codes,
        kv_codes,
        kv_codes,
    )


def project_kernel(info, normed, own, other, *refs):
    *outs, weight = refs
    rows = own.shape[1]
    core = info[0]
    weight[pl.ds(pl.multiple_of(core * rows, GROUP_ROWS), rows), :] = own[0]
    weight[pl.ds(pl.multiple_of((1 - core) * rows, GROUP_ROWS), rows), :] = other[0]
    product = jnp.dot(normed[...], weight[...], preferred_element_type=F32)
    start = 0
    for out in outs:
        out[0] = product[start : start + out.shape[1]].astype(out.dtype)
        start += out.shape[1]


def project(core, normed, own, first, other, out_type):
    count, width = normed.shape
    blocks, rows, columns = other.shape
    return pl.pallas_call(
        project_kernel,
        grid=(blocks,),
        in_specs=[
            SMEM,
            pl.BlockSpec((count, width), lambda k: (0, 0)),
            pl.BlockSpec((1, rows, columns), lambda k: (first + k, 0, 0)),
            pl.BlockSpec((1, rows, columns), lambda k: (k, 0, 0)),
        ],
        out_specs=[pl.BlockSpec((1, part, columns), lambda k: (k, 0, 0)) for part in PART_ROWS],
        scratch_shapes=[pltpu.VMEM((width, columns), BF)],
        out_shape=[jax.ShapeDtypeStruct((blocks, part, columns), out_type) for part in PART_ROWS],
        compiler_params=PARAMS,
        cost_estimate=cost(
            2 * blocks * count * width * columns, 2 * blocks * columns * (width + count)
        ),
        name="project",
    )(core.reshape(1), normed, own, other)


def join_kernel(own, got, kept, *sent):
    kept[...] = own[0] + got[0].astype(F32)
    for block, out in enumerate(sent):
        out[...] = (own[block + 1] + got[block + 1].astype(F32)).astype(BF)


def join_partials(own, got):
    blocks, rows, columns = got.shape
    vmem = pl.BlockSpec(memory_space=pltpu.VMEM)
    return pl.pallas_call(
        join_kernel,
        in_specs=[vmem, vmem],
        out_shape=[jax.ShapeDtypeStruct((rows, columns), F32)]
        + [jax.ShapeDtypeStruct((rows, columns), BF)] * (blocks - 1),
        compiler_params=PARAMS,
        cost_estimate=cost(2 * blocks * rows * columns, 8 * blocks * rows * columns),
        name="join_partials",
    )(own, got)


def turn(values, cosine, sine):
    return values * cosine + pltpu.roll(values, HEAD_SIZE // 2, 1) * sine


def normalise(values, gain):
    mean_square = jnp.mean(values * values, axis=-1, keepdims=True)
    return values * lax.rsqrt(mean_square + eps_norm) * gain


def heads_kernel(start, info, *refs):
    *parts, q_gain, k_gain, cosine, sine, q_out, kv_out = refs
    total = parts[0][...]
    for part in parts[1:]:
        total = total + part[...].astype(F32)
    heads, count, _ = q_out.shape
    cos, sin = cosine[start : start + count, :], sine[start : start + count, :]
    last = total[:, heads * HEAD_SIZE :]

    @pl.when(info[0] == 0)
    def _():
        kv_out[...] = turn(normalise(last, k_gain[...]), cos, sin).astype(BF)

    @pl.when(info[0] == 1)
    def _():
        kv_out[...] = last.astype(BF)

    for head in range(heads):
        values = total[:, head * HEAD_SIZE : (head + 1) * HEAD_SIZE]
        q_out[head] = turn(normalise(values, q_gain[...]), cos, sin).astype(BF)


def make_heads(core, parts, start, q_gain, k_gain, cosine, sine):
    count, columns = parts[0].shape
    heads = columns // HEAD_SIZE - 1
    vmem = pl.BlockSpec(memory_space=pltpu.VMEM)
    return pl.pallas_call(
        functools.partial(heads_kernel, start),
        out_shape=(
            jax.ShapeDtypeStruct((heads, count, HEAD_SIZE), BF),
            jax.ShapeDtypeStruct((count, HEAD_SIZE), BF),
        ),
        in_specs=[SMEM] + [vmem] * (len(parts) + 4),
        compiler_params=PARAMS,
        cost_estimate=cost(20 * count * columns, 14 * count * columns),
        name="make_heads",
    )(core.reshape(1), *parts, q_gain.reshape(1, -1), k_gain.reshape(1, -1), cosine, sine)


def attend_kernel(length, start, share, info, queries, *refs):
    *rows, kept, sent = refs
    parts = len(rows) // 2
    own = jnp.concatenate([ref[...] for ref in rows[:parts]], axis=0)
    other = jnp.concatenate([ref[...] for ref in rows[parts:]], axis=0)
    first = info[0] == 0
    keys, values = jnp.where(first, own, other), jnp.where(first, other, own)
    count = queries.shape[1]
    here = lax.broadcasted_iota(jnp.int32, (count, keys.shape[0]), 0) + start
    there = lax.broadcasted_iota(jnp.int32, (count, keys.shape[0]), 1)
    allowed = here >= there
    for prompt in range(1, (start + count + length - 1) // length):
        allowed = allowed & ((here < prompt * length) | (there >= prompt * length))
    for head in range(queries.shape[0]):
        scores = lax.dot_general(
            queries[head], keys, (((1,), (1,)), ((), ())), preferred_element_type=F32
        ) * HEAD_SIZE ** (-0.5)
        weights = jnp.where(allowed, jnp.exp(scores), 0.0)
        probabilities = (weights / jnp.sum(weights, axis=-1, keepdims=True)).astype(BF)
        result = jnp.dot(probabilities, values, preferred_element_type=F32)
        shares = [result[at : at + share] for at in range(0, count, share)]
        even = jnp.concatenate(shares[0::2], axis=0)
        odd = jnp.concatenate(shares[1::2], axis=0)
        span = slice(head * HEAD_SIZE, (head + 1) * HEAD_SIZE)
        kept[:, span] = jnp.where(first, even, odd).astype(BF)
        sent[:, span] = jnp.where(first, odd, even).astype(BF)


def attend_heads(core, queries, start, own, other, share):
    heads, count, width = queries.shape
    vmem = pl.BlockSpec(memory_space=pltpu.VMEM)
    return pl.pallas_call(
        functools.partial(attend_kernel, LEN, start, share),
        out_shape=[jax.ShapeDtypeStruct((count // 2, heads * width), BF)] * 2,
        in_specs=[SMEM] + [vmem] * (1 + len(own) + len(other)),
        compiler_params=PARAMS,
        cost_estimate=cost(4 * heads * count * (start + count) * width, 4 * heads * count * width),
        name="attend",
    )(core.reshape(1), queries, *own, *other)


def out_weight_kernel(info, scales, codes, out):
    step, rank = pl.program_id(0), info[0]
    blocks, rows, width = out.shape
    tiles = width // TILE_SIDE
    for group in range(rows // GROUP_ROWS):
        span = slice(group * GROUP_ROWS, (group + 1) * GROUP_ROWS)
        column = (rank * rows + group * GROUP_ROWS) // TILE_SIDE
        for tile in range(blocks * tiles):
            codes_here = codes[span, tile * TILE_SIDE : (tile + 1) * TILE_SIDE].astype(F32)
            lanes = slice(tile % tiles * TILE_SIDE, (tile % tiles + 1) * TILE_SIDE)
            scale = scales[step * blocks * tiles + tile, column]
            out[tile // tiles, span, lanes] = (codes_here * scale).astype(BF)


def prepare_out(rank, wo_rows, wo_scale, width):
    columns, rows = wo_rows.shape
    blocks = 4
    return pl.pallas_call(
        out_weight_kernel,
        grid_spec=pltpu.PrefetchScalarGridSpec(
            num_scalar_prefetch=2,
            grid=(rows // width // blocks,),
            in_specs=[pl.BlockSpec((columns, blocks * width), lambda i, *_: (0, i))],
            out_specs=pl.BlockSpec((blocks, columns, width), lambda i, *_: (i, 0, 0)),
        ),
        out_shape=jax.ShapeDtypeStruct((rows // width, columns, width), BF),
        compiler_params=PARAMS,
        cost_estimate=cost(4 * rows * columns, 4 * rows * columns),
        name="prepare_out",
    )(rank.reshape(1), wo_scale, wo_rows)


def out_kernel(blocks, has_start, last, info, *refs):
    attended = refs[:blocks]
    weights = refs[blocks : blocks + 2]
    out, held, arrived = refs[-3:]
    core = info[0]
    columns, width = held.shape[2:]
    halves = [(block, half) for block in range(blocks) for half in range(2)]
    copies = []
    for number, (block, half) in enumerate(halves):
        rank = 2 * info[1 + block] + (core ^ half)
        for side in range(2):
            copy = pltpu.make_async_copy(
                weights[side].at[rank], held.at[number, side], arrived.at[number, side]
            )
            copy.start()
            copies.append(copy)
    totals = [None, None]
    for number, (block, half) in enumerate(halves):
        rows = attended[block][:, half * width : (half + 1) * width]
        for side in range(2):
            copies[2 * number + side].wait()
            term = lax.dot_general(
                held[number, side], rows, (((1,), (1,)), ((), ())), preferred_element_type=F32
            )
            totals[side] = term if totals[side] is None else totals[side] + term
    if has_start:
        start = refs[blocks + 2]
        totals = [total + start[side] for side, total in enumerate(totals)]
    if last:
        first = core == 0
        both = jnp.concatenate(
            [jnp.where(first, totals[0], totals[1]), jnp.where(first, totals[1], totals[0])], axis=0
        )
        out[...] = both.T.astype(out.dtype)
    else:
        for side in range(2):
            out[side] = totals[side]


def out_project(core, attended, chips_of, weights, start, last):
    count, both = attended[0].shape
    blocks = len(attended)
    _, columns, width = weights[0].shape
    vmem = pl.BlockSpec(memory_space=pltpu.VMEM)
    extra = [] if start is None else [start]
    shape = (count, 2 * columns) if last else (2, columns, count)
    return pl.pallas_call(
        functools.partial(out_kernel, blocks, bool(extra), last),
        out_shape=jax.ShapeDtypeStruct(shape, BF if last else F32),
        in_specs=[SMEM]
        + [vmem] * blocks
        + [pl.BlockSpec(memory_space=pl.ANY)] * 2
        + [vmem] * len(extra),
        scratch_shapes=[
            pltpu.VMEM((2 * blocks, 2, columns, width), BF),
            pltpu.SemaphoreType.DMA((2 * blocks, 2)),
        ],
        compiler_params=PARAMS,
        cost_estimate=cost(4 * blocks * count * both * columns, 4 * blocks * both * columns),
        name="out_project",
    )(jnp.concatenate([core.reshape(1), chips_of]), *attended, *weights, *extra)


def rotation_tables(count):
    half_width = HEAD_SIZE // 2
    positions = (jnp.arange(count) % LEN).astype(F32)
    frequency = theta_base ** (-jnp.arange(half_width, dtype=F32) * 2.0 / HEAD_SIZE)
    angles = positions[:, None] * frequency[None, :]
    cosine, sine = jnp.cos(angles), jnp.sin(angles)
    return jnp.concatenate([cosine, cosine], axis=1), jnp.concatenate([-sine, sine], axis=1)


Z_COUNT = 4
PART_ROWS = (192, 192)
SPLIT_GATHER = False


def after(values, *earlier):
    return lax.optimization_barrier((values, *earlier))[0]


def chip_plan(
    token_ids,
    key_value_of_block,
    vocab_table,
    in_gain,
    q_gain,
    k_gain,
    wq_codes,
    wq_scale,
    key_value_codes,
    key_value_scale,
    wo_codes,
    wo_scale,
):
    ranks = lax.axis_size("fsdp")
    chips = ranks // 2
    y_count = chips // Z_COUNT
    my_rank = lax.axis_index("fsdp").astype(jnp.int32)
    core, chip = my_rank % 2, my_rank // 2
    count = token_ids.shape[0]
    vocab_rows = vocab_table.shape[0]
    same_core = [[2 * chip + side for chip in range(chips)] for side in range(2)]

    def swap(values, bits):
        return lax.ppermute(values, "fsdp", [(i, i ^ bits) for i in range(ranks)])

    def swap_groups(values):
        return lax.ppermute(values, "groups", [(0, 1), (1, 0)])

    def to_chips(values):
        return lax.all_to_all(
            values, "fsdp", split_axis=0, concat_axis=0, tiled=True, axis_index_groups=same_core
        )

    def exchange(sent):
        own = to_chips(sent)
        return own, swap(own, 1)

    owners, rows, most = find_slots(token_ids, my_rank, ranks, vocab_rows)
    sent = pick_rows(rows, jnp.int32(0), in_gain, vocab_table, chips)
    most = jnp.maximum(most, swap_groups(after(most, sent)))[0, 0]
    own, other = exchange(sent)
    normed = place_rows(owners, jnp.int32(0), core, own, other)

    def one_more(state):
        base, total = state
        more = exchange(pick_rows(rows, base, in_gain, vocab_table, chips))
        return base + SLOTS, total + place_rows(owners, base, core, *more)

    _, normed = lax.while_loop(
        lambda state: state[0].astype(F32) < most, one_more, (jnp.int32(SLOTS), normed)
    )

    near = jnp.arange(Z_COUNT, dtype=jnp.int32) * y_count
    order = after(chip, sent) ^ jnp.concatenate([near ^ 1, near])
    own_weight, away_weight, home_weight, sent_keys = prepare_weights(
        core, my_rank, order, key_value_of_block, wq_codes, wq_scale, key_value_codes, key_value_scale
    )
    away_weight = swap(after(away_weight, own), 1)
    home_weight = swap(after(home_weight, own), 1)

    half = sent_keys.shape[1] // 2
    group = lax.axis_index("groups")
    my_half = lax.dynamic_slice_in_dim(sent_keys, group * half, half, 1)
    my_z = chip // y_count

    def keys_for(z):
        return lax.dynamic_slice_in_dim(my_half, z * y_count, y_count, 0)

    by_z = [keys_for(my_z)] + [swap(keys_for(my_z ^ k), 2 * y_count * k) for k in range(1, Z_COUNT)]

    away = project(core, normed, own_weight, 0, away_weight, BF)
    got = [swap(part, 2) for part in away]
    home = project(after(core, *away), normed, own_weight, Z_COUNT, home_weight, F32)
    got[0], *by_z = lax.optimization_barrier((got[0], *by_z))

    cosine, sine = rotation_tables(count)
    heads_width = wq_codes.shape[1] // ranks
    own_kv, other_kv, held = [], [], []
    start, share = 0, count // ranks
    for part, part_rows in enumerate(PART_ROWS):
        kept, *sums = join_partials(home[part], got[part])
        sums = [swap(value, 4 * (k + 1)) for k, value in enumerate(sums)]
        queries, kv = make_heads(core, [kept, *sums], start, q_gain, k_gain, cosine, sine)
        own_kv.append(kv)
        other_kv.append(swap(kv, 1))
        kept, sent_rows = attend_heads(core, queries, start, own_kv, other_kv, share)
        held.append(jnp.concatenate([kept, swap(sent_rows, 1)], axis=1))
        start += part_rows
    wo_rows = wo_codes.T
    out_weights = [
        prepare_out(rank, codes, wo_scale, heads_width)
        for rank, codes in ((my_rank, wo_rows), (my_rank ^ 1, swap(wo_rows, 1)))
    ]

    by_z = jnp.stack(by_z)
    my_y = chip % y_count
    here = lax.dynamic_index_in_dim(by_z, my_y, 1, keepdims=False)
    there = swap(lax.dynamic_index_in_dim(by_z, 1 - my_y, 1, keepdims=False), 2)
    own_keys = jnp.stack([here, there], axis=1).reshape(chips, half, HEAD_SIZE)
    far_keys = swap_groups(own_keys)
    own_keys = (own_keys, far_keys)
    synced = collect_keys(
        jnp.stack([core, group, chip]), [*own_keys, *(swap(value, 1) for value in own_keys)]
    )

    if not SPLIT_GATHER:
        held = [jnp.concatenate(held, axis=0)]
    columns = []
    for block in held:
        blocks = gather_chips(block, chips, y_count)
        total = None
        for chosen in ((0, 1, 2, 3), (4, 6), (5, 7)):
            total = out_project(
                core,
                [blocks[bits] for bits in chosen],
                chip ^ jnp.array(chosen, jnp.int32),
                out_weights,
                total,
                chosen == (5, 7),
            )
        columns.append(total)
    columns = to_chips(jnp.concatenate(columns, axis=0).reshape(chips, share, -1))
    attn_out = jnp.transpose(columns, (1, 0, 2)).reshape(share, -1)
    return attn_out, synced


def collect_kernel(info, own, far, other, other_far, out):
    core, group = info[0], info[1]
    out[0, core, group] = own[0]
    out[0, core, 1 - group] = far[0]
    out[0, 1 - core, group] = other[0]
    out[0, 1 - core, 1 - group] = other_far[0]


def collect_keys(info, parts):
    chips, half, width = parts[0].shape
    part = pl.BlockSpec((1, half, width), lambda i, info: (i ^ info[2], 0, 0))
    out = pl.pallas_call(
        collect_kernel,
        grid_spec=pltpu.PrefetchScalarGridSpec(
            num_scalar_prefetch=1,
            grid=(chips,),
            in_specs=[part] * 4,
            out_specs=pl.BlockSpec((1, 2, 2, half, width), lambda i, info: (i, 0, 0, 0, 0)),
        ),
        out_shape=jax.ShapeDtypeStruct((chips, 2, 2, half, width), BF),
        compiler_params=PARAMS,
        cost_estimate=cost(0, 16 * chips * half * width),
        name="collect_keys",
    )(info, *parts)
    return out.reshape(1, -1, width)


def gather_chips(block, chips, y_count):
    ranks = 2 * chips
    along = 2 * y_count

    def swap(values, bits):
        return lax.ppermute(values, "fsdp", [(i, i ^ bits) for i in range(ranks)])

    def hop(values, pairs):
        return lax.ppermute(
            values,
            "fsdp",
            [(a * along + rest, b * along + rest) for a, b in pairs for rest in range(along)],
        )

    middle, outward = [(1, 2), (2, 1)], [(1, 0), (2, 3)]
    z_index = lax.axis_index("fsdp") // along
    at_end = (z_index == 0) | (z_index == Z_COUNT - 1)
    across = swap(block, 2)
    one = swap(block, along)
    inner = hop(block, middle)
    two_end = hop(inner, outward)
    two_inner = hop(one, middle)
    one_across = swap(one, 2)
    two = jnp.where(at_end, two_end, two_inner)
    three_end = hop(two, outward)
    two_across = swap(two, 2)
    three = jnp.where(at_end, three_end, inner)
    three_across = swap(three, 2)
    return {
        0: block,
        1: across,
        2: one,
        3: one_across,
        4: two,
        5: two_across,
        6: three,
        7: three_across,
    }


def solution(mesh):
    sizes = dict(mesh.shape)
    small = sizes["fsdp"] == 2 * KEY_VALUE_HEADS and sizes["groups"] == 2
    return jax.shard_map(
        chip_plan if small else general_plan,
        mesh=mesh,
        in_specs=(
            P("groups"),
            P(),
            P("fsdp", None),
            P(),
            P(),
            P(),
            P("fsdp", None),
            P(),
            P("fsdp", None),
            P(),
            P(None, "fsdp"),
            P(),
        ),
        out_specs=(P(("groups", "fsdp"), None), P(("groups", "fsdp"), None, None)),
        check_vma=False,
    )
```

time: 251 us -> 214 us (0.85)
  blocking collectives: 50.6 us -> 0 us
  starting transfers between devices: 15.5 us -> 62.2 us
  between operations: 14.3 us -> 1.12 us
  waiting for transfers between devices: 88 us -> 75.7 us
  local copies, waits for them, and re-layouts: 21.7 us -> 11 us
  Pallas kernels: 56.9 us -> 59.5 us
    all_to_all x2 -> x0, blocking collectives: 50.6 us -> none  [the longest x1 32.3 us: chip_plan(): lax.all_to_all(sent_keys, 'fsdp', split_axis=0, concat_axis=0, tiled=True...]
    ppermute x7 -> x33, starting transfers between devices: 3.78 us -> 48.9 us  [the longest x27 41.7 us: swap(): return lax.ppermute(values, 'fsdp', [(i, i ^ bits) for i in range(ranks)])]
    ppermute x7 -> x33, waiting for transfers between devices: 40.7 us -> 75.1 us  [the longest x27 56.1 us: swap(): return lax.ppermute(values, 'fsdp', [(i, i ^ bits) for i in range(ranks)])]
    all_to_all x3 -> x2, waiting for transfers between devices: 29.9 us -> 0.59 us  [to_chips(): lax.all_to_all(values, 'fsdp', split_axis=0, concat_axis=0, tiled=True, a...]
    all_gather x1 -> x0, waiting for transfers between devices: 17.4 us -> none  [chip_plan(): columns = out_project(lax.all_gather(attended, 'fsdp'), out_weight)]
    unnamed x30 -> x36, local copies, waits for them, and re-layouts: 18.2 us -> 8.93 us
    pallas_call x9 -> x15, Pallas kernels: 46.2 us -> 49 us  [the longest x3 13.6 us: out_project(): pl.pallas_call(functools.partial(out_kernel, blocks, bool(extra), last),...]
    all_to_all x3 -> x2, starting transfers between devices: 11.8 us -> 13.3 us  [to_chips(): lax.all_to_all(values, 'fsdp', split_axis=0, concat_axis=0, tiled=True, a...]
  transfers between devices with their start and end apart: 11 -> 35, of which waited for: 7 -> 16; matrix products, arithmetic and copies ran while one was open for 5% -> 2% of each run, Pallas kernels for 15% -> 25%
where the time goes in v2:
time: 214 us; the launch traced here: 213 us
  waiting for transfers between devices  75.7 us (35%)
  starting transfers between devices  62.2 us (29%)
  Pallas kernels  59.5 us (28%)
  local copies, waits for them, and re-layouts  11 us (5%)
  other arithmetic  2.62 us (1%)
    ppermute x27, waiting for transfers between devices, swap(): return lax.ppermute(values, 'fsdp', [(i, i ^ bits) for i in range(ranks)])  56.1 us
    ppermute x27, starting transfers between devices, swap(): return lax.ppermute(values, 'fsdp', [(i, i ^ bits) for i in range(ranks)])  41.7 us
    ppermute x4, waiting for transfers between devices, hop(): lax.ppermute(values, 'fsdp', [(a * along + rest, b * along + rest) for a,...  17.2 us
    pallas_call x3, Pallas kernels, out_project(): pl.pallas_call(functools.partial(out_kernel, blocks, bool(extra), last),...  13.6 us
    all_to_all x2, starting transfers between devices, to_chips(): lax.all_to_all(values, 'fsdp', split_axis=0, concat_axis=0, tiled=True, a...  13.3 us
    pallas_call x2, Pallas kernels, project(): pl.pallas_call(project_kernel, grid=(blocks,), in_specs=[SMEM, pl.BlockSp...  9.75 us
    pallas_call x2, Pallas kernels, prepare_out(): pl.pallas_call(out_weight_kernel, grid_spec=pltpu.PrefetchScalarGridSpec(...  9.61 us
    unnamed x36, local copies, waits for them, and re-layouts  8.93 us
  transfers between devices with their start and end apart: 35, of which 16 were waited for; matrix products, arithmetic and copies ran while one was open for 2% of the time, Pallas kernels for 25%

profile of v2, /device:TPU:0, one launch (start us, length us, event | category | flops | bytes accessed | tf_op | source)
XLA Modules:
  0.0 212.8 jit_solution(15329456896461081412)
XLA Ops:
  2.1 5.3 %pick_rows.2 = bf16[8,32,640]{2,1,0:T(8,128)(2,1)} custom-call(s32[1]{0:T(128)} %constant.154.clone.1.info, f32[8,384]{1,0:T(8,128)S(1)} %get-tuple-element.206.rows, f32[1,5120]{1,0:T(1,128)} %bitcast.56, bf16[600,5120]{1,0:T(8,128)(2,1)} %table.1), custom_call_target="tpu_custom_call" | custom-call | flops 196608000 | bytes 6144000 | tf_op jit(solution)/shard_map/pick_rows/pallas_call | solution.py:281
  7.5 7.3 %all-to-all-start.1 = ((bf16[8,32,640]{2,1,0:T(8,128)(2,1)}), bf16[8,32,640]{2,1,0:T(8,128)(2,1)S(1)}, u32[]{:S(2)}, u32[]{:S(2)}) async-start(bf16[8,32,640]{2,1,0:T(8,128)(2,1)} %pick_rows.2), calls=%async_computation.1 | async-start | bytes 655360 | tf_op jit(solution)/shard_map/all_to_all | solution.py:707
  15.0 8.5 %prepare_weights.1 = (bf16[8,320,640]{2,1,0:T(8,128)(2,1)}, bf16[4,320,640]{2,1,0:T(8,128)(2,1)S(1)}, bf16[4,320,640]{2,1,0:T(8,128)(2,1)S(1)}, bf16[8,320,128]{2,1,0:T(8,128)(2,1)S(1)}) custom-call(s32[2]{0:T(128)S(1)} %pad_add_fusion.3.info, s32[8]{0:T(128)S(1)} %add_xor_fusion.order, s32[8]{0:T(128)S(1)} %copy-done.8, f32[40,64]{1,0:T(8,128)S(1)} %copy-done.5, ...), custom_call_target="tpu_custom_call" | custom-call | flops 20971520 | bytes 15728640 | tf_op jit(solution)/shard_map/prepare_weights/pallas_call | solution.py:379
  29.0 1.8 collective-permute-done.2
  34.3 5.5 %project.2 = (bf16[4,192,640]{2,1,0:T(8,128)(2,1)}, bf16[4,192,640]{2,1,0:T(8,128)(2,1)}) custom-call(s32[1]{0:T(128)} %bitcast.5.info, bf16[384,640]{1,0:T(8,128)(2,1)} %copy-done.11, bf16[8,320,640]{2,1,0:T(8,128)(2,1)} %get-tuple-element.88.own, bf16[4,320,640]{2,1,0:T(8,128)(2,1)} %collective-permute-done.3.other), custom_call_target="tpu_custom_call" | custom-call | flops 1258291200 | bytes 5242880 | tf_op jit(solution)/shard_map/project/pallas_call | solution.py:435
  39.8 2.0 collective-permute-start.5
  42.0 2.0 collective-permute-start.6
  44.0 2.5 %collective-permute-done.6 = bf16[2,160,128]{2,1,0:T(8,128)(2,1)S(1)} collective-permute-done((bf16[2,160,128]{2,1,0:T(8,128)(2,1)S(1)}, bf16[2,160,128]{2,1,0:T(8,128)(2,1)S(1)}, u32[]{:S(2)}, u32[]{:S(2)}) %collective-permute-start.6) | collective-permute-done | bytes 81952 | tf_op jit(solution)/shard_map/ppermute | solution.py:701
  46.5 2.9 %collective-permute-start.7 = (bf16[2,160,128]{2,1,0:T(8,128)(2,1)S(1)}, bf16[2,160,128]{2,1,0:T(8,128)(2,1)S(1)}, u32[]{:S(2)}, u32[]{:S(2)}) collective-permute-start(bf16[2,160,128]{2,1,0:T(8,128)(2,1)S(1)} %get-tuple-element.137), channel_id=1, source_target_pairs={{0,8},{1,9},{2,10},{3,11},{4,12},{5,13},{6,14},{7,15},{8,0},{9,1},... | collective-permute-start | bytes 245768 | tf_op jit(solution)/shard_map/ppermute | solution.py:701
  50.9 4.2 %project.3 = (f32[4,192,640]{2,1,0:T(8,128)S(1)}, f32[4,192,640]{2,1,0:T(8,128)S(1)}) custom-call(s32[1]{0:T(128)} %bitcast.11.info, bf16[384,640]{1,0:T(8,128)(2,1)} %copy-done.11, bf16[8,320,640]{2,1,0:T(8,128)(2,1)} %get-tuple-element.88.own, bf16[4,320,640]{2,1,0:T(8,128)(2,1)S(1)} %collective-permute-done.4.other), custom_call_target="tpu_custom_call" | custom-call | flops 1258291200 | bytes 5242880 | tf_op jit(solution)/shard_map/project/pallas_call | solution.py:435
  55.7 9.0 %collective-permute-done.5.got = bf16[4,192,640]{2,1,0:T(8,128)(2,1)} collective-permute-done((bf16[4,192,640]{2,1,0:T(8,128)(2,1)}, bf16[4,192,640]{2,1,0:T(8,128)(2,1)}, u32[]{:S(2)}, u32[]{:S(2)}) %collective-permute-start.5) | collective-permute-done | bytes 983072 | tf_op jit(solution)/shard_map/ppermute | solution.py:701
  66.1 2.1 collective-permute-start.9
  68.2 2.4 %collective-permute-start.10 = (bf16[192,640]{1,0:T(8,128)(2,1)S(1)}, bf16[192,640]{1,0:T(8,128)(2,1)S(1)}, u32[]{:S(2)}, u32[]{:S(2)}) collective-permute-start(bf16[192,640]{1,0:T(8,128)(2,1)S(1)} %get-tuple-element.101), channel_id=1, source_target_pairs={{0,8},{1,9},{2,10},{3,11},{4,12},{5,13},{6,14},{7,15},{8,0},{9,1},... | collective-permute-start | bytes 737288 | tf_op jit(solution)/shard_map/ppermute | solution.py:701
  70.6 14.6 %collective-permute-done.14.got = bf16[4,192,640]{2,1,0:T(8,128)(2,1)S(1)} collective-permute-done((bf16[4,192,640]{2,1,0:T(8,128)(2,1)}, bf16[4,192,640]{2,1,0:T(8,128)(2,1)S(1)}, u32[]{:S(2)}, u32[]{:S(2)}) %collective-permute-start.14) | collective-permute-done | bytes 983072 | tf_op jit(solution)/shard_map/ppermute | solution.py:701
  85.4 1.8 collective-permute-start.15
  87.2 2.4 %collective-permute-start.16 = (bf16[192,640]{1,0:T(8,128)(2,1)S(1)}, bf16[192,640]{1,0:T(8,128)(2,1)S(1)}, u32[]{:S(2)}, u32[]{:S(2)}) collective-permute-start(bf16[192,640]{1,0:T(8,128)(2,1)S(1)} %get-tuple-element.110), channel_id=1, source_target_pairs={{0,8},{1,9},{2,10},{3,11},{4,12},{5,13},{6,14},{7,15},{8,0},{9,1},... | collective-permute-start | bytes 737288 | tf_op jit(solution)/shard_map/ppermute | solution.py:701
  89.9 3.5 %collective-permute-start.11 = (bf16[192,640]{1,0:T(8,128)(2,1)S(1)}, bf16[192,640]{1,0:T(8,128)(2,1)S(1)}, u32[]{:S(2)}, u32[]{:S(2)}) collective-permute-start(bf16[192,640]{1,0:T(8,128)(2,1)S(1)} %get-tuple-element.102), channel_id=1, source_target_pairs={{0,12},{1,13},{2,14},{3,15},{4,8},{5,9},{6,10},{7,11},{8,4},{9,5},... | collective-permute-start | bytes 737288 | tf_op jit(solution)/shard_map/ppermute | solution.py:701
  94.4 16.3 %collective-permute-done.11.refs_3_ = bf16[192,640]{1,0:T(8,128)(2,1)S(1)} collective-permute-done((bf16[192,640]{1,0:T(8,128)(2,1)S(1)}, bf16[192,640]{1,0:T(8,128)(2,1)S(1)}, u32[]{:S(2)}, u32[]{:S(2)}) %collective-permute-start.11) | collective-permute-done | bytes 245792 | tf_op jit(solution)/shard_map/ppermute | solution.py:701
  119.4 13.1 %collective-permute-start.22 = (bf16[192,1024]{1,0:T(8,128)(2,1)S(1)}, bf16[192,1024]{1,0:T(8,128)(2,1)S(1)}, u32[]{:S(2)}, u32[]{:S(2)}) collective-permute-start(bf16[192,1024]{1,0:T(8,128)(2,1)S(1)} %maximum_maximum_fusion.refs_0_), channel_id=1, source_target_pairs={{0,4},{1,5},{2,6},{3,7},{4,0},{5,1},{6,2},{7,3},{8,12},{9,13},{10,... | collective-permute-start | bytes 1179656 | tf_op jit(solution)/shard_map/ppermute | solution.py:836
  133.8 7.9 %collective-permute-done.22.refs_2_ = bf16[192,1024]{1,0:T(8,128)(2,1)S(1)} collective-permute-done((bf16[192,1024]{1,0:T(8,128)(2,1)S(1)}, bf16[192,1024]{1,0:T(8,128)(2,1)S(1)}, u32[]{:S(2)}, u32[]{:S(2)}) %collective-permute-start.22) | collective-permute-done | bytes 393248 | tf_op jit(solution)/shard_map/ppermute | solution.py:836
  142.5 9.6 %collective-permute-done.21 = bf16[192,1024]{1,0:T(8,128)(2,1)S(1)} collective-permute-done((bf16[192,1024]{1,0:T(8,128)(2,1)S(1)}, bf16[192,1024]{1,0:T(8,128)(2,1)S(1)}, u32[]{:S(2)}, u32[]{:S(2)}) %collective-permute-start.21) | collective-permute-done | bytes 393248 | tf_op jit(solution)/shard_map/ppermute | solution.py:839
  157.4 7.5 %collective-permute-done.25 = bf16[192,1024]{1,0:T(8,128)(2,1)} collective-permute-done((bf16[192,1024]{1,0:T(8,128)(2,1)S(1)}, bf16[192,1024]{1,0:T(8,128)(2,1)}, u32[]{:S(2)}, u32[]{:S(2)}) %collective-permute-start.25) | collective-permute-done | bytes 393248 | tf_op jit(solution)/shard_map/ppermute | solution.py:839
  168.2 1.6 collective-permute-start.31
  169.9 4.8 %prepare_out.2.refs_4_.refs_2_ = bf16[16,320,512]{2,1,0:T(8,128)(2,1)S(1)} custom-call(s32[1]{0:T(128)} %bitcast.6.info, f32[64,40]{1,0:T(8,128)S(1)} %copy.18.scales, bf16[320,8192]{1,0:T(8,128)(2,1)} %bitcast.53), custom_call_target="tpu_custom_call" | custom-call | flops 10485760 | bytes 10485760 | tf_op jit(solution)/shard_map/prepare_out/pallas_call | solution.py:581
  174.7 2.4 %copy-done = bf16[16,320,512]{2,1,0:T(8,128)(2,1)} copy-done((bf16[16,320,512]{2,1,0:T(8,128)(2,1)}, bf16[16,320,512]{2,1,0:T(8,128)(2,1)S(1)}, u32[]{:S(2)}) %copy-start) | copy-done | bytes 5242904
  177.1 4.8 %prepare_out.3.refs_5_.refs_3_ = bf16[16,320,512]{2,1,0:T(8,128)(2,1)S(1)} custom-call(s32[1]{0:T(128)} %bitcast.15.info, f32[64,40]{1,0:T(8,128)S(1)} %copy.18.scales, bf16[320,8192]{1,0:T(8,128)(2,1)} %collective-permute-done.27.codes), custom_call_target="tpu_custom_call" | custom-call | flops 10485760 | bytes 10485760 | tf_op jit(solution)/shard_map/prepare_out/pallas_call | solution.py:581
  181.9 2.3 %copy-done.1 = bf16[16,320,512]{2,1,0:T(8,128)(2,1)} copy-done((bf16[16,320,512]{2,1,0:T(8,128)(2,1)}, bf16[16,320,512]{2,1,0:T(8,128)(2,1)S(1)}, u32[]{:S(2)}) %copy-start.1) | copy-done | bytes 5242904
  184.3 5.5 %out_project.3.refs_4_ = f32[2,320,192]{2,1,0:T(8,128)S(1)} custom-call(s32[5]{0:T(128)S(1)} %pad_add_fusion.5.info, bf16[192,1024]{1,0:T(8,128)(2,1)S(1)} %maximum_maximum_fusion.refs_0_, bf16[192,1024]{1,0:T(8,128)(2,1)S(1)} %collective-permute-done.28.refs_1_, bf16[192,1024]{1,0:T(8,128)(2,1)S(1)} %collective-permute-done.22.refs_2_, ...), custom_call_target="tpu_custom_call" | custom-call | flops 1006632960 | bytes 5242880 | tf_op jit(solution)/shard_map/out_project/pallas_call | solution.py:642
  189.8 3.7 %out_project.4.refs_4_ = f32[2,320,192]{2,1,0:T(8,128)S(1)} custom-call(s32[3]{0:T(128)S(1)} %get-tuple-element.146.info, bf16[192,1024]{1,0:T(8,128)(2,1)S(1)} %broadcast_select_fusion.1.refs_0_, bf16[192,1024]{1,0:T(8,128)(2,1)S(1)} %broadcast_select_fusion.refs_1_, bf16[16,320,512]{2,1,0:T(8,128)(2,1)} %copy-done, bf16[16,320,512]{2,1,0:T(8,128)(2,1)} %copy-done.1, ...), custom_call_target="tpu_custom_call" | custom-call | flops 503316480 | bytes 2621440 | tf_op jit(solution)/shard_map/out_project/pallas_call | solution.py:642
  193.5 4.5 %out_project.5 = bf16[192,640]{1,0:T(8,128)(2,1)} custom-call(s32[3]{0:T(128)S(1)} %get-tuple-element.145.info, bf16[192,1024]{1,0:T(8,128)(2,1)S(1)} %collective-permute-done.24.refs_0_, bf16[192,1024]{1,0:T(8,128)(2,1)S(1)} %collective-permute-done.26.refs_1_, bf16[16,320,512]{2,1,0:T(8,128)(2,1)} %copy-done, bf16[16,320,512]{2,1,0:T(8,128)(2,1)} %copy-done.1, ...), custom_call_target="tpu_custom_call" | custom-call | flops 503316480 | bytes 2621440 | tf_op jit(solution)/shard_map/out_project/pallas_call | solution.py:642
  197.9 6.1 %all-to-all-start.2 = ((bf16[8,24,640]{2,1,0:T(8,128)(2,1)}), bf16[8,24,640]{2,1,0:T(8,128)(2,1)S(1)}, u32[]{:S(2)}, u32[]{:S(2)}) async-start(bf16[8,24,640]{2,1,0:T(8,128)(2,1)} %bitcast.16), calls=%async_computation.2 | async-start | bytes 491520 | tf_op jit(solution)/shard_map/all_to_all | solution.py:707
  206.3 5.2 %collect_keys.1 = bf16[8,2,2,160,128]{4,3,2,1,0:T(8,128)(2,1)} custom-call(s32[3]{0:T(128)S(1)} %pad_add_fusion.6.info, bf16[8,160,128]{2,1,0:T(8,128)(2,1)S(1)} %bitcast.46, bf16[8,160,128]{2,1,0:T(8,128)(2,1)} %collective-permute-done.31.far, bf16[8,160,128]{2,1,0:T(8,128)(2,1)S(1)} %collective-permute-done.32.other, ...), custom_call_target="tpu_custom_call" | custom-call | bytes 2621440 | tf_op jit(solution)/shard_map/collect_keys/pallas_call | solution.py:815
  (118 shorter events, 38.6 us)
Async XLA Ops:
  7.5 19.3 %all-to-all-start.1 = ((bf16[8,32,640]{2,1,0:T(8,128)(2,1)}), bf16[8,32,640]{2,1,0:T(8,128)(2,1)S(1)}, u32[]{:S(2)}, u32[]{:S(2)}) async-start(bf16[8,32,640]{2,1,0:T(8,128)(2,1)} %pick_rows.2), calls=%async_computation.1 | async-start | bytes 655360 | tf_op jit(solution)/shard_map/all_to_all | solution.py:707
  26.7 6.8 %collective-permute-start.3 = (bf16[4,320,640]{2,1,0:T(8,128)(2,1)}, bf16[4,320,640]{2,1,0:T(8,128)(2,1)}, u32[]{:S(2)}, u32[]{:S(2)}) collective-permute-start(bf16[4,320,640]{2,1,0:T(8,128)(2,1)} %copy-done.10), channel_id=1, source_target_pairs={{0,1},{1,0},{2,3},{3,2},{4,5},{5,4},{6,7},{7,6},{8,9},{9,8},{10,11... | collective-permute-start | bytes 4915208 | tf_op jit(solution)/shard_map/ppermute | solution.py:701
  26.7 141.4 %collective-permute-start.27 = (bf16[320,8192]{1,0:T(8,128)(2,1)}, bf16[320,8192]{1,0:T(8,128)(2,1)}, u32[]{:S(2)}, u32[]{:S(2)}) collective-permute-start(bf16[320,8192]{1,0:T(8,128)(2,1)} %bitcast.52), channel_id=1, source_target_pairs={{0,1},{1,0},{2,3},{3,2},{4,5},{5,4},{6,7},{7,6},{8,9},{9,8},{10,11... | collective-permute-start | bytes 15728648 | tf_op jit(solution)/shard_map/ppermute | solution.py:701
  27.2 4.4 %collective-permute-start.1 = (bf16[8,32,640]{2,1,0:T(8,128)(2,1)S(1)}, bf16[8,32,640]{2,1,0:T(8,128)(2,1)S(1)}, u32[]{:S(2)}, u32[]{:S(2)}) collective-permute-start(bf16[8,32,640]{2,1,0:T(8,128)(2,1)S(1)} %all-to-all-done.1), channel_id=1, source_target_pairs={{0,1},{1,0},{2,3},{3,2},{4,5},{5,4},{6,7},{7,6},{8,9},{9,8},{10,11... | collective-permute-start | bytes 983048 | tf_op jit(solution)/shard_map/ppermute | solution.py:701
  27.2 3.6 %collective-permute-start.2 = (f32[8,128]{1,0:T(8,128)S(1)}, f32[8,128]{1,0:T(8,128)S(1)}, u32[]{:S(2)}, u32[]{:S(2)}) collective-permute-start(f32[8,128]{1,0:T(8,128)S(1)} %get-tuple-element.85), channel_id=1, source_target_pairs={{0,16},{16,0},{1,17},{17,1},{2,18},{18,2},{3,19},{19,3},{4,20},{20... | collective-permute-start | bytes 12296 | tf_op jit(solution)/shard_map/ppermute | solution.py:704
  28.7 20.7 %collective-permute-start.4 = (bf16[4,320,640]{2,1,0:T(8,128)(2,1)}, bf16[4,320,640]{2,1,0:T(8,128)(2,1)S(1)}, u32[]{:S(2)}, u32[]{:S(2)}) collective-permute-start(bf16[4,320,640]{2,1,0:T(8,128)(2,1)} %copy-done.9), channel_id=1, source_target_pairs={{0,1},{1,0},{2,3},{3,2},{4,5},{5,4},{6,7},{7,6},{8,9},{9,8},{10,11... | collective-permute-start | bytes 4915208 | tf_op jit(solution)/shard_map/ppermute | solution.py:701
  39.8 24.9 %collective-permute-start.5 = (bf16[4,192,640]{2,1,0:T(8,128)(2,1)}, bf16[4,192,640]{2,1,0:T(8,128)(2,1)}, u32[]{:S(2)}, u32[]{:S(2)}) collective-permute-start(bf16[4,192,640]{2,1,0:T(8,128)(2,1)} %get-tuple-element.91), channel_id=1, source_target_pairs={{0,2},{1,3},{2,0},{3,1},{4,6},{5,7},{6,4},{7,5},{8,10},{9,11},{10,... | collective-permute-start | bytes 2949128 | tf_op jit(solution)/shard_map/ppermute | solution.py:701
  41.9 43.3 %collective-permute-start.14 = (bf16[4,192,640]{2,1,0:T(8,128)(2,1)}, bf16[4,192,640]{2,1,0:T(8,128)(2,1)S(1)}, u32[]{:S(2)}, u32[]{:S(2)}) collective-permute-start(bf16[4,192,640]{2,1,0:T(8,128)(2,1)} %get-tuple-element.92), channel_id=1, source_target_pairs={{0,2},{1,3},{2,0},{3,1},{4,6},{5,7},{6,4},{7,5},{8,10},{9,11},{10,... | collective-permute-start | bytes 2949128 | tf_op jit(solution)/shard_map/ppermute | solution.py:701
  42.0 4.5 %collective-permute-start.6 = (bf16[2,160,128]{2,1,0:T(8,128)(2,1)S(1)}, bf16[2,160,128]{2,1,0:T(8,128)(2,1)S(1)}, u32[]{:S(2)}, u32[]{:S(2)}) collective-permute-start(bf16[2,160,128]{2,1,0:T(8,128)(2,1)S(1)} %get-tuple-element.138), channel_id=1, source_target_pairs={{0,4},{1,5},{2,6},{3,7},{4,0},{5,1},{6,2},{7,3},{8,12},{9,13},{10,... | collective-permute-start | bytes 245768 | tf_op jit(solution)/shard_map/ppermute | solution.py:701
  46.5 8.6 %collective-permute-start.7 = (bf16[2,160,128]{2,1,0:T(8,128)(2,1)S(1)}, bf16[2,160,128]{2,1,0:T(8,128)(2,1)S(1)}, u32[]{:S(2)}, u32[]{:S(2)}) collective-permute-start(bf16[2,160,128]{2,1,0:T(8,128)(2,1)S(1)} %get-tuple-element.137), channel_id=1, source_target_pairs={{0,8},{1,9},{2,10},{3,11},{4,12},{5,13},{6,14},{7,15},{8,0},{9,1},... | collective-permute-start | bytes 245768 | tf_op jit(solution)/shard_map/ppermute | solution.py:701
  49.4 6.3 %collective-permute-start.8 = (bf16[2,160,128]{2,1,0:T(8,128)(2,1)S(1)}, bf16[2,160,128]{2,1,0:T(8,128)(2,1)S(1)}, u32[]{:S(2)}, u32[]{:S(2)}) collective-permute-start(bf16[2,160,128]{2,1,0:T(8,128)(2,1)S(1)} %get-tuple-element.136), channel_id=1, source_target_pairs={{0,12},{1,13},{2,14},{3,15},{4,8},{5,9},{6,10},{7,11},{8,4},{9,5},... | collective-permute-start | bytes 245768 | tf_op jit(solution)/shard_map/ppermute | solution.py:701
  66.1 23.5 %collective-permute-start.9 = (bf16[192,640]{1,0:T(8,128)(2,1)S(1)}, bf16[192,640]{1,0:T(8,128)(2,1)S(1)}, u32[]{:S(2)}, u32[]{:S(2)}) collective-permute-start(bf16[192,640]{1,0:T(8,128)(2,1)S(1)} %get-tuple-element.100), channel_id=1, source_target_pairs={{0,4},{1,5},{2,6},{3,7},{4,0},{5,1},{6,2},{7,3},{8,12},{9,13},{10,... | collective-permute-start | bytes 737288 | tf_op jit(solution)/shard_map/ppermute | solution.py:701
  68.2 21.7 %collective-permute-start.10 = (bf16[192,640]{1,0:T(8,128)(2,1)S(1)}, bf16[192,640]{1,0:T(8,128)(2,1)S(1)}, u32[]{:S(2)}, u32[]{:S(2)}) collective-permute-start(bf16[192,640]{1,0:T(8,128)(2,1)S(1)} %get-tuple-element.101), channel_id=1, source_target_pairs={{0,8},{1,9},{2,10},{3,11},{4,12},{5,13},{6,14},{7,15},{8,0},{9,1},... | collective-permute-start | bytes 737288 | tf_op jit(solution)/shard_map/ppermute | solution.py:701
  85.4 26.2 %collective-permute-start.15 = (bf16[192,640]{1,0:T(8,128)(2,1)S(1)}, bf16[192,640]{1,0:T(8,128)(2,1)S(1)}, u32[]{:S(2)}, u32[]{:S(2)}) collective-permute-start(bf16[192,640]{1,0:T(8,128)(2,1)S(1)} %get-tuple-element.109), channel_id=1, source_target_pairs={{0,4},{1,5},{2,6},{3,7},{4,0},{5,1},{6,2},{7,3},{8,12},{9,13},{10,... | collective-permute-start | bytes 737288 | tf_op jit(solution)/shard_map/ppermute | solution.py:701
  87.2 25.6 %collective-permute-start.16 = (bf16[192,640]{1,0:T(8,128)(2,1)S(1)}, bf16[192,640]{1,0:T(8,128)(2,1)S(1)}, u32[]{:S(2)}, u32[]{:S(2)}) collective-permute-start(bf16[192,640]{1,0:T(8,128)(2,1)S(1)} %get-tuple-element.110), channel_id=1, source_target_pairs={{0,8},{1,9},{2,10},{3,11},{4,12},{5,13},{6,14},{7,15},{8,0},{9,1},... | collective-permute-start | bytes 737288 | tf_op jit(solution)/shard_map/ppermute | solution.py:701
  89.6 23.2 %collective-permute-start.17 = (bf16[192,640]{1,0:T(8,128)(2,1)S(1)}, bf16[192,640]{1,0:T(8,128)(2,1)S(1)}, u32[]{:S(2)}, u32[]{:S(2)}) collective-permute-start(bf16[192,640]{1,0:T(8,128)(2,1)S(1)} %get-tuple-element.111), channel_id=1, source_target_pairs={{0,12},{1,13},{2,14},{3,15},{4,8},{5,9},{6,10},{7,11},{8,4},{9,5},... | collective-permute-start | bytes 737288 | tf_op jit(solution)/shard_map/ppermute | solution.py:701
  89.9 20.8 %collective-permute-start.11 = (bf16[192,640]{1,0:T(8,128)(2,1)S(1)}, bf16[192,640]{1,0:T(8,128)(2,1)S(1)}, u32[]{:S(2)}, u32[]{:S(2)}) collective-permute-start(bf16[192,640]{1,0:T(8,128)(2,1)S(1)} %get-tuple-element.102), channel_id=1, source_target_pairs={{0,12},{1,13},{2,14},{3,15},{4,8},{5,9},{6,10},{7,11},{8,4},{9,5},... | collective-permute-start | bytes 737288 | tf_op jit(solution)/shard_map/ppermute | solution.py:701
  111.6 2.3 %collective-permute-start.12 = (bf16[192,128]{1,0:T(8,128)(2,1)S(1)}, bf16[192,128]{1,0:T(8,128)(2,1)S(1)}, u32[]{:S(2)}, u32[]{:S(2)}) collective-permute-start(bf16[192,128]{1,0:T(8,128)(2,1)S(1)} %get-tuple-element.104.refs_0_), channel_id=1, source_target_pairs={{0,1},{1,0},{2,3},{3,2},{4,5},{5,4},{6,7},{7,6},{8,9},{9,8},{10,11... | collective-permute-start | bytes 147464 | tf_op jit(solution)/shard_map/ppermute | solution.py:701
  118.8 13.8 %collective-permute-start.20 = (bf16[192,1024]{1,0:T(8,128)(2,1)S(1)}, bf16[192,1024]{1,0:T(8,128)(2,1)S(1)}, u32[]{:S(2)}, u32[]{:S(2)}) collective-permute-start(bf16[192,1024]{1,0:T(8,128)(2,1)S(1)} %maximum_maximum_fusion.refs_0_), channel_id=1, source_target_pairs={{4,8},{5,9},{6,10},{7,11},{8,4},{9,5},{10,6},{11,7},{20,24},{21,25... | collective-permute-start | bytes 1179656 | tf_op jit(solution)/shard_map/ppermute | solution.py:839
  119.4 22.3 %collective-permute-start.22 = (bf16[192,1024]{1,0:T(8,128)(2,1)S(1)}, bf16[192,1024]{1,0:T(8,128)(2,1)S(1)}, u32[]{:S(2)}, u32[]{:S(2)}) collective-permute-start(bf16[192,1024]{1,0:T(8,128)(2,1)S(1)} %maximum_maximum_fusion.refs_0_), channel_id=1, source_target_pairs={{0,4},{1,5},{2,6},{3,7},{4,0},{5,1},{6,2},{7,3},{8,12},{9,13},{10,... | collective-permute-start | bytes 1179656 | tf_op jit(solution)/shard_map/ppermute | solution.py:836
  132.5 19.6 %collective-permute-start.21 = (bf16[192,1024]{1,0:T(8,128)(2,1)S(1)}, bf16[192,1024]{1,0:T(8,128)(2,1)S(1)}, u32[]{:S(2)}, u32[]{:S(2)}) collective-permute-start(bf16[192,1024]{1,0:T(8,128)(2,1)S(1)} %collective-permute-done.20), channel_id=1, source_target_pairs={{4,0},{5,1},{6,2},{7,3},{8,12},{9,13},{10,14},{11,15},{20,16},{21,... | collective-permute-start | bytes 1179656 | tf_op jit(solution)/shard_map/ppermute | solution.py:839
  141.7 10.4 %collective-permute-start.23 = (bf16[192,1024]{1,0:T(8,128)(2,1)S(1)}, bf16[192,1024]{1,0:T(8,128)(2,1)S(1)}, u32[]{:S(2)}, u32[]{:S(2)}) collective-permute-start(bf16[192,1024]{1,0:T(8,128)(2,1)S(1)} %collective-permute-done.22.refs_2_), channel_id=1, source_target_pairs={{4,8},{5,9},{6,10},{7,11},{8,4},{9,5},{10,6},{11,7},{20,24},{21,25... | collective-permute-start | bytes 1179656 | tf_op jit(solution)/shard_map/ppermute | solution.py:839
  152.2 12.8 %collective-permute-start.25 = (bf16[192,1024]{1,0:T(8,128)(2,1)S(1)}, bf16[192,1024]{1,0:T(8,128)(2,1)}, u32[]{:S(2)}, u32[]{:S(2)}) collective-permute-start(bf16[192,1024]{1,0:T(8,128)(2,1)S(1)} %broadcast_select_fusion.1.refs_0_), channel_id=1, source_target_pairs={{4,0},{5,1},{6,2},{7,3},{8,12},{9,13},{10,14},{11,15},{20,16},{21,... | collective-permute-start | bytes 1179656 | tf_op jit(solution)/shard_map/ppermute | solution.py:839
  153.9 13.7 %collective-permute-start.30 = (bf16[4,160,128]{2,1,0:T(8,128)(2,1)S(1)}, bf16[4,160,128]{2,1,0:T(8,128)(2,1)S(1)}, u32[]{:S(2)}, u32[]{:S(2)}) collective-permute-start(bf16[4,160,128]{2,1,0:T(8,128)(2,1)S(1)} %get-tuple-element.141), channel_id=1, source_target_pairs={{0,2},{1,3},{2,0},{3,1},{4,6},{5,7},{6,4},{7,5},{8,10},{9,11},{10,... | collective-permute-start | bytes 491528 | tf_op jit(solution)/shard_map/ppermute | solution.py:701
  155.4 28.9 %collective-permute-start.28 = (bf16[192,1024]{1,0:T(8,128)(2,1)S(1)}, bf16[192,1024]{1,0:T(8,128)(2,1)S(1)}, u32[]{:S(2)}, u32[]{:S(2)}) collective-permute-start(bf16[192,1024]{1,0:T(8,128)(2,1)S(1)} %maximum_maximum_fusion.refs_0_), channel_id=1, source_target_pairs={{0,2},{1,3},{2,0},{3,1},{4,6},{5,7},{6,4},{7,5},{8,10},{9,11},{10,... | collective-permute-start | bytes 1179656 | tf_op jit(solution)/shard_map/ppermute | solution.py:836
  155.9 28.3 %collective-permute-start.29 = (bf16[192,1024]{1,0:T(8,128)(2,1)S(1)}, bf16[192,1024]{1,0:T(8,128)(2,1)S(1)}, u32[]{:S(2)}, u32[]{:S(2)}) collective-permute-start(bf16[192,1024]{1,0:T(8,128)(2,1)S(1)} %collective-permute-done.22.refs_2_), channel_id=1, source_target_pairs={{0,2},{1,3},{2,0},{3,1},{4,6},{5,7},{6,4},{7,5},{8,10},{9,11},{10,... | collective-permute-start | bytes 1179656 | tf_op jit(solution)/shard_map/ppermute | solution.py:836
  165.0 28.5 %collective-permute-start.24 = (bf16[192,1024]{1,0:T(8,128)(2,1)S(1)}, bf16[192,1024]{1,0:T(8,128)(2,1)S(1)}, u32[]{:S(2)}, u32[]{:S(2)}) collective-permute-start(bf16[192,1024]{1,0:T(8,128)(2,1)S(1)} %broadcast_select_fusion.1.refs_0_), channel_id=1, source_target_pairs={{0,2},{1,3},{2,0},{3,1},{4,6},{5,7},{6,4},{7,5},{8,10},{9,11},{10,... | collective-permute-start | bytes 1179656 | tf_op jit(solution)/shard_map/ppermute | solution.py:836
  167.5 25.9 %collective-permute-start.26 = (bf16[192,1024]{1,0:T(8,128)(2,1)S(1)}, bf16[192,1024]{1,0:T(8,128)(2,1)S(1)}, u32[]{:S(2)}, u32[]{:S(2)}) collective-permute-start(bf16[192,1024]{1,0:T(8,128)(2,1)S(1)} %broadcast_select_fusion.refs_1_), channel_id=1, source_target_pairs={{0,2},{1,3},{2,0},{3,1},{4,6},{5,7},{6,4},{7,5},{8,10},{9,11},{10,... | collective-permute-start | bytes 1179656 | tf_op jit(solution)/shard_map/ppermute | solution.py:836
  168.2 35.8 %collective-permute-start.31 = (bf16[8,160,128]{2,1,0:T(8,128)(2,1)S(1)}, bf16[8,160,128]{2,1,0:T(8,128)(2,1)}, u32[]{:S(2)}, u32[]{:S(2)}) collective-permute-start(bf16[8,160,128]{2,1,0:T(8,128)(2,1)S(1)} %bitcast.44), channel_id=1, source_target_pairs={{0,16},{16,0},{1,17},{17,1},{2,18},{18,2},{3,19},{19,3},{4,20},{20... | collective-permute-start | bytes 983048 | tf_op jit(solution)/shard_map/ppermute | solution.py:704
  197.9 14.2 %all-to-all-start.2 = ((bf16[8,24,640]{2,1,0:T(8,128)(2,1)}), bf16[8,24,640]{2,1,0:T(8,128)(2,1)S(1)}, u32[]{:S(2)}, u32[]{:S(2)}) async-start(bf16[8,24,640]{2,1,0:T(8,128)(2,1)} %bitcast.16), calls=%async_computation.2 | async-start | bytes 491520 | tf_op jit(solution)/shard_map/all_to_all | solution.py:707
  204.0 1.6 collective-permute-start.32
  204.0 2.3 %collective-permute-start.33 = (bf16[8,160,128]{2,1,0:T(8,128)(2,1)}, bf16[8,160,128]{2,1,0:T(8,128)(2,1)S(1)}, u32[]{:S(2)}, u32[]{:S(2)}) collective-permute-start(bf16[8,160,128]{2,1,0:T(8,128)(2,1)} %collective-permute-done.31.far), channel_id=1, source_target_pairs={{0,1},{1,0},{2,3},{3,2},{4,5},{5,4},{6,7},{7,6},{8,9},{9,8},{10,11... | collective-permute-start | bytes 983048 | tf_op jit(solution)/shard_map/ppermute | solution.py:701
  (20 other events, 239.7 us)

commit v3 on v2

--- a/solution.py
+++ b/solution.py
@@ -561,63 +561,52 @@
     )(core.reshape(1), queries, *own, *other)
 
 
-def out_weight_kernel(info, scales, codes, out):
-    step, rank = pl.program_id(0), info[0]
-    blocks, rows, width = out.shape
+def out_kernel(blocks, has_start, last, width, info, scales, *refs):
+    attended = refs[:blocks]
+    codes = refs[blocks : blocks + 2]
+    out, held, arrived = refs[-3:]
+    core, my_rank = info[0], info[1]
+    columns = held.shape[1]
     tiles = width // TILE_SIDE
-    for group in range(rows // GROUP_ROWS):
-        span = slice(group * GROUP_ROWS, (group + 1) * GROUP_ROWS)
-        column = (rank * rows + group * GROUP_ROWS) // TILE_SIDE
-        for tile in range(blocks * tiles):
-            codes_here = codes[span, tile * TILE_SIDE : (tile + 1) * TILE_SIDE].astype(F32)
-            lanes = slice(tile % tiles * TILE_SIDE, (tile % tiles + 1) * TILE_SIDE)
-            scale = scales[step * blocks * tiles + tile, column]
-            out[tile // tiles, span, lanes] = (codes_here * scale).astype(BF)
-
-
-def prepare_out(rank, wo_rows, wo_scale, width):
-    columns, rows = wo_rows.shape
-    blocks = 4
-    return pl.pallas_call(
-        out_weight_kernel,
-        grid_spec=pltpu.PrefetchScalarGridSpec(
-            num_scalar_prefetch=2,
-            grid=(rows // width // blocks,),
-            in_specs=[pl.BlockSpec((columns, blocks * width), lambda i, *_: (0, i))],
-            out_specs=pl.BlockSpec((blocks, columns, width), lambda i, *_: (i, 0, 0)),
-        ),
-        out_shape=jax.ShapeDtypeStruct((rows // width, columns, width), BF),
-        compiler_params=PARAMS,
-        cost_estimate=cost(4 * rows * columns, 4 * rows * columns),
-        name="prepare_out",
-    )(rank.reshape(1), wo_scale, wo_rows)
-
-
-def out_kernel(blocks, has_start, last, info, *refs):
-    attended = refs[:blocks]
-    weights = refs[blocks : blocks + 2]
-    out, held, arrived = refs[-3:]
-    core = info[0]
-    columns, width = held.shape[2:]
-    halves = [(block, half) for block in range(blocks) for half in range(2)]
+    pieces = [(block, half, side) for block in range(blocks) for half in range(2) for side in range(2)]
     copies = []
-    for number, (block, half) in enumerate(halves):
-        rank = 2 * info[1 + block] + (core ^ half)
-        for side in range(2):
-            copy = pltpu.make_async_copy(
-                weights[side].at[rank], held.at[number, side], arrived.at[number, side]
+    for number, (block, half, side) in enumerate(pieces):
+        start = (2 * info[2 + block] + (core ^ half)) * width
+        copy = pltpu.make_async_copy(
+            codes[side].at[:, pl.ds(pl.multiple_of(start, width), width)],
+            held.at[number],
+            arrived.at[number],
+        )
+        copy.start()
+        copies.append(copy)
+    totals = [None, None]
+    for number, (block, half, side) in enumerate(pieces):
+        rows = attended[block][:, half * width : (half + 1) * width]
+        first_tile = (2 * info[2 + block] + (core ^ half)) * tiles
+        copies[number].wait()
+        weight = []
+        for group in range(columns // GROUP_ROWS):
+            column = ((my_rank ^ side) * columns + group * GROUP_ROWS) // TILE_SIDE
+            span = slice(group * GROUP_ROWS, (group + 1) * GROUP_ROWS)
+            weight.append(
+                jnp.concatenate(
+                    [
+                        (
+                            held[number, span, tile * TILE_SIDE : (tile + 1) * TILE_SIDE].astype(F32)
+                            * scales[first_tile + tile, column]
+                        ).astype(BF)
+                        for tile in range(tiles)
+                    ],
+                    axis=1,
+                )
             )
-            copy.start()
-            copies.append(copy)
-    totals = [None, None]
-    for number, (block, half) in enumerate(halves):
-        rows = attended[block][:, half * width : (half + 1) * width]
-        for side in range(2):
-            copies[2 * number + side].wait()
-            term = lax.dot_general(
-                held[number, side], rows, (((1,), (1,)), ((), ())), preferred_element_type=F32
-            )
-            totals[side] = term if totals[side] is None else totals[side] + term
+        term = lax.dot_general(
+            jnp.concatenate(weight, axis=0),
+            rows,
+            (((1,), (1,)), ((), ())),
+            preferred_element_type=F32,
+        )
+        totals[side] = term if totals[side] is None else totals[side] + term
     if has_start:
         start = refs[blocks + 2]
         totals = [total + start[side] for side, total in enumerate(totals)]
@@ -632,28 +621,28 @@
             out[side] = totals[side]
 
 
-def out_project(core, attended, chips_of, weights, start, last):
+def out_project(core, my_rank, attended, chips_of, codes, scales, start, last):
     count, both = attended[0].shape
     blocks = len(attended)
-    _, columns, width = weights[0].shape
+    columns = codes[0].shape[0]
     vmem = pl.BlockSpec(memory_space=pltpu.VMEM)
     extra = [] if start is None else [start]
     shape = (count, 2 * columns) if last else (2, columns, count)
     return pl.pallas_call(
-        functools.partial(out_kernel, blocks, bool(extra), last),
+        functools.partial(out_kernel, blocks, bool(extra), last, both // 2),
         out_shape=jax.ShapeDtypeStruct(shape, BF if last else F32),
-        in_specs=[SMEM]
+        in_specs=[SMEM, SMEM]
         + [vmem] * blocks
         + [pl.BlockSpec(memory_space=pl.ANY)] * 2
         + [vmem] * len(extra),
         scratch_shapes=[
-            pltpu.VMEM((2 * blocks, 2, columns, width), BF),
-            pltpu.SemaphoreType.DMA((2 * blocks, 2)),
+            pltpu.VMEM((4 * blocks, columns, both // 2), BF),
+            pltpu.SemaphoreType.DMA((4 * blocks,)),
         ],
         compiler_params=PARAMS,
         cost_estimate=cost(4 * blocks * count * both * columns, 4 * blocks * both * columns),
         name="out_project",
-    )(jnp.concatenate([core.reshape(1), chips_of]), *attended, *weights, *extra)
+    )(jnp.concatenate([jnp.stack([core, my_rank]), chips_of]), scales, *attended, *codes, *extra)
 
 
 def rotation_tables(count):
@@ -668,6 +657,8 @@
 Z_COUNT = 4
 PART_ROWS = (192, 192)
 SPLIT_GATHER = False
+TIE_SUMS = True
+CALLS = ((0, 1, 2), (3, 4, 5, 6), (7,))
 
 
 def after(values, *earlier):
@@ -757,6 +748,8 @@
     for part, part_rows in enumerate(PART_ROWS):
         kept, *sums = join_partials(home[part], got[part])
         sums = [swap(value, 4 * (k + 1)) for k, value in enumerate(sums)]
+        if TIE_SUMS and part + 1 < len(PART_ROWS):
+            got[part + 1], *sums = lax.optimization_barrier((got[part + 1], *sums))
         queries, kv = make_heads(core, [kept, *sums], start, q_gain, k_gain, cosine, sine)
         own_kv.append(kv)
         other_kv.append(swap(kv, 1))
@@ -764,10 +757,7 @@
         held.append(jnp.concatenate([kept, swap(sent_rows, 1)], axis=1))
         start += part_rows
     wo_rows = wo_codes.T
-    out_weights = [
-        prepare_out(rank, codes, wo_scale, heads_width)
-        for rank, codes in ((my_rank, wo_rows), (my_rank ^ 1, swap(wo_rows, 1)))
-    ]
+    out_codes = [wo_rows, swap(wo_rows, 1)]
 
     by_z = jnp.stack(by_z)
     my_y = chip % y_count
@@ -786,14 +776,16 @@
     for block in held:
         blocks = gather_chips(block, chips, y_count)
         total = None
-        for chosen in ((0, 1, 2, 3), (4, 6), (5, 7)):
+        for chosen in CALLS:
             total = out_project(
                 core,
+                my_rank,
                 [blocks[bits] for bits in chosen],
                 chip ^ jnp.array(chosen, jnp.int32),
-                out_weights,
+                out_codes,
+                wo_scale,
                 total,
-                chosen == (5, 7),
+                chosen == CALLS[-1],
             )
         columns.append(total)
     columns = to_chips(jnp.concatenate(columns, axis=0).reshape(chips, share, -1))
@@ -848,12 +840,15 @@
     across = swap(block, 2)
     one = swap(block, along)
     inner = hop(block, middle)
+    across, one, inner = lax.optimization_barrier((across, one, inner))
     two_end = hop(inner, outward)
     two_inner = hop(one, middle)
     one_across = swap(one, 2)
+    two_end, two_inner, one_across = lax.optimization_barrier((two_end, two_inner, one_across))
     two = jnp.where(at_end, two_end, two_inner)
     three_end = hop(two, outward)
     two_across = swap(two, 2)
+    three_end, two_across = lax.optimization_barrier((three_end, two_across))
     three = jnp.where(at_end, three_end, inner)
     three_across = swap(three, 2)
     return {

time: 214 us -> 194 us (0.907)
  starting transfers between devices: 62.2 us -> 50.9 us
  Pallas kernels: 59.5 us -> 51.7 us
  local copies, waits for them, and re-layouts: 11 us -> 7.62 us
  waiting for transfers between devices: 75.7 us -> 78.6 us
    ppermute x27, starting transfers between devices: 41.7 us -> 28.8 us  [swap(): return lax.ppermute(values, 'fsdp', [(i, i ^ bits) for i in range(ranks)])]
    pallas_call x5 -> x3, Pallas kernels: 23.2 us -> 15.3 us  [out_project(): pl.pallas_call(functools.partial(out_kernel, blocks, bool(extra), last, b...]
    unnamed x36 -> x34, local copies, waits for them, and re-layouts: 8.93 us -> 4.95 us
    ppermute x4, waiting for transfers between devices: 17.2 us -> 20.4 us  [hop(): lax.ppermute(values, 'fsdp', [(a * along + rest, b * along + rest) for a,...]
  transfers between devices with their start and end apart: 35 -> 35, of which waited for: 16 -> 17; matrix products, arithmetic and copies ran while one was open for 2% -> 2% of each run, Pallas kernels for 25% -> 24%
where the time goes in v3:
time: 194 us; the launch traced here: 193 us
  waiting for transfers between devices  78.6 us (41%)
  Pallas kernels  51.7 us (27%)
  starting transfers between devices  50.9 us (26%)
  local copies, waits for them, and re-layouts  7.62 us (4%)
  other arithmetic  2.69 us (1%)
    ppermute x27, waiting for transfers between devices, swap(): return lax.ppermute(values, 'fsdp', [(i, i ^ bits) for i in range(ranks)])  55.8 us
    ppermute x27, starting transfers between devices, swap(): return lax.ppermute(values, 'fsdp', [(i, i ^ bits) for i in range(ranks)])  28.8 us
    ppermute x4, waiting for transfers between devices, hop(): lax.ppermute(values, 'fsdp', [(a * along + rest, b * along + rest) for a,...  20.4 us
    pallas_call x3, Pallas kernels, out_project(): pl.pallas_call(functools.partial(out_kernel, blocks, bool(extra), last, b...  15.3 us
    all_to_all x2, starting transfers between devices, to_chips(): lax.all_to_all(values, 'fsdp', split_axis=0, concat_axis=0, tiled=True, a...  15 us
    pallas_call x2, Pallas kernels, project(): pl.pallas_call(project_kernel, grid=(blocks,), in_specs=[SMEM, pl.BlockSp...  9.75 us
    pallas_call x1, Pallas kernels, prepare_weights(): pl.pallas_call(weight_kernel, grid_spec=pltpu.PrefetchScalarGridSpec(num_...  8.51 us
    pallas_call x1, Pallas kernels, pick_rows(): pl.pallas_call(functools.partial(pick_kernel, width), grid=(steps,), out_...  5.35 us
  transfers between devices with their start and end apart: 35, of which 17 were waited for; matrix products, arithmetic and copies ran while one was open for 2% of the time, Pallas kernels for 24%

profile of v3, /device:TPU:0, one launch (start us, length us, event | category | flops | bytes accessed | tf_op | source)
XLA Modules:
  0.0 193.2 jit_solution(2170068262149573308)
XLA Ops:
  2.1 5.3 %pick_rows.2 = bf16[8,32,640]{2,1,0:T(8,128)(2,1)} custom-call(s32[1]{0:T(128)} %constant.154.clone.1.info, f32[8,384]{1,0:T(8,128)S(1)} %get-tuple-element.228.rows, f32[1,5120]{1,0:T(1,128)} %bitcast.57, bf16[600,5120]{1,0:T(8,128)(2,1)} %table.1), custom_call_target="tpu_custom_call" | custom-call | flops 196608000 | bytes 6144000 | tf_op jit(solution)/shard_map/pick_rows/pallas_call | solution.py:281
  7.5 7.3 %all-to-all-start.1 = ((bf16[8,32,640]{2,1,0:T(8,128)(2,1)}), bf16[8,32,640]{2,1,0:T(8,128)(2,1)S(1)}, u32[]{:S(2)}, u32[]{:S(2)}) async-start(bf16[8,32,640]{2,1,0:T(8,128)(2,1)} %pick_rows.2), calls=%async_computation.1 | async-start | bytes 655360 | tf_op jit(solution)/shard_map/all_to_all | solution.py:698
  15.0 8.5 %prepare_weights.1 = (bf16[8,320,640]{2,1,0:T(8,128)(2,1)}, bf16[4,320,640]{2,1,0:T(8,128)(2,1)S(1)}, bf16[4,320,640]{2,1,0:T(8,128)(2,1)S(1)}, bf16[8,320,128]{2,1,0:T(8,128)(2,1)S(1)}) custom-call(s32[2]{0:T(128)S(1)} %pad_add_fusion.3.info, s32[8]{0:T(128)S(1)} %add_xor_fusion.order, s32[8]{0:T(128)S(1)} %copy-done.6, f32[40,64]{1,0:T(8,128)S(1)} %copy-done.3, ...), custom_call_target="tpu_custom_call" | custom-call | flops 20971520 | bytes 15728640 | tf_op jit(solution)/shard_map/prepare_weights/pallas_call | solution.py:379
  27.2 1.5 collective-permute-start.2
  29.0 1.8 collective-permute-done.2
  34.4 5.5 %project.2 = (bf16[4,192,640]{2,1,0:T(8,128)(2,1)}, bf16[4,192,640]{2,1,0:T(8,128)(2,1)}) custom-call(s32[1]{0:T(128)} %bitcast.5.info, bf16[384,640]{1,0:T(8,128)(2,1)} %copy-done.9, bf16[8,320,640]{2,1,0:T(8,128)(2,1)} %get-tuple-element.100.own, bf16[4,320,640]{2,1,0:T(8,128)(2,1)} %collective-permute-done.3.other), custom_call_target="tpu_custom_call" | custom-call | flops 1258291200 | bytes 5242880 | tf_op jit(solution)/shard_map/project/pallas_call | solution.py:435
  39.9 2.0 %collective-permute-start.5 = (bf16[4,192,640]{2,1,0:T(8,128)(2,1)}, bf16[4,192,640]{2,1,0:T(8,128)(2,1)}, u32[]{:S(2)}, u32[]{:S(2)}) collective-permute-start(bf16[4,192,640]{2,1,0:T(8,128)(2,1)} %get-tuple-element.103), channel_id=1, source_target_pairs={{0,2},{1,3},{2,0},{3,1},{4,6},{5,7},{6,4},{7,5},{8,10},{9,11},{10,... | collective-permute-start | bytes 2949128 | tf_op jit(solution)/shard_map/ppermute | solution.py:692
  42.7 2.0 %collective-permute-start.6 = (bf16[2,160,128]{2,1,0:T(8,128)(2,1)S(1)}, bf16[2,160,128]{2,1,0:T(8,128)(2,1)S(1)}, u32[]{:S(2)}, u32[]{:S(2)}) collective-permute-start(bf16[2,160,128]{2,1,0:T(8,128)(2,1)S(1)} %get-tuple-element.162), channel_id=1, source_target_pairs={{0,4},{1,5},{2,6},{3,7},{4,0},{5,1},{6,2},{7,3},{8,12},{9,13},{10,... | collective-permute-start | bytes 245768 | tf_op jit(solution)/shard_map/ppermute | solution.py:692
  44.6 2.5 %collective-permute-done.6 = bf16[2,160,128]{2,1,0:T(8,128)(2,1)S(1)} collective-permute-done((bf16[2,160,128]{2,1,0:T(8,128)(2,1)S(1)}, bf16[2,160,128]{2,1,0:T(8,128)(2,1)S(1)}, u32[]{:S(2)}, u32[]{:S(2)}) %collective-permute-start.6) | collective-permute-done | bytes 81952 | tf_op jit(solution)/shard_map/ppermute | solution.py:692
  47.1 2.9 %collective-permute-start.7 = (bf16[2,160,128]{2,1,0:T(8,128)(2,1)S(1)}, bf16[2,160,128]{2,1,0:T(8,128)(2,1)S(1)}, u32[]{:S(2)}, u32[]{:S(2)}) collective-permute-start(bf16[2,160,128]{2,1,0:T(8,128)(2,1)S(1)} %get-tuple-element.161), channel_id=1, source_target_pairs={{0,8},{1,9},{2,10},{3,11},{4,12},{5,13},{6,14},{7,15},{8,0},{9,1},... | collective-permute-start | bytes 245768 | tf_op jit(solution)/shard_map/ppermute | solution.py:692
  51.5 4.3 %project.3 = (f32[4,192,640]{2,1,0:T(8,128)S(1)}, f32[4,192,640]{2,1,0:T(8,128)S(1)}) custom-call(s32[1]{0:T(128)} %bitcast.12.info, bf16[384,640]{1,0:T(8,128)(2,1)} %copy-done.9, bf16[8,320,640]{2,1,0:T(8,128)(2,1)} %get-tuple-element.100.own, bf16[4,320,640]{2,1,0:T(8,128)(2,1)S(1)} %collective-permute-done.4.other), custom_call_target="tpu_custom_call" | custom-call | flops 1258291200 | bytes 5242880 | tf_op jit(solution)/shard_map/project/pallas_call | solution.py:435
  56.3 8.4 %collective-permute-done.5.got = bf16[4,192,640]{2,1,0:T(8,128)(2,1)} collective-permute-done((bf16[4,192,640]{2,1,0:T(8,128)(2,1)}, bf16[4,192,640]{2,1,0:T(8,128)(2,1)}, u32[]{:S(2)}, u32[]{:S(2)}) %collective-permute-start.5) | collective-permute-done | bytes 983072 | tf_op jit(solution)/shard_map/ppermute | solution.py:692
  66.2 2.1 %collective-permute-start.10 = (bf16[192,640]{1,0:T(8,128)(2,1)S(1)}, bf16[192,640]{1,0:T(8,128)(2,1)S(1)}, u32[]{:S(2)}, u32[]{:S(2)}) collective-permute-start(bf16[192,640]{1,0:T(8,128)(2,1)S(1)} %get-tuple-element.112), channel_id=1, source_target_pairs={{0,4},{1,5},{2,6},{3,7},{4,0},{5,1},{6,2},{7,3},{8,12},{9,13},{10,... | collective-permute-start | bytes 737288 | tf_op jit(solution)/shard_map/ppermute | solution.py:692
  68.3 2.4 %collective-permute-start.11 = (bf16[192,640]{1,0:T(8,128)(2,1)S(1)}, bf16[192,640]{1,0:T(8,128)(2,1)S(1)}, u32[]{:S(2)}, u32[]{:S(2)}) collective-permute-start(bf16[192,640]{1,0:T(8,128)(2,1)S(1)} %get-tuple-element.113), channel_id=1, source_target_pairs={{0,8},{1,9},{2,10},{3,11},{4,12},{5,13},{6,14},{7,15},{8,0},{9,1},... | collective-permute-start | bytes 737288 | tf_op jit(solution)/shard_map/ppermute | solution.py:692
  70.8 14.5 %collective-permute-done.9.got = bf16[4,192,640]{2,1,0:T(8,128)(2,1)S(1)} collective-permute-done((bf16[4,192,640]{2,1,0:T(8,128)(2,1)}, bf16[4,192,640]{2,1,0:T(8,128)(2,1)S(1)}, u32[]{:S(2)}, u32[]{:S(2)}) %collective-permute-start.9) | collective-permute-done | bytes 983072 | tf_op jit(solution)/shard_map/ppermute | solution.py:692
  85.2 3.2 %collective-permute-done.11.refs_2_ = bf16[192,640]{1,0:T(8,128)(2,1)S(1)} collective-permute-done((bf16[192,640]{1,0:T(8,128)(2,1)S(1)}, bf16[192,640]{1,0:T(8,128)(2,1)S(1)}, u32[]{:S(2)}, u32[]{:S(2)}) %collective-permute-start.11) | collective-permute-done | bytes 245792 | tf_op jit(solution)/shard_map/ppermute | solution.py:692
  88.7 3.3 %collective-permute-start.15 = (bf16[192,640]{1,0:T(8,128)(2,1)S(1)}, bf16[192,640]{1,0:T(8,128)(2,1)S(1)}, u32[]{:S(2)}, u32[]{:S(2)}) collective-permute-start(bf16[192,640]{1,0:T(8,128)(2,1)S(1)} %get-tuple-element.125), channel_id=1, source_target_pairs={{0,4},{1,5},{2,6},{3,7},{4,0},{5,1},{6,2},{7,3},{8,12},{9,13},{10,... | collective-permute-start | bytes 737288 | tf_op jit(solution)/shard_map/ppermute | solution.py:692
  96.4 2.4 %collective-permute-done.15.refs_1_ = bf16[192,640]{1,0:T(8,128)(2,1)S(1)} collective-permute-done((bf16[192,640]{1,0:T(8,128)(2,1)S(1)}, bf16[192,640]{1,0:T(8,128)(2,1)S(1)}, u32[]{:S(2)}, u32[]{:S(2)}) %collective-permute-start.15) | collective-permute-done | bytes 245792 | tf_op jit(solution)/shard_map/ppermute | solution.py:692
  98.8 12.4 %collective-permute-done.16.refs_2_ = bf16[192,640]{1,0:T(8,128)(2,1)S(1)} collective-permute-done((bf16[192,640]{1,0:T(8,128)(2,1)S(1)}, bf16[192,640]{1,0:T(8,128)(2,1)S(1)}, u32[]{:S(2)}, u32[]{:S(2)}) %collective-permute-start.16) | collective-permute-done | bytes 245792 | tf_op jit(solution)/shard_map/ppermute | solution.py:692
  117.5 3.2 %collective-permute-start.21 = (bf16[192,1024]{1,0:T(8,128)(2,1)S(1)}, bf16[192,1024]{1,0:T(8,128)(2,1)S(1)}, u32[]{:S(2)}, u32[]{:S(2)}) collective-permute-start(bf16[192,1024]{1,0:T(8,128)(2,1)S(1)} %maximum_maximum_fusion.refs_0_), channel_id=1, source_target_pairs={{0,4},{1,5},{2,6},{3,7},{4,0},{5,1},{6,2},{7,3},{8,12},{9,13},{10,... | collective-permute-start | bytes 1179656 | tf_op jit(solution)/shard_map/ppermute | solution.py:828
  121.3 6.2 %collective-permute-done.20.refs_1_ = bf16[192,1024]{1,0:T(8,128)(2,1)S(1)} collective-permute-done((bf16[192,1024]{1,0:T(8,128)(2,1)S(1)}, bf16[192,1024]{1,0:T(8,128)(2,1)S(1)}, u32[]{:S(2)}, u32[]{:S(2)}) %collective-permute-start.20) | collective-permute-done | bytes 393248 | tf_op jit(solution)/shard_map/ppermute | solution.py:828
  127.5 2.3 %collective-permute-done.21.refs_2_ = bf16[192,1024]{1,0:T(8,128)(2,1)S(1)} collective-permute-done((bf16[192,1024]{1,0:T(8,128)(2,1)S(1)}, bf16[192,1024]{1,0:T(8,128)(2,1)S(1)}, u32[]{:S(2)}, u32[]{:S(2)}) %collective-permute-start.21) | collective-permute-done | bytes 393248 | tf_op jit(solution)/shard_map/ppermute | solution.py:828
  132.8 11.0 %collective-permute-done.23 = bf16[192,1024]{1,0:T(8,128)(2,1)S(1)} collective-permute-done((bf16[192,1024]{1,0:T(8,128)(2,1)S(1)}, bf16[192,1024]{1,0:T(8,128)(2,1)S(1)}, u32[]{:S(2)}, u32[]{:S(2)}) %collective-permute-start.23) | collective-permute-done | bytes 393248 | tf_op jit(solution)/shard_map/ppermute | solution.py:831
  143.9 1.5 collective-permute-start.26
  146.1 1.6 collective-permute-start.30
  147.8 9.4 %collective-permute-done.26 = bf16[192,1024]{1,0:T(8,128)(2,1)S(1)} collective-permute-done((bf16[192,1024]{1,0:T(8,128)(2,1)S(1)}, bf16[192,1024]{1,0:T(8,128)(2,1)S(1)}, u32[]{:S(2)}, u32[]{:S(2)}) %collective-permute-start.26) | collective-permute-done | bytes 393248 | tf_op jit(solution)/shard_map/ppermute | solution.py:831
  159.6 1.5 collective-permute-start.31
  161.3 5.1 %out_project.3.refs_6_ = f32[2,320,192]{2,1,0:T(8,128)S(1)} custom-call(s32[5]{0:T(128)S(1)} %pad_add_fusion.5.info, f32[64,40]{1,0:T(8,128)S(1)} %copy.20.scales, bf16[192,1024]{1,0:T(8,128)(2,1)S(1)} %maximum_maximum_fusion.refs_0_, bf16[192,1024]{1,0:T(8,128)(2,1)S(1)} %collective-permute-done.20.refs_1_, ...), custom_call_target="tpu_custom_call" | custom-call | flops 754974720 | bytes 3932160 | tf_op jit(solution)/shard_map/out_project/pallas_call | solution.py:631
  166.5 6.1 %out_project.4.refs_3_ = f32[2,320,192]{2,1,0:T(8,128)S(1)} custom-call(s32[6]{0:T(128)S(1)} %pad_add_fusion.4.info, f32[64,40]{1,0:T(8,128)S(1)} %copy.20.scales, bf16[192,1024]{1,0:T(8,128)(2,1)S(1)} %collective-permute-done.25.refs_0_, bf16[192,1024]{1,0:T(8,128)(2,1)S(1)} %broadcast_select_fusion.1.refs_1_, ...), custom_call_target="tpu_custom_call" | custom-call | flops 1006632960 | bytes 5242880 | tf_op jit(solution)/shard_map/out_project/pallas_call | solution.py:631
  172.5 4.1 %out_project.5 = bf16[192,640]{1,0:T(8,128)(2,1)} custom-call(s32[3]{0:T(128)S(1)} %pad_add_fusion.1.info, f32[64,40]{1,0:T(8,128)S(1)} %copy.20.scales, bf16[192,1024]{1,0:T(8,128)(2,1)S(1)} %collective-permute-done.28.refs_0_, bf16[320,8192]{1,0:T(8,128)(2,1)} %bitcast.54, bf16[320,8192]{1,0:T(8,128)(2,1)} %collective-permute-done.29.refs_4_.refs_5_.refs_2_, ...), custom_call_target="tpu_custom_call" | custom-call | flops 251658240 | bytes 1310720 | tf_op jit(solution)/shard_map/out_project/pallas_call | solution.py:631
  176.7 7.7 %all-to-all-start.2 = ((bf16[8,24,640]{2,1,0:T(8,128)(2,1)}), bf16[8,24,640]{2,1,0:T(8,128)(2,1)S(1)}, u32[]{:S(2)}, u32[]{:S(2)}) async-start(bf16[8,24,640]{2,1,0:T(8,128)(2,1)} %bitcast.16), calls=%async_computation.2 | async-start | bytes 491520 | tf_op jit(solution)/shard_map/all_to_all | solution.py:698
  186.7 5.2 %collect_keys.1 = bf16[8,2,2,160,128]{4,3,2,1,0:T(8,128)(2,1)} custom-call(s32[3]{0:T(128)S(1)} %pad_add_fusion.6.info, bf16[8,160,128]{2,1,0:T(8,128)(2,1)S(1)} %bitcast.45, bf16[8,160,128]{2,1,0:T(8,128)(2,1)} %collective-permute-done.31.far, bf16[8,160,128]{2,1,0:T(8,128)(2,1)S(1)} %collective-permute-done.32.other, ...), custom_call_target="tpu_custom_call" | custom-call | bytes 2621440 | tf_op jit(solution)/shard_map/collect_keys/pallas_call | solution.py:807
  (114 shorter events, 35.0 us)
Async XLA Ops:
  7.5 19.3 %all-to-all-start.1 = ((bf16[8,32,640]{2,1,0:T(8,128)(2,1)}), bf16[8,32,640]{2,1,0:T(8,128)(2,1)S(1)}, u32[]{:S(2)}, u32[]{:S(2)}) async-start(bf16[8,32,640]{2,1,0:T(8,128)(2,1)} %pick_rows.2), calls=%async_computation.1 | async-start | bytes 655360 | tf_op jit(solution)/shard_map/all_to_all | solution.py:698
  26.7 6.9 %collective-permute-start.3 = (bf16[4,320,640]{2,1,0:T(8,128)(2,1)}, bf16[4,320,640]{2,1,0:T(8,128)(2,1)}, u32[]{:S(2)}, u32[]{:S(2)}) collective-permute-start(bf16[4,320,640]{2,1,0:T(8,128)(2,1)} %copy-done.8), channel_id=1, source_target_pairs={{0,1},{1,0},{2,3},{3,2},{4,5},{5,4},{6,7},{7,6},{8,9},{9,8},{10,11... | collective-permute-start | bytes 4915208 | tf_op jit(solution)/shard_map/ppermute | solution.py:692
  26.7 134.6 %collective-permute-start.29 = (bf16[320,8192]{1,0:T(8,128)(2,1)}, bf16[320,8192]{1,0:T(8,128)(2,1)}, u32[]{:S(2)}, u32[]{:S(2)}) collective-permute-start(bf16[320,8192]{1,0:T(8,128)(2,1)} %bitcast.51), channel_id=1, source_target_pairs={{0,1},{1,0},{2,3},{3,2},{4,5},{5,4},{6,7},{7,6},{8,9},{9,8},{10,11... | collective-permute-start | bytes 15728648 | tf_op jit(solution)/shard_map/ppermute | solution.py:692
  27.2 4.4 %collective-permute-start.1 = (bf16[8,32,640]{2,1,0:T(8,128)(2,1)S(1)}, bf16[8,32,640]{2,1,0:T(8,128)(2,1)S(1)}, u32[]{:S(2)}, u32[]{:S(2)}) collective-permute-start(bf16[8,32,640]{2,1,0:T(8,128)(2,1)S(1)} %all-to-all-done.1), channel_id=1, source_target_pairs={{0,1},{1,0},{2,3},{3,2},{4,5},{5,4},{6,7},{7,6},{8,9},{9,8},{10,11... | collective-permute-start | bytes 983048 | tf_op jit(solution)/shard_map/ppermute | solution.py:692
  27.2 3.6 %collective-permute-start.2 = (f32[8,128]{1,0:T(8,128)S(1)}, f32[8,128]{1,0:T(8,128)S(1)}, u32[]{:S(2)}, u32[]{:S(2)}) collective-permute-start(f32[8,128]{1,0:T(8,128)S(1)} %get-tuple-element.97), channel_id=1, source_target_pairs={{0,16},{16,0},{1,17},{17,1},{2,18},{18,2},{3,19},{19,3},{4,20},{20... | collective-permute-start | bytes 12296 | tf_op jit(solution)/shard_map/ppermute | solution.py:695
  28.7 21.3 %collective-permute-start.4 = (bf16[4,320,640]{2,1,0:T(8,128)(2,1)}, bf16[4,320,640]{2,1,0:T(8,128)(2,1)S(1)}, u32[]{:S(2)}, u32[]{:S(2)}) collective-permute-start(bf16[4,320,640]{2,1,0:T(8,128)(2,1)} %copy-done.7), channel_id=1, source_target_pairs={{0,1},{1,0},{2,3},{3,2},{4,5},{5,4},{6,7},{7,6},{8,9},{9,8},{10,11... | collective-permute-start | bytes 4915208 | tf_op jit(solution)/shard_map/ppermute | solution.py:692
  39.9 24.9 %collective-permute-start.5 = (bf16[4,192,640]{2,1,0:T(8,128)(2,1)}, bf16[4,192,640]{2,1,0:T(8,128)(2,1)}, u32[]{:S(2)}, u32[]{:S(2)}) collective-permute-start(bf16[4,192,640]{2,1,0:T(8,128)(2,1)} %get-tuple-element.103), channel_id=1, source_target_pairs={{0,2},{1,3},{2,0},{3,1},{4,6},{5,7},{6,4},{7,5},{8,10},{9,11},{10,... | collective-permute-start | bytes 2949128 | tf_op jit(solution)/shard_map/ppermute | solution.py:692
  41.9 43.3 %collective-permute-start.9 = (bf16[4,192,640]{2,1,0:T(8,128)(2,1)}, bf16[4,192,640]{2,1,0:T(8,128)(2,1)S(1)}, u32[]{:S(2)}, u32[]{:S(2)}) collective-permute-start(bf16[4,192,640]{2,1,0:T(8,128)(2,1)} %get-tuple-element.104), channel_id=1, source_target_pairs={{0,2},{1,3},{2,0},{3,1},{4,6},{5,7},{6,4},{7,5},{8,10},{9,11},{10,... | collective-permute-start | bytes 2949128 | tf_op jit(solution)/shard_map/ppermute | solution.py:692
  42.7 4.4 %collective-permute-start.6 = (bf16[2,160,128]{2,1,0:T(8,128)(2,1)S(1)}, bf16[2,160,128]{2,1,0:T(8,128)(2,1)S(1)}, u32[]{:S(2)}, u32[]{:S(2)}) collective-permute-start(bf16[2,160,128]{2,1,0:T(8,128)(2,1)S(1)} %get-tuple-element.162), channel_id=1, source_target_pairs={{0,4},{1,5},{2,6},{3,7},{4,0},{5,1},{6,2},{7,3},{8,12},{9,13},{10,... | collective-permute-start | bytes 245768 | tf_op jit(solution)/shard_map/ppermute | solution.py:692
  47.1 8.6 %collective-permute-start.7 = (bf16[2,160,128]{2,1,0:T(8,128)(2,1)S(1)}, bf16[2,160,128]{2,1,0:T(8,128)(2,1)S(1)}, u32[]{:S(2)}, u32[]{:S(2)}) collective-permute-start(bf16[2,160,128]{2,1,0:T(8,128)(2,1)S(1)} %get-tuple-element.161), channel_id=1, source_target_pairs={{0,8},{1,9},{2,10},{3,11},{4,12},{5,13},{6,14},{7,15},{8,0},{9,1},... | collective-permute-start | bytes 245768 | tf_op jit(solution)/shard_map/ppermute | solution.py:692
  50.0 6.3 %collective-permute-start.8 = (bf16[2,160,128]{2,1,0:T(8,128)(2,1)S(1)}, bf16[2,160,128]{2,1,0:T(8,128)(2,1)S(1)}, u32[]{:S(2)}, u32[]{:S(2)}) collective-permute-start(bf16[2,160,128]{2,1,0:T(8,128)(2,1)S(1)} %get-tuple-element.160), channel_id=1, source_target_pairs={{0,12},{1,13},{2,14},{3,15},{4,8},{5,9},{6,10},{7,11},{8,4},{9,5},... | collective-permute-start | bytes 245768 | tf_op jit(solution)/shard_map/ppermute | solution.py:692
  66.2 19.1 %collective-permute-start.10 = (bf16[192,640]{1,0:T(8,128)(2,1)S(1)}, bf16[192,640]{1,0:T(8,128)(2,1)S(1)}, u32[]{:S(2)}, u32[]{:S(2)}) collective-permute-start(bf16[192,640]{1,0:T(8,128)(2,1)S(1)} %get-tuple-element.112), channel_id=1, source_target_pairs={{0,4},{1,5},{2,6},{3,7},{4,0},{5,1},{6,2},{7,3},{8,12},{9,13},{10,... | collective-permute-start | bytes 737288 | tf_op jit(solution)/shard_map/ppermute | solution.py:692
  68.3 20.2 %collective-permute-start.11 = (bf16[192,640]{1,0:T(8,128)(2,1)S(1)}, bf16[192,640]{1,0:T(8,128)(2,1)S(1)}, u32[]{:S(2)}, u32[]{:S(2)}) collective-permute-start(bf16[192,640]{1,0:T(8,128)(2,1)S(1)} %get-tuple-element.113), channel_id=1, source_target_pairs={{0,8},{1,9},{2,10},{3,11},{4,12},{5,13},{6,14},{7,15},{8,0},{9,1},... | collective-permute-start | bytes 737288 | tf_op jit(solution)/shard_map/ppermute | solution.py:692
  70.7 17.8 %collective-permute-start.12 = (bf16[192,640]{1,0:T(8,128)(2,1)S(1)}, bf16[192,640]{1,0:T(8,128)(2,1)S(1)}, u32[]{:S(2)}, u32[]{:S(2)}) collective-permute-start(bf16[192,640]{1,0:T(8,128)(2,1)S(1)} %get-tuple-element.114), channel_id=1, source_target_pairs={{0,12},{1,13},{2,14},{3,15},{4,8},{5,9},{6,10},{7,11},{8,4},{9,5},... | collective-permute-start | bytes 737288 | tf_op jit(solution)/shard_map/ppermute | solution.py:692
  88.7 10.1 %collective-permute-start.15 = (bf16[192,640]{1,0:T(8,128)(2,1)S(1)}, bf16[192,640]{1,0:T(8,128)(2,1)S(1)}, u32[]{:S(2)}, u32[]{:S(2)}) collective-permute-start(bf16[192,640]{1,0:T(8,128)(2,1)S(1)} %get-tuple-element.125), channel_id=1, source_target_pairs={{0,4},{1,5},{2,6},{3,7},{4,0},{5,1},{6,2},{7,3},{8,12},{9,13},{10,... | collective-permute-start | bytes 737288 | tf_op jit(solution)/shard_map/ppermute | solution.py:692
  92.0 19.2 %collective-permute-start.16 = (bf16[192,640]{1,0:T(8,128)(2,1)S(1)}, bf16[192,640]{1,0:T(8,128)(2,1)S(1)}, u32[]{:S(2)}, u32[]{:S(2)}) collective-permute-start(bf16[192,640]{1,0:T(8,128)(2,1)S(1)} %get-tuple-element.126), channel_id=1, source_target_pairs={{0,8},{1,9},{2,10},{3,11},{4,12},{5,13},{6,14},{7,15},{8,0},{9,1},... | collective-permute-start | bytes 737288 | tf_op jit(solution)/shard_map/ppermute | solution.py:692
  93.0 18.2 %collective-permute-start.17 = (bf16[192,640]{1,0:T(8,128)(2,1)S(1)}, bf16[192,640]{1,0:T(8,128)(2,1)S(1)}, u32[]{:S(2)}, u32[]{:S(2)}) collective-permute-start(bf16[192,640]{1,0:T(8,128)(2,1)S(1)} %get-tuple-element.127), channel_id=1, source_target_pairs={{0,12},{1,13},{2,14},{3,15},{4,8},{5,9},{6,10},{7,11},{8,4},{9,5},... | collective-permute-start | bytes 737288 | tf_op jit(solution)/shard_map/ppermute | solution.py:692
  96.3 15.9 %collective-permute-start.13 = (bf16[192,128]{1,0:T(8,128)(2,1)S(1)}, bf16[192,128]{1,0:T(8,128)(2,1)S(1)}, u32[]{:S(2)}, u32[]{:S(2)}) collective-permute-start(bf16[192,128]{1,0:T(8,128)(2,1)S(1)} %get-tuple-element.119.refs_0_), channel_id=1, source_target_pairs={{0,1},{1,0},{2,3},{3,2},{4,5},{5,4},{6,7},{7,6},{8,9},{9,8},{10,11... | collective-permute-start | bytes 147464 | tf_op jit(solution)/shard_map/ppermute | solution.py:692
  113.0 1.9 %collective-permute-start.14 = (bf16[96,512]{1,0:T(8,128)(2,1)S(1)}, bf16[96,512]{1,0:T(8,128)(2,1)S(1)}, u32[]{:S(2)}, u32[]{:S(2)}) collective-permute-start(bf16[96,512]{1,0:T(8,128)(2,1)S(1)} %get-tuple-element.121), channel_id=1, source_target_pairs={{0,1},{1,0},{2,3},{3,2},{4,5},{5,4},{6,7},{7,6},{8,9},{9,8},{10,11... | collective-permute-start | bytes 294920 | tf_op jit(solution)/shard_map/ppermute | solution.py:692
  116.3 11.2 %collective-permute-start.20 = (bf16[192,1024]{1,0:T(8,128)(2,1)S(1)}, bf16[192,1024]{1,0:T(8,128)(2,1)S(1)}, u32[]{:S(2)}, u32[]{:S(2)}) collective-permute-start(bf16[192,1024]{1,0:T(8,128)(2,1)S(1)} %maximum_maximum_fusion.refs_0_), channel_id=1, source_target_pairs={{0,2},{1,3},{2,0},{3,1},{4,6},{5,7},{6,4},{7,5},{8,10},{9,11},{10,... | collective-permute-start | bytes 1179656 | tf_op jit(solution)/shard_map/ppermute | solution.py:828
  117.5 12.3 %collective-permute-start.21 = (bf16[192,1024]{1,0:T(8,128)(2,1)S(1)}, bf16[192,1024]{1,0:T(8,128)(2,1)S(1)}, u32[]{:S(2)}, u32[]{:S(2)}) collective-permute-start(bf16[192,1024]{1,0:T(8,128)(2,1)S(1)} %maximum_maximum_fusion.refs_0_), channel_id=1, source_target_pairs={{0,4},{1,5},{2,6},{3,7},{4,0},{5,1},{6,2},{7,3},{8,12},{9,13},{10,... | collective-permute-start | bytes 1179656 | tf_op jit(solution)/shard_map/ppermute | solution.py:828
  120.7 9.2 %collective-permute-start.22 = (bf16[192,1024]{1,0:T(8,128)(2,1)S(1)}, bf16[192,1024]{1,0:T(8,128)(2,1)S(1)}, u32[]{:S(2)}, u32[]{:S(2)}) collective-permute-start(bf16[192,1024]{1,0:T(8,128)(2,1)S(1)} %maximum_maximum_fusion.refs_0_), channel_id=1, source_target_pairs={{4,8},{5,9},{6,10},{7,11},{8,4},{9,5},{10,6},{11,7},{20,24},{21,25... | collective-permute-start | bytes 1179656 | tf_op jit(solution)/shard_map/ppermute | solution.py:831
  129.8 14.0 %collective-permute-start.23 = (bf16[192,1024]{1,0:T(8,128)(2,1)S(1)}, bf16[192,1024]{1,0:T(8,128)(2,1)S(1)}, u32[]{:S(2)}, u32[]{:S(2)}) collective-permute-start(bf16[192,1024]{1,0:T(8,128)(2,1)S(1)} %collective-permute-done.22), channel_id=1, source_target_pairs={{4,0},{5,1},{6,2},{7,3},{8,12},{9,13},{10,14},{11,15},{20,16},{21,... | collective-permute-start | bytes 1179656 | tf_op jit(solution)/shard_map/ppermute | solution.py:831
  131.1 12.7 %collective-permute-start.24 = (bf16[192,1024]{1,0:T(8,128)(2,1)S(1)}, bf16[192,1024]{1,0:T(8,128)(2,1)S(1)}, u32[]{:S(2)}, u32[]{:S(2)}) collective-permute-start(bf16[192,1024]{1,0:T(8,128)(2,1)S(1)} %collective-permute-done.21.refs_2_), channel_id=1, source_target_pairs={{4,8},{5,9},{6,10},{7,11},{8,4},{9,5},{10,6},{11,7},{20,24},{21,25... | collective-permute-start | bytes 1179656 | tf_op jit(solution)/shard_map/ppermute | solution.py:831
  131.8 12.0 %collective-permute-start.25 = (bf16[192,1024]{1,0:T(8,128)(2,1)S(1)}, bf16[192,1024]{1,0:T(8,128)(2,1)S(1)}, u32[]{:S(2)}, u32[]{:S(2)}) collective-permute-start(bf16[192,1024]{1,0:T(8,128)(2,1)S(1)} %collective-permute-done.21.refs_2_), channel_id=1, source_target_pairs={{0,2},{1,3},{2,0},{3,1},{4,6},{5,7},{6,4},{7,5},{8,10},{9,11},{10,... | collective-permute-start | bytes 1179656 | tf_op jit(solution)/shard_map/ppermute | solution.py:828
  143.9 13.2 %collective-permute-start.26 = (bf16[192,1024]{1,0:T(8,128)(2,1)S(1)}, bf16[192,1024]{1,0:T(8,128)(2,1)S(1)}, u32[]{:S(2)}, u32[]{:S(2)}) collective-permute-start(bf16[192,1024]{1,0:T(8,128)(2,1)S(1)} %broadcast_select_fusion.1.refs_1_), channel_id=1, source_target_pairs={{4,0},{5,1},{6,2},{7,3},{8,12},{9,13},{10,14},{11,15},{20,16},{21,... | collective-permute-start | bytes 1179656 | tf_op jit(solution)/shard_map/ppermute | solution.py:831
  145.3 12.5 %collective-permute-start.27 = (bf16[192,1024]{1,0:T(8,128)(2,1)S(1)}, bf16[192,1024]{1,0:T(8,128)(2,1)S(1)}, u32[]{:S(2)}, u32[]{:S(2)}) collective-permute-start(bf16[192,1024]{1,0:T(8,128)(2,1)S(1)} %broadcast_select_fusion.1.refs_1_), channel_id=1, source_target_pairs={{0,2},{1,3},{2,0},{3,1},{4,6},{5,7},{6,4},{7,5},{8,10},{9,11},{10,... | collective-permute-start | bytes 1179656 | tf_op jit(solution)/shard_map/ppermute | solution.py:828
  146.1 13.4 %collective-permute-start.30 = (bf16[4,160,128]{2,1,0:T(8,128)(2,1)S(1)}, bf16[4,160,128]{2,1,0:T(8,128)(2,1)S(1)}, u32[]{:S(2)}, u32[]{:S(2)}) collective-permute-start(bf16[4,160,128]{2,1,0:T(8,128)(2,1)S(1)} %get-tuple-element.165), channel_id=1, source_target_pairs={{0,2},{1,3},{2,0},{3,1},{4,6},{5,7},{6,4},{7,5},{8,10},{9,11},{10,... | collective-permute-start | bytes 491528 | tf_op jit(solution)/shard_map/ppermute | solution.py:692
  158.9 13.6 %collective-permute-start.28 = (bf16[192,1024]{1,0:T(8,128)(2,1)S(1)}, bf16[192,1024]{1,0:T(8,128)(2,1)S(1)}, u32[]{:S(2)}, u32[]{:S(2)}) collective-permute-start(bf16[192,1024]{1,0:T(8,128)(2,1)S(1)} %broadcast_select_fusion.refs_3_), channel_id=1, source_target_pairs={{0,2},{1,3},{2,0},{3,1},{4,6},{5,7},{6,4},{7,5},{8,10},{9,11},{10,... | collective-permute-start | bytes 1179656 | tf_op jit(solution)/shard_map/ppermute | solution.py:828
  159.6 24.8 %collective-permute-start.31 = (bf16[8,160,128]{2,1,0:T(8,128)(2,1)S(1)}, bf16[8,160,128]{2,1,0:T(8,128)(2,1)}, u32[]{:S(2)}, u32[]{:S(2)}) collective-permute-start(bf16[8,160,128]{2,1,0:T(8,128)(2,1)S(1)} %bitcast.43), channel_id=1, source_target_pairs={{0,16},{16,0},{1,17},{17,1},{2,18},{18,2},{3,19},{19,3},{4,20},{20... | collective-permute-start | bytes 983048 | tf_op jit(solution)/shard_map/ppermute | solution.py:695
  176.7 15.8 %all-to-all-start.2 = ((bf16[8,24,640]{2,1,0:T(8,128)(2,1)}), bf16[8,24,640]{2,1,0:T(8,128)(2,1)S(1)}, u32[]{:S(2)}, u32[]{:S(2)}) async-start(bf16[8,24,640]{2,1,0:T(8,128)(2,1)} %bitcast.16), calls=%async_computation.2 | async-start | bytes 491520 | tf_op jit(solution)/shard_map/all_to_all | solution.py:698
  184.4 2.3 %collective-permute-start.33 = (bf16[8,160,128]{2,1,0:T(8,128)(2,1)}, bf16[8,160,128]{2,1,0:T(8,128)(2,1)S(1)}, u32[]{:S(2)}, u32[]{:S(2)}) collective-permute-start(bf16[8,160,128]{2,1,0:T(8,128)(2,1)} %collective-permute-done.31.far), channel_id=1, source_target_pairs={{0,1},{1,0},{2,3},{3,2},{4,5},{5,4},{6,7},{7,6},{8,9},{9,8},{10,11... | collective-permute-start | bytes 983048 | tf_op jit(solution)/shard_map/ppermute | solution.py:692
  (19 other events, 199.6 us)

commit v4 on v3

--- a/solution.py
+++ b/solution.py
@@ -656,9 +656,9 @@
 
 Z_COUNT = 4
 PART_ROWS = (192, 192)
-SPLIT_GATHER = False
-TIE_SUMS = True
-CALLS = ((0, 1, 2), (3, 4, 5, 6), (7,))
+TIE_FIRST = True
+TIE_SECOND = False
+TIE_KEYS = True
 
 
 def after(values, *earlier):
@@ -743,13 +743,19 @@
 
     cosine, sine = rotation_tables(count)
     heads_width = wq_codes.shape[1] // ranks
+    by_z = jnp.stack(by_z)
+    my_y = chip % y_count
+    here = lax.dynamic_index_in_dim(by_z, my_y, 1, keepdims=False)
+    there = swap(lax.dynamic_index_in_dim(by_z, 1 - my_y, 1, keepdims=False), 2)
     own_kv, other_kv, held = [], [], []
     start, share = 0, count // ranks
     for part, part_rows in enumerate(PART_ROWS):
         kept, *sums = join_partials(home[part], got[part])
         sums = [swap(value, 4 * (k + 1)) for k, value in enumerate(sums)]
-        if TIE_SUMS and part + 1 < len(PART_ROWS):
+        if part + 1 < len(PART_ROWS):
             got[part + 1], *sums = lax.optimization_barrier((got[part + 1], *sums))
+        if part == 1 and TIE_KEYS:
+            kept, there = lax.optimization_barrier((kept, there))
         queries, kv = make_heads(core, [kept, *sums], start, q_gain, k_gain, cosine, sine)
         own_kv.append(kv)
         other_kv.append(swap(kv, 1))
@@ -759,10 +765,6 @@
     wo_rows = wo_codes.T
     out_codes = [wo_rows, swap(wo_rows, 1)]
 
-    by_z = jnp.stack(by_z)
-    my_y = chip % y_count
-    here = lax.dynamic_index_in_dim(by_z, my_y, 1, keepdims=False)
-    there = swap(lax.dynamic_index_in_dim(by_z, 1 - my_y, 1, keepdims=False), 2)
     own_keys = jnp.stack([here, there], axis=1).reshape(chips, half, HEAD_SIZE)
     far_keys = swap_groups(own_keys)
     own_keys = (own_keys, far_keys)
@@ -770,25 +772,14 @@
         jnp.stack([core, group, chip]), [*own_keys, *(swap(value, 1) for value in own_keys)]
     )
 
-    if not SPLIT_GATHER:
-        held = [jnp.concatenate(held, axis=0)]
-    columns = []
-    for block in held:
-        blocks = gather_chips(block, chips, y_count)
-        total = None
-        for chosen in CALLS:
-            total = out_project(
-                core,
-                my_rank,
-                [blocks[bits] for bits in chosen],
-                chip ^ jnp.array(chosen, jnp.int32),
-                out_codes,
-                wo_scale,
-                total,
-                chosen == CALLS[-1],
-            )
-        columns.append(total)
-    columns = to_chips(jnp.concatenate(columns, axis=0).reshape(chips, share, -1))
+    def add_blocks(total, blocks, numbers, last=False):
+        chips_of = chip ^ jnp.array(numbers, jnp.int32)
+        return out_project(
+            core, my_rank, blocks, chips_of, out_codes, wo_scale, total, last
+        )
+
+    total = gather_project(jnp.concatenate(held, axis=0), add_blocks, y_count)
+    columns = to_chips(total.reshape(chips, share, -1))
     attn_out = jnp.transpose(columns, (1, 0, 2)).reshape(share, -1)
     return attn_out, synced
 
@@ -820,47 +811,52 @@
     return out.reshape(1, -1, width)
 
 
-def gather_chips(block, chips, y_count):
-    ranks = 2 * chips
+def hop(values, pairs, along, ranks):
+    moves = [(a * along + rest, b * along + rest) for a, b in pairs for rest in range(along)]
+    return lax.ppermute(values, "fsdp", moves)
+
+
+NEXT = [(0, 1), (1, 0), (2, 3), (3, 2)]
+MIDDLE = [(1, 2), (2, 1)]
+OUTWARD = [(1, 0), (2, 3)]
+
+
+def gather_project(block, add_blocks, y_count):
     along = 2 * y_count
-
-    def swap(values, bits):
-        return lax.ppermute(values, "fsdp", [(i, i ^ bits) for i in range(ranks)])
-
-    def hop(values, pairs):
-        return lax.ppermute(
-            values,
-            "fsdp",
-            [(a * along + rest, b * along + rest) for a, b in pairs for rest in range(along)],
-        )
-
-    middle, outward = [(1, 2), (2, 1)], [(1, 0), (2, 3)]
+    ranks = Z_COUNT * along
+    together = lax.optimization_barrier
+
+    def swap_y(values):
+        return lax.ppermute(values, "fsdp", [(i, i ^ 2) for i in range(ranks)])
+
     z_index = lax.axis_index("fsdp") // along
     at_end = (z_index == 0) | (z_index == Z_COUNT - 1)
-    across = swap(block, 2)
-    one = swap(block, along)
-    inner = hop(block, middle)
-    across, one, inner = lax.optimization_barrier((across, one, inner))
-    two_end = hop(inner, outward)
-    two_inner = hop(one, middle)
-    one_across = swap(one, 2)
-    two_end, two_inner, one_across = lax.optimization_barrier((two_end, two_inner, one_across))
+    across, one, inner = together(
+        (swap_y(block), hop(block, NEXT, along, ranks), hop(block, MIDDLE, along, ranks))
+    )
+    total = add_blocks(None, [block, across, one], (0, 1, 2))
+    two_end, two_inner, one_across = (
+        hop(inner, OUTWARD, along, ranks),
+        hop(one, MIDDLE, along, ranks),
+        swap_y(one),
+    )
+    if TIE_FIRST:
+        two_end, two_inner, one_across, total = together((two_end, two_inner, one_across, total))
+    else:
+        two_end, two_inner, one_across = together((two_end, two_inner, one_across))
     two = jnp.where(at_end, two_end, two_inner)
-    three_end = hop(two, outward)
-    two_across = swap(two, 2)
-    three_end, two_across = lax.optimization_barrier((three_end, two_across))
+    three_end, two_across = hop(two, OUTWARD, along, ranks), swap_y(two)
+    if TIE_SECOND:
+        total = add_blocks(total, [one_across, two], (3, 4))
+        three_end, two_across, total = together((three_end, two_across, total))
+        rest, numbers = [two_across], (5, 6)
+    else:
+        three_end, two_across = together((three_end, two_across))
+        rest, numbers = [one_across, two, two_across], (3, 4, 5, 6)
     three = jnp.where(at_end, three_end, inner)
-    three_across = swap(three, 2)
-    return {
-        0: block,
-        1: across,
-        2: one,
-        3: one_across,
-        4: two,
-        5: two_across,
-        6: three,
-        7: three_across,
-    }
+    three_across = swap_y(three)
+    total = add_blocks(total, [*rest, three], numbers)
+    return add_blocks(total, [three_across], (7,), True)
 
 
 def solution(mesh):

time: 194 us -> 184 us (0.948)
  waiting for transfers between devices: 78.6 us -> 69.6 us
  starting transfers between devices: 50.9 us -> 47.7 us
  local copies, waits for them, and re-layouts: 7.62 us -> 10.1 us
    ppermute x27 -> x22, waiting for transfers between devices: 55.8 us -> 39.3 us  [swap(): return lax.ppermute(values, 'fsdp', [(i, i ^ bits) for i in range(ranks)])]
    ppermute x4 -> x9, starting transfers between devices: 4.11 us -> 10.7 us  [the longest x5 7.3 us: hop(): return lax.ppermute(values, 'fsdp', moves)]
    ppermute x27 -> x22, starting transfers between devices: 28.8 us -> 22.7 us  [swap(): return lax.ppermute(values, 'fsdp', [(i, i ^ bits) for i in range(ranks)])]
    ppermute x4 -> x9, waiting for transfers between devices: 20.4 us -> 25.5 us  [the longest x5 19.7 us: hop(): return lax.ppermute(values, 'fsdp', moves)]
    all_to_all x2, starting transfers between devices: 15 us -> 11.2 us  [to_chips(): lax.all_to_all(values, 'fsdp', split_axis=0, concat_axis=0, tiled=True, a...]
    all_to_all x2, waiting for transfers between devices: 0.59 us -> 2.69 us  [to_chips(): lax.all_to_all(values, 'fsdp', split_axis=0, concat_axis=0, tiled=True, a...]
    unnamed x34 -> x50, local copies, waits for them, and re-layouts: 4.95 us -> 6.81 us
  transfers between devices with their start and end apart: 35 -> 35, of which waited for: 17 -> 15; matrix products, arithmetic and copies ran while one was open for 2% -> 3% of each run, Pallas kernels for 24% -> 28%
where the time goes in v4:
time: 184 us; the launch traced here: 183 us
  waiting for transfers between devices  69.6 us (38%)
  Pallas kernels  51.3 us (28%)
  starting transfers between devices  47.7 us (26%)
  local copies, waits for them, and re-layouts  10.1 us (5%)
  other arithmetic  2.66 us (1%)
    ppermute x22, waiting for transfers between devices, swap(): return lax.ppermute(values, 'fsdp', [(i, i ^ bits) for i in range(ranks)])  39.3 us
    ppermute x22, starting transfers between devices, swap(): return lax.ppermute(values, 'fsdp', [(i, i ^ bits) for i in range(ranks)])  22.7 us
    ppermute x5, waiting for transfers between devices, hop(): return lax.ppermute(values, 'fsdp', moves)  19.7 us
    pallas_call x3, Pallas kernels, out_project(): pl.pallas_call(functools.partial(out_kernel, blocks, bool(extra), last, b...  15.3 us
    all_to_all x2, starting transfers between devices, to_chips(): lax.all_to_all(values, 'fsdp', split_axis=0, concat_axis=0, tiled=True, a...  11.2 us
    pallas_call x2, Pallas kernels, project(): pl.pallas_call(project_kernel, grid=(blocks,), in_specs=[SMEM, pl.BlockSp...  9.75 us
    pallas_call x1, Pallas kernels, prepare_weights(): pl.pallas_call(weight_kernel, grid_spec=pltpu.PrefetchScalarGridSpec(num_...  8.51 us
    ppermute x5, starting transfers between devices, hop(): return lax.ppermute(values, 'fsdp', moves)  7.3 us
  transfers between devices with their start and end apart: 35, of which 15 were waited for; matrix products, arithmetic and copies ran while one was open for 3% of the time, Pallas kernels for 28%

profile of v4, /device:TPU:0, one launch (start us, length us, event | category | flops | bytes accessed | tf_op | source)
XLA Modules:
  0.0 183.1 jit_solution(14221662217214368802)
XLA Ops:
  2.6 5.3 %pick_rows.2 = bf16[8,32,640]{2,1,0:T(8,128)(2,1)} custom-call(s32[1]{0:T(128)} %constant.154.clone.1.info, f32[8,384]{1,0:T(8,128)S(1)} %get-tuple-element.234.rows, f32[1,5120]{1,0:T(1,128)} %bitcast.57, bf16[600,5120]{1,0:T(8,128)(2,1)} %table.1), custom_call_target="tpu_custom_call" | custom-call | flops 196608000 | bytes 6144000 | tf_op jit(solution)/shard_map/pick_rows/pallas_call | solution.py:281
  8.0 6.8 %all-to-all-start.1 = ((bf16[8,32,640]{2,1,0:T(8,128)(2,1)}), bf16[8,32,640]{2,1,0:T(8,128)(2,1)S(1)}, u32[]{:S(2)}, u32[]{:S(2)}) async-start(bf16[8,32,640]{2,1,0:T(8,128)(2,1)} %pick_rows.2), calls=%async_computation.1 | async-start | bytes 655360 | tf_op jit(solution)/shard_map/all_to_all | solution.py:698
  15.1 8.5 %prepare_weights.1 = (bf16[8,320,640]{2,1,0:T(8,128)(2,1)}, bf16[4,320,640]{2,1,0:T(8,128)(2,1)S(1)}, bf16[4,320,640]{2,1,0:T(8,128)(2,1)S(1)}, bf16[8,320,128]{2,1,0:T(8,128)(2,1)S(1)}) custom-call(s32[2]{0:T(128)S(1)} %pad_add_fusion.3.info, s32[8]{0:T(128)S(1)} %add_xor_fusion.order, s32[8]{0:T(128)S(1)} %copy-done.10, f32[40,64]{1,0:T(8,128)S(1)} %copy-done.7, ...), custom_call_target="tpu_custom_call" | custom-call | flops 20971520 | bytes 15728640 | tf_op jit(solution)/shard_map/prepare_weights/pallas_call | solution.py:379
  28.9 2.0 %collective-permute-done.2 = f32[8,128]{1,0:T(8,128)S(1)} collective-permute-done((f32[8,128]{1,0:T(8,128)S(1)}, f32[8,128]{1,0:T(8,128)S(1)}, u32[]{:S(2)}, u32[]{:S(2)}) %collective-permute-start.2) | collective-permute-done | bytes 4128 | tf_op jit(solution)/shard_map/ppermute | solution.py:695
  33.4 5.5 %project.2 = (bf16[4,192,640]{2,1,0:T(8,128)(2,1)}, bf16[4,192,640]{2,1,0:T(8,128)(2,1)}) custom-call(s32[1]{0:T(128)} %bitcast.5.info, bf16[384,640]{1,0:T(8,128)(2,1)S(1)} %get-tuple-element.101.normed, bf16[8,320,640]{2,1,0:T(8,128)(2,1)} %get-tuple-element.103.own, bf16[4,320,640]{2,1,0:T(8,128)(2,1)} %collective-permute-done.3.other), custom_call_target="tpu_custom_call" | custom-call | flops 1258291200 | bytes 5242880 | tf_op jit(solution)/shard_map/project/pallas_call | solution.py:435
  38.9 2.0 %collective-permute-start.5 = (bf16[4,192,640]{2,1,0:T(8,128)(2,1)}, bf16[4,192,640]{2,1,0:T(8,128)(2,1)}, u32[]{:S(2)}, u32[]{:S(2)}) collective-permute-start(bf16[4,192,640]{2,1,0:T(8,128)(2,1)} %get-tuple-element.106), channel_id=1, source_target_pairs={{0,2},{1,3},{2,0},{3,1},{4,6},{5,7},{6,4},{7,5},{8,10},{9,11},{10,... | collective-permute-start | bytes 2949128 | tf_op jit(solution)/shard_map/ppermute | solution.py:692
  41.7 2.0 %collective-permute-start.6 = (bf16[2,160,128]{2,1,0:T(8,128)(2,1)S(1)}, bf16[2,160,128]{2,1,0:T(8,128)(2,1)}, u32[]{:S(2)}, u32[]{:S(2)}) collective-permute-start(bf16[2,160,128]{2,1,0:T(8,128)(2,1)S(1)} %get-tuple-element.168), channel_id=1, source_target_pairs={{0,4},{1,5},{2,6},{3,7},{4,0},{5,1},{6,2},{7,3},{8,12},{9,13},{10,... | collective-permute-start | bytes 245768 | tf_op jit(solution)/shard_map/ppermute | solution.py:692
  43.7 2.6 %collective-permute-done.6 = bf16[2,160,128]{2,1,0:T(8,128)(2,1)} collective-permute-done((bf16[2,160,128]{2,1,0:T(8,128)(2,1)S(1)}, bf16[2,160,128]{2,1,0:T(8,128)(2,1)}, u32[]{:S(2)}, u32[]{:S(2)}) %collective-permute-start.6) | collective-permute-done | bytes 81952 | tf_op jit(solution)/shard_map/ppermute | solution.py:692
  46.3 2.9 %collective-permute-start.7 = (bf16[2,160,128]{2,1,0:T(8,128)(2,1)S(1)}, bf16[2,160,128]{2,1,0:T(8,128)(2,1)S(1)}, u32[]{:S(2)}, u32[]{:S(2)}) collective-permute-start(bf16[2,160,128]{2,1,0:T(8,128)(2,1)S(1)} %get-tuple-element.167), channel_id=1, source_target_pairs={{0,8},{1,9},{2,10},{3,11},{4,12},{5,13},{6,14},{7,15},{8,0},{9,1},... | collective-permute-start | bytes 245768 | tf_op jit(solution)/shard_map/ppermute | solution.py:692
  53.2 4.3 %project.3 = (f32[4,192,640]{2,1,0:T(8,128)S(1)}, f32[4,192,640]{2,1,0:T(8,128)S(1)}) custom-call(s32[1]{0:T(128)} %bitcast.12.info, bf16[384,640]{1,0:T(8,128)(2,1)} %copy-done.13, bf16[8,320,640]{2,1,0:T(8,128)(2,1)} %get-tuple-element.103.own, bf16[4,320,640]{2,1,0:T(8,128)(2,1)S(1)} %copy-done.2), custom_call_target="tpu_custom_call" | custom-call | flops 1258291200 | bytes 5242880 | tf_op jit(solution)/shard_map/project/pallas_call | solution.py:435
  57.5 6.3 %collective-permute-done.5.got = bf16[4,192,640]{2,1,0:T(8,128)(2,1)} collective-permute-done((bf16[4,192,640]{2,1,0:T(8,128)(2,1)}, bf16[4,192,640]{2,1,0:T(8,128)(2,1)}, u32[]{:S(2)}, u32[]{:S(2)}) %collective-permute-start.5) | collective-permute-done | bytes 983072 | tf_op jit(solution)/shard_map/ppermute | solution.py:692
  63.8 2.1 %join_partials.2 = (f32[192,640]{1,0:T(8,128)S(1)}, bf16[192,640]{1,0:T(8,128)(2,1)}, bf16[192,640]{1,0:T(8,128)(2,1)}, bf16[192,640]{1,0:T(8,128)(2,1)}) custom-call(f32[4,192,640]{2,1,0:T(8,128)S(1)} %get-tuple-element.111.own, bf16[4,192,640]{2,1,0:T(8,128)(2,1)} %collective-permute-done.5.got), custom_call_target="tpu_custom_call" | custom-call | flops 983040 | bytes 3932160 | tf_op jit(solution)/shard_map/join_partials/pallas_call | solution.py:464
  66.7 2.1 %collective-permute-start.10 = (bf16[192,640]{1,0:T(8,128)(2,1)}, bf16[192,640]{1,0:T(8,128)(2,1)S(1)}, u32[]{:S(2)}, u32[]{:S(2)}) collective-permute-start(bf16[192,640]{1,0:T(8,128)(2,1)} %get-tuple-element.115), channel_id=1, source_target_pairs={{0,4},{1,5},{2,6},{3,7},{4,0},{5,1},{6,2},{7,3},{8,12},{9,13},{10,... | collective-permute-start | bytes 737288 | tf_op jit(solution)/shard_map/ppermute | solution.py:692
  68.8 2.4 %collective-permute-start.11 = (bf16[192,640]{1,0:T(8,128)(2,1)}, bf16[192,640]{1,0:T(8,128)(2,1)S(1)}, u32[]{:S(2)}, u32[]{:S(2)}) collective-permute-start(bf16[192,640]{1,0:T(8,128)(2,1)} %get-tuple-element.116), channel_id=1, source_target_pairs={{0,8},{1,9},{2,10},{3,11},{4,12},{5,13},{6,14},{7,15},{8,0},{9,1},... | collective-permute-start | bytes 737288 | tf_op jit(solution)/shard_map/ppermute | solution.py:692
  72.9 11.0 %collective-permute-done.9.got = bf16[4,192,640]{2,1,0:T(8,128)(2,1)S(1)} collective-permute-done((bf16[4,192,640]{2,1,0:T(8,128)(2,1)}, bf16[4,192,640]{2,1,0:T(8,128)(2,1)S(1)}, u32[]{:S(2)}, u32[]{:S(2)}) %collective-permute-start.9) | collective-permute-done | bytes 983072 | tf_op jit(solution)/shard_map/ppermute | solution.py:692
  83.9 1.7 collective-permute-start.15
  85.7 2.7 %collective-permute-done.11.refs_2_ = bf16[192,640]{1,0:T(8,128)(2,1)S(1)} collective-permute-done((bf16[192,640]{1,0:T(8,128)(2,1)}, bf16[192,640]{1,0:T(8,128)(2,1)S(1)}, u32[]{:S(2)}, u32[]{:S(2)}) %collective-permute-start.11) | collective-permute-done | bytes 245792 | tf_op jit(solution)/shard_map/ppermute | solution.py:692
  88.6 3.4 %collective-permute-start.16 = (bf16[192,640]{1,0:T(8,128)(2,1)S(1)}, bf16[192,640]{1,0:T(8,128)(2,1)S(1)}, u32[]{:S(2)}, u32[]{:S(2)}) collective-permute-start(bf16[192,640]{1,0:T(8,128)(2,1)S(1)} %get-tuple-element.133), channel_id=1, source_target_pairs={{0,4},{1,5},{2,6},{3,7},{4,0},{5,1},{6,2},{7,3},{8,12},{9,13},{10,... | collective-permute-start | bytes 737288 | tf_op jit(solution)/shard_map/ppermute | solution.py:692
  95.4 1.8 %make_heads.2 = (bf16[4,192,128]{2,1,0:T(8,128)(2,1)S(1)}, bf16[192,128]{1,0:T(8,128)(2,1)S(1)}) custom-call(s32[1]{0:T(128)} %bitcast.5.info, f32[192,640]{1,0:T(8,128)S(1)} %copy-done.4, bf16[192,640]{1,0:T(8,128)(2,1)S(1)} %collective-permute-done.10.refs_1_, bf16[192,640]{1,0:T(8,128)(2,1)S(1)} %collective-permute-done.11.refs_2_, ...), custom_call_target="tpu_custom_call" | custom-call | flops 2457600 | bytes 1720320 | tf_op jit(solution)/shard_map/make_heads/pallas_call | solution.py:510
  98.8 12.4 %collective-permute-done.17.refs_2_ = bf16[192,640]{1,0:T(8,128)(2,1)S(1)} collective-permute-done((bf16[192,640]{1,0:T(8,128)(2,1)S(1)}, bf16[192,640]{1,0:T(8,128)(2,1)S(1)}, u32[]{:S(2)}, u32[]{:S(2)}) %collective-permute-start.17) | collective-permute-done | bytes 245792 | tf_op jit(solution)/shard_map/ppermute | solution.py:692
  117.7 3.2 %collective-permute-start.22 = (bf16[192,1024]{1,0:T(8,128)(2,1)S(1)}, bf16[192,1024]{1,0:T(8,128)(2,1)S(1)}, u32[]{:S(2)}, u32[]{:S(2)}) collective-permute-start(bf16[192,1024]{1,0:T(8,128)(2,1)S(1)} %maximum_maximum_fusion.refs_0_), channel_id=1, source_target_pairs={{0,4},{1,5},{2,6},{3,7},{4,0},{5,1},{6,2},{7,3},{8,12},{9,13},{10,... | collective-permute-start | bytes 1179656 | tf_op jit(solution)/shard_map/ppermute | solution.py:816
  121.6 5.8 %collective-permute-done.21.refs_1_ = bf16[192,1024]{1,0:T(8,128)(2,1)S(1)} collective-permute-done((bf16[192,1024]{1,0:T(8,128)(2,1)S(1)}, bf16[192,1024]{1,0:T(8,128)(2,1)S(1)}, u32[]{:S(2)}, u32[]{:S(2)}) %collective-permute-start.21) | collective-permute-done | bytes 393248 | tf_op jit(solution)/shard_map/ppermute | solution.py:830
  127.4 2.6 %collective-permute-done.22.refs_2_ = bf16[192,1024]{1,0:T(8,128)(2,1)S(1)} collective-permute-done((bf16[192,1024]{1,0:T(8,128)(2,1)S(1)}, bf16[192,1024]{1,0:T(8,128)(2,1)S(1)}, u32[]{:S(2)}, u32[]{:S(2)}) %collective-permute-start.22) | collective-permute-done | bytes 393248 | tf_op jit(solution)/shard_map/ppermute | solution.py:816
  133.1 5.2 %out_project.3.refs_6_ = f32[2,320,192]{2,1,0:T(8,128)S(1)} custom-call(s32[5]{0:T(128)S(1)} %pad_add_fusion.4.info, f32[64,40]{1,0:T(8,128)S(1)} %copy.20.scales, bf16[192,1024]{1,0:T(8,128)(2,1)S(1)} %maximum_maximum_fusion.refs_0_, bf16[192,1024]{1,0:T(8,128)(2,1)S(1)} %collective-permute-done.21.refs_1_, ...), custom_call_target="tpu_custom_call" | custom-call | flops 754974720 | bytes 3932160 | tf_op jit(solution)/shard_map/out_project/pallas_call | solution.py:631
  138.2 5.5 %collective-permute-done.24 = bf16[192,1024]{1,0:T(8,128)(2,1)S(1)} collective-permute-done((bf16[192,1024]{1,0:T(8,128)(2,1)S(1)}, bf16[192,1024]{1,0:T(8,128)(2,1)S(1)}, u32[]{:S(2)}, u32[]{:S(2)}) %collective-permute-start.24) | collective-permute-done | bytes 393248 | tf_op jit(solution)/shard_map/ppermute | solution.py:816
  145.7 11.6 %collective-permute-done.28 = bf16[192,1024]{1,0:T(8,128)(2,1)S(1)} collective-permute-done((bf16[192,1024]{1,0:T(8,128)(2,1)S(1)}, bf16[192,1024]{1,0:T(8,128)(2,1)S(1)}, u32[]{:S(2)}, u32[]{:S(2)}) %collective-permute-start.28) | collective-permute-done | bytes 393248 | tf_op jit(solution)/shard_map/ppermute | solution.py:816
  158.1 1.6 collective-permute-start.31
  159.7 6.1 %out_project.4.refs_3_ = f32[2,320,192]{2,1,0:T(8,128)S(1)} custom-call(s32[6]{0:T(128)S(1)} %pad_add_fusion.5.info, f32[64,40]{1,0:T(8,128)S(1)} %copy.20.scales, bf16[192,1024]{1,0:T(8,128)(2,1)S(1)} %collective-permute-done.26.refs_0_, bf16[192,1024]{1,0:T(8,128)(2,1)S(1)} %broadcast_select_fusion.1.refs_1_, ...), custom_call_target="tpu_custom_call" | custom-call | flops 1006632960 | bytes 5242880 | tf_op jit(solution)/shard_map/out_project/pallas_call | solution.py:631
  165.8 4.1 %out_project.5 = bf16[192,640]{1,0:T(8,128)(2,1)} custom-call(s32[3]{0:T(128)S(1)} %pad_add_fusion.1.info, f32[64,40]{1,0:T(8,128)S(1)} %copy.20.scales, bf16[192,1024]{1,0:T(8,128)(2,1)S(1)} %collective-permute-done.30.refs_0_, bf16[320,8192]{1,0:T(8,128)(2,1)} %bitcast.54, bf16[320,8192]{1,0:T(8,128)(2,1)} %collective-permute-done.27.refs_4_.refs_5_.refs_2_, ...), custom_call_target="tpu_custom_call" | custom-call | flops 251658240 | bytes 1310720 | tf_op jit(solution)/shard_map/out_project/pallas_call | solution.py:631
  169.9 4.4 %all-to-all-start.2 = ((bf16[8,24,640]{2,1,0:T(8,128)(2,1)}), bf16[8,24,640]{2,1,0:T(8,128)(2,1)S(1)}, u32[]{:S(2)}, u32[]{:S(2)}) async-start(bf16[8,24,640]{2,1,0:T(8,128)(2,1)} %bitcast.21), calls=%async_computation.2 | async-start | bytes 491520 | tf_op jit(solution)/shard_map/all_to_all | solution.py:698
  176.4 3.3 %collect_keys.1 = bf16[8,2,2,160,128]{4,3,2,1,0:T(8,128)(2,1)} custom-call(s32[3]{0:T(128)S(1)} %pad_add_fusion.6.info, bf16[8,160,128]{2,1,0:T(8,128)(2,1)S(1)} %bitcast.45, bf16[8,160,128]{2,1,0:T(8,128)(2,1)S(1)} %collective-permute-done.31.far, bf16[8,160,128]{2,1,0:T(8,128)(2,1)S(1)} %collective-permute-done.32.other, ...), custom_call_target="tpu_custom_call" | custom-call | bytes 2621440 | tf_op jit(solution)/shard_map/collect_keys/pallas_call | solution.py:798
  179.7 2.7 %all-to-all-done.2 = bf16[8,24,640]{2,1,0:T(8,128)(2,1)S(1)} async-done(((bf16[8,24,640]{2,1,0:T(8,128)(2,1)}), bf16[8,24,640]{2,1,0:T(8,128)(2,1)S(1)}, u32[]{:S(2)}, u32[]{:S(2)}) %all-to-all-start.2) | async-done | bytes 245792 | tf_op jit(solution)/shard_map/all_to_all | solution.py:698
  (130 shorter events, 38.2 us)
Async XLA Ops:
  0.6 132.4 %collective-permute-start.27 = (bf16[320,8192]{1,0:T(8,128)(2,1)}, bf16[320,8192]{1,0:T(8,128)(2,1)}, u32[]{:S(2)}, u32[]{:S(2)}) collective-permute-start(bf16[320,8192]{1,0:T(8,128)(2,1)} %bitcast.51), channel_id=1, source_target_pairs={{0,1},{1,0},{2,3},{3,2},{4,5},{5,4},{6,7},{7,6},{8,9},{9,8},{10,11... | collective-permute-start | bytes 15728648 | tf_op jit(solution)/shard_map/ppermute | solution.py:692
  8.0 18.8 %all-to-all-start.1 = ((bf16[8,32,640]{2,1,0:T(8,128)(2,1)}), bf16[8,32,640]{2,1,0:T(8,128)(2,1)S(1)}, u32[]{:S(2)}, u32[]{:S(2)}) async-start(bf16[8,32,640]{2,1,0:T(8,128)(2,1)} %pick_rows.2), calls=%async_computation.1 | async-start | bytes 655360 | tf_op jit(solution)/shard_map/all_to_all | solution.py:698
  26.8 6.6 %collective-permute-start.3 = (bf16[4,320,640]{2,1,0:T(8,128)(2,1)}, bf16[4,320,640]{2,1,0:T(8,128)(2,1)}, u32[]{:S(2)}, u32[]{:S(2)}) collective-permute-start(bf16[4,320,640]{2,1,0:T(8,128)(2,1)} %copy-done.12), channel_id=1, source_target_pairs={{0,1},{1,0},{2,3},{3,2},{4,5},{5,4},{6,7},{7,6},{8,9},{9,8},{10,11... | collective-permute-start | bytes 4915208 | tf_op jit(solution)/shard_map/ppermute | solution.py:692
  27.0 4.4 %collective-permute-start.1 = (bf16[8,32,640]{2,1,0:T(8,128)(2,1)S(1)}, bf16[8,32,640]{2,1,0:T(8,128)(2,1)S(1)}, u32[]{:S(2)}, u32[]{:S(2)}) collective-permute-start(bf16[8,32,640]{2,1,0:T(8,128)(2,1)S(1)} %all-to-all-done.1), channel_id=1, source_target_pairs={{0,1},{1,0},{2,3},{3,2},{4,5},{5,4},{6,7},{7,6},{8,9},{9,8},{10,11... | collective-permute-start | bytes 983048 | tf_op jit(solution)/shard_map/ppermute | solution.py:692
  27.3 3.6 %collective-permute-start.2 = (f32[8,128]{1,0:T(8,128)S(1)}, f32[8,128]{1,0:T(8,128)S(1)}, u32[]{:S(2)}, u32[]{:S(2)}) collective-permute-start(f32[8,128]{1,0:T(8,128)S(1)} %get-tuple-element.100), channel_id=1, source_target_pairs={{0,16},{16,0},{1,17},{17,1},{2,18},{18,2},{3,19},{19,3},{4,20},{20... | collective-permute-start | bytes 12296 | tf_op jit(solution)/shard_map/ppermute | solution.py:695
  28.8 20.3 %collective-permute-start.4 = (bf16[4,320,640]{2,1,0:T(8,128)(2,1)}, bf16[4,320,640]{2,1,0:T(8,128)(2,1)S(1)}, u32[]{:S(2)}, u32[]{:S(2)}) collective-permute-start(bf16[4,320,640]{2,1,0:T(8,128)(2,1)} %copy-done.11), channel_id=1, source_target_pairs={{0,1},{1,0},{2,3},{3,2},{4,5},{5,4},{6,7},{7,6},{8,9},{9,8},{10,11... | collective-permute-start | bytes 4915208 | tf_op jit(solution)/shard_map/ppermute | solution.py:692
  38.9 24.9 %collective-permute-start.5 = (bf16[4,192,640]{2,1,0:T(8,128)(2,1)}, bf16[4,192,640]{2,1,0:T(8,128)(2,1)}, u32[]{:S(2)}, u32[]{:S(2)}) collective-permute-start(bf16[4,192,640]{2,1,0:T(8,128)(2,1)} %get-tuple-element.106), channel_id=1, source_target_pairs={{0,2},{1,3},{2,0},{3,1},{4,6},{5,7},{6,4},{7,5},{8,10},{9,11},{10,... | collective-permute-start | bytes 2949128 | tf_op jit(solution)/shard_map/ppermute | solution.py:692
  40.9 43.0 %collective-permute-start.9 = (bf16[4,192,640]{2,1,0:T(8,128)(2,1)}, bf16[4,192,640]{2,1,0:T(8,128)(2,1)S(1)}, u32[]{:S(2)}, u32[]{:S(2)}) collective-permute-start(bf16[4,192,640]{2,1,0:T(8,128)(2,1)} %get-tuple-element.107), channel_id=1, source_target_pairs={{0,2},{1,3},{2,0},{3,1},{4,6},{5,7},{6,4},{7,5},{8,10},{9,11},{10,... | collective-permute-start | bytes 2949128 | tf_op jit(solution)/shard_map/ppermute | solution.py:692
  41.7 4.5 %collective-permute-start.6 = (bf16[2,160,128]{2,1,0:T(8,128)(2,1)S(1)}, bf16[2,160,128]{2,1,0:T(8,128)(2,1)}, u32[]{:S(2)}, u32[]{:S(2)}) collective-permute-start(bf16[2,160,128]{2,1,0:T(8,128)(2,1)S(1)} %get-tuple-element.168), channel_id=1, source_target_pairs={{0,4},{1,5},{2,6},{3,7},{4,0},{5,1},{6,2},{7,3},{8,12},{9,13},{10,... | collective-permute-start | bytes 245768 | tf_op jit(solution)/shard_map/ppermute | solution.py:692
  46.3 11.2 %collective-permute-start.7 = (bf16[2,160,128]{2,1,0:T(8,128)(2,1)S(1)}, bf16[2,160,128]{2,1,0:T(8,128)(2,1)S(1)}, u32[]{:S(2)}, u32[]{:S(2)}) collective-permute-start(bf16[2,160,128]{2,1,0:T(8,128)(2,1)S(1)} %get-tuple-element.167), channel_id=1, source_target_pairs={{0,8},{1,9},{2,10},{3,11},{4,12},{5,13},{6,14},{7,15},{8,0},{9,1},... | collective-permute-start | bytes 245768 | tf_op jit(solution)/shard_map/ppermute | solution.py:692
  50.3 7.2 %collective-permute-start.8 = (bf16[2,160,128]{2,1,0:T(8,128)(2,1)S(1)}, bf16[2,160,128]{2,1,0:T(8,128)(2,1)S(1)}, u32[]{:S(2)}, u32[]{:S(2)}) collective-permute-start(bf16[2,160,128]{2,1,0:T(8,128)(2,1)S(1)} %get-tuple-element.166), channel_id=1, source_target_pairs={{0,12},{1,13},{2,14},{3,15},{4,8},{5,9},{6,10},{7,11},{8,4},{9,5},... | collective-permute-start | bytes 245768 | tf_op jit(solution)/shard_map/ppermute | solution.py:692
  66.7 19.0 %collective-permute-start.10 = (bf16[192,640]{1,0:T(8,128)(2,1)}, bf16[192,640]{1,0:T(8,128)(2,1)S(1)}, u32[]{:S(2)}, u32[]{:S(2)}) collective-permute-start(bf16[192,640]{1,0:T(8,128)(2,1)} %get-tuple-element.115), channel_id=1, source_target_pairs={{0,4},{1,5},{2,6},{3,7},{4,0},{5,1},{6,2},{7,3},{8,12},{9,13},{10,... | collective-permute-start | bytes 737288 | tf_op jit(solution)/shard_map/ppermute | solution.py:692
  68.8 19.6 %collective-permute-start.11 = (bf16[192,640]{1,0:T(8,128)(2,1)}, bf16[192,640]{1,0:T(8,128)(2,1)S(1)}, u32[]{:S(2)}, u32[]{:S(2)}) collective-permute-start(bf16[192,640]{1,0:T(8,128)(2,1)} %get-tuple-element.116), channel_id=1, source_target_pairs={{0,8},{1,9},{2,10},{3,11},{4,12},{5,13},{6,14},{7,15},{8,0},{9,1},... | collective-permute-start | bytes 737288 | tf_op jit(solution)/shard_map/ppermute | solution.py:692
  71.1 17.3 %collective-permute-start.12 = (bf16[192,640]{1,0:T(8,128)(2,1)}, bf16[192,640]{1,0:T(8,128)(2,1)}, u32[]{:S(2)}, u32[]{:S(2)}) collective-permute-start(bf16[192,640]{1,0:T(8,128)(2,1)} %get-tuple-element.117), channel_id=1, source_target_pairs={{0,12},{1,13},{2,14},{3,15},{4,8},{5,9},{6,10},{7,11},{8,4},{9,5},... | collective-permute-start | bytes 737288 | tf_op jit(solution)/shard_map/ppermute | solution.py:692
  83.9 13.3 %collective-permute-start.15 = (bf16[4,160,128]{2,1,0:T(8,128)(2,1)S(1)}, bf16[4,160,128]{2,1,0:T(8,128)(2,1)S(1)}, u32[]{:S(2)}, u32[]{:S(2)}) collective-permute-start(bf16[4,160,128]{2,1,0:T(8,128)(2,1)S(1)} %get-tuple-element.171), channel_id=1, source_target_pairs={{0,2},{1,3},{2,0},{3,1},{4,6},{5,7},{6,4},{7,5},{8,10},{9,11},{10,... | collective-permute-start | bytes 491528 | tf_op jit(solution)/shard_map/ppermute | solution.py:692
  88.6 10.2 %collective-permute-start.16 = (bf16[192,640]{1,0:T(8,128)(2,1)S(1)}, bf16[192,640]{1,0:T(8,128)(2,1)S(1)}, u32[]{:S(2)}, u32[]{:S(2)}) collective-permute-start(bf16[192,640]{1,0:T(8,128)(2,1)S(1)} %get-tuple-element.133), channel_id=1, source_target_pairs={{0,4},{1,5},{2,6},{3,7},{4,0},{5,1},{6,2},{7,3},{8,12},{9,13},{10,... | collective-permute-start | bytes 737288 | tf_op jit(solution)/shard_map/ppermute | solution.py:692
  92.0 19.2 %collective-permute-start.17 = (bf16[192,640]{1,0:T(8,128)(2,1)S(1)}, bf16[192,640]{1,0:T(8,128)(2,1)S(1)}, u32[]{:S(2)}, u32[]{:S(2)}) collective-permute-start(bf16[192,640]{1,0:T(8,128)(2,1)S(1)} %get-tuple-element.134), channel_id=1, source_target_pairs={{0,8},{1,9},{2,10},{3,11},{4,12},{5,13},{6,14},{7,15},{8,0},{9,1},... | collective-permute-start | bytes 737288 | tf_op jit(solution)/shard_map/ppermute | solution.py:692
  92.9 18.2 %collective-permute-start.18 = (bf16[192,640]{1,0:T(8,128)(2,1)S(1)}, bf16[192,640]{1,0:T(8,128)(2,1)S(1)}, u32[]{:S(2)}, u32[]{:S(2)}) collective-permute-start(bf16[192,640]{1,0:T(8,128)(2,1)S(1)} %get-tuple-element.135), channel_id=1, source_target_pairs={{0,12},{1,13},{2,14},{3,15},{4,8},{5,9},{6,10},{7,11},{8,4},{9,5},... | collective-permute-start | bytes 737288 | tf_op jit(solution)/shard_map/ppermute | solution.py:692
  97.3 14.9 %collective-permute-start.13 = (bf16[192,128]{1,0:T(8,128)(2,1)S(1)}, bf16[192,128]{1,0:T(8,128)(2,1)S(1)}, u32[]{:S(2)}, u32[]{:S(2)}) collective-permute-start(bf16[192,128]{1,0:T(8,128)(2,1)S(1)} %get-tuple-element.122.refs_0_), channel_id=1, source_target_pairs={{0,1},{1,0},{2,3},{3,2},{4,5},{5,4},{6,7},{7,6},{8,9},{9,8},{10,11... | collective-permute-start | bytes 147464 | tf_op jit(solution)/shard_map/ppermute | solution.py:692
  113.0 1.9 %collective-permute-start.14 = (bf16[96,512]{1,0:T(8,128)(2,1)S(1)}, bf16[96,512]{1,0:T(8,128)(2,1)S(1)}, u32[]{:S(2)}, u32[]{:S(2)}) collective-permute-start(bf16[96,512]{1,0:T(8,128)(2,1)S(1)} %get-tuple-element.124), channel_id=1, source_target_pairs={{0,1},{1,0},{2,3},{3,2},{4,5},{5,4},{6,7},{7,6},{8,9},{9,8},{10,11... | collective-permute-start | bytes 294920 | tf_op jit(solution)/shard_map/ppermute | solution.py:692
  116.2 11.2 %collective-permute-start.21 = (bf16[192,1024]{1,0:T(8,128)(2,1)S(1)}, bf16[192,1024]{1,0:T(8,128)(2,1)S(1)}, u32[]{:S(2)}, u32[]{:S(2)}) collective-permute-start(bf16[192,1024]{1,0:T(8,128)(2,1)S(1)} %maximum_maximum_fusion.refs_0_), channel_id=1, source_target_pairs={{0,2},{1,3},{2,0},{3,1},{4,6},{5,7},{6,4},{7,5},{8,10},{9,11},{10,... | collective-permute-start | bytes 1179656 | tf_op jit(solution)/shard_map/ppermute | solution.py:830
  117.7 12.3 %collective-permute-start.22 = (bf16[192,1024]{1,0:T(8,128)(2,1)S(1)}, bf16[192,1024]{1,0:T(8,128)(2,1)S(1)}, u32[]{:S(2)}, u32[]{:S(2)}) collective-permute-start(bf16[192,1024]{1,0:T(8,128)(2,1)S(1)} %maximum_maximum_fusion.refs_0_), channel_id=1, source_target_pairs={{0,4},{1,5},{2,6},{3,7},{4,0},{5,1},{6,2},{7,3},{8,12},{9,13},{10,... | collective-permute-start | bytes 1179656 | tf_op jit(solution)/shard_map/ppermute | solution.py:816
  120.9 9.2 %collective-permute-start.23 = (bf16[192,1024]{1,0:T(8,128)(2,1)S(1)}, bf16[192,1024]{1,0:T(8,128)(2,1)S(1)}, u32[]{:S(2)}, u32[]{:S(2)}) collective-permute-start(bf16[192,1024]{1,0:T(8,128)(2,1)S(1)} %maximum_maximum_fusion.refs_0_), channel_id=1, source_target_pairs={{4,8},{5,9},{6,10},{7,11},{8,4},{9,5},{10,6},{11,7},{20,24},{21,25... | collective-permute-start | bytes 1179656 | tf_op jit(solution)/shard_map/ppermute | solution.py:816
  130.1 13.6 %collective-permute-start.24 = (bf16[192,1024]{1,0:T(8,128)(2,1)S(1)}, bf16[192,1024]{1,0:T(8,128)(2,1)S(1)}, u32[]{:S(2)}, u32[]{:S(2)}) collective-permute-start(bf16[192,1024]{1,0:T(8,128)(2,1)S(1)} %collective-permute-done.23), channel_id=1, source_target_pairs={{4,0},{5,1},{6,2},{7,3},{8,12},{9,13},{10,14},{11,15},{20,16},{21,... | collective-permute-start | bytes 1179656 | tf_op jit(solution)/shard_map/ppermute | solution.py:816
  131.4 12.3 %collective-permute-start.25 = (bf16[192,1024]{1,0:T(8,128)(2,1)S(1)}, bf16[192,1024]{1,0:T(8,128)(2,1)S(1)}, u32[]{:S(2)}, u32[]{:S(2)}) collective-permute-start(bf16[192,1024]{1,0:T(8,128)(2,1)S(1)} %collective-permute-done.22.refs_2_), channel_id=1, source_target_pairs={{4,8},{5,9},{6,10},{7,11},{8,4},{9,5},{10,6},{11,7},{20,24},{21,25... | collective-permute-start | bytes 1179656 | tf_op jit(solution)/shard_map/ppermute | solution.py:816
  132.3 11.5 %collective-permute-start.26 = (bf16[192,1024]{1,0:T(8,128)(2,1)S(1)}, bf16[192,1024]{1,0:T(8,128)(2,1)S(1)}, u32[]{:S(2)}, u32[]{:S(2)}) collective-permute-start(bf16[192,1024]{1,0:T(8,128)(2,1)S(1)} %collective-permute-done.22.refs_2_), channel_id=1, source_target_pairs={{0,2},{1,3},{2,0},{3,1},{4,6},{5,7},{6,4},{7,5},{8,10},{9,11},{10,... | collective-permute-start | bytes 1179656 | tf_op jit(solution)/shard_map/ppermute | solution.py:830
  143.8 13.5 %collective-permute-start.28 = (bf16[192,1024]{1,0:T(8,128)(2,1)S(1)}, bf16[192,1024]{1,0:T(8,128)(2,1)S(1)}, u32[]{:S(2)}, u32[]{:S(2)}) collective-permute-start(bf16[192,1024]{1,0:T(8,128)(2,1)S(1)} %broadcast_select_fusion.1.refs_1_), channel_id=1, source_target_pairs={{4,0},{5,1},{6,2},{7,3},{8,12},{9,13},{10,14},{11,15},{20,16},{21,... | collective-permute-start | bytes 1179656 | tf_op jit(solution)/shard_map/ppermute | solution.py:816
  145.1 12.2 %collective-permute-start.29 = (bf16[192,1024]{1,0:T(8,128)(2,1)S(1)}, bf16[192,1024]{1,0:T(8,128)(2,1)S(1)}, u32[]{:S(2)}, u32[]{:S(2)}) collective-permute-start(bf16[192,1024]{1,0:T(8,128)(2,1)S(1)} %broadcast_select_fusion.1.refs_1_), channel_id=1, source_target_pairs={{0,2},{1,3},{2,0},{3,1},{4,6},{5,7},{6,4},{7,5},{8,10},{9,11},{10,... | collective-permute-start | bytes 1179656 | tf_op jit(solution)/shard_map/ppermute | solution.py:830
  157.3 8.5 %collective-permute-start.30 = (bf16[192,1024]{1,0:T(8,128)(2,1)S(1)}, bf16[192,1024]{1,0:T(8,128)(2,1)S(1)}, u32[]{:S(2)}, u32[]{:S(2)}) collective-permute-start(bf16[192,1024]{1,0:T(8,128)(2,1)S(1)} %broadcast_select_fusion.refs_3_), channel_id=1, source_target_pairs={{0,2},{1,3},{2,0},{3,1},{4,6},{5,7},{6,4},{7,5},{8,10},{9,11},{10,... | collective-permute-start | bytes 1179656 | tf_op jit(solution)/shard_map/ppermute | solution.py:830
  158.1 16.2 %collective-permute-start.31 = (bf16[8,160,128]{2,1,0:T(8,128)(2,1)S(1)}, bf16[8,160,128]{2,1,0:T(8,128)(2,1)S(1)}, u32[]{:S(2)}, u32[]{:S(2)}) collective-permute-start(bf16[8,160,128]{2,1,0:T(8,128)(2,1)S(1)} %bitcast.43), channel_id=1, source_target_pairs={{0,16},{16,0},{1,17},{17,1},{2,18},{18,2},{3,19},{19,3},{4,20},{20... | collective-permute-start | bytes 983048 | tf_op jit(solution)/shard_map/ppermute | solution.py:695
  169.9 12.5 %all-to-all-start.2 = ((bf16[8,24,640]{2,1,0:T(8,128)(2,1)}), bf16[8,24,640]{2,1,0:T(8,128)(2,1)S(1)}, u32[]{:S(2)}, u32[]{:S(2)}) async-start(bf16[8,24,640]{2,1,0:T(8,128)(2,1)} %bitcast.21), calls=%async_computation.2 | async-start | bytes 491520 | tf_op jit(solution)/shard_map/all_to_all | solution.py:698
  174.3 2.1 %collective-permute-start.33 = (bf16[8,160,128]{2,1,0:T(8,128)(2,1)S(1)}, bf16[8,160,128]{2,1,0:T(8,128)(2,1)S(1)}, u32[]{:S(2)}, u32[]{:S(2)}) collective-permute-start(bf16[8,160,128]{2,1,0:T(8,128)(2,1)S(1)} %collective-permute-done.31.far), channel_id=1, source_target_pairs={{0,1},{1,0},{2,3},{3,2},{4,5},{5,4},{6,7},{7,6},{8,9},{9,8},{10,11... | collective-permute-start | bytes 983048 | tf_op jit(solution)/shard_map/ppermute | solution.py:692
  (27 other events, 269.9 us)

commit v5 on v4

--- a/solution.py
+++ b/solution.py
@@ -329,17 +329,14 @@
     )
 
 
-def weight_kernel(
-    info, order, head_of, wq_scale, kv_scale, wq, kv, kv_key, own, first, second, key_out
-):
-    step = pl.program_id(0)
-    block, key_head = order[step], head_of[step]
+def weight_kernel(flips, info, order, wq_scale, kv_scale, wq, kv, *outs):
+    block = order[pl.program_id(0)]
     core, rank = info[0], info[1]
     rows = wq.shape[0]
     half = wq.shape[1] // 2
     tiles = half // TILE_SIDE
-
-    def fill(target, side):
+    for flip, out in zip(flips, outs):
+        side = core ^ flip
         for group in range(rows // GROUP_ROWS):
             tile_row = (rank * (rows // GROUP_ROWS) + group) // 2
             span = slice(group * GROUP_ROWS, (group + 1) * GROUP_ROWS)
@@ -347,103 +344,109 @@
                 scale = wq_scale[tile_row, (2 * block + side) * tiles + tile]
                 start = pl.multiple_of(side * half + tile * TILE_SIDE, TILE_SIDE)
                 codes = wq[span, pl.ds(start, TILE_SIDE)].astype(F32)
-                target[0, span, tile * TILE_SIDE : (tile + 1) * TILE_SIDE] = (codes * scale).astype(BF)
+                out[0, span, tile * TILE_SIDE : (tile + 1) * TILE_SIDE] = (codes * scale).astype(BF)
             scale = kv_scale[tile_row, 2 * block + side]
             start = pl.multiple_of(side * TILE_SIDE, TILE_SIDE)
             codes = kv[span, pl.ds(start, TILE_SIDE)].astype(F32)
-            target[0, span, half : half + TILE_SIDE] = (codes * scale).astype(BF)
-
-    fill(own, core)
-
-    @pl.when(step < pl.num_programs(0) // 2)
-    def _():
-        fill(first, 1 - core)
-
-    @pl.when(step >= pl.num_programs(0) // 2)
-    def _():
-        fill(second, 1 - core)
-
-    for group in range(rows // GROUP_ROWS):
-        tile_row = (rank * (rows // GROUP_ROWS) + group) // 2
-        span = slice(group * GROUP_ROWS, (group + 1) * GROUP_ROWS)
-        scale = kv_scale[tile_row, 2 * key_head]
-        key_out[0, span, :] = (kv_key[span, :].astype(F32) * scale).astype(BF)
-
-
-def prepare_weights(core, my_rank, order, key_value_of_block, wq_codes, wq_scale, kv_codes, kv_scale):
-    chips = order.shape[0]
+            out[0, span, half : half + TILE_SIDE] = (codes * scale).astype(BF)
+
+
+def prepare_weights(flips, core, my_rank, order, chips, wq_codes, wq_scale, kv_codes, kv_scale):
     rows = wq_codes.shape[0]
     half = wq_codes.shape[1] // (2 * chips)
-    middle = chips // 2
+    blocks = order.shape[0]
     block = (1, rows, half + TILE_SIDE)
     return pl.pallas_call(
-        weight_kernel,
+        functools.partial(weight_kernel, flips),
         grid_spec=pltpu.PrefetchScalarGridSpec(
-            num_scalar_prefetch=5,
-            grid=(chips,),
+            num_scalar_prefetch=4,
+            grid=(blocks,),
             in_specs=[
                 pl.BlockSpec((rows, 2 * half), lambda i, info, order, *_: (0, order[i])),
                 pl.BlockSpec((rows, 2 * TILE_SIDE), lambda i, info, order, *_: (0, order[i])),
-                pl.BlockSpec(
-                    (rows, TILE_SIDE), lambda i, info, order, head_of, *_: (0, 2 * head_of[i])
-                ),
             ],
-            out_specs=[
-                pl.BlockSpec(block, lambda i, *_: (i, 0, 0)),
-                pl.BlockSpec(block, lambda i, *_: (jnp.minimum(i, middle - 1), 0, 0)),
-                pl.BlockSpec(block, lambda i, *_: (jnp.maximum(i - middle, 0), 0, 0)),
-                pl.BlockSpec((1, rows, TILE_SIDE), lambda i, *_: (i, 0, 0)),
+            out_specs=[pl.BlockSpec(block, lambda i, *_: (i, 0, 0))] * len(flips),
+        ),
+        out_shape=[jax.ShapeDtypeStruct((blocks, *block[1:]), BF)] * len(flips),
+        compiler_params=PARAMS,
+        cost_estimate=cost(rows * wq_codes.shape[1] * 4, rows * wq_codes.shape[1] * 3),
+        name="prepare_weights",
+    )(jnp.stack([core, my_rank]), order, wq_scale, kv_scale, wq_codes, kv_codes)
+
+
+def key_kernel(info, head_of, kv_scale, codes, out):
+    step = pl.program_id(0)
+    rows = codes.shape[0]
+    for group in range(rows // GROUP_ROWS):
+        tile_row = (info[0] * (rows // GROUP_ROWS) + group) // 2
+        span = slice(group * GROUP_ROWS, (group + 1) * GROUP_ROWS)
+        scale = kv_scale[tile_row, 2 * head_of[step]]
+        out[0, span, :] = (codes[span, :].astype(F32) * scale).astype(BF)
+
+
+def prepare_keys(my_rank, key_value_of_block, kv_codes, kv_scale):
+    rows = kv_codes.shape[0]
+    chips = key_value_of_block.shape[0]
+    return pl.pallas_call(
+        key_kernel,
+        grid_spec=pltpu.PrefetchScalarGridSpec(
+            num_scalar_prefetch=3,
+            grid=(chips,),
+            in_specs=[
+                pl.BlockSpec((rows, TILE_SIDE), lambda i, info, head_of, *_: (0, 2 * head_of[i]))
             ],
+            out_specs=pl.BlockSpec((1, rows, TILE_SIDE), lambda i, *_: (i, 0, 0)),
         ),
-        out_shape=[
-            jax.ShapeDtypeStruct((chips, *block[1:]), BF),
-            jax.ShapeDtypeStruct((middle, *block[1:]), BF),
-            jax.ShapeDtypeStruct((middle, *block[1:]), BF),
-            jax.ShapeDtypeStruct((chips, rows, TILE_SIDE), BF),
-        ],
-        compiler_params=PARAMS,
-        cost_estimate=cost(rows * wq_codes.shape[1] * 8, rows * wq_codes.shape[1] * 6),
-        name="prepare_weights",
-    )(
-        jnp.stack([core, my_rank]),
-        order,
-        key_value_of_block,
-        wq_scale,
-        kv_scale,
-        wq_codes,
-        kv_codes,
-        kv_codes,
-    )
-
-
-def project_kernel(info, normed, own, other, *refs):
-    *outs, weight = refs
+        out_shape=jax.ShapeDtypeStruct((chips, rows, TILE_SIDE), BF),
+        compiler_params=PARAMS,
+        cost_estimate=cost(2 * chips * rows * TILE_SIDE, 4 * chips * rows * TILE_SIDE),
+        name="prepare_keys",
+    )(my_rank.reshape(1), key_value_of_block, kv_scale, kv_codes)
+
+
+def project_kernel(info, normed, own, other, first, sent, kept, weight):
+    step = pl.program_id(0)
     rows = own.shape[1]
     core = info[0]
     weight[pl.ds(pl.multiple_of(core * rows, GROUP_ROWS), rows), :] = own[0]
     weight[pl.ds(pl.multiple_of((1 - core) * rows, GROUP_ROWS), rows), :] = other[0]
     product = jnp.dot(normed[...], weight[...], preferred_element_type=F32)
-    start = 0
-    for out in outs:
-        out[0] = product[start : start + out.shape[1]].astype(out.dtype)
-        start += out.shape[1]
-
-
-def project(core, normed, own, first, other, out_type):
+    first[0] = product[: first.shape[1]].astype(first.dtype)
+    second = product[first.shape[1] :]
+
+    @pl.when(step < 2)
+    def _():
+        sent[0] = second.astype(BF)
+
+    @pl.when(step >= 2)
+    def _():
+        kept[0] = second
+
+
+def project(core, normed, own, other, first_type):
     count, width = normed.shape
     blocks, rows, columns = other.shape
+    first, second = PART_ROWS
     return pl.pallas_call(
         project_kernel,
         grid=(blocks,),
         in_specs=[
             SMEM,
             pl.BlockSpec((count, width), lambda k: (0, 0)),
-            pl.BlockSpec((1, rows, columns), lambda k: (first + k, 0, 0)),
+            pl.BlockSpec((1, rows, columns), lambda k: (k, 0, 0)),
             pl.BlockSpec((1, rows, columns), lambda k: (k, 0, 0)),
         ],
-        out_specs=[pl.BlockSpec((1, part, columns), lambda k: (k, 0, 0)) for part in PART_ROWS],
+        out_specs=[
+            pl.BlockSpec((1, first, columns), lambda k: (k, 0, 0)),
+            pl.BlockSpec((1, second, columns), lambda k: (jnp.minimum(k, 1), 0, 0)),
+            pl.BlockSpec((1, second, columns), lambda k: (jnp.maximum(k - 2, 0), 0, 0)),
+        ],
         scratch_shapes=[pltpu.VMEM((width, columns), BF)],
-        out_shape=[jax.ShapeDtypeStruct((blocks, part, columns), out_type) for part in PART_ROWS],
+        out_shape=[
+            jax.ShapeDtypeStruct((blocks, first, columns), first_type),
+            jax.ShapeDtypeStruct((2, second, columns), BF),
+            jax.ShapeDtypeStruct((2, second, columns), F32),
+        ],
         compiler_params=PARAMS,
         cost_estimate=cost(
             2 * blocks * count * width * columns, 2 * blocks * columns * (width + count)
@@ -452,24 +455,62 @@
     )(core.reshape(1), normed, own, other)
 
 
-def join_kernel(own, got, kept, *sent):
-    kept[...] = own[0] + got[0].astype(F32)
-    for block, out in enumerate(sent):
-        out[...] = (own[block + 1] + got[block + 1].astype(F32)).astype(BF)
+def join_kernel(own, got, kept, near, far, middle):
+    for block, out in enumerate((near, far, kept, middle)):
+        out[...] = (own[block] + got[block].astype(F32)).astype(out.dtype)
 
 
 def join_partials(own, got):
-    blocks, rows, columns = got.shape
+    _, rows, columns = got.shape
     vmem = pl.BlockSpec(memory_space=pltpu.VMEM)
-    return pl.pallas_call(
+    sent = jax.ShapeDtypeStruct((rows, columns), BF)
+    kept, near, far, middle = pl.pallas_call(
         join_kernel,
         in_specs=[vmem, vmem],
-        out_shape=[jax.ShapeDtypeStruct((rows, columns), F32)]
-        + [jax.ShapeDtypeStruct((rows, columns), BF)] * (blocks - 1),
-        compiler_params=PARAMS,
-        cost_estimate=cost(2 * blocks * rows * columns, 8 * blocks * rows * columns),
+        out_shape=[jax.ShapeDtypeStruct((rows, columns), F32), sent, sent, sent],
+        compiler_params=PARAMS,
+        cost_estimate=cost(8 * rows * columns, 32 * rows * columns),
         name="join_partials",
     )(own, got)
+    return kept, near, middle, far
+
+
+def pair_kernel(away, home, got_away, got_home, sent, kept):
+    sent[...] = (away[...] + got_away[...].astype(F32)).astype(BF)
+    kept[...] = home[...] + got_home[...].astype(F32)
+
+
+def join_pair(away, home, got_away, got_home):
+    vmem = pl.BlockSpec(memory_space=pltpu.VMEM)
+    return pl.pallas_call(
+        pair_kernel,
+        in_specs=[vmem] * 4,
+        out_shape=[jax.ShapeDtypeStruct(away.shape, BF), jax.ShapeDtypeStruct(home.shape, F32)],
+        compiler_params=PARAMS,
+        cost_estimate=cost(2 * home.size, 16 * home.size),
+        name="join_pair",
+    )(away, home, got_away, got_home)
+
+
+def last_kernel(kept, got, own, sent):
+    own[...] = kept[0] + got[0].astype(F32)
+    sent[...] = (kept[1] + got[1].astype(F32)).astype(BF)
+
+
+def join_last(kept, got):
+    _, rows, columns = kept.shape
+    vmem = pl.BlockSpec(memory_space=pltpu.VMEM)
+    return pl.pallas_call(
+        last_kernel,
+        in_specs=[vmem, vmem],
+        out_shape=[
+            jax.ShapeDtypeStruct((rows, columns), F32),
+            jax.ShapeDtypeStruct((rows, columns), BF),
+        ],
+        compiler_params=PARAMS,
+        cost_estimate=cost(2 * kept.size, 8 * kept.size),
+        name="join_last",
+    )(kept, got)
 
 
 def turn(values, cosine, sine):
@@ -658,7 +699,8 @@
 PART_ROWS = (192, 192)
 TIE_FIRST = True
 TIE_SECOND = False
-TIE_KEYS = True
+TIE_AWAY = True
+TIE_SUMS = False
 
 
 def after(values, *earlier):
@@ -706,7 +748,42 @@
     owners, rows, most = find_slots(token_ids, my_rank, ranks, vocab_rows)
     sent = pick_rows(rows, jnp.int32(0), in_gain, vocab_table, chips)
     most = jnp.maximum(most, swap_groups(after(most, sent)))[0, 0]
-    own, other = exchange(sent)
+
+    sent_keys = prepare_keys(
+        after(my_rank, sent), key_value_of_block, key_value_codes, key_value_scale
+    )
+    half = sent_keys.shape[1] // 2
+    group = lax.axis_index("groups")
+    my_half = lax.dynamic_slice_in_dim(sent_keys, group * half, half, 1)
+    my_z = chip // y_count
+
+    def keys_for(z):
+        return lax.dynamic_slice_in_dim(my_half, z * y_count, y_count, 0)
+
+    by_z = [keys_for(my_z)] + [swap(keys_for(my_z ^ k), 2 * y_count * k) for k in range(1, Z_COUNT)]
+
+    near = jnp.array([1, 3, 0, 2], jnp.int32) * y_count
+
+    def weights_of(flips, order):
+        return prepare_weights(
+            flips,
+            core,
+            my_rank,
+            order,
+            chips,
+            wq_codes,
+            wq_scale,
+            key_value_codes,
+            key_value_scale,
+        )
+
+    away_own, away_other = weights_of((0, 1), after(chip, sent) ^ 1 ^ near)
+    (home_other,) = weights_of((1,), after(chip, sent) ^ near)
+    own = to_chips(sent)
+    own, away_other, home_other, *by_z = lax.optimization_barrier(
+        (own, away_other, home_other, *by_z)
+    )
+    other = swap(own, 1)
     normed = place_rows(owners, jnp.int32(0), core, own, other)
 
     def one_more(state):
@@ -718,28 +795,18 @@
         lambda state: state[0].astype(F32) < most, one_more, (jnp.int32(SLOTS), normed)
     )
 
-    near = jnp.arange(Z_COUNT, dtype=jnp.int32) * y_count
-    order = after(chip, sent) ^ jnp.concatenate([near ^ 1, near])
-    own_weight, away_weight, home_weight, sent_keys = prepare_weights(
-        core, my_rank, order, key_value_of_block, wq_codes, wq_scale, key_value_codes, key_value_scale
-    )
-    away_weight = swap(after(away_weight, own), 1)
-    home_weight = swap(after(home_weight, own), 1)
-
-    half = sent_keys.shape[1] // 2
-    group = lax.axis_index("groups")
-    my_half = lax.dynamic_slice_in_dim(sent_keys, group * half, half, 1)
-    my_z = chip // y_count
-
-    def keys_for(z):
-        return lax.dynamic_slice_in_dim(my_half, z * y_count, y_count, 0)
-
-    by_z = [keys_for(my_z)] + [swap(keys_for(my_z ^ k), 2 * y_count * k) for k in range(1, Z_COUNT)]
-
-    away = project(core, normed, own_weight, 0, away_weight, BF)
-    got = [swap(part, 2) for part in away]
-    home = project(after(core, *away), normed, own_weight, Z_COUNT, home_weight, F32)
-    got[0], *by_z = lax.optimization_barrier((got[0], *by_z))
+    away_other = swap(away_other, 1)
+    home_other = swap(home_other, 1)
+    away, away_sent, away_kept = project(core, normed, away_own, away_other, BF)
+    got = swap(away, 2)
+    got_away = swap(away_sent, 2 * y_count)
+    (home_own,) = weights_of((0,), after(chip, away) ^ near)
+    home, home_sent, home_kept = project(
+        after(core, away), normed, home_own, home_other, F32
+    )
+    got_home = swap(home_sent, 2 * y_count)
+    if TIE_AWAY:
+        got, got_away = lax.optimization_barrier((got, got_away))
 
     cosine, sine = rotation_tables(count)
     heads_width = wq_codes.shape[1] // ranks
@@ -747,30 +814,30 @@
     my_y = chip % y_count
     here = lax.dynamic_index_in_dim(by_z, my_y, 1, keepdims=False)
     there = swap(lax.dynamic_index_in_dim(by_z, 1 - my_y, 1, keepdims=False), 2)
+    wo_rows = wo_codes.T
+    out_codes = [wo_rows, swap(wo_rows, 1)]
     own_kv, other_kv, held = [], [], []
-    start, share = 0, count // ranks
-    for part, part_rows in enumerate(PART_ROWS):
-        kept, *sums = join_partials(home[part], got[part])
-        sums = [swap(value, 4 * (k + 1)) for k, value in enumerate(sums)]
-        if part + 1 < len(PART_ROWS):
-            got[part + 1], *sums = lax.optimization_barrier((got[part + 1], *sums))
-        if part == 1 and TIE_KEYS:
-            kept, there = lax.optimization_barrier((kept, there))
-        queries, kv = make_heads(core, [kept, *sums], start, q_gain, k_gain, cosine, sine)
+    share = count // ranks
+
+    def attend_part(start, sums):
+        queries, kv = make_heads(core, sums, start, q_gain, k_gain, cosine, sine)
         own_kv.append(kv)
         other_kv.append(swap(kv, 1))
         kept, sent_rows = attend_heads(core, queries, start, own_kv, other_kv, share)
         held.append(jnp.concatenate([kept, swap(sent_rows, 1)], axis=1))
-        start += part_rows
-    wo_rows = wo_codes.T
-    out_codes = [wo_rows, swap(wo_rows, 1)]
-
-    own_keys = jnp.stack([here, there], axis=1).reshape(chips, half, HEAD_SIZE)
-    far_keys = swap_groups(own_keys)
-    own_keys = (own_keys, far_keys)
-    synced = collect_keys(
-        jnp.stack([core, group, chip]), [*own_keys, *(swap(value, 1) for value in own_keys)]
-    )
+
+    kept, *sums = join_partials(home, got)
+    got_away, got_home = lax.optimization_barrier((got_away, got_home, *sums))[:2]
+    pair_sent, pair_kept = join_pair(away_kept, home_kept, got_away, got_home)
+    sums = [swap(value, 2 * y_count * (k + 1)) for k, value in enumerate(sums)]
+    pair_got = swap(pair_sent, 2)
+    if TIE_SUMS:
+        pair_got, *sums = lax.optimization_barrier((pair_got, *sums))
+    attend_part(0, [kept, *sums])
+    kept, last_sent = join_last(pair_kept, pair_got)
+    last_got = swap(last_sent, 4 * y_count)
+    kept, there = lax.optimization_barrier((kept, there))
+    attend_part(PART_ROWS[0], [kept, last_got])
 
     def add_blocks(total, blocks, numbers, last=False):
         chips_of = chip ^ jnp.array(numbers, jnp.int32)
@@ -778,7 +845,17 @@
             core, my_rank, blocks, chips_of, out_codes, wo_scale, total, last
         )
 
-    total = gather_project(jnp.concatenate(held, axis=0), add_blocks, y_count)
+    own_keys = jnp.stack([here, there], axis=1).reshape(chips, half, HEAD_SIZE)
+
+    def finish_keys(far_keys):
+        return collect_keys(
+            jnp.stack([core, group, chip]),
+            [own_keys, far_keys, swap(own_keys, 1), swap(far_keys, 1)],
+        )
+
+    total, synced = gather_project(
+        jnp.concatenate(held, axis=0), add_blocks, y_count, swap_groups(own_keys), finish_keys
+    )
     columns = to_chips(total.reshape(chips, share, -1))
     attn_out = jnp.transpose(columns, (1, 0, 2)).reshape(share, -1)
     return attn_out, synced
@@ -821,7 +898,7 @@
 OUTWARD = [(1, 0), (2, 3)]
 
 
-def gather_project(block, add_blocks, y_count):
+def gather_project(block, add_blocks, y_count, beside, finish):
     along = 2 * y_count
     ranks = Z_COUNT * along
     together = lax.optimization_barrier
@@ -841,22 +918,29 @@
         swap_y(one),
     )
     if TIE_FIRST:
-        two_end, two_inner, one_across, total = together((two_end, two_inner, one_across, total))
+        two_end, two_inner, one_across, total, beside = together(
+            (two_end, two_inner, one_across, total, beside)
+        )
     else:
-        two_end, two_inner, one_across = together((two_end, two_inner, one_across))
+        two_end, two_inner, one_across, beside = together(
+            (two_end, two_inner, one_across, beside)
+        )
+    finished = finish(beside)
     two = jnp.where(at_end, two_end, two_inner)
     three_end, two_across = hop(two, OUTWARD, along, ranks), swap_y(two)
     if TIE_SECOND:
         total = add_blocks(total, [one_across, two], (3, 4))
-        three_end, two_across, total = together((three_end, two_across, total))
+        three_end, two_across, total, finished = together(
+            (three_end, two_across, total, finished)
+        )
         rest, numbers = [two_across], (5, 6)
     else:
-        three_end, two_across = together((three_end, two_across))
+        three_end, two_across, finished = together((three_end, two_across, finished))
         rest, numbers = [one_across, two, two_across], (3, 4, 5, 6)
     three = jnp.where(at_end, three_end, inner)
     three_across = swap_y(three)
     total = add_blocks(total, [*rest, three], numbers)
-    return add_blocks(total, [three_across], (7,), True)
+    return add_blocks(total, [three_across], (7,), True), finished
 
 
 def solution(mesh):

time: 184 us -> 179 us (0.973)
  blocking collectives: 0 us -> 11.9 us
  waiting for transfers between devices: 69.6 us -> 60.2 us
  starting transfers between devices: 47.7 us -> 39.9 us
  Pallas kernels: 51.3 us -> 54.6 us
  local copies, waits for them, and re-layouts: 10.1 us -> 7.04 us
    all_to_all x0 -> x1, blocking collectives: none -> 11.9 us  [to_chips(): lax.all_to_all(values, 'fsdp', split_axis=0, concat_axis=0, tiled=True, a...]
    ppermute x5, waiting for transfers between devices: 19.7 us -> 8.6 us  [hop(): return lax.ppermute(values, 'fsdp', moves)]
    pallas_call x1 -> x6, Pallas kernels: 8.51 us -> 16.1 us  [the longest x3 14.3 us: prepare_weights(): pl.pallas_call(functools.partial(weight_kernel, flips), grid_spec=pltpu.P...]
    ppermute x4, waiting for transfers between devices: 5.84 us -> 10.4 us  [swap_y(): return lax.ppermute(values, 'fsdp', [(i, i ^ 2) for i in range(ranks)])]
    all_to_all x2 -> x1, starting transfers between devices: 11.2 us -> 6.98 us  [to_chips(): lax.all_to_all(values, 'fsdp', split_axis=0, concat_axis=0, tiled=True, a...]
    ppermute x5, starting transfers between devices: 7.3 us -> 4.1 us  [hop(): return lax.ppermute(values, 'fsdp', moves)]
    all_to_all x2 -> x1, waiting for transfers between devices: 2.69 us -> 0.01 us  [to_chips(): lax.all_to_all(values, 'fsdp', split_axis=0, concat_axis=0, tiled=True, a...]
    ppermute x22, starting transfers between devices: 22.7 us -> 20.5 us  [swap(): return lax.ppermute(values, 'fsdp', [(i, i ^ bits) for i in range(ranks)])]
  transfers between devices with their start and end apart: 35 -> 34, of which waited for: 15 -> 15; matrix products, arithmetic and copies ran while one was open for 3% -> 2% of each run, Pallas kernels for 28% -> 29%
where the time goes in v5:
time: 179 us; the launch traced here: 178 us
  waiting for transfers between devices  60.2 us (34%)
  Pallas kernels  54.6 us (31%)
  starting transfers between devices  39.9 us (22%)
  blocking collectives  11.9 us (7%)
  local copies, waits for them, and re-layouts  7.04 us (4%)
  other arithmetic  2.58 us (1%)
    ppermute x22, waiting for transfers between devices, swap(): return lax.ppermute(values, 'fsdp', [(i, i ^ bits) for i in range(ranks)])  37.6 us
    ppermute x22, starting transfers between devices, swap(): return lax.ppermute(values, 'fsdp', [(i, i ^ bits) for i in range(ranks)])  20.5 us
    pallas_call x3, Pallas kernels, out_project(): pl.pallas_call(functools.partial(out_kernel, blocks, bool(extra), last, b...  14.6 us
    pallas_call x3, Pallas kernels, prepare_weights(): pl.pallas_call(functools.partial(weight_kernel, flips), grid_spec=pltpu.P...  14.3 us
    all_to_all x1, blocking collectives, to_chips(): lax.all_to_all(values, 'fsdp', split_axis=0, concat_axis=0, tiled=True, a...  11.9 us
    ppermute x4, waiting for transfers between devices, swap_y(): return lax.ppermute(values, 'fsdp', [(i, i ^ 2) for i in range(ranks)])  10.4 us
    pallas_call x2, Pallas kernels, project(): pl.pallas_call(project_kernel, grid=(blocks,), in_specs=[SMEM, pl.BlockSp...  9.29 us
    ppermute x5, waiting for transfers between devices, hop(): return lax.ppermute(values, 'fsdp', moves)  8.6 us
  transfers between devices with their start and end apart: 34, of which 15 were waited for; matrix products, arithmetic and copies ran while one was open for 2% of the time, Pallas kernels for 29%

profile of v5, /device:TPU:0, one launch (start us, length us, event | category | flops | bytes accessed | tf_op | source)
XLA Modules:
  0.0 177.9 jit_solution(11406543335644288660)
XLA Ops:
  2.6 5.4 %pick_rows.2 = bf16[8,32,640]{2,1,0:T(8,128)(2,1)} custom-call(s32[1]{0:T(128)} %constant.155.clone.1.info, f32[8,384]{1,0:T(8,128)S(1)} %get-tuple-element.242.rows, f32[1,5120]{1,0:T(1,128)} %bitcast.59, bf16[600,5120]{1,0:T(8,128)(2,1)} %table.1), custom_call_target="tpu_custom_call" | custom-call | flops 196608000 | bytes 6144000 | tf_op jit(solution)/shard_map/pick_rows/pallas_call | solution.py:281
  8.0 7.0 %all-to-all-start.1 = ((bf16[8,32,640]{2,1,0:T(8,128)(2,1)}), bf16[8,32,640]{2,1,0:T(8,128)(2,1)S(1)}, u32[]{:S(2)}, u32[]{:S(2)}) async-start(bf16[8,32,640]{2,1,0:T(8,128)(2,1)} %pick_rows.2), calls=%async_computation.1 | async-start | bytes 655360 | tf_op jit(solution)/shard_map/all_to_all | solution.py:740
  15.0 1.6 prepare_keys.1
  16.7 2.1 %collective-permute-start.1 = (bf16[2,160,128]{2,1,0:T(8,128)(2,1)S(1)}, bf16[2,160,128]{2,1,0:T(8,128)(2,1)}, u32[]{:S(2)}, u32[]{:S(2)}) collective-permute-start(bf16[2,160,128]{2,1,0:T(8,128)(2,1)S(1)} %get-tuple-element.176), channel_id=1, source_target_pairs={{0,4},{1,5},{2,6},{3,7},{4,0},{5,1},{6,2},{7,3},{8,12},{9,13},{10,... | collective-permute-start | bytes 245768 | tf_op jit(solution)/shard_map/ppermute | solution.py:734
  18.8 2.4 %collective-permute-start.2 = (bf16[2,160,128]{2,1,0:T(8,128)(2,1)S(1)}, bf16[2,160,128]{2,1,0:T(8,128)(2,1)}, u32[]{:S(2)}, u32[]{:S(2)}) collective-permute-start(bf16[2,160,128]{2,1,0:T(8,128)(2,1)S(1)} %get-tuple-element.175), channel_id=1, source_target_pairs={{0,8},{1,9},{2,10},{3,11},{4,12},{5,13},{6,14},{7,15},{8,0},{9,1},... | collective-permute-start | bytes 245768 | tf_op jit(solution)/shard_map/ppermute | solution.py:734
  21.3 5.2 %prepare_weights.3 = (bf16[4,320,640]{2,1,0:T(8,128)(2,1)S(1)}, bf16[4,320,640]{2,1,0:T(8,128)(2,1)}) custom-call(s32[2]{0:T(128)S(1)} %pad_add_fusion.3.info, s32[4]{0:T(128)S(1)} %get-tuple-element.184.order, f32[40,64]{1,0:T(8,128)S(1)} %copy-done.2, f32[40,16]{1,0:T(8,128)S(1)} %copy.18.kv_scale, bf16[320,8192]{1,0:T(8,128)(2,1)} %wq.5, ...), custom_call_target="tpu_custom_call" | custom-call | flops 10485760 | bytes 7864320 | tf_op jit(solution)/shard_map/prepare_weights/pallas_call | solution.py:359
  27.8 5.2 %prepare_weights.4 = bf16[4,320,640]{2,1,0:T(8,128)(2,1)} custom-call(s32[2]{0:T(128)S(1)} %pad_add_fusion.3.info, s32[4]{0:T(128)S(1)} %get-tuple-element.183.order, f32[40,64]{1,0:T(8,128)S(1)} %copy-done.2, f32[40,16]{1,0:T(8,128)S(1)} %copy.18.kv_scale, bf16[320,8192]{1,0:T(8,128)(2,1)} %wq.5, bf16[320,2048]{1,0:T(8,128)(2,1)S(1)} %copy-done), custom_call_target="tpu_custom_call" | custom-call | flops 10485760 | bytes 7864320 | tf_op jit(solution)/shard_map/prepare_weights/pallas_call | solution.py:359
  35.7 2.0 %collective-permute-done.5 = f32[8,128]{1,0:T(8,128)S(1)} collective-permute-done((f32[8,128]{1,0:T(8,128)S(1)}, f32[8,128]{1,0:T(8,128)S(1)}, u32[]{:S(2)}, u32[]{:S(2)}) %collective-permute-start.5) | collective-permute-done | bytes 4128 | tf_op jit(solution)/shard_map/ppermute | solution.py:737
  41.7 4.2 %project.2 = (bf16[4,192,640]{2,1,0:T(8,128)(2,1)S(1)}, bf16[2,192,640]{2,1,0:T(8,128)(2,1)S(1)}, f32[2,192,640]{2,1,0:T(8,128)S(1)}) custom-call(s32[1]{0:T(128)} %bitcast.5.info, bf16[384,640]{1,0:T(8,128)(2,1)S(1)} %get-tuple-element.109.normed, bf16[4,320,640]{2,1,0:T(8,128)(2,1)S(1)} %copy-done.7, bf16[4,320,640]{2,1,0:T(8,128)(2,1)} %collective-permute-done.6.other), custom_call_target="tpu_custom_call" | custom-call | flops 1258291200 | bytes 5242880 | tf_op jit(solution)/shard_map/project/pallas_call | solution.py:430
  45.8 2.0 %collective-permute-start.8 = (bf16[4,192,640]{2,1,0:T(8,128)(2,1)S(1)}, bf16[4,192,640]{2,1,0:T(8,128)(2,1)S(1)}, u32[]{:S(2)}, u32[]{:S(2)}) collective-permute-start(bf16[4,192,640]{2,1,0:T(8,128)(2,1)S(1)} %get-tuple-element.112), channel_id=1, source_target_pairs={{0,2},{1,3},{2,0},{3,1},{4,6},{5,7},{6,4},{7,5},{8,10},{9,11},{10,... | collective-permute-start | bytes 2949128 | tf_op jit(solution)/shard_map/ppermute | solution.py:734
  48.4 3.9 %prepare_weights.5.own = bf16[4,320,640]{2,1,0:T(8,128)(2,1)S(1)} custom-call(s32[2]{0:T(128)S(1)} %pad_add_fusion.3.info, s32[4]{0:T(128)S(1)} %broadcast_xor_fusion.1.order, f32[40,64]{1,0:T(8,128)S(1)} %copy-done.2, f32[40,16]{1,0:T(8,128)S(1)} %copy.18.kv_scale, bf16[320,8192]{1,0:T(8,128)(2,1)} %wq.5, bf16[320,2048]{1,0:T(8,128)(2,1)S(1)} %copy-done), custom_call_target="tpu_custom_call" | custom-call | flops 10485760 | bytes 7864320 | tf_op jit(solution)/shard_map/prepare_weights/pallas_call | solution.py:359
  52.3 5.1 %project.3 = (f32[4,192,640]{2,1,0:T(8,128)}, bf16[2,192,640]{2,1,0:T(8,128)(2,1)S(1)}, f32[2,192,640]{2,1,0:T(8,128)S(1)}) custom-call(s32[1]{0:T(128)} %bitcast.13.info, bf16[384,640]{1,0:T(8,128)(2,1)S(1)} %get-tuple-element.109.normed, bf16[4,320,640]{2,1,0:T(8,128)(2,1)S(1)} %prepare_weights.5.own, bf16[4,320,640]{2,1,0:T(8,128)(2,1)} %collective-permute-done.7.other), custom_call_target="tpu_custom_call" | custom-call | flops 1258291200 | bytes 5242880 | tf_op jit(solution)/shard_map/project/pallas_call | solution.py:430
  58.9 2.2 %collective-permute-done.9.got_away = bf16[2,192,640]{2,1,0:T(8,128)(2,1)S(1)} collective-permute-done((bf16[2,192,640]{2,1,0:T(8,128)(2,1)S(1)}, bf16[2,192,640]{2,1,0:T(8,128)(2,1)S(1)}, u32[]{:S(2)}, u32[]{:S(2)}) %collective-permute-start.9) | collective-permute-done | bytes 491552 | tf_op jit(solution)/shard_map/ppermute | solution.py:734
  61.2 7.9 %collective-permute-done.8.got = bf16[4,192,640]{2,1,0:T(8,128)(2,1)S(1)} collective-permute-done((bf16[4,192,640]{2,1,0:T(8,128)(2,1)S(1)}, bf16[4,192,640]{2,1,0:T(8,128)(2,1)S(1)}, u32[]{:S(2)}, u32[]{:S(2)}) %collective-permute-start.8) | collective-permute-done | bytes 983072 | tf_op jit(solution)/shard_map/ppermute | solution.py:734
  69.1 1.5 copy-done.1
  71.0 1.8 %collective-permute-start.16 = (bf16[2,192,640]{2,1,0:T(8,128)(2,1)S(1)}, bf16[2,192,640]{2,1,0:T(8,128)(2,1)S(1)}, u32[]{:S(2)}, u32[]{:S(2)}) collective-permute-start(bf16[2,192,640]{2,1,0:T(8,128)(2,1)S(1)} %get-tuple-element.134), channel_id=1, source_target_pairs={{0,2},{1,3},{2,0},{3,1},{4,6},{5,7},{6,4},{7,5},{8,10},{9,11},{10,... | collective-permute-start | bytes 1474568 | tf_op jit(solution)/shard_map/ppermute | solution.py:734
  75.1 3.3 %collective-permute-start.11 = (bf16[192,640]{1,0:T(8,128)(2,1)S(1)}, bf16[192,640]{1,0:T(8,128)(2,1)S(1)}, u32[]{:S(2)}, u32[]{:S(2)}) collective-permute-start(bf16[192,640]{1,0:T(8,128)(2,1)S(1)} %get-tuple-element.121), channel_id=1, source_target_pairs={{0,8},{1,9},{2,10},{3,11},{4,12},{5,13},{6,14},{7,15},{8,0},{9,1},... | collective-permute-start | bytes 737288 | tf_op jit(solution)/shard_map/ppermute | solution.py:734
  78.4 6.3 %collective-permute-done.16.got = bf16[2,192,640]{2,1,0:T(8,128)(2,1)S(1)} collective-permute-done((bf16[2,192,640]{2,1,0:T(8,128)(2,1)S(1)}, bf16[2,192,640]{2,1,0:T(8,128)(2,1)S(1)}, u32[]{:S(2)}, u32[]{:S(2)}) %collective-permute-start.16) | collective-permute-done | bytes 491552 | tf_op jit(solution)/shard_map/ppermute | solution.py:734
  84.7 3.2 %collective-permute-start.12 = (bf16[192,640]{1,0:T(8,128)(2,1)S(1)}, bf16[192,640]{1,0:T(8,128)(2,1)S(1)}, u32[]{:S(2)}, u32[]{:S(2)}) collective-permute-start(bf16[192,640]{1,0:T(8,128)(2,1)S(1)} %get-tuple-element.122), channel_id=1, source_target_pairs={{0,12},{1,13},{2,14},{3,15},{4,8},{5,9},{6,10},{7,11},{8,4},{9,5},... | collective-permute-start | bytes 737288 | tf_op jit(solution)/shard_map/ppermute | solution.py:734
  89.0 10.5 %collective-permute-done.11.refs_2_ = bf16[192,640]{1,0:T(8,128)(2,1)S(1)} collective-permute-done((bf16[192,640]{1,0:T(8,128)(2,1)S(1)}, bf16[192,640]{1,0:T(8,128)(2,1)S(1)}, u32[]{:S(2)}, u32[]{:S(2)}) %collective-permute-start.11) | collective-permute-done | bytes 245792 | tf_op jit(solution)/shard_map/ppermute | solution.py:734
  100.5 7.9 %collective-permute-done.18.refs_1_ = bf16[192,640]{1,0:T(8,128)(2,1)S(1)} collective-permute-done((bf16[192,640]{1,0:T(8,128)(2,1)S(1)}, bf16[192,640]{1,0:T(8,128)(2,1)S(1)}, u32[]{:S(2)}, u32[]{:S(2)}) %collective-permute-start.18) | collective-permute-done | bytes 245792 | tf_op jit(solution)/shard_map/ppermute | solution.py:734
  113.3 1.5 collective-permute-start.21
  115.5 9.0 %collective-permute-done.21.refs_1_ = bf16[192,1024]{1,0:T(8,128)(2,1)S(1)} collective-permute-done((bf16[192,1024]{1,0:T(8,128)(2,1)S(1)}, bf16[192,1024]{1,0:T(8,128)(2,1)S(1)}, u32[]{:S(2)}, u32[]{:S(2)}) %collective-permute-start.21) | collective-permute-done | bytes 393248 | tf_op jit(solution)/shard_map/ppermute | solution.py:907
  128.6 1.6 collective-permute-start.28
  130.3 5.1 %out_project.3.refs_6_ = f32[2,320,192]{2,1,0:T(8,128)S(1)} custom-call(s32[5]{0:T(128)S(1)} %pad_add_fusion.4.info, f32[64,40]{1,0:T(8,128)S(1)} %copy.24.scales, bf16[192,1024]{1,0:T(8,128)(2,1)S(1)} %maximum_maximum_fusion.refs_0_, bf16[192,1024]{1,0:T(8,128)(2,1)S(1)} %collective-permute-done.21.refs_1_, ...), custom_call_target="tpu_custom_call" | custom-call | flops 754974720 | bytes 3932160 | tf_op jit(solution)/shard_map/out_project/pallas_call | solution.py:672
  135.4 1.6 collective-permute-done.28.far
  137.0 5.3 %collective-permute-done.24 = bf16[192,1024]{1,0:T(8,128)(2,1)S(1)} collective-permute-done((bf16[192,1024]{1,0:T(8,128)(2,1)S(1)}, bf16[192,1024]{1,0:T(8,128)(2,1)S(1)}, u32[]{:S(2)}, u32[]{:S(2)}) %collective-permute-start.24) | collective-permute-done | bytes 393248 | tf_op jit(solution)/shard_map/ppermute | solution.py:893
  147.3 3.3 %collect_keys.1 = bf16[8,2,2,160,128]{4,3,2,1,0:T(8,128)(2,1)} custom-call(s32[3]{0:T(128)S(1)} %pad_add_fusion.5.info, bf16[8,160,128]{2,1,0:T(8,128)(2,1)S(1)} %bitcast.46, bf16[8,160,128]{2,1,0:T(8,128)(2,1)S(1)} %collective-permute-done.28.far, bf16[8,160,128]{2,1,0:T(8,128)(2,1)S(1)} %collective-permute-done.31.other, ...), custom_call_target="tpu_custom_call" | custom-call | bytes 2621440 | tf_op jit(solution)/shard_map/collect_keys/pallas_call | solution.py:875
  150.6 2.1 %collective-permute-done.29 = bf16[192,1024]{1,0:T(8,128)(2,1)S(1)} collective-permute-done((bf16[192,1024]{1,0:T(8,128)(2,1)S(1)}, bf16[192,1024]{1,0:T(8,128)(2,1)S(1)}, u32[]{:S(2)}, u32[]{:S(2)}) %collective-permute-start.29) | collective-permute-done | bytes 393248 | tf_op jit(solution)/shard_map/ppermute | solution.py:893
  154.5 6.0 %out_project.4.refs_3_ = f32[2,320,192]{2,1,0:T(8,128)S(1)} custom-call(s32[6]{0:T(128)S(1)} %pad_add_fusion.6.info, f32[64,40]{1,0:T(8,128)S(1)} %copy.24.scales, bf16[192,1024]{1,0:T(8,128)(2,1)S(1)} %collective-permute-done.26.refs_0_, bf16[192,1024]{1,0:T(8,128)(2,1)S(1)} %broadcast_select_fusion.1.refs_1_, ...), custom_call_target="tpu_custom_call" | custom-call | flops 1006632960 | bytes 5242880 | tf_op jit(solution)/shard_map/out_project/pallas_call | solution.py:672
  161.9 3.4 %out_project.5 = bf16[192,640]{1,0:T(8,128)(2,1)S(1)} custom-call(s32[3]{0:T(128)S(1)} %pad_add_fusion.1.info, f32[64,40]{1,0:T(8,128)S(1)} %copy.24.scales, bf16[192,1024]{1,0:T(8,128)(2,1)S(1)} %collective-permute-done.33.refs_0_, bf16[320,8192]{1,0:T(8,128)(2,1)} %bitcast.56, bf16[320,8192]{1,0:T(8,128)(2,1)} %collective-permute-done.27.refs_4_.refs_5_.refs_2_, ...), custom_call_target="tpu_custom_call" | custom-call | flops 251658240 | bytes 1310720 | tf_op jit(solution)/shard_map/out_project/pallas_call | solution.py:672
  165.3 11.9 %all_to_all.16 = bf16[8,24,640]{2,1,0:T(8,128)(2,1)S(1)} all-to-all(bf16[8,24,640]{2,1,0:T(8,128)(2,1)S(1)} %bitcast.47), channel_id=1, replica_groups={{0,2,4,6,8,10,12,14},{1,3,5,7,9,11,13,15},{16,18,20,22,24,26,28,30},{17..., dimensions={0} | all-to-all | bytes 491520 | tf_op jit(solution)/shard_map/all_to_all | solution.py:740
  (113 shorter events, 35.3 us)
Async XLA Ops:
  0.6 129.7 %collective-permute-start.27 = (bf16[320,8192]{1,0:T(8,128)(2,1)}, bf16[320,8192]{1,0:T(8,128)(2,1)}, u32[]{:S(2)}, u32[]{:S(2)}) collective-permute-start(bf16[320,8192]{1,0:T(8,128)(2,1)} %bitcast.53), channel_id=1, source_target_pairs={{0,1},{1,0},{2,3},{3,2},{4,5},{5,4},{6,7},{7,6},{8,9},{9,8},{10,11... | collective-permute-start | bytes 15728648 | tf_op jit(solution)/shard_map/ppermute | solution.py:734
  8.0 25.0 %all-to-all-start.1 = ((bf16[8,32,640]{2,1,0:T(8,128)(2,1)}), bf16[8,32,640]{2,1,0:T(8,128)(2,1)S(1)}, u32[]{:S(2)}, u32[]{:S(2)}) async-start(bf16[8,32,640]{2,1,0:T(8,128)(2,1)} %pick_rows.2), calls=%async_computation.1 | async-start | bytes 655360 | tf_op jit(solution)/shard_map/all_to_all | solution.py:740
  16.7 16.3 %collective-permute-start.1 = (bf16[2,160,128]{2,1,0:T(8,128)(2,1)S(1)}, bf16[2,160,128]{2,1,0:T(8,128)(2,1)}, u32[]{:S(2)}, u32[]{:S(2)}) collective-permute-start(bf16[2,160,128]{2,1,0:T(8,128)(2,1)S(1)} %get-tuple-element.176), channel_id=1, source_target_pairs={{0,4},{1,5},{2,6},{3,7},{4,0},{5,1},{6,2},{7,3},{8,12},{9,13},{10,... | collective-permute-start | bytes 245768 | tf_op jit(solution)/shard_map/ppermute | solution.py:734
  18.8 14.2 %collective-permute-start.2 = (bf16[2,160,128]{2,1,0:T(8,128)(2,1)S(1)}, bf16[2,160,128]{2,1,0:T(8,128)(2,1)}, u32[]{:S(2)}, u32[]{:S(2)}) collective-permute-start(bf16[2,160,128]{2,1,0:T(8,128)(2,1)S(1)} %get-tuple-element.175), channel_id=1, source_target_pairs={{0,8},{1,9},{2,10},{3,11},{4,12},{5,13},{6,14},{7,15},{8,0},{9,1},... | collective-permute-start | bytes 245768 | tf_op jit(solution)/shard_map/ppermute | solution.py:734
  21.2 11.8 %collective-permute-start.3 = (bf16[2,160,128]{2,1,0:T(8,128)(2,1)S(1)}, bf16[2,160,128]{2,1,0:T(8,128)(2,1)S(1)}, u32[]{:S(2)}, u32[]{:S(2)}) collective-permute-start(bf16[2,160,128]{2,1,0:T(8,128)(2,1)S(1)} %get-tuple-element.174), channel_id=1, source_target_pairs={{0,12},{1,13},{2,14},{3,15},{4,8},{5,9},{6,10},{7,11},{8,4},{9,5},... | collective-permute-start | bytes 245768 | tf_op jit(solution)/shard_map/ppermute | solution.py:734
  33.0 7.2 %collective-permute-start.6 = (bf16[4,320,640]{2,1,0:T(8,128)(2,1)}, bf16[4,320,640]{2,1,0:T(8,128)(2,1)}, u32[]{:S(2)}, u32[]{:S(2)}) collective-permute-start(bf16[4,320,640]{2,1,0:T(8,128)(2,1)} %get-tuple-element.111), channel_id=1, source_target_pairs={{0,1},{1,0},{2,3},{3,2},{4,5},{5,4},{6,7},{7,6},{8,9},{9,8},{10,11... | collective-permute-start | bytes 4915208 | tf_op jit(solution)/shard_map/ppermute | solution.py:734
  33.6 18.7 %collective-permute-start.7 = (bf16[4,320,640]{2,1,0:T(8,128)(2,1)}, bf16[4,320,640]{2,1,0:T(8,128)(2,1)}, u32[]{:S(2)}, u32[]{:S(2)}) collective-permute-start(bf16[4,320,640]{2,1,0:T(8,128)(2,1)} %prepare_weights.4), channel_id=1, source_target_pairs={{0,1},{1,0},{2,3},{3,2},{4,5},{5,4},{6,7},{7,6},{8,9},{9,8},{10,11... | collective-permute-start | bytes 4915208 | tf_op jit(solution)/shard_map/ppermute | solution.py:734
  33.6 4.7 %collective-permute-start.4 = (bf16[8,32,640]{2,1,0:T(8,128)(2,1)S(1)}, bf16[8,32,640]{2,1,0:T(8,128)(2,1)S(1)}, u32[]{:S(2)}, u32[]{:S(2)}) collective-permute-start(bf16[8,32,640]{2,1,0:T(8,128)(2,1)S(1)} %all-to-all-done.1), channel_id=1, source_target_pairs={{0,1},{1,0},{2,3},{3,2},{4,5},{5,4},{6,7},{7,6},{8,9},{9,8},{10,11... | collective-permute-start | bytes 983048 | tf_op jit(solution)/shard_map/ppermute | solution.py:734
  34.1 3.6 %collective-permute-start.5 = (f32[8,128]{1,0:T(8,128)S(1)}, f32[8,128]{1,0:T(8,128)S(1)}, u32[]{:S(2)}, u32[]{:S(2)}) collective-permute-start(f32[8,128]{1,0:T(8,128)S(1)} %get-tuple-element.108), channel_id=1, source_target_pairs={{0,16},{16,0},{1,17},{17,1},{2,18},{18,2},{3,19},{19,3},{4,20},{20... | collective-permute-start | bytes 12296 | tf_op jit(solution)/shard_map/ppermute | solution.py:737
  45.8 23.3 %collective-permute-start.8 = (bf16[4,192,640]{2,1,0:T(8,128)(2,1)S(1)}, bf16[4,192,640]{2,1,0:T(8,128)(2,1)S(1)}, u32[]{:S(2)}, u32[]{:S(2)}) collective-permute-start(bf16[4,192,640]{2,1,0:T(8,128)(2,1)S(1)} %get-tuple-element.112), channel_id=1, source_target_pairs={{0,2},{1,3},{2,0},{3,1},{4,6},{5,7},{6,4},{7,5},{8,10},{9,11},{10,... | collective-permute-start | bytes 2949128 | tf_op jit(solution)/shard_map/ppermute | solution.py:734
  47.9 13.3 %collective-permute-start.9 = (bf16[2,192,640]{2,1,0:T(8,128)(2,1)S(1)}, bf16[2,192,640]{2,1,0:T(8,128)(2,1)S(1)}, u32[]{:S(2)}, u32[]{:S(2)}) collective-permute-start(bf16[2,192,640]{2,1,0:T(8,128)(2,1)S(1)} %get-tuple-element.117), channel_id=1, source_target_pairs={{0,4},{1,5},{2,6},{3,7},{4,0},{5,1},{6,2},{7,3},{8,12},{9,13},{10,... | collective-permute-start | bytes 1474568 | tf_op jit(solution)/shard_map/ppermute | solution.py:734
  57.5 13.4 %collective-permute-start.15 = (bf16[2,192,640]{2,1,0:T(8,128)(2,1)S(1)}, bf16[2,192,640]{2,1,0:T(8,128)(2,1)S(1)}, u32[]{:S(2)}, u32[]{:S(2)}) collective-permute-start(bf16[2,192,640]{2,1,0:T(8,128)(2,1)S(1)} %get-tuple-element.130), channel_id=1, source_target_pairs={{0,4},{1,5},{2,6},{3,7},{4,0},{5,1},{6,2},{7,3},{8,12},{9,13},{10,... | collective-permute-start | bytes 1474568 | tf_op jit(solution)/shard_map/ppermute | solution.py:734
  71.0 13.7 %collective-permute-start.16 = (bf16[2,192,640]{2,1,0:T(8,128)(2,1)S(1)}, bf16[2,192,640]{2,1,0:T(8,128)(2,1)S(1)}, u32[]{:S(2)}, u32[]{:S(2)}) collective-permute-start(bf16[2,192,640]{2,1,0:T(8,128)(2,1)S(1)} %get-tuple-element.134), channel_id=1, source_target_pairs={{0,2},{1,3},{2,0},{3,1},{4,6},{5,7},{6,4},{7,5},{8,10},{9,11},{10,... | collective-permute-start | bytes 1474568 | tf_op jit(solution)/shard_map/ppermute | solution.py:734
  72.8 15.2 %collective-permute-start.10 = (bf16[192,640]{1,0:T(8,128)(2,1)S(1)}, bf16[192,640]{1,0:T(8,128)(2,1)S(1)}, u32[]{:S(2)}, u32[]{:S(2)}) collective-permute-start(bf16[192,640]{1,0:T(8,128)(2,1)S(1)} %get-tuple-element.120), channel_id=1, source_target_pairs={{0,4},{1,5},{2,6},{3,7},{4,0},{5,1},{6,2},{7,3},{8,12},{9,13},{10,... | collective-permute-start | bytes 737288 | tf_op jit(solution)/shard_map/ppermute | solution.py:734
  74.5 26.0 %collective-permute-start.17 = (bf16[4,160,128]{2,1,0:T(8,128)(2,1)S(1)}, bf16[4,160,128]{2,1,0:T(8,128)(2,1)S(1)}, u32[]{:S(2)}, u32[]{:S(2)}) collective-permute-start(bf16[4,160,128]{2,1,0:T(8,128)(2,1)S(1)} %get-tuple-element.179), channel_id=1, source_target_pairs={{0,2},{1,3},{2,0},{3,1},{4,6},{5,7},{6,4},{7,5},{8,10},{9,11},{10,... | collective-permute-start | bytes 491528 | tf_op jit(solution)/shard_map/ppermute | solution.py:734
  75.1 24.4 %collective-permute-start.11 = (bf16[192,640]{1,0:T(8,128)(2,1)S(1)}, bf16[192,640]{1,0:T(8,128)(2,1)S(1)}, u32[]{:S(2)}, u32[]{:S(2)}) collective-permute-start(bf16[192,640]{1,0:T(8,128)(2,1)S(1)} %get-tuple-element.121), channel_id=1, source_target_pairs={{0,8},{1,9},{2,10},{3,11},{4,12},{5,13},{6,14},{7,15},{8,0},{9,1},... | collective-permute-start | bytes 737288 | tf_op jit(solution)/shard_map/ppermute | solution.py:734
  84.7 14.8 %collective-permute-start.12 = (bf16[192,640]{1,0:T(8,128)(2,1)S(1)}, bf16[192,640]{1,0:T(8,128)(2,1)S(1)}, u32[]{:S(2)}, u32[]{:S(2)}) collective-permute-start(bf16[192,640]{1,0:T(8,128)(2,1)S(1)} %get-tuple-element.122), channel_id=1, source_target_pairs={{0,12},{1,13},{2,14},{3,15},{4,8},{5,9},{6,10},{7,11},{8,4},{9,5},... | collective-permute-start | bytes 737288 | tf_op jit(solution)/shard_map/ppermute | solution.py:734
  88.0 20.4 %collective-permute-start.18 = (bf16[192,640]{1,0:T(8,128)(2,1)S(1)}, bf16[192,640]{1,0:T(8,128)(2,1)S(1)}, u32[]{:S(2)}, u32[]{:S(2)}) collective-permute-start(bf16[192,640]{1,0:T(8,128)(2,1)S(1)} %get-tuple-element.141), channel_id=1, source_target_pairs={{0,8},{1,9},{2,10},{3,11},{4,12},{5,13},{6,14},{7,15},{8,0},{9,1},... | collective-permute-start | bytes 737288 | tf_op jit(solution)/shard_map/ppermute | solution.py:734
  100.4 8.8 %collective-permute-start.13 = (bf16[192,128]{1,0:T(8,128)(2,1)S(1)}, bf16[192,128]{1,0:T(8,128)(2,1)S(1)}, u32[]{:S(2)}, u32[]{:S(2)}) collective-permute-start(bf16[192,128]{1,0:T(8,128)(2,1)S(1)} %get-tuple-element.124.refs_0_), channel_id=1, source_target_pairs={{0,1},{1,0},{2,3},{3,2},{4,5},{5,4},{6,7},{7,6},{8,9},{9,8},{10,11... | collective-permute-start | bytes 147464 | tf_op jit(solution)/shard_map/ppermute | solution.py:734
  110.1 1.9 %collective-permute-start.14 = (bf16[96,512]{1,0:T(8,128)(2,1)S(1)}, bf16[96,512]{1,0:T(8,128)(2,1)S(1)}, u32[]{:S(2)}, u32[]{:S(2)}) collective-permute-start(bf16[96,512]{1,0:T(8,128)(2,1)S(1)} %get-tuple-element.126), channel_id=1, source_target_pairs={{0,1},{1,0},{2,3},{3,2},{4,5},{5,4},{6,7},{7,6},{8,9},{9,8},{10,11... | collective-permute-start | bytes 294920 | tf_op jit(solution)/shard_map/ppermute | solution.py:734
  113.3 11.2 %collective-permute-start.21 = (bf16[192,1024]{1,0:T(8,128)(2,1)S(1)}, bf16[192,1024]{1,0:T(8,128)(2,1)S(1)}, u32[]{:S(2)}, u32[]{:S(2)}) collective-permute-start(bf16[192,1024]{1,0:T(8,128)(2,1)S(1)} %maximum_maximum_fusion.refs_0_), channel_id=1, source_target_pairs={{0,2},{1,3},{2,0},{3,1},{4,6},{5,7},{6,4},{7,5},{8,10},{9,11},{10,... | collective-permute-start | bytes 1179656 | tf_op jit(solution)/shard_map/ppermute | solution.py:907
  114.8 10.9 %collective-permute-start.22 = (bf16[192,1024]{1,0:T(8,128)(2,1)S(1)}, bf16[192,1024]{1,0:T(8,128)(2,1)S(1)}, u32[]{:S(2)}, u32[]{:S(2)}) collective-permute-start(bf16[192,1024]{1,0:T(8,128)(2,1)S(1)} %maximum_maximum_fusion.refs_0_), channel_id=1, source_target_pairs={{0,4},{1,5},{2,6},{3,7},{4,0},{5,1},{6,2},{7,3},{8,12},{9,13},{10,... | collective-permute-start | bytes 1179656 | tf_op jit(solution)/shard_map/ppermute | solution.py:893
  114.8 10.9 %collective-permute-start.23 = (bf16[192,1024]{1,0:T(8,128)(2,1)S(1)}, bf16[192,1024]{1,0:T(8,128)(2,1)S(1)}, u32[]{:S(2)}, u32[]{:S(2)}) collective-permute-start(bf16[192,1024]{1,0:T(8,128)(2,1)S(1)} %maximum_maximum_fusion.refs_0_), channel_id=1, source_target_pairs={{4,8},{5,9},{6,10},{7,11},{8,4},{9,5},{10,6},{11,7},{20,24},{21,25... | collective-permute-start | bytes 1179656 | tf_op jit(solution)/shard_map/ppermute | solution.py:893
  125.7 16.5 %collective-permute-start.25 = (bf16[192,1024]{1,0:T(8,128)(2,1)S(1)}, bf16[192,1024]{1,0:T(8,128)(2,1)S(1)}, u32[]{:S(2)}, u32[]{:S(2)}) collective-permute-start(bf16[192,1024]{1,0:T(8,128)(2,1)S(1)} %collective-permute-done.22.refs_2_), channel_id=1, source_target_pairs={{4,8},{5,9},{6,10},{7,11},{8,4},{9,5},{10,6},{11,7},{20,24},{21,25... | collective-permute-start | bytes 1179656 | tf_op jit(solution)/shard_map/ppermute | solution.py:893
  126.6 15.7 %collective-permute-start.26 = (bf16[192,1024]{1,0:T(8,128)(2,1)S(1)}, bf16[192,1024]{1,0:T(8,128)(2,1)S(1)}, u32[]{:S(2)}, u32[]{:S(2)}) collective-permute-start(bf16[192,1024]{1,0:T(8,128)(2,1)S(1)} %collective-permute-done.22.refs_2_), channel_id=1, source_target_pairs={{0,2},{1,3},{2,0},{3,1},{4,6},{5,7},{6,4},{7,5},{8,10},{9,11},{10,... | collective-permute-start | bytes 1179656 | tf_op jit(solution)/shard_map/ppermute | solution.py:907
  127.2 15.0 %collective-permute-start.24 = (bf16[192,1024]{1,0:T(8,128)(2,1)S(1)}, bf16[192,1024]{1,0:T(8,128)(2,1)S(1)}, u32[]{:S(2)}, u32[]{:S(2)}) collective-permute-start(bf16[192,1024]{1,0:T(8,128)(2,1)S(1)} %collective-permute-done.23), channel_id=1, source_target_pairs={{4,0},{5,1},{6,2},{7,3},{8,12},{9,13},{10,14},{11,15},{20,16},{21,... | collective-permute-start | bytes 1179656 | tf_op jit(solution)/shard_map/ppermute | solution.py:893
  128.6 8.5 %collective-permute-start.28 = (bf16[8,160,128]{2,1,0:T(8,128)(2,1)S(1)}, bf16[8,160,128]{2,1,0:T(8,128)(2,1)S(1)}, u32[]{:S(2)}, u32[]{:S(2)}) collective-permute-start(bf16[8,160,128]{2,1,0:T(8,128)(2,1)S(1)} %bitcast.44), channel_id=1, source_target_pairs={{0,16},{16,0},{1,17},{17,1},{2,18},{18,2},{3,19},{19,3},{4,20},{20... | collective-permute-start | bytes 983048 | tf_op jit(solution)/shard_map/ppermute | solution.py:737
  142.3 10.4 %collective-permute-start.29 = (bf16[192,1024]{1,0:T(8,128)(2,1)S(1)}, bf16[192,1024]{1,0:T(8,128)(2,1)S(1)}, u32[]{:S(2)}, u32[]{:S(2)}) collective-permute-start(bf16[192,1024]{1,0:T(8,128)(2,1)S(1)} %broadcast_select_fusion.1.refs_1_), channel_id=1, source_target_pairs={{4,0},{5,1},{6,2},{7,3},{8,12},{9,13},{10,14},{11,15},{20,16},{21,... | collective-permute-start | bytes 1179656 | tf_op jit(solution)/shard_map/ppermute | solution.py:893
  143.6 9.1 %collective-permute-start.30 = (bf16[192,1024]{1,0:T(8,128)(2,1)S(1)}, bf16[192,1024]{1,0:T(8,128)(2,1)S(1)}, u32[]{:S(2)}, u32[]{:S(2)}) collective-permute-start(bf16[192,1024]{1,0:T(8,128)(2,1)S(1)} %broadcast_select_fusion.1.refs_1_), channel_id=1, source_target_pairs={{0,2},{1,3},{2,0},{3,1},{4,6},{5,7},{6,4},{7,5},{8,10},{9,11},{10,... | collective-permute-start | bytes 1179656 | tf_op jit(solution)/shard_map/ppermute | solution.py:907
  145.2 1.6 collective-permute-start.31
  145.2 2.1 %collective-permute-start.32 = (bf16[8,160,128]{2,1,0:T(8,128)(2,1)S(1)}, bf16[8,160,128]{2,1,0:T(8,128)(2,1)S(1)}, u32[]{:S(2)}, u32[]{:S(2)}) collective-permute-start(bf16[8,160,128]{2,1,0:T(8,128)(2,1)S(1)} %collective-permute-done.28.far), channel_id=1, source_target_pairs={{0,1},{1,0},{2,3},{3,2},{4,5},{5,4},{6,7},{7,6},{8,9},{9,8},{10,11... | collective-permute-start | bytes 983048 | tf_op jit(solution)/shard_map/ppermute | solution.py:734
  152.8 9.1 %collective-permute-start.33 = (bf16[192,1024]{1,0:T(8,128)(2,1)S(1)}, bf16[192,1024]{1,0:T(8,128)(2,1)S(1)}, u32[]{:S(2)}, u32[]{:S(2)}) collective-permute-start(bf16[192,1024]{1,0:T(8,128)(2,1)S(1)} %broadcast_select_fusion.refs_3_), channel_id=1, source_target_pairs={{0,2},{1,3},{2,0},{3,1},{4,6},{5,7},{6,4},{7,5},{8,10},{9,11},{10,... | collective-permute-start | bytes 1179656 | tf_op jit(solution)/shard_map/ppermute | solution.py:907
  (16 other events, 171.7 us)

commit v6 on v5

--- a/solution.py
+++ b/solution.py
@@ -329,47 +329,45 @@
     )
 
 
-def weight_kernel(flips, info, order, wq_scale, kv_scale, wq, kv, *outs):
-    block = order[pl.program_id(0)]
+def weight_kernel(info, order, wq_scale, kv_scale, wq, kv, *outs):
     core, rank = info[0], info[1]
-    rows = wq.shape[0]
-    half = wq.shape[1] // 2
+    blocks, rows, columns = outs[0].shape
+    half = columns - TILE_SIDE
     tiles = half // TILE_SIDE
-    for flip, out in zip(flips, outs):
-        side = core ^ flip
-        for group in range(rows // GROUP_ROWS):
-            tile_row = (rank * (rows // GROUP_ROWS) + group) // 2
-            span = slice(group * GROUP_ROWS, (group + 1) * GROUP_ROWS)
+    tile_row = (rank * pl.num_programs(0) + pl.program_id(0)) // 2
+    for number, out in enumerate(outs):
+        side = core ^ (number % 2)
+        for at in range(blocks):
+            column = 2 * order[number // 2 * blocks + at] + side
             for tile in range(tiles):
-                scale = wq_scale[tile_row, (2 * block + side) * tiles + tile]
-                start = pl.multiple_of(side * half + tile * TILE_SIDE, TILE_SIDE)
-                codes = wq[span, pl.ds(start, TILE_SIDE)].astype(F32)
-                out[0, span, tile * TILE_SIDE : (tile + 1) * TILE_SIDE] = (codes * scale).astype(BF)
-            scale = kv_scale[tile_row, 2 * block + side]
-            start = pl.multiple_of(side * TILE_SIDE, TILE_SIDE)
-            codes = kv[span, pl.ds(start, TILE_SIDE)].astype(F32)
-            out[0, span, half : half + TILE_SIDE] = (codes * scale).astype(BF)
-
-
-def prepare_weights(flips, core, my_rank, order, chips, wq_codes, wq_scale, kv_codes, kv_scale):
-    rows = wq_codes.shape[0]
-    half = wq_codes.shape[1] // (2 * chips)
-    blocks = order.shape[0]
-    block = (1, rows, half + TILE_SIDE)
-    return pl.pallas_call(
-        functools.partial(weight_kernel, flips),
+                scale = wq_scale[tile_row, column * tiles + tile]
+                start = pl.multiple_of(column * half + tile * TILE_SIDE, TILE_SIDE)
+                codes = wq[:, pl.ds(start, TILE_SIDE)].astype(F32)
+                out[at, :, tile * TILE_SIDE : (tile + 1) * TILE_SIDE] = (codes * scale).astype(BF)
+            start = pl.multiple_of(column * TILE_SIDE, TILE_SIDE)
+            codes = kv[:, pl.ds(start, TILE_SIDE)].astype(F32)
+            out[at, :, half:] = (codes * kv_scale[tile_row, column]).astype(BF)
+
+
+def prepare_weights(core, my_rank, order, wq_codes, wq_scale, kv_codes, kv_scale):
+    rows, width = wq_codes.shape
+    chips = order.shape[0]
+    columns = width // (2 * chips) + TILE_SIDE
+    blocks = chips // 2
+    return pl.pallas_call(
+        weight_kernel,
         grid_spec=pltpu.PrefetchScalarGridSpec(
             num_scalar_prefetch=4,
-            grid=(blocks,),
+            grid=(rows // GROUP_ROWS,),
             in_specs=[
-                pl.BlockSpec((rows, 2 * half), lambda i, info, order, *_: (0, order[i])),
-                pl.BlockSpec((rows, 2 * TILE_SIDE), lambda i, info, order, *_: (0, order[i])),
+                pl.BlockSpec((GROUP_ROWS, width), lambda i, *_: (i, 0)),
+                pl.BlockSpec((GROUP_ROWS, kv_codes.shape[1]), lambda i, *_: (i, 0)),
             ],
-            out_specs=[pl.BlockSpec(block, lambda i, *_: (i, 0, 0))] * len(flips),
+            out_specs=[pl.BlockSpec((blocks, GROUP_ROWS, columns), lambda i, *_: (0, i, 0))] * 4,
         ),
-        out_shape=[jax.ShapeDtypeStruct((blocks, *block[1:]), BF)] * len(flips),
-        compiler_params=PARAMS,
-        cost_estimate=cost(rows * wq_codes.shape[1] * 4, rows * wq_codes.shape[1] * 3),
+        out_shape=[jax.ShapeDtypeStruct((blocks, rows, columns), BF)] * 4,
+        compiler_params=PARAMS,
+        cost_estimate=cost(rows * width * 4, rows * width * 5),
         name="prepare_weights",
     )(jnp.stack([core, my_rank]), order, wq_scale, kv_scale, wq_codes, kv_codes)
 
@@ -609,45 +607,38 @@
     core, my_rank = info[0], info[1]
     columns = held.shape[1]
     tiles = width // TILE_SIDE
-    pieces = [(block, half, side) for block in range(blocks) for half in range(2) for side in range(2)]
+    pieces = [(block, side) for block in range(blocks) for side in range(2)]
     copies = []
-    for number, (block, half, side) in enumerate(pieces):
-        start = (2 * info[2 + block] + (core ^ half)) * width
+    for number, (block, side) in enumerate(pieces):
+        start = pl.multiple_of(info[2 + block] * (2 * width), 2 * width)
         copy = pltpu.make_async_copy(
-            codes[side].at[:, pl.ds(pl.multiple_of(start, width), width)],
-            held.at[number],
-            arrived.at[number],
+            codes[side].at[:, pl.ds(start, 2 * width)], held.at[number], arrived.at[number]
         )
         copy.start()
         copies.append(copy)
     totals = [None, None]
-    for number, (block, half, side) in enumerate(pieces):
-        rows = attended[block][:, half * width : (half + 1) * width]
-        first_tile = (2 * info[2 + block] + (core ^ half)) * tiles
+    for number, (block, side) in enumerate(pieces):
         copies[number].wait()
-        weight = []
-        for group in range(columns // GROUP_ROWS):
-            column = ((my_rank ^ side) * columns + group * GROUP_ROWS) // TILE_SIDE
-            span = slice(group * GROUP_ROWS, (group + 1) * GROUP_ROWS)
-            weight.append(
-                jnp.concatenate(
-                    [
-                        (
-                            held[number, span, tile * TILE_SIDE : (tile + 1) * TILE_SIDE].astype(F32)
-                            * scales[first_tile + tile, column]
-                        ).astype(BF)
-                        for tile in range(tiles)
-                    ],
-                    axis=1,
-                )
+        for half in range(2):
+            rows = attended[block][:, half * width : (half + 1) * width]
+            first_tile = (2 * info[2 + block] + (core ^ half)) * tiles
+            weight = []
+            for group in range(columns // GROUP_ROWS):
+                column = ((my_rank ^ side) * columns + group * GROUP_ROWS) // TILE_SIDE
+                span = slice(group * GROUP_ROWS, (group + 1) * GROUP_ROWS)
+                parts = []
+                for tile in range(tiles):
+                    lane = pl.multiple_of((core ^ half) * width + tile * TILE_SIDE, TILE_SIDE)
+                    code = held[number, span, pl.ds(lane, TILE_SIDE)].astype(F32)
+                    parts.append((code * scales[first_tile + tile, column]).astype(BF))
+                weight.append(jnp.concatenate(parts, axis=1))
+            term = lax.dot_general(
+                jnp.concatenate(weight, axis=0),
+                rows,
+                (((1,), (1,)), ((), ())),
+                preferred_element_type=F32,
             )
-        term = lax.dot_general(
-            jnp.concatenate(weight, axis=0),
-            rows,
-            (((1,), (1,)), ((), ())),
-            preferred_element_type=F32,
-        )
-        totals[side] = term if totals[side] is None else totals[side] + term
+            totals[side] = term if totals[side] is None else totals[side] + term
     if has_start:
         start = refs[blocks + 2]
         totals = [total + start[side] for side, total in enumerate(totals)]
@@ -677,8 +668,8 @@
         + [pl.BlockSpec(memory_space=pl.ANY)] * 2
         + [vmem] * len(extra),
         scratch_shapes=[
-            pltpu.VMEM((4 * blocks, columns, both // 2), BF),
-            pltpu.SemaphoreType.DMA((4 * blocks,)),
+            pltpu.VMEM((2 * blocks, columns, both), BF),
+            pltpu.SemaphoreType.DMA((2 * blocks,)),
         ],
         compiler_params=PARAMS,
         cost_estimate=cost(4 * blocks * count * both * columns, 4 * blocks * both * columns),
@@ -764,21 +755,15 @@
 
     near = jnp.array([1, 3, 0, 2], jnp.int32) * y_count
 
-    def weights_of(flips, order):
-        return prepare_weights(
-            flips,
-            core,
-            my_rank,
-            order,
-            chips,
-            wq_codes,
-            wq_scale,
-            key_value_codes,
-            key_value_scale,
-        )
-
-    away_own, away_other = weights_of((0, 1), after(chip, sent) ^ 1 ^ near)
-    (home_other,) = weights_of((1,), after(chip, sent) ^ near)
+    away_own, away_other, home_own, home_other = prepare_weights(
+        core,
+        my_rank,
+        after(chip, sent) ^ jnp.concatenate([near ^ 1, near]),
+        wq_codes,
+        wq_scale,
+        key_value_codes,
+        key_value_scale,
+    )
     own = to_chips(sent)
     own, away_other, home_other, *by_z = lax.optimization_barrier(
         (own, away_other, home_other, *by_z)
@@ -800,7 +785,6 @@
     away, away_sent, away_kept = project(core, normed, away_own, away_other, BF)
     got = swap(away, 2)
     got_away = swap(away_sent, 2 * y_count)
-    (home_own,) = weights_of((0,), after(chip, away) ^ near)
     home, home_sent, home_kept = project(
         after(core, away), normed, home_own, home_other, F32
     )

time: 179 us -> 177 us (0.989)
  waiting for transfers between devices: 60.2 us -> 67.4 us
  Pallas kernels: 54.6 us -> 47.9 us
  starting transfers between devices: 39.9 us -> 38.1 us
    ppermute x22, waiting for transfers between devices: 37.6 us -> 44.7 us  [swap(): return lax.ppermute(values, 'fsdp', [(i, i ^ bits) for i in range(ranks)])]
    pallas_call x3 -> x1, Pallas kernels: 14.3 us -> 7.94 us  [prepare_weights(): pl.pallas_call(weight_kernel, grid_spec=pltpu.PrefetchScalarGridSpec(num_...]
    unnamed x30 -> x32, local copies, waits for them, and re-layouts: 4.93 us -> 2.95 us
  transfers between devices with their start and end apart: 34 -> 34, of which waited for: 15 -> 16; matrix products, arithmetic and copies ran while one was open for 2% -> 3% of each run, Pallas kernels for 29% -> 25%
where the time goes in v6:
time: 177 us; the launch traced here: 176 us
  waiting for transfers between devices  67.4 us (38%)
  Pallas kernels  47.9 us (27%)
  starting transfers between devices  38.1 us (22%)
  blocking collectives  12.6 us (7%)
  local copies, waits for them, and re-layouts  5.68 us (3%)
  other arithmetic  2.58 us (1%)
    ppermute x22, waiting for transfers between devices, swap(): return lax.ppermute(values, 'fsdp', [(i, i ^ bits) for i in range(ranks)])  44.7 us
    ppermute x22, starting transfers between devices, swap(): return lax.ppermute(values, 'fsdp', [(i, i ^ bits) for i in range(ranks)])  19.2 us
    pallas_call x3, Pallas kernels, out_project(): pl.pallas_call(functools.partial(out_kernel, blocks, bool(extra), last, b...  13.8 us
    all_to_all x1, blocking collectives, to_chips(): lax.all_to_all(values, 'fsdp', split_axis=0, concat_axis=0, tiled=True, a...  12.6 us
    ppermute x4, waiting for transfers between devices, swap_y(): return lax.ppermute(values, 'fsdp', [(i, i ^ 2) for i in range(ranks)])  10.9 us
    pallas_call x2, Pallas kernels, project(): pl.pallas_call(project_kernel, grid=(blocks,), in_specs=[SMEM, pl.BlockSp...  9.68 us
    ppermute x5, waiting for transfers between devices, hop(): return lax.ppermute(values, 'fsdp', moves)  8.03 us
    pallas_call x1, Pallas kernels, prepare_weights(): pl.pallas_call(weight_kernel, grid_spec=pltpu.PrefetchScalarGridSpec(num_...  7.94 us
  transfers between devices with their start and end apart: 34, of which 16 were waited for; matrix products, arithmetic and copies ran while one was open for 3% of the time, Pallas kernels for 25%

profile of v6, /device:TPU:0, one launch (start us, length us, event | category | flops | bytes accessed | tf_op | source)
XLA Modules:
  0.0 175.9 jit_solution(3731867344198838739)
XLA Ops:
  2.6 5.4 %pick_rows.2 = bf16[8,32,640]{2,1,0:T(8,128)(2,1)} custom-call(s32[1]{0:T(128)} %constant.156.clone.1.info, f32[8,384]{1,0:T(8,128)S(1)} %get-tuple-element.242.rows, f32[1,5120]{1,0:T(1,128)} %bitcast.59, bf16[600,5120]{1,0:T(8,128)(2,1)} %table.1), custom_call_target="tpu_custom_call" | custom-call | flops 196608000 | bytes 6144000 | tf_op jit(solution)/shard_map/pick_rows/pallas_call | solution.py:281
  8.0 7.0 %all-to-all-start.1 = ((bf16[8,32,640]{2,1,0:T(8,128)(2,1)}), bf16[8,32,640]{2,1,0:T(8,128)(2,1)S(1)}, u32[]{:S(2)}, u32[]{:S(2)}) async-start(bf16[8,32,640]{2,1,0:T(8,128)(2,1)} %pick_rows.2), calls=%async_computation.1 | async-start | bytes 655360 | tf_op jit(solution)/shard_map/all_to_all | solution.py:731
  15.0 1.6 prepare_keys.1
  17.4 2.0 %collective-permute-start.1 = (bf16[2,160,128]{2,1,0:T(8,128)(2,1)}, bf16[2,160,128]{2,1,0:T(8,128)(2,1)}, u32[]{:S(2)}, u32[]{:S(2)}) collective-permute-start(bf16[2,160,128]{2,1,0:T(8,128)(2,1)} %get-tuple-element.178), channel_id=1, source_target_pairs={{0,4},{1,5},{2,6},{3,7},{4,0},{5,1},{6,2},{7,3},{8,12},{9,13},{10,... | collective-permute-start | bytes 245768 | tf_op jit(solution)/shard_map/ppermute | solution.py:725
  19.4 2.4 %collective-permute-start.2 = (bf16[2,160,128]{2,1,0:T(8,128)(2,1)}, bf16[2,160,128]{2,1,0:T(8,128)(2,1)}, u32[]{:S(2)}, u32[]{:S(2)}) collective-permute-start(bf16[2,160,128]{2,1,0:T(8,128)(2,1)} %get-tuple-element.177), channel_id=1, source_target_pairs={{0,8},{1,9},{2,10},{3,11},{4,12},{5,13},{6,14},{7,15},{8,0},{9,1},... | collective-permute-start | bytes 245768 | tf_op jit(solution)/shard_map/ppermute | solution.py:725
  21.9 7.9 %prepare_weights.1 = (bf16[4,320,640]{2,1,0:T(8,128)(2,1)S(1)}, bf16[4,320,640]{2,1,0:T(8,128)(2,1)S(1)}, bf16[4,320,640]{2,1,0:T(8,128)(2,1)}, bf16[4,320,640]{2,1,0:T(8,128)(2,1)}) custom-call(s32[2]{0:T(128)S(1)} %pad_add_fusion.3.info, s32[8]{0:T(128)S(1)} %broadcast_xor_fusion.1.order, f32[40,64]{1,0:T(8,128)S(1)} %copy-done.2, ...), custom_call_target="tpu_custom_call" | custom-call | flops 10485760 | bytes 13107200 | tf_op jit(solution)/shard_map/prepare_weights/pallas_call | solution.py:357
  34.1 2.0 %collective-permute-done.5 = f32[8,128]{1,0:T(8,128)S(1)} collective-permute-done((f32[8,128]{1,0:T(8,128)S(1)}, f32[8,128]{1,0:T(8,128)S(1)}, u32[]{:S(2)}, u32[]{:S(2)}) %collective-permute-start.5) | collective-permute-done | bytes 4128 | tf_op jit(solution)/shard_map/ppermute | solution.py:728
  38.7 4.4 %project.2 = (bf16[4,192,640]{2,1,0:T(8,128)(2,1)S(1)}, bf16[2,192,640]{2,1,0:T(8,128)(2,1)S(1)}, f32[2,192,640]{2,1,0:T(8,128)S(1)}) custom-call(s32[1]{0:T(128)} %bitcast.5.info, bf16[384,640]{1,0:T(8,128)(2,1)S(1)} %get-tuple-element.111.normed, bf16[4,320,640]{2,1,0:T(8,128)(2,1)S(1)} %get-tuple-element.112.own, ...), custom_call_target="tpu_custom_call" | custom-call | flops 1258291200 | bytes 5242880 | tf_op jit(solution)/shard_map/project/pallas_call | solution.py:428
  43.1 1.5 collective-permute-start.8
  44.6 1.5 collective-permute-start.9
  46.1 5.3 %project.3 = (f32[4,192,640]{2,1,0:T(8,128)}, bf16[2,192,640]{2,1,0:T(8,128)(2,1)S(1)}, f32[2,192,640]{2,1,0:T(8,128)S(1)}) custom-call(s32[1]{0:T(128)} %bitcast.13.info, bf16[384,640]{1,0:T(8,128)(2,1)} %copy-done.8, bf16[4,320,640]{2,1,0:T(8,128)(2,1)S(1)} %copy-done.6, bf16[4,320,640]{2,1,0:T(8,128)(2,1)} %collective-permute-done.7.other), custom_call_target="tpu_custom_call" | custom-call | flops 1258291200 | bytes 5242880 | tf_op jit(solution)/shard_map/project/pallas_call | solution.py:428
  51.9 6.8 %collective-permute-done.9.got_away = bf16[2,192,640]{2,1,0:T(8,128)(2,1)S(1)} collective-permute-done((bf16[2,192,640]{2,1,0:T(8,128)(2,1)S(1)}, bf16[2,192,640]{2,1,0:T(8,128)(2,1)S(1)}, u32[]{:S(2)}, u32[]{:S(2)}) %collective-permute-start.9) | collective-permute-done | bytes 491552 | tf_op jit(solution)/shard_map/ppermute | solution.py:725
  58.7 7.9 %collective-permute-done.8.got = bf16[4,192,640]{2,1,0:T(8,128)(2,1)S(1)} collective-permute-done((bf16[4,192,640]{2,1,0:T(8,128)(2,1)S(1)}, bf16[4,192,640]{2,1,0:T(8,128)(2,1)S(1)}, u32[]{:S(2)}, u32[]{:S(2)}) %collective-permute-start.8) | collective-permute-done | bytes 983072 | tf_op jit(solution)/shard_map/ppermute | solution.py:725
  66.7 1.5 copy-done.1
  68.6 1.5 collective-permute-start.16
  70.1 1.6 collective-permute-start.10
  73.4 1.9 %collective-permute-start.11 = (bf16[192,640]{1,0:T(8,128)(2,1)S(1)}, bf16[192,640]{1,0:T(8,128)(2,1)S(1)}, u32[]{:S(2)}, u32[]{:S(2)}) collective-permute-start(bf16[192,640]{1,0:T(8,128)(2,1)S(1)} %get-tuple-element.123), channel_id=1, source_target_pairs={{0,8},{1,9},{2,10},{3,11},{4,12},{5,13},{6,14},{7,15},{8,0},{9,1},... | collective-permute-start | bytes 737288 | tf_op jit(solution)/shard_map/ppermute | solution.py:725
  75.3 7.2 %collective-permute-done.16.got = bf16[2,192,640]{2,1,0:T(8,128)(2,1)S(1)} collective-permute-done((bf16[2,192,640]{2,1,0:T(8,128)(2,1)S(1)}, bf16[2,192,640]{2,1,0:T(8,128)(2,1)S(1)}, u32[]{:S(2)}, u32[]{:S(2)}) %collective-permute-start.16) | collective-permute-done | bytes 491552 | tf_op jit(solution)/shard_map/ppermute | solution.py:725
  82.5 2.9 %collective-permute-start.12 = (bf16[192,640]{1,0:T(8,128)(2,1)S(1)}, bf16[192,640]{1,0:T(8,128)(2,1)S(1)}, u32[]{:S(2)}, u32[]{:S(2)}) collective-permute-start(bf16[192,640]{1,0:T(8,128)(2,1)S(1)} %get-tuple-element.124), channel_id=1, source_target_pairs={{0,12},{1,13},{2,14},{3,15},{4,8},{5,9},{6,10},{7,11},{8,4},{9,5},... | collective-permute-start | bytes 737288 | tf_op jit(solution)/shard_map/ppermute | solution.py:725
  86.8 11.1 %collective-permute-done.11.refs_2_ = bf16[192,640]{1,0:T(8,128)(2,1)S(1)} collective-permute-done((bf16[192,640]{1,0:T(8,128)(2,1)S(1)}, bf16[192,640]{1,0:T(8,128)(2,1)S(1)}, u32[]{:S(2)}, u32[]{:S(2)}) %collective-permute-start.11) | collective-permute-done | bytes 245792 | tf_op jit(solution)/shard_map/ppermute | solution.py:725
  98.9 7.8 %collective-permute-done.18.refs_1_ = bf16[192,640]{1,0:T(8,128)(2,1)S(1)} collective-permute-done((bf16[192,640]{1,0:T(8,128)(2,1)S(1)}, bf16[192,640]{1,0:T(8,128)(2,1)S(1)}, u32[]{:S(2)}, u32[]{:S(2)}) %collective-permute-start.18) | collective-permute-done | bytes 245792 | tf_op jit(solution)/shard_map/ppermute | solution.py:725
  113.8 9.1 %collective-permute-done.21.refs_1_ = bf16[192,1024]{1,0:T(8,128)(2,1)S(1)} collective-permute-done((bf16[192,1024]{1,0:T(8,128)(2,1)S(1)}, bf16[192,1024]{1,0:T(8,128)(2,1)S(1)}, u32[]{:S(2)}, u32[]{:S(2)}) %collective-permute-start.21) | collective-permute-done | bytes 393248 | tf_op jit(solution)/shard_map/ppermute | solution.py:891
  126.9 1.6 collective-permute-start.28
  128.7 4.8 %out_project.3.refs_6_ = f32[2,320,192]{2,1,0:T(8,128)S(1)} custom-call(s32[5]{0:T(128)S(1)} %pad_add_fusion.4.info, f32[64,40]{1,0:T(8,128)S(1)} %copy.22.scales, bf16[192,1024]{1,0:T(8,128)(2,1)S(1)} %maximum_maximum_fusion.refs_0_, bf16[192,1024]{1,0:T(8,128)(2,1)S(1)} %collective-permute-done.21.refs_1_, ...), custom_call_target="tpu_custom_call" | custom-call | flops 754974720 | bytes 3932160 | tf_op jit(solution)/shard_map/out_project/pallas_call | solution.py:663
  133.5 1.9 %collective-permute-done.28.far = bf16[8,160,128]{2,1,0:T(8,128)(2,1)S(1)} collective-permute-done((bf16[8,160,128]{2,1,0:T(8,128)(2,1)S(1)}, bf16[8,160,128]{2,1,0:T(8,128)(2,1)S(1)}, u32[]{:S(2)}, u32[]{:S(2)}) %collective-permute-start.28) | collective-permute-done | bytes 327712 | tf_op jit(solution)/shard_map/ppermute | solution.py:728
  135.3 4.5 %collective-permute-done.24 = bf16[192,1024]{1,0:T(8,128)(2,1)S(1)} collective-permute-done((bf16[192,1024]{1,0:T(8,128)(2,1)S(1)}, bf16[192,1024]{1,0:T(8,128)(2,1)S(1)}, u32[]{:S(2)}, u32[]{:S(2)}) %collective-permute-start.24) | collective-permute-done | bytes 393248 | tf_op jit(solution)/shard_map/ppermute | solution.py:877
  144.6 3.3 %collect_keys.1 = bf16[8,2,2,160,128]{4,3,2,1,0:T(8,128)(2,1)} custom-call(s32[3]{0:T(128)S(1)} %pad_add_fusion.5.info, bf16[8,160,128]{2,1,0:T(8,128)(2,1)S(1)} %bitcast.46, bf16[8,160,128]{2,1,0:T(8,128)(2,1)S(1)} %collective-permute-done.28.far, bf16[8,160,128]{2,1,0:T(8,128)(2,1)S(1)} %collective-permute-done.31.other, ...), custom_call_target="tpu_custom_call" | custom-call | bytes 2621440 | tf_op jit(solution)/shard_map/collect_keys/pallas_call | solution.py:859
  148.0 2.4 %collective-permute-done.29 = bf16[192,1024]{1,0:T(8,128)(2,1)S(1)} collective-permute-done((bf16[192,1024]{1,0:T(8,128)(2,1)S(1)}, bf16[192,1024]{1,0:T(8,128)(2,1)S(1)}, u32[]{:S(2)}, u32[]{:S(2)}) %collective-permute-start.29) | collective-permute-done | bytes 393248 | tf_op jit(solution)/shard_map/ppermute | solution.py:877
  151.9 5.6 %out_project.4.refs_3_ = f32[2,320,192]{2,1,0:T(8,128)S(1)} custom-call(s32[6]{0:T(128)S(1)} %pad_add_fusion.6.info, f32[64,40]{1,0:T(8,128)S(1)} %copy.22.scales, bf16[192,1024]{1,0:T(8,128)(2,1)S(1)} %collective-permute-done.26.refs_0_, bf16[192,1024]{1,0:T(8,128)(2,1)S(1)} %broadcast_select_fusion.1.refs_1_, ...), custom_call_target="tpu_custom_call" | custom-call | flops 1006632960 | bytes 5242880 | tf_op jit(solution)/shard_map/out_project/pallas_call | solution.py:663
  157.5 1.8 collective-permute-done.33.refs_0_
  159.2 3.3 %out_project.5 = bf16[192,640]{1,0:T(8,128)(2,1)S(1)} custom-call(s32[3]{0:T(128)S(1)} %pad_add_fusion.1.info, f32[64,40]{1,0:T(8,128)S(1)} %copy.22.scales, bf16[192,1024]{1,0:T(8,128)(2,1)S(1)} %collective-permute-done.33.refs_0_, bf16[320,8192]{1,0:T(8,128)(2,1)} %bitcast.56, bf16[320,8192]{1,0:T(8,128)(2,1)} %collective-permute-done.27.refs_4_.refs_5_.refs_2_, ...), custom_call_target="tpu_custom_call" | custom-call | flops 251658240 | bytes 1310720 | tf_op jit(solution)/shard_map/out_project/pallas_call | solution.py:663
  162.6 12.6 %all_to_all.16 = bf16[8,24,640]{2,1,0:T(8,128)(2,1)S(1)} all-to-all(bf16[8,24,640]{2,1,0:T(8,128)(2,1)S(1)} %bitcast.47), channel_id=1, replica_groups={{0,2,4,6,8,10,12,14},{1,3,5,7,9,11,13,15},{16,18,20,22,24,26,28,30},{17..., dimensions={0} | all-to-all | bytes 491520 | tf_op jit(solution)/shard_map/all_to_all | solution.py:731
  (112 shorter events, 32.6 us)
Async XLA Ops:
  0.6 128.1 %collective-permute-start.27 = (bf16[320,8192]{1,0:T(8,128)(2,1)}, bf16[320,8192]{1,0:T(8,128)(2,1)}, u32[]{:S(2)}, u32[]{:S(2)}) collective-permute-start(bf16[320,8192]{1,0:T(8,128)(2,1)} %bitcast.53), channel_id=1, source_target_pairs={{0,1},{1,0},{2,3},{3,2},{4,5},{5,4},{6,7},{7,6},{8,9},{9,8},{10,11... | collective-permute-start | bytes 15728648 | tf_op jit(solution)/shard_map/ppermute | solution.py:725
  8.0 24.0 %all-to-all-start.1 = ((bf16[8,32,640]{2,1,0:T(8,128)(2,1)}), bf16[8,32,640]{2,1,0:T(8,128)(2,1)S(1)}, u32[]{:S(2)}, u32[]{:S(2)}) async-start(bf16[8,32,640]{2,1,0:T(8,128)(2,1)} %pick_rows.2), calls=%async_computation.1 | async-start | bytes 655360 | tf_op jit(solution)/shard_map/all_to_all | solution.py:731
  17.4 13.6 %collective-permute-start.1 = (bf16[2,160,128]{2,1,0:T(8,128)(2,1)}, bf16[2,160,128]{2,1,0:T(8,128)(2,1)}, u32[]{:S(2)}, u32[]{:S(2)}) collective-permute-start(bf16[2,160,128]{2,1,0:T(8,128)(2,1)} %get-tuple-element.178), channel_id=1, source_target_pairs={{0,4},{1,5},{2,6},{3,7},{4,0},{5,1},{6,2},{7,3},{8,12},{9,13},{10,... | collective-permute-start | bytes 245768 | tf_op jit(solution)/shard_map/ppermute | solution.py:725
  19.4 12.6 %collective-permute-start.2 = (bf16[2,160,128]{2,1,0:T(8,128)(2,1)}, bf16[2,160,128]{2,1,0:T(8,128)(2,1)}, u32[]{:S(2)}, u32[]{:S(2)}) collective-permute-start(bf16[2,160,128]{2,1,0:T(8,128)(2,1)} %get-tuple-element.177), channel_id=1, source_target_pairs={{0,8},{1,9},{2,10},{3,11},{4,12},{5,13},{6,14},{7,15},{8,0},{9,1},... | collective-permute-start | bytes 245768 | tf_op jit(solution)/shard_map/ppermute | solution.py:725
  21.8 10.2 %collective-permute-start.3 = (bf16[2,160,128]{2,1,0:T(8,128)(2,1)}, bf16[2,160,128]{2,1,0:T(8,128)(2,1)}, u32[]{:S(2)}, u32[]{:S(2)}) collective-permute-start(bf16[2,160,128]{2,1,0:T(8,128)(2,1)} %get-tuple-element.176), channel_id=1, source_target_pairs={{0,12},{1,13},{2,14},{3,15},{4,8},{5,9},{6,10},{7,11},{8,4},{9,5},... | collective-permute-start | bytes 245768 | tf_op jit(solution)/shard_map/ppermute | solution.py:725
  32.0 6.7 %collective-permute-start.6 = (bf16[4,320,640]{2,1,0:T(8,128)(2,1)}, bf16[4,320,640]{2,1,0:T(8,128)(2,1)}, u32[]{:S(2)}, u32[]{:S(2)}) collective-permute-start(bf16[4,320,640]{2,1,0:T(8,128)(2,1)} %copy-done.7), channel_id=1, source_target_pairs={{0,1},{1,0},{2,3},{3,2},{4,5},{5,4},{6,7},{7,6},{8,9},{9,8},{10,11... | collective-permute-start | bytes 4915208 | tf_op jit(solution)/shard_map/ppermute | solution.py:725
  32.0 14.1 %collective-permute-start.7 = (bf16[4,320,640]{2,1,0:T(8,128)(2,1)}, bf16[4,320,640]{2,1,0:T(8,128)(2,1)}, u32[]{:S(2)}, u32[]{:S(2)}) collective-permute-start(bf16[4,320,640]{2,1,0:T(8,128)(2,1)} %get-tuple-element.117), channel_id=1, source_target_pairs={{0,1},{1,0},{2,3},{3,2},{4,5},{5,4},{6,7},{7,6},{8,9},{9,8},{10,11... | collective-permute-start | bytes 4915208 | tf_op jit(solution)/shard_map/ppermute | solution.py:725
  32.5 4.2 %collective-permute-start.4 = (bf16[8,32,640]{2,1,0:T(8,128)(2,1)S(1)}, bf16[8,32,640]{2,1,0:T(8,128)(2,1)S(1)}, u32[]{:S(2)}, u32[]{:S(2)}) collective-permute-start(bf16[8,32,640]{2,1,0:T(8,128)(2,1)S(1)} %all-to-all-done.1), channel_id=1, source_target_pairs={{0,1},{1,0},{2,3},{3,2},{4,5},{5,4},{6,7},{7,6},{8,9},{9,8},{10,11... | collective-permute-start | bytes 983048 | tf_op jit(solution)/shard_map/ppermute | solution.py:725
  32.6 3.6 %collective-permute-start.5 = (f32[8,128]{1,0:T(8,128)S(1)}, f32[8,128]{1,0:T(8,128)S(1)}, u32[]{:S(2)}, u32[]{:S(2)}) collective-permute-start(f32[8,128]{1,0:T(8,128)S(1)} %get-tuple-element.110), channel_id=1, source_target_pairs={{0,16},{16,0},{1,17},{17,1},{2,18},{18,2},{3,19},{19,3},{4,20},{20... | collective-permute-start | bytes 12296 | tf_op jit(solution)/shard_map/ppermute | solution.py:728
  43.1 23.6 %collective-permute-start.8 = (bf16[4,192,640]{2,1,0:T(8,128)(2,1)S(1)}, bf16[4,192,640]{2,1,0:T(8,128)(2,1)S(1)}, u32[]{:S(2)}, u32[]{:S(2)}) collective-permute-start(bf16[4,192,640]{2,1,0:T(8,128)(2,1)S(1)} %get-tuple-element.114), channel_id=1, source_target_pairs={{0,2},{1,3},{2,0},{3,1},{4,6},{5,7},{6,4},{7,5},{8,10},{9,11},{10,... | collective-permute-start | bytes 2949128 | tf_op jit(solution)/shard_map/ppermute | solution.py:725
  44.6 14.1 %collective-permute-start.9 = (bf16[2,192,640]{2,1,0:T(8,128)(2,1)S(1)}, bf16[2,192,640]{2,1,0:T(8,128)(2,1)S(1)}, u32[]{:S(2)}, u32[]{:S(2)}) collective-permute-start(bf16[2,192,640]{2,1,0:T(8,128)(2,1)S(1)} %get-tuple-element.119), channel_id=1, source_target_pairs={{0,4},{1,5},{2,6},{3,7},{4,0},{5,1},{6,2},{7,3},{8,12},{9,13},{10,... | collective-permute-start | bytes 1474568 | tf_op jit(solution)/shard_map/ppermute | solution.py:725
  51.4 17.0 %collective-permute-start.15 = (bf16[2,192,640]{2,1,0:T(8,128)(2,1)S(1)}, bf16[2,192,640]{2,1,0:T(8,128)(2,1)S(1)}, u32[]{:S(2)}, u32[]{:S(2)}) collective-permute-start(bf16[2,192,640]{2,1,0:T(8,128)(2,1)S(1)} %get-tuple-element.132), channel_id=1, source_target_pairs={{0,4},{1,5},{2,6},{3,7},{4,0},{5,1},{6,2},{7,3},{8,12},{9,13},{10,... | collective-permute-start | bytes 1474568 | tf_op jit(solution)/shard_map/ppermute | solution.py:725
  68.6 13.9 %collective-permute-start.16 = (bf16[2,192,640]{2,1,0:T(8,128)(2,1)S(1)}, bf16[2,192,640]{2,1,0:T(8,128)(2,1)S(1)}, u32[]{:S(2)}, u32[]{:S(2)}) collective-permute-start(bf16[2,192,640]{2,1,0:T(8,128)(2,1)S(1)} %get-tuple-element.136), channel_id=1, source_target_pairs={{0,2},{1,3},{2,0},{3,1},{4,6},{5,7},{6,4},{7,5},{8,10},{9,11},{10,... | collective-permute-start | bytes 1474568 | tf_op jit(solution)/shard_map/ppermute | solution.py:725
  70.1 15.5 %collective-permute-start.10 = (bf16[192,640]{1,0:T(8,128)(2,1)S(1)}, bf16[192,640]{1,0:T(8,128)(2,1)S(1)}, u32[]{:S(2)}, u32[]{:S(2)}) collective-permute-start(bf16[192,640]{1,0:T(8,128)(2,1)S(1)} %get-tuple-element.122), channel_id=1, source_target_pairs={{0,4},{1,5},{2,6},{3,7},{4,0},{5,1},{6,2},{7,3},{8,12},{9,13},{10,... | collective-permute-start | bytes 737288 | tf_op jit(solution)/shard_map/ppermute | solution.py:725
  72.8 26.1 %collective-permute-start.17 = (bf16[4,160,128]{2,1,0:T(8,128)(2,1)S(1)}, bf16[4,160,128]{2,1,0:T(8,128)(2,1)S(1)}, u32[]{:S(2)}, u32[]{:S(2)}) collective-permute-start(bf16[4,160,128]{2,1,0:T(8,128)(2,1)S(1)} %get-tuple-element.181), channel_id=1, source_target_pairs={{0,2},{1,3},{2,0},{3,1},{4,6},{5,7},{6,4},{7,5},{8,10},{9,11},{10,... | collective-permute-start | bytes 491528 | tf_op jit(solution)/shard_map/ppermute | solution.py:725
  73.4 24.5 %collective-permute-start.11 = (bf16[192,640]{1,0:T(8,128)(2,1)S(1)}, bf16[192,640]{1,0:T(8,128)(2,1)S(1)}, u32[]{:S(2)}, u32[]{:S(2)}) collective-permute-start(bf16[192,640]{1,0:T(8,128)(2,1)S(1)} %get-tuple-element.123), channel_id=1, source_target_pairs={{0,8},{1,9},{2,10},{3,11},{4,12},{5,13},{6,14},{7,15},{8,0},{9,1},... | collective-permute-start | bytes 737288 | tf_op jit(solution)/shard_map/ppermute | solution.py:725
  82.5 15.4 %collective-permute-start.12 = (bf16[192,640]{1,0:T(8,128)(2,1)S(1)}, bf16[192,640]{1,0:T(8,128)(2,1)S(1)}, u32[]{:S(2)}, u32[]{:S(2)}) collective-permute-start(bf16[192,640]{1,0:T(8,128)(2,1)S(1)} %get-tuple-element.124), channel_id=1, source_target_pairs={{0,12},{1,13},{2,14},{3,15},{4,8},{5,9},{6,10},{7,11},{8,4},{9,5},... | collective-permute-start | bytes 737288 | tf_op jit(solution)/shard_map/ppermute | solution.py:725
  85.6 21.2 %collective-permute-start.18 = (bf16[192,640]{1,0:T(8,128)(2,1)S(1)}, bf16[192,640]{1,0:T(8,128)(2,1)S(1)}, u32[]{:S(2)}, u32[]{:S(2)}) collective-permute-start(bf16[192,640]{1,0:T(8,128)(2,1)S(1)} %get-tuple-element.143), channel_id=1, source_target_pairs={{0,8},{1,9},{2,10},{3,11},{4,12},{5,13},{6,14},{7,15},{8,0},{9,1},... | collective-permute-start | bytes 737288 | tf_op jit(solution)/shard_map/ppermute | solution.py:725
  98.8 8.8 %collective-permute-start.13 = (bf16[192,128]{1,0:T(8,128)(2,1)S(1)}, bf16[192,128]{1,0:T(8,128)(2,1)S(1)}, u32[]{:S(2)}, u32[]{:S(2)}) collective-permute-start(bf16[192,128]{1,0:T(8,128)(2,1)S(1)} %get-tuple-element.126.refs_0_), channel_id=1, source_target_pairs={{0,1},{1,0},{2,3},{3,2},{4,5},{5,4},{6,7},{7,6},{8,9},{9,8},{10,11... | collective-permute-start | bytes 147464 | tf_op jit(solution)/shard_map/ppermute | solution.py:725
  108.4 1.9 %collective-permute-start.14 = (bf16[96,512]{1,0:T(8,128)(2,1)S(1)}, bf16[96,512]{1,0:T(8,128)(2,1)S(1)}, u32[]{:S(2)}, u32[]{:S(2)}) collective-permute-start(bf16[96,512]{1,0:T(8,128)(2,1)S(1)} %get-tuple-element.128), channel_id=1, source_target_pairs={{0,1},{1,0},{2,3},{3,2},{4,5},{5,4},{6,7},{7,6},{8,9},{9,8},{10,11... | collective-permute-start | bytes 294920 | tf_op jit(solution)/shard_map/ppermute | solution.py:725
  111.7 11.2 %collective-permute-start.21 = (bf16[192,1024]{1,0:T(8,128)(2,1)S(1)}, bf16[192,1024]{1,0:T(8,128)(2,1)S(1)}, u32[]{:S(2)}, u32[]{:S(2)}) collective-permute-start(bf16[192,1024]{1,0:T(8,128)(2,1)S(1)} %maximum_maximum_fusion.refs_0_), channel_id=1, source_target_pairs={{0,2},{1,3},{2,0},{3,1},{4,6},{5,7},{6,4},{7,5},{8,10},{9,11},{10,... | collective-permute-start | bytes 1179656 | tf_op jit(solution)/shard_map/ppermute | solution.py:891
  113.1 10.9 %collective-permute-start.22 = (bf16[192,1024]{1,0:T(8,128)(2,1)S(1)}, bf16[192,1024]{1,0:T(8,128)(2,1)S(1)}, u32[]{:S(2)}, u32[]{:S(2)}) collective-permute-start(bf16[192,1024]{1,0:T(8,128)(2,1)S(1)} %maximum_maximum_fusion.refs_0_), channel_id=1, source_target_pairs={{0,4},{1,5},{2,6},{3,7},{4,0},{5,1},{6,2},{7,3},{8,12},{9,13},{10,... | collective-permute-start | bytes 1179656 | tf_op jit(solution)/shard_map/ppermute | solution.py:877
  113.1 10.9 %collective-permute-start.23 = (bf16[192,1024]{1,0:T(8,128)(2,1)S(1)}, bf16[192,1024]{1,0:T(8,128)(2,1)S(1)}, u32[]{:S(2)}, u32[]{:S(2)}) collective-permute-start(bf16[192,1024]{1,0:T(8,128)(2,1)S(1)} %maximum_maximum_fusion.refs_0_), channel_id=1, source_target_pairs={{4,8},{5,9},{6,10},{7,11},{8,4},{9,5},{10,6},{11,7},{20,24},{21,25... | collective-permute-start | bytes 1179656 | tf_op jit(solution)/shard_map/ppermute | solution.py:877
  124.0 15.9 %collective-permute-start.25 = (bf16[192,1024]{1,0:T(8,128)(2,1)S(1)}, bf16[192,1024]{1,0:T(8,128)(2,1)S(1)}, u32[]{:S(2)}, u32[]{:S(2)}) collective-permute-start(bf16[192,1024]{1,0:T(8,128)(2,1)S(1)} %collective-permute-done.22.refs_2_), channel_id=1, source_target_pairs={{4,8},{5,9},{6,10},{7,11},{8,4},{9,5},{10,6},{11,7},{20,24},{21,25... | collective-permute-start | bytes 1179656 | tf_op jit(solution)/shard_map/ppermute | solution.py:877
  124.7 15.2 %collective-permute-start.26 = (bf16[192,1024]{1,0:T(8,128)(2,1)S(1)}, bf16[192,1024]{1,0:T(8,128)(2,1)S(1)}, u32[]{:S(2)}, u32[]{:S(2)}) collective-permute-start(bf16[192,1024]{1,0:T(8,128)(2,1)S(1)} %collective-permute-done.22.refs_2_), channel_id=1, source_target_pairs={{0,2},{1,3},{2,0},{3,1},{4,6},{5,7},{6,4},{7,5},{8,10},{9,11},{10,... | collective-permute-start | bytes 1179656 | tf_op jit(solution)/shard_map/ppermute | solution.py:891
  125.4 14.5 %collective-permute-start.24 = (bf16[192,1024]{1,0:T(8,128)(2,1)S(1)}, bf16[192,1024]{1,0:T(8,128)(2,1)S(1)}, u32[]{:S(2)}, u32[]{:S(2)}) collective-permute-start(bf16[192,1024]{1,0:T(8,128)(2,1)S(1)} %collective-permute-done.23), channel_id=1, source_target_pairs={{4,0},{5,1},{6,2},{7,3},{8,12},{9,13},{10,14},{11,15},{20,16},{21,... | collective-permute-start | bytes 1179656 | tf_op jit(solution)/shard_map/ppermute | solution.py:877
  126.9 8.4 %collective-permute-start.28 = (bf16[8,160,128]{2,1,0:T(8,128)(2,1)S(1)}, bf16[8,160,128]{2,1,0:T(8,128)(2,1)S(1)}, u32[]{:S(2)}, u32[]{:S(2)}) collective-permute-start(bf16[8,160,128]{2,1,0:T(8,128)(2,1)S(1)} %bitcast.44), channel_id=1, source_target_pairs={{0,16},{16,0},{1,17},{17,1},{2,18},{18,2},{3,19},{19,3},{4,20},{20... | collective-permute-start | bytes 983048 | tf_op jit(solution)/shard_map/ppermute | solution.py:728
  139.9 10.4 %collective-permute-start.29 = (bf16[192,1024]{1,0:T(8,128)(2,1)S(1)}, bf16[192,1024]{1,0:T(8,128)(2,1)S(1)}, u32[]{:S(2)}, u32[]{:S(2)}) collective-permute-start(bf16[192,1024]{1,0:T(8,128)(2,1)S(1)} %broadcast_select_fusion.1.refs_1_), channel_id=1, source_target_pairs={{4,0},{5,1},{6,2},{7,3},{8,12},{9,13},{10,14},{11,15},{20,16},{21,... | collective-permute-start | bytes 1179656 | tf_op jit(solution)/shard_map/ppermute | solution.py:877
  141.2 9.1 %collective-permute-start.30 = (bf16[192,1024]{1,0:T(8,128)(2,1)S(1)}, bf16[192,1024]{1,0:T(8,128)(2,1)S(1)}, u32[]{:S(2)}, u32[]{:S(2)}) collective-permute-start(bf16[192,1024]{1,0:T(8,128)(2,1)S(1)} %broadcast_select_fusion.1.refs_1_), channel_id=1, source_target_pairs={{0,2},{1,3},{2,0},{3,1},{4,6},{5,7},{6,4},{7,5},{8,10},{9,11},{10,... | collective-permute-start | bytes 1179656 | tf_op jit(solution)/shard_map/ppermute | solution.py:891
  142.5 1.6 collective-permute-start.31
  142.5 2.1 %collective-permute-start.32 = (bf16[8,160,128]{2,1,0:T(8,128)(2,1)S(1)}, bf16[8,160,128]{2,1,0:T(8,128)(2,1)S(1)}, u32[]{:S(2)}, u32[]{:S(2)}) collective-permute-start(bf16[8,160,128]{2,1,0:T(8,128)(2,1)S(1)} %collective-permute-done.28.far), channel_id=1, source_target_pairs={{0,1},{1,0},{2,3},{3,2},{4,5},{5,4},{6,7},{7,6},{8,9},{9,8},{10,11... | collective-permute-start | bytes 983048 | tf_op jit(solution)/shard_map/ppermute | solution.py:725
  150.4 8.9 %collective-permute-start.33 = (bf16[192,1024]{1,0:T(8,128)(2,1)S(1)}, bf16[192,1024]{1,0:T(8,128)(2,1)S(1)}, u32[]{:S(2)}, u32[]{:S(2)}) collective-permute-start(bf16[192,1024]{1,0:T(8,128)(2,1)S(1)} %broadcast_select_fusion.refs_3_), channel_id=1, source_target_pairs={{0,2},{1,3},{2,0},{3,1},{4,6},{5,7},{6,4},{7,5},{8,10},{9,11},{10,... | collective-permute-start | bytes 1179656 | tf_op jit(solution)/shard_map/ppermute | solution.py:891
  (17 other events, 190.3 us)

commit v7 on v6

--- a/solution.py
+++ b/solution.py
@@ -450,6 +450,35 @@
             2 * blocks * count * width * columns, 2 * blocks * columns * (width + count)
         ),
         name="project",
+    )(core.reshape(1), normed, own, other)
+
+
+def project_first_kernel(info, normed, own, other, out, weight):
+    rows = own.shape[1]
+    core = info[0]
+    weight[pl.ds(pl.multiple_of(core * rows, GROUP_ROWS), rows), :] = own[0]
+    weight[pl.ds(pl.multiple_of((1 - core) * rows, GROUP_ROWS), rows), :] = other[0]
+    product = jnp.dot(normed[...], weight[...], preferred_element_type=F32)
+    out[0] = product.astype(out.dtype)
+
+
+def project_part(core, normed, part, own, other, first_block, blocks, out_type):
+    width = normed.shape[1]
+    _, rows, columns = other.shape
+    count = PART_ROWS[part]
+    weight = pl.BlockSpec((1, rows, columns), lambda k: (first_block + k, 0, 0))
+    return pl.pallas_call(
+        project_first_kernel,
+        grid=(blocks,),
+        in_specs=[SMEM, pl.BlockSpec((count, width), lambda k: (part, 0)), weight, weight],
+        out_specs=pl.BlockSpec((1, count, columns), lambda k: (k, 0, 0)),
+        scratch_shapes=[pltpu.VMEM((width, columns), BF)],
+        out_shape=jax.ShapeDtypeStruct((blocks, count, columns), out_type),
+        compiler_params=PARAMS,
+        cost_estimate=cost(
+            2 * blocks * count * width * columns, 2 * blocks * columns * (width + count)
+        ),
+        name="project_part",
     )(core.reshape(1), normed, own, other)
 
 
@@ -691,7 +720,6 @@
 TIE_FIRST = True
 TIE_SECOND = False
 TIE_AWAY = True
-TIE_SUMS = False
 
 
 def after(values, *earlier):
@@ -782,11 +810,13 @@
 
     away_other = swap(away_other, 1)
     home_other = swap(home_other, 1)
-    away, away_sent, away_kept = project(core, normed, away_own, away_other, BF)
+    away = project_part(core, normed, 0, away_own, away_other, 0, Z_COUNT, BF)
     got = swap(away, 2)
+    away_sent = project_part(after(core, away), normed, 1, away_own, away_other, 0, 2, BF)
     got_away = swap(away_sent, 2 * y_count)
+    away_kept = project_part(after(core, away_sent), normed, 1, away_own, away_other, 2, 2, F32)
     home, home_sent, home_kept = project(
-        after(core, away), normed, home_own, home_other, F32
+        after(core, away_sent), normed, home_own, home_other, F32
     )
     got_home = swap(home_sent, 2 * y_count)
     if TIE_AWAY:
@@ -815,8 +845,7 @@
     pair_sent, pair_kept = join_pair(away_kept, home_kept, got_away, got_home)
     sums = [swap(value, 2 * y_count * (k + 1)) for k, value in enumerate(sums)]
     pair_got = swap(pair_sent, 2)
-    if TIE_SUMS:
-        pair_got, *sums = lax.optimization_barrier((pair_got, *sums))
+    pair_got, sums[0], sums[1] = lax.optimization_barrier((pair_got, sums[0], sums[1]))
     attend_part(0, [kept, *sums])
     kept, last_sent = join_last(pair_kept, pair_got)
     last_got = swap(last_sent, 4 * y_count)

time: 177 us -> 175 us (0.989)
  waiting for transfers between devices: 67.4 us -> 63.1 us
  Pallas kernels: 47.9 us -> 51.9 us
    pallas_call x0 -> x3, Pallas kernels: none -> 7.74 us  [project_part(): pl.pallas_call(project_first_kernel, grid=(blocks,), in_specs=[SMEM, pl.B...]
    ppermute x22, waiting for transfers between devices: 44.7 us -> 40.3 us  [swap(): return lax.ppermute(values, 'fsdp', [(i, i ^ bits) for i in range(ranks)])]
    pallas_call x2 -> x1, Pallas kernels: 9.68 us -> 5.35 us  [project(): pl.pallas_call(project_kernel, grid=(blocks,), in_specs=[SMEM, pl.BlockSp...]
  transfers between devices with their start and end apart: 34 -> 34, of which waited for: 16 -> 17; matrix products, arithmetic and copies ran while one was open for 3% -> 3% of each run, Pallas kernels for 25% -> 28%
where the time goes in v7:
time: 175 us; the launch traced here: 174 us
  waiting for transfers between devices  63.1 us (36%)
  Pallas kernels  51.9 us (30%)
  starting transfers between devices  38.3 us (22%)
  blocking collectives  12.4 us (7%)
  local copies, waits for them, and re-layouts  4.14 us (2%)
  other arithmetic  2.58 us (1%)
    ppermute x22, waiting for transfers between devices, swap(): return lax.ppermute(values, 'fsdp', [(i, i ^ bits) for i in range(ranks)])  40.3 us
    ppermute x22, starting transfers between devices, swap(): return lax.ppermute(values, 'fsdp', [(i, i ^ bits) for i in range(ranks)])  19.1 us
    pallas_call x3, Pallas kernels, out_project(): pl.pallas_call(functools.partial(out_kernel, blocks, bool(extra), last, b...  13.8 us
    all_to_all x1, blocking collectives, to_chips(): lax.all_to_all(values, 'fsdp', split_axis=0, concat_axis=0, tiled=True, a...  12.4 us
    ppermute x4, waiting for transfers between devices, swap_y(): return lax.ppermute(values, 'fsdp', [(i, i ^ 2) for i in range(ranks)])  10.7 us
    ppermute x5, waiting for transfers between devices, hop(): return lax.ppermute(values, 'fsdp', moves)  8.13 us
    pallas_call x1, Pallas kernels, prepare_weights(): pl.pallas_call(weight_kernel, grid_spec=pltpu.PrefetchScalarGridSpec(num_...  7.94 us
    pallas_call x3, Pallas kernels, project_part(): pl.pallas_call(project_first_kernel, grid=(blocks,), in_specs=[SMEM, pl.B...  7.74 us
  transfers between devices with their start and end apart: 34, of which 17 were waited for; matrix products, arithmetic and copies ran while one was open for 3% of the time, Pallas kernels for 28%

profile of v7, /device:TPU:0, one launch (start us, length us, event | category | flops | bytes accessed | tf_op | source)
XLA Modules:
  0.0 174.1 jit_solution(1663416799090409794)
XLA Ops:
  2.6 5.4 %pick_rows.2 = bf16[8,32,640]{2,1,0:T(8,128)(2,1)} custom-call(s32[1]{0:T(128)} %constant.156.clone.1.info, f32[8,384]{1,0:T(8,128)S(1)} %get-tuple-element.244.rows, f32[1,5120]{1,0:T(1,128)} %bitcast.60, bf16[600,5120]{1,0:T(8,128)(2,1)} %table.1), custom_call_target="tpu_custom_call" | custom-call | flops 196608000 | bytes 6144000 | tf_op jit(solution)/shard_map/pick_rows/pallas_call | solution.py:281
  8.0 7.0 %all-to-all-start.1 = ((bf16[8,32,640]{2,1,0:T(8,128)(2,1)}), bf16[8,32,640]{2,1,0:T(8,128)(2,1)S(1)}, u32[]{:S(2)}, u32[]{:S(2)}) async-start(bf16[8,32,640]{2,1,0:T(8,128)(2,1)} %pick_rows.2), calls=%async_computation.1 | async-start | bytes 655360 | tf_op jit(solution)/shard_map/all_to_all | solution.py:759
  15.0 1.6 prepare_keys.1
  17.4 2.0 %collective-permute-start.1 = (bf16[2,160,128]{2,1,0:T(8,128)(2,1)}, bf16[2,160,128]{2,1,0:T(8,128)(2,1)}, u32[]{:S(2)}, u32[]{:S(2)}) collective-permute-start(bf16[2,160,128]{2,1,0:T(8,128)(2,1)} %get-tuple-element.180), channel_id=1, source_target_pairs={{0,4},{1,5},{2,6},{3,7},{4,0},{5,1},{6,2},{7,3},{8,12},{9,13},{10,... | collective-permute-start | bytes 245768 | tf_op jit(solution)/shard_map/ppermute | solution.py:753
  19.4 2.4 %collective-permute-start.2 = (bf16[2,160,128]{2,1,0:T(8,128)(2,1)}, bf16[2,160,128]{2,1,0:T(8,128)(2,1)}, u32[]{:S(2)}, u32[]{:S(2)}) collective-permute-start(bf16[2,160,128]{2,1,0:T(8,128)(2,1)} %get-tuple-element.179), channel_id=1, source_target_pairs={{0,8},{1,9},{2,10},{3,11},{4,12},{5,13},{6,14},{7,15},{8,0},{9,1},... | collective-permute-start | bytes 245768 | tf_op jit(solution)/shard_map/ppermute | solution.py:753
  21.9 7.9 %prepare_weights.1 = (bf16[4,320,640]{2,1,0:T(8,128)(2,1)S(1)}, bf16[4,320,640]{2,1,0:T(8,128)(2,1)S(1)}, bf16[4,320,640]{2,1,0:T(8,128)(2,1)}, bf16[4,320,640]{2,1,0:T(8,128)(2,1)}) custom-call(s32[2]{0:T(128)S(1)} %pad_add_fusion.3.info, s32[8]{0:T(128)S(1)} %broadcast_xor_fusion.1.order, f32[40,64]{1,0:T(8,128)S(1)} %copy-done.2, ...), custom_call_target="tpu_custom_call" | custom-call | flops 10485760 | bytes 13107200 | tf_op jit(solution)/shard_map/prepare_weights/pallas_call | solution.py:357
  34.1 2.0 %collective-permute-done.5 = f32[8,128]{1,0:T(8,128)S(1)} collective-permute-done((f32[8,128]{1,0:T(8,128)S(1)}, f32[8,128]{1,0:T(8,128)S(1)}, u32[]{:S(2)}, u32[]{:S(2)}) %collective-permute-start.5) | collective-permute-done | bytes 4128 | tf_op jit(solution)/shard_map/ppermute | solution.py:756
  38.7 3.6 %project_part.3 = bf16[4,192,640]{2,1,0:T(8,128)(2,1)S(1)} custom-call(s32[1]{0:T(128)} %bitcast.5.info, bf16[384,640]{1,0:T(8,128)(2,1)S(1)} %get-tuple-element.112.normed, bf16[4,320,640]{2,1,0:T(8,128)(2,1)S(1)} %get-tuple-element.113.own, bf16[4,320,640]{2,1,0:T(8,128)(2,1)} %collective-permute-done.6.other), custom_call_target="tpu_custom_call" | custom-call | flops 629145600 | bytes 4259840 | tf_op jit(solution)/shard_map/project_part/pallas_call | solution.py:470
  43.8 2.1 %project_part.4 = bf16[2,192,640]{2,1,0:T(8,128)(2,1)S(1)} custom-call(s32[1]{0:T(128)} %bitcast.13.info, bf16[384,640]{1,0:T(8,128)(2,1)S(1)} %get-tuple-element.112.normed, bf16[4,320,640]{2,1,0:T(8,128)(2,1)S(1)} %get-tuple-element.113.own, bf16[4,320,640]{2,1,0:T(8,128)(2,1)} %collective-permute-done.6.other), custom_call_target="tpu_custom_call" | custom-call | flops 314572800 | bytes 2129920 | tf_op jit(solution)/shard_map/project_part/pallas_call | solution.py:470
  45.9 1.6 collective-permute-start.9
  47.5 5.4 %project.1 = (f32[4,192,640]{2,1,0:T(8,128)}, bf16[2,192,640]{2,1,0:T(8,128)(2,1)S(1)}, f32[2,192,640]{2,1,0:T(8,128)S(1)}) custom-call(s32[1]{0:T(128)} %bitcast.14.info, bf16[384,640]{1,0:T(8,128)(2,1)} %copy-done.8, bf16[4,320,640]{2,1,0:T(8,128)(2,1)S(1)} %copy-done.6, bf16[4,320,640]{2,1,0:T(8,128)(2,1)} %collective-permute-done.7.other), custom_call_target="tpu_custom_call" | custom-call | flops 1258291200 | bytes 5242880 | tf_op jit(solution)/shard_map/project/pallas_call | solution.py:428
  53.4 2.0 %project_part.5.away = f32[2,192,640]{2,1,0:T(8,128)S(1)} custom-call(s32[1]{0:T(128)} %bitcast.14.info, bf16[384,640]{1,0:T(8,128)(2,1)S(1)} %copy-done.9, bf16[4,320,640]{2,1,0:T(8,128)(2,1)S(1)} %get-tuple-element.113.own, bf16[4,320,640]{2,1,0:T(8,128)(2,1)} %collective-permute-done.6.other), custom_call_target="tpu_custom_call" | custom-call | flops 314572800 | bytes 2129920 | tf_op jit(solution)/shard_map/project_part/pallas_call | solution.py:470
  55.4 4.7 %collective-permute-done.9.got_away = bf16[2,192,640]{2,1,0:T(8,128)(2,1)S(1)} collective-permute-done((bf16[2,192,640]{2,1,0:T(8,128)(2,1)S(1)}, bf16[2,192,640]{2,1,0:T(8,128)(2,1)S(1)}, u32[]{:S(2)}, u32[]{:S(2)}) %collective-permute-start.9) | collective-permute-done | bytes 491552 | tf_op jit(solution)/shard_map/ppermute | solution.py:753
  60.1 5.8 %collective-permute-done.8.got = bf16[4,192,640]{2,1,0:T(8,128)(2,1)S(1)} collective-permute-done((bf16[4,192,640]{2,1,0:T(8,128)(2,1)S(1)}, bf16[4,192,640]{2,1,0:T(8,128)(2,1)S(1)}, u32[]{:S(2)}, u32[]{:S(2)}) %collective-permute-start.8) | collective-permute-done | bytes 983072 | tf_op jit(solution)/shard_map/ppermute | solution.py:753
  66.7 2.5 %collective-permute-done.10.got_home = bf16[2,192,640]{2,1,0:T(8,128)(2,1)S(1)} collective-permute-done((bf16[2,192,640]{2,1,0:T(8,128)(2,1)S(1)}, bf16[2,192,640]{2,1,0:T(8,128)(2,1)S(1)}, u32[]{:S(2)}, u32[]{:S(2)}) %collective-permute-start.10) | collective-permute-done | bytes 491552 | tf_op jit(solution)/shard_map/ppermute | solution.py:753
  70.0 1.6 collective-permute-start.12
  71.6 1.9 %collective-permute-start.13 = (bf16[192,640]{1,0:T(8,128)(2,1)S(1)}, bf16[192,640]{1,0:T(8,128)(2,1)S(1)}, u32[]{:S(2)}, u32[]{:S(2)}) collective-permute-start(bf16[192,640]{1,0:T(8,128)(2,1)S(1)} %get-tuple-element.126), channel_id=1, source_target_pairs={{0,8},{1,9},{2,10},{3,11},{4,12},{5,13},{6,14},{7,15},{8,0},{9,1},... | collective-permute-start | bytes 737288 | tf_op jit(solution)/shard_map/ppermute | solution.py:753
  76.1 5.1 %collective-permute-done.12.refs_1_ = bf16[192,640]{1,0:T(8,128)(2,1)S(1)} collective-permute-done((bf16[192,640]{1,0:T(8,128)(2,1)}, bf16[192,640]{1,0:T(8,128)(2,1)S(1)}, u32[]{:S(2)}, u32[]{:S(2)}) %collective-permute-start.12) | collective-permute-done | bytes 245792 | tf_op jit(solution)/shard_map/ppermute | solution.py:753
  81.2 3.0 %collective-permute-start.14 = (bf16[192,640]{1,0:T(8,128)(2,1)S(1)}, bf16[192,640]{1,0:T(8,128)(2,1)S(1)}, u32[]{:S(2)}, u32[]{:S(2)}) collective-permute-start(bf16[192,640]{1,0:T(8,128)(2,1)S(1)} %get-tuple-element.127), channel_id=1, source_target_pairs={{0,12},{1,13},{2,14},{3,15},{4,8},{5,9},{6,10},{7,11},{8,4},{9,5},... | collective-permute-start | bytes 737288 | tf_op jit(solution)/shard_map/ppermute | solution.py:753
  84.2 10.6 %collective-permute-done.13.refs_2_ = bf16[192,640]{1,0:T(8,128)(2,1)S(1)} collective-permute-done((bf16[192,640]{1,0:T(8,128)(2,1)S(1)}, bf16[192,640]{1,0:T(8,128)(2,1)S(1)}, u32[]{:S(2)}, u32[]{:S(2)}) %collective-permute-start.13) | collective-permute-done | bytes 245792 | tf_op jit(solution)/shard_map/ppermute | solution.py:753
  97.0 7.9 %collective-permute-done.18.refs_1_ = bf16[192,640]{1,0:T(8,128)(2,1)S(1)} collective-permute-done((bf16[192,640]{1,0:T(8,128)(2,1)S(1)}, bf16[192,640]{1,0:T(8,128)(2,1)S(1)}, u32[]{:S(2)}, u32[]{:S(2)}) %collective-permute-start.18) | collective-permute-done | bytes 245792 | tf_op jit(solution)/shard_map/ppermute | solution.py:753
  112.3 8.8 %collective-permute-done.21.refs_1_ = bf16[192,1024]{1,0:T(8,128)(2,1)S(1)} collective-permute-done((bf16[192,1024]{1,0:T(8,128)(2,1)S(1)}, bf16[192,1024]{1,0:T(8,128)(2,1)S(1)}, u32[]{:S(2)}, u32[]{:S(2)}) %collective-permute-start.21) | collective-permute-done | bytes 393248 | tf_op jit(solution)/shard_map/ppermute | solution.py:920
  124.9 1.6 collective-permute-start.28
  126.7 4.8 %out_project.3.refs_6_ = f32[2,320,192]{2,1,0:T(8,128)S(1)} custom-call(s32[5]{0:T(128)S(1)} %pad_add_fusion.4.info, f32[64,40]{1,0:T(8,128)S(1)} %copy.22.scales, bf16[192,1024]{1,0:T(8,128)(2,1)S(1)} %maximum_maximum_fusion.refs_0_, bf16[192,1024]{1,0:T(8,128)(2,1)S(1)} %collective-permute-done.21.refs_1_, ...), custom_call_target="tpu_custom_call" | custom-call | flops 754974720 | bytes 3932160 | tf_op jit(solution)/shard_map/out_project/pallas_call | solution.py:692
  131.5 1.9 %collective-permute-done.28.far = bf16[8,160,128]{2,1,0:T(8,128)(2,1)S(1)} collective-permute-done((bf16[8,160,128]{2,1,0:T(8,128)(2,1)S(1)}, bf16[8,160,128]{2,1,0:T(8,128)(2,1)S(1)}, u32[]{:S(2)}, u32[]{:S(2)}) %collective-permute-start.28) | collective-permute-done | bytes 327712 | tf_op jit(solution)/shard_map/ppermute | solution.py:756
  133.4 4.7 %collective-permute-done.24 = bf16[192,1024]{1,0:T(8,128)(2,1)S(1)} collective-permute-done((bf16[192,1024]{1,0:T(8,128)(2,1)S(1)}, bf16[192,1024]{1,0:T(8,128)(2,1)S(1)}, u32[]{:S(2)}, u32[]{:S(2)}) %collective-permute-start.24) | collective-permute-done | bytes 393248 | tf_op jit(solution)/shard_map/ppermute | solution.py:906
  143.0 3.3 %collect_keys.1 = bf16[8,2,2,160,128]{4,3,2,1,0:T(8,128)(2,1)} custom-call(s32[3]{0:T(128)S(1)} %pad_add_fusion.5.info, bf16[8,160,128]{2,1,0:T(8,128)(2,1)S(1)} %bitcast.47, bf16[8,160,128]{2,1,0:T(8,128)(2,1)S(1)} %collective-permute-done.28.far, bf16[8,160,128]{2,1,0:T(8,128)(2,1)S(1)} %collective-permute-done.31.other, ...), custom_call_target="tpu_custom_call" | custom-call | bytes 2621440 | tf_op jit(solution)/shard_map/collect_keys/pallas_call | solution.py:888
  146.3 2.2 %collective-permute-done.29 = bf16[192,1024]{1,0:T(8,128)(2,1)S(1)} collective-permute-done((bf16[192,1024]{1,0:T(8,128)(2,1)S(1)}, bf16[192,1024]{1,0:T(8,128)(2,1)S(1)}, u32[]{:S(2)}, u32[]{:S(2)}) %collective-permute-start.29) | collective-permute-done | bytes 393248 | tf_op jit(solution)/shard_map/ppermute | solution.py:906
  150.1 5.6 %out_project.4.refs_3_ = f32[2,320,192]{2,1,0:T(8,128)S(1)} custom-call(s32[6]{0:T(128)S(1)} %pad_add_fusion.6.info, f32[64,40]{1,0:T(8,128)S(1)} %copy.22.scales, bf16[192,1024]{1,0:T(8,128)(2,1)S(1)} %collective-permute-done.26.refs_0_, bf16[192,1024]{1,0:T(8,128)(2,1)S(1)} %broadcast_select_fusion.1.refs_1_, ...), custom_call_target="tpu_custom_call" | custom-call | flops 1006632960 | bytes 5242880 | tf_op jit(solution)/shard_map/out_project/pallas_call | solution.py:692
  155.8 1.8 %collective-permute-done.33.refs_0_ = bf16[192,1024]{1,0:T(8,128)(2,1)S(1)} collective-permute-done((bf16[192,1024]{1,0:T(8,128)(2,1)S(1)}, bf16[192,1024]{1,0:T(8,128)(2,1)S(1)}, u32[]{:S(2)}, u32[]{:S(2)}) %collective-permute-start.33) | collective-permute-done | bytes 393248 | tf_op jit(solution)/shard_map/ppermute | solution.py:920
  157.6 3.3 %out_project.5 = bf16[192,640]{1,0:T(8,128)(2,1)S(1)} custom-call(s32[3]{0:T(128)S(1)} %pad_add_fusion.1.info, f32[64,40]{1,0:T(8,128)S(1)} %copy.22.scales, bf16[192,1024]{1,0:T(8,128)(2,1)S(1)} %collective-permute-done.33.refs_0_, bf16[320,8192]{1,0:T(8,128)(2,1)} %bitcast.57, bf16[320,8192]{1,0:T(8,128)(2,1)} %collective-permute-done.27.refs_4_.refs_5_.refs_2_, ...), custom_call_target="tpu_custom_call" | custom-call | flops 251658240 | bytes 1310720 | tf_op jit(solution)/shard_map/out_project/pallas_call | solution.py:692
  160.9 12.4 %all_to_all.16 = bf16[8,24,640]{2,1,0:T(8,128)(2,1)S(1)} all-to-all(bf16[8,24,640]{2,1,0:T(8,128)(2,1)S(1)} %bitcast.48), channel_id=1, replica_groups={{0,2,4,6,8,10,12,14},{1,3,5,7,9,11,13,15},{16,18,20,22,24,26,28,30},{17..., dimensions={0} | all-to-all | bytes 491520 | tf_op jit(solution)/shard_map/all_to_all | solution.py:759
  (116 shorter events, 36.4 us)
Async XLA Ops:
  0.6 126.0 %collective-permute-start.27 = (bf16[320,8192]{1,0:T(8,128)(2,1)}, bf16[320,8192]{1,0:T(8,128)(2,1)}, u32[]{:S(2)}, u32[]{:S(2)}) collective-permute-start(bf16[320,8192]{1,0:T(8,128)(2,1)} %bitcast.54), channel_id=1, source_target_pairs={{0,1},{1,0},{2,3},{3,2},{4,5},{5,4},{6,7},{7,6},{8,9},{9,8},{10,11... | collective-permute-start | bytes 15728648 | tf_op jit(solution)/shard_map/ppermute | solution.py:753
  8.0 24.0 %all-to-all-start.1 = ((bf16[8,32,640]{2,1,0:T(8,128)(2,1)}), bf16[8,32,640]{2,1,0:T(8,128)(2,1)S(1)}, u32[]{:S(2)}, u32[]{:S(2)}) async-start(bf16[8,32,640]{2,1,0:T(8,128)(2,1)} %pick_rows.2), calls=%async_computation.1 | async-start | bytes 655360 | tf_op jit(solution)/shard_map/all_to_all | solution.py:759
  17.4 13.6 %collective-permute-start.1 = (bf16[2,160,128]{2,1,0:T(8,128)(2,1)}, bf16[2,160,128]{2,1,0:T(8,128)(2,1)}, u32[]{:S(2)}, u32[]{:S(2)}) collective-permute-start(bf16[2,160,128]{2,1,0:T(8,128)(2,1)} %get-tuple-element.180), channel_id=1, source_target_pairs={{0,4},{1,5},{2,6},{3,7},{4,0},{5,1},{6,2},{7,3},{8,12},{9,13},{10,... | collective-permute-start | bytes 245768 | tf_op jit(solution)/shard_map/ppermute | solution.py:753
  19.4 12.6 %collective-permute-start.2 = (bf16[2,160,128]{2,1,0:T(8,128)(2,1)}, bf16[2,160,128]{2,1,0:T(8,128)(2,1)}, u32[]{:S(2)}, u32[]{:S(2)}) collective-permute-start(bf16[2,160,128]{2,1,0:T(8,128)(2,1)} %get-tuple-element.179), channel_id=1, source_target_pairs={{0,8},{1,9},{2,10},{3,11},{4,12},{5,13},{6,14},{7,15},{8,0},{9,1},... | collective-permute-start | bytes 245768 | tf_op jit(solution)/shard_map/ppermute | solution.py:753
  21.8 10.2 %collective-permute-start.3 = (bf16[2,160,128]{2,1,0:T(8,128)(2,1)}, bf16[2,160,128]{2,1,0:T(8,128)(2,1)}, u32[]{:S(2)}, u32[]{:S(2)}) collective-permute-start(bf16[2,160,128]{2,1,0:T(8,128)(2,1)} %get-tuple-element.178), channel_id=1, source_target_pairs={{0,12},{1,13},{2,14},{3,15},{4,8},{5,9},{6,10},{7,11},{8,4},{9,5},... | collective-permute-start | bytes 245768 | tf_op jit(solution)/shard_map/ppermute | solution.py:753
  32.0 6.7 %collective-permute-start.6 = (bf16[4,320,640]{2,1,0:T(8,128)(2,1)}, bf16[4,320,640]{2,1,0:T(8,128)(2,1)}, u32[]{:S(2)}, u32[]{:S(2)}) collective-permute-start(bf16[4,320,640]{2,1,0:T(8,128)(2,1)} %copy-done.7), channel_id=1, source_target_pairs={{0,1},{1,0},{2,3},{3,2},{4,5},{5,4},{6,7},{7,6},{8,9},{9,8},{10,11... | collective-permute-start | bytes 4915208 | tf_op jit(solution)/shard_map/ppermute | solution.py:753
  32.0 15.5 %collective-permute-start.7 = (bf16[4,320,640]{2,1,0:T(8,128)(2,1)}, bf16[4,320,640]{2,1,0:T(8,128)(2,1)}, u32[]{:S(2)}, u32[]{:S(2)}) collective-permute-start(bf16[4,320,640]{2,1,0:T(8,128)(2,1)} %get-tuple-element.118), channel_id=1, source_target_pairs={{0,1},{1,0},{2,3},{3,2},{4,5},{5,4},{6,7},{7,6},{8,9},{9,8},{10,11... | collective-permute-start | bytes 4915208 | tf_op jit(solution)/shard_map/ppermute | solution.py:753
  32.5 4.2 %collective-permute-start.4 = (bf16[8,32,640]{2,1,0:T(8,128)(2,1)S(1)}, bf16[8,32,640]{2,1,0:T(8,128)(2,1)S(1)}, u32[]{:S(2)}, u32[]{:S(2)}) collective-permute-start(bf16[8,32,640]{2,1,0:T(8,128)(2,1)S(1)} %all-to-all-done.1), channel_id=1, source_target_pairs={{0,1},{1,0},{2,3},{3,2},{4,5},{5,4},{6,7},{7,6},{8,9},{9,8},{10,11... | collective-permute-start | bytes 983048 | tf_op jit(solution)/shard_map/ppermute | solution.py:753
  32.6 3.6 %collective-permute-start.5 = (f32[8,128]{1,0:T(8,128)S(1)}, f32[8,128]{1,0:T(8,128)S(1)}, u32[]{:S(2)}, u32[]{:S(2)}) collective-permute-start(f32[8,128]{1,0:T(8,128)S(1)} %get-tuple-element.111), channel_id=1, source_target_pairs={{0,16},{16,0},{1,17},{17,1},{2,18},{18,2},{3,19},{19,3},{4,20},{20... | collective-permute-start | bytes 12296 | tf_op jit(solution)/shard_map/ppermute | solution.py:756
  42.3 23.6 %collective-permute-start.8 = (bf16[4,192,640]{2,1,0:T(8,128)(2,1)S(1)}, bf16[4,192,640]{2,1,0:T(8,128)(2,1)S(1)}, u32[]{:S(2)}, u32[]{:S(2)}) collective-permute-start(bf16[4,192,640]{2,1,0:T(8,128)(2,1)S(1)} %project_part.3), channel_id=1, source_target_pairs={{0,2},{1,3},{2,0},{3,1},{4,6},{5,7},{6,4},{7,5},{8,10},{9,11},{10,... | collective-permute-start | bytes 2949128 | tf_op jit(solution)/shard_map/ppermute | solution.py:753
  45.9 14.2 %collective-permute-start.9 = (bf16[2,192,640]{2,1,0:T(8,128)(2,1)S(1)}, bf16[2,192,640]{2,1,0:T(8,128)(2,1)S(1)}, u32[]{:S(2)}, u32[]{:S(2)}) collective-permute-start(bf16[2,192,640]{2,1,0:T(8,128)(2,1)S(1)} %project_part.4), channel_id=1, source_target_pairs={{0,4},{1,5},{2,6},{3,7},{4,0},{5,1},{6,2},{7,3},{8,12},{9,13},{10,... | collective-permute-start | bytes 1474568 | tf_op jit(solution)/shard_map/ppermute | solution.py:753
  52.9 16.4 %collective-permute-start.10 = (bf16[2,192,640]{2,1,0:T(8,128)(2,1)S(1)}, bf16[2,192,640]{2,1,0:T(8,128)(2,1)S(1)}, u32[]{:S(2)}, u32[]{:S(2)}) collective-permute-start(bf16[2,192,640]{2,1,0:T(8,128)(2,1)S(1)} %get-tuple-element.124), channel_id=1, source_target_pairs={{0,4},{1,5},{2,6},{3,7},{4,0},{5,1},{6,2},{7,3},{8,12},{9,13},{10,... | collective-permute-start | bytes 1474568 | tf_op jit(solution)/shard_map/ppermute | solution.py:753
  69.4 25.4 %collective-permute-start.11 = (bf16[2,192,640]{2,1,0:T(8,128)(2,1)S(1)}, bf16[2,192,640]{2,1,0:T(8,128)(2,1)S(1)}, u32[]{:S(2)}, u32[]{:S(2)}) collective-permute-start(bf16[2,192,640]{2,1,0:T(8,128)(2,1)S(1)} %get-tuple-element.130), channel_id=1, source_target_pairs={{0,2},{1,3},{2,0},{3,1},{4,6},{5,7},{6,4},{7,5},{8,10},{9,11},{10,... | collective-permute-start | bytes 1474568 | tf_op jit(solution)/shard_map/ppermute | solution.py:753
  70.0 11.2 %collective-permute-start.12 = (bf16[192,640]{1,0:T(8,128)(2,1)}, bf16[192,640]{1,0:T(8,128)(2,1)S(1)}, u32[]{:S(2)}, u32[]{:S(2)}) collective-permute-start(bf16[192,640]{1,0:T(8,128)(2,1)} %get-tuple-element.125), channel_id=1, source_target_pairs={{0,4},{1,5},{2,6},{3,7},{4,0},{5,1},{6,2},{7,3},{8,12},{9,13},{10,... | collective-permute-start | bytes 737288 | tf_op jit(solution)/shard_map/ppermute | solution.py:753
  71.6 23.2 %collective-permute-start.13 = (bf16[192,640]{1,0:T(8,128)(2,1)S(1)}, bf16[192,640]{1,0:T(8,128)(2,1)S(1)}, u32[]{:S(2)}, u32[]{:S(2)}) collective-permute-start(bf16[192,640]{1,0:T(8,128)(2,1)S(1)} %get-tuple-element.126), channel_id=1, source_target_pairs={{0,8},{1,9},{2,10},{3,11},{4,12},{5,13},{6,14},{7,15},{8,0},{9,1},... | collective-permute-start | bytes 737288 | tf_op jit(solution)/shard_map/ppermute | solution.py:753
  74.6 22.4 %collective-permute-start.17 = (bf16[4,160,128]{2,1,0:T(8,128)(2,1)S(1)}, bf16[4,160,128]{2,1,0:T(8,128)(2,1)S(1)}, u32[]{:S(2)}, u32[]{:S(2)}) collective-permute-start(bf16[4,160,128]{2,1,0:T(8,128)(2,1)S(1)} %get-tuple-element.183), channel_id=1, source_target_pairs={{0,2},{1,3},{2,0},{3,1},{4,6},{5,7},{6,4},{7,5},{8,10},{9,11},{10,... | collective-permute-start | bytes 491528 | tf_op jit(solution)/shard_map/ppermute | solution.py:753
  81.2 14.7 %collective-permute-start.14 = (bf16[192,640]{1,0:T(8,128)(2,1)S(1)}, bf16[192,640]{1,0:T(8,128)(2,1)S(1)}, u32[]{:S(2)}, u32[]{:S(2)}) collective-permute-start(bf16[192,640]{1,0:T(8,128)(2,1)S(1)} %get-tuple-element.127), channel_id=1, source_target_pairs={{0,12},{1,13},{2,14},{3,15},{4,8},{5,9},{6,10},{7,11},{8,4},{9,5},... | collective-permute-start | bytes 737288 | tf_op jit(solution)/shard_map/ppermute | solution.py:753
  94.9 10.0 %collective-permute-start.18 = (bf16[192,640]{1,0:T(8,128)(2,1)S(1)}, bf16[192,640]{1,0:T(8,128)(2,1)S(1)}, u32[]{:S(2)}, u32[]{:S(2)}) collective-permute-start(bf16[192,640]{1,0:T(8,128)(2,1)S(1)} %get-tuple-element.145), channel_id=1, source_target_pairs={{0,8},{1,9},{2,10},{3,11},{4,12},{5,13},{6,14},{7,15},{8,0},{9,1},... | collective-permute-start | bytes 737288 | tf_op jit(solution)/shard_map/ppermute | solution.py:753
  96.9 8.9 %collective-permute-start.15 = (bf16[192,128]{1,0:T(8,128)(2,1)S(1)}, bf16[192,128]{1,0:T(8,128)(2,1)S(1)}, u32[]{:S(2)}, u32[]{:S(2)}) collective-permute-start(bf16[192,128]{1,0:T(8,128)(2,1)S(1)} %get-tuple-element.134.refs_0_), channel_id=1, source_target_pairs={{0,1},{1,0},{2,3},{3,2},{4,5},{5,4},{6,7},{7,6},{8,9},{9,8},{10,11... | collective-permute-start | bytes 147464 | tf_op jit(solution)/shard_map/ppermute | solution.py:753
  106.6 1.9 %collective-permute-start.16 = (bf16[96,512]{1,0:T(8,128)(2,1)S(1)}, bf16[96,512]{1,0:T(8,128)(2,1)S(1)}, u32[]{:S(2)}, u32[]{:S(2)}) collective-permute-start(bf16[96,512]{1,0:T(8,128)(2,1)S(1)} %get-tuple-element.136), channel_id=1, source_target_pairs={{0,1},{1,0},{2,3},{3,2},{4,5},{5,4},{6,7},{7,6},{8,9},{9,8},{10,11... | collective-permute-start | bytes 294920 | tf_op jit(solution)/shard_map/ppermute | solution.py:753
  109.9 11.2 %collective-permute-start.21 = (bf16[192,1024]{1,0:T(8,128)(2,1)S(1)}, bf16[192,1024]{1,0:T(8,128)(2,1)S(1)}, u32[]{:S(2)}, u32[]{:S(2)}) collective-permute-start(bf16[192,1024]{1,0:T(8,128)(2,1)S(1)} %maximum_maximum_fusion.refs_0_), channel_id=1, source_target_pairs={{0,2},{1,3},{2,0},{3,1},{4,6},{5,7},{6,4},{7,5},{8,10},{9,11},{10,... | collective-permute-start | bytes 1179656 | tf_op jit(solution)/shard_map/ppermute | solution.py:920
  111.4 10.9 %collective-permute-start.22 = (bf16[192,1024]{1,0:T(8,128)(2,1)S(1)}, bf16[192,1024]{1,0:T(8,128)(2,1)S(1)}, u32[]{:S(2)}, u32[]{:S(2)}) collective-permute-start(bf16[192,1024]{1,0:T(8,128)(2,1)S(1)} %maximum_maximum_fusion.refs_0_), channel_id=1, source_target_pairs={{0,4},{1,5},{2,6},{3,7},{4,0},{5,1},{6,2},{7,3},{8,12},{9,13},{10,... | collective-permute-start | bytes 1179656 | tf_op jit(solution)/shard_map/ppermute | solution.py:906
  111.4 10.9 %collective-permute-start.23 = (bf16[192,1024]{1,0:T(8,128)(2,1)S(1)}, bf16[192,1024]{1,0:T(8,128)(2,1)S(1)}, u32[]{:S(2)}, u32[]{:S(2)}) collective-permute-start(bf16[192,1024]{1,0:T(8,128)(2,1)S(1)} %maximum_maximum_fusion.refs_0_), channel_id=1, source_target_pairs={{4,8},{5,9},{6,10},{7,11},{8,4},{9,5},{10,6},{11,7},{20,24},{21,25... | collective-permute-start | bytes 1179656 | tf_op jit(solution)/shard_map/ppermute | solution.py:906
  122.3 15.8 %collective-permute-start.25 = (bf16[192,1024]{1,0:T(8,128)(2,1)S(1)}, bf16[192,1024]{1,0:T(8,128)(2,1)S(1)}, u32[]{:S(2)}, u32[]{:S(2)}) collective-permute-start(bf16[192,1024]{1,0:T(8,128)(2,1)S(1)} %collective-permute-done.22.refs_2_), channel_id=1, source_target_pairs={{4,8},{5,9},{6,10},{7,11},{8,4},{9,5},{10,6},{11,7},{20,24},{21,25... | collective-permute-start | bytes 1179656 | tf_op jit(solution)/shard_map/ppermute | solution.py:906
  123.0 15.1 %collective-permute-start.26 = (bf16[192,1024]{1,0:T(8,128)(2,1)S(1)}, bf16[192,1024]{1,0:T(8,128)(2,1)S(1)}, u32[]{:S(2)}, u32[]{:S(2)}) collective-permute-start(bf16[192,1024]{1,0:T(8,128)(2,1)S(1)} %collective-permute-done.22.refs_2_), channel_id=1, source_target_pairs={{0,2},{1,3},{2,0},{3,1},{4,6},{5,7},{6,4},{7,5},{8,10},{9,11},{10,... | collective-permute-start | bytes 1179656 | tf_op jit(solution)/shard_map/ppermute | solution.py:920
  123.6 14.5 %collective-permute-start.24 = (bf16[192,1024]{1,0:T(8,128)(2,1)S(1)}, bf16[192,1024]{1,0:T(8,128)(2,1)S(1)}, u32[]{:S(2)}, u32[]{:S(2)}) collective-permute-start(bf16[192,1024]{1,0:T(8,128)(2,1)S(1)} %collective-permute-done.23), channel_id=1, source_target_pairs={{4,0},{5,1},{6,2},{7,3},{8,12},{9,13},{10,14},{11,15},{20,16},{21,... | collective-permute-start | bytes 1179656 | tf_op jit(solution)/shard_map/ppermute | solution.py:906
  124.9 8.5 %collective-permute-start.28 = (bf16[8,160,128]{2,1,0:T(8,128)(2,1)S(1)}, bf16[8,160,128]{2,1,0:T(8,128)(2,1)S(1)}, u32[]{:S(2)}, u32[]{:S(2)}) collective-permute-start(bf16[8,160,128]{2,1,0:T(8,128)(2,1)S(1)} %bitcast.45), channel_id=1, source_target_pairs={{0,16},{16,0},{1,17},{17,1},{2,18},{18,2},{3,19},{19,3},{4,20},{20... | collective-permute-start | bytes 983048 | tf_op jit(solution)/shard_map/ppermute | solution.py:756
  138.2 10.4 %collective-permute-start.29 = (bf16[192,1024]{1,0:T(8,128)(2,1)S(1)}, bf16[192,1024]{1,0:T(8,128)(2,1)S(1)}, u32[]{:S(2)}, u32[]{:S(2)}) collective-permute-start(bf16[192,1024]{1,0:T(8,128)(2,1)S(1)} %broadcast_select_fusion.1.refs_1_), channel_id=1, source_target_pairs={{4,0},{5,1},{6,2},{7,3},{8,12},{9,13},{10,14},{11,15},{20,16},{21,... | collective-permute-start | bytes 1179656 | tf_op jit(solution)/shard_map/ppermute | solution.py:906
  139.5 9.1 %collective-permute-start.30 = (bf16[192,1024]{1,0:T(8,128)(2,1)S(1)}, bf16[192,1024]{1,0:T(8,128)(2,1)S(1)}, u32[]{:S(2)}, u32[]{:S(2)}) collective-permute-start(bf16[192,1024]{1,0:T(8,128)(2,1)S(1)} %broadcast_select_fusion.1.refs_1_), channel_id=1, source_target_pairs={{0,2},{1,3},{2,0},{3,1},{4,6},{5,7},{6,4},{7,5},{8,10},{9,11},{10,... | collective-permute-start | bytes 1179656 | tf_op jit(solution)/shard_map/ppermute | solution.py:920
  140.9 1.6 collective-permute-start.31
  140.9 2.1 %collective-permute-start.32 = (bf16[8,160,128]{2,1,0:T(8,128)(2,1)S(1)}, bf16[8,160,128]{2,1,0:T(8,128)(2,1)S(1)}, u32[]{:S(2)}, u32[]{:S(2)}) collective-permute-start(bf16[8,160,128]{2,1,0:T(8,128)(2,1)S(1)} %collective-permute-done.28.far), channel_id=1, source_target_pairs={{0,1},{1,0},{2,3},{3,2},{4,5},{5,4},{6,7},{7,6},{8,9},{9,8},{10,11... | collective-permute-start | bytes 983048 | tf_op jit(solution)/shard_map/ppermute | solution.py:753
  148.6 9.0 %collective-permute-start.33 = (bf16[192,1024]{1,0:T(8,128)(2,1)S(1)}, bf16[192,1024]{1,0:T(8,128)(2,1)S(1)}, u32[]{:S(2)}, u32[]{:S(2)}) collective-permute-start(bf16[192,1024]{1,0:T(8,128)(2,1)S(1)} %broadcast_select_fusion.refs_3_), channel_id=1, source_target_pairs={{0,2},{1,3},{2,0},{3,1},{4,6},{5,7},{6,4},{7,5},{8,10},{9,11},{10,... | collective-permute-start | bytes 1179656 | tf_op jit(solution)/shard_map/ppermute | solution.py:920
  (18 other events, 200.5 us)

commit v8 on v7

--- a/solution.py
+++ b/solution.py
@@ -845,7 +845,7 @@
     pair_sent, pair_kept = join_pair(away_kept, home_kept, got_away, got_home)
     sums = [swap(value, 2 * y_count * (k + 1)) for k, value in enumerate(sums)]
     pair_got = swap(pair_sent, 2)
-    pair_got, sums[0], sums[1] = lax.optimization_barrier((pair_got, sums[0], sums[1]))
+    pair_got, sums[0], sums[2] = lax.optimization_barrier((pair_got, sums[0], sums[2]))
     attend_part(0, [kept, *sums])
     kept, last_sent = join_last(pair_kept, pair_got)
     last_got = swap(last_sent, 4 * y_count)

time: 175 us -> 174 us (level)
  starting transfers between devices: 38.3 us -> 46.1 us
  waiting for transfers between devices: 63.1 us -> 55.3 us
    ppermute x22, waiting for transfers between devices: 40.3 us -> 31.8 us  [swap(): return lax.ppermute(values, 'fsdp', [(i, i ^ bits) for i in range(ranks)])]
    ppermute x22, starting transfers between devices: 19.1 us -> 26.8 us  [swap(): return lax.ppermute(values, 'fsdp', [(i, i ^ bits) for i in range(ranks)])]
  transfers between devices with their start and end apart: 34 -> 34, of which waited for: 17 -> 18; matrix products, arithmetic and copies ran while one was open for 3% -> 3% of each run, Pallas kernels for 28% -> 28%
where the time goes in v8:
time: 174 us; the launch traced here: 173 us
  waiting for transfers between devices  55.3 us (32%)
  Pallas kernels  51.9 us (30%)
  starting transfers between devices  46.1 us (26%)
  blocking collectives  11.9 us (7%)
  local copies, waits for them, and re-layouts  4.14 us (2%)
  other arithmetic  2.58 us (1%)
    ppermute x22, waiting for transfers between devices, swap(): return lax.ppermute(values, 'fsdp', [(i, i ^ bits) for i in range(ranks)])  31.8 us
    ppermute x22, starting transfers between devices, swap(): return lax.ppermute(values, 'fsdp', [(i, i ^ bits) for i in range(ranks)])  26.8 us
    pallas_call x3, Pallas kernels, out_project(): pl.pallas_call(functools.partial(out_kernel, blocks, bool(extra), last, b...  13.8 us
    all_to_all x1, blocking collectives, to_chips(): lax.all_to_all(values, 'fsdp', split_axis=0, concat_axis=0, tiled=True, a...  11.9 us
    ppermute x4, waiting for transfers between devices, swap_y(): return lax.ppermute(values, 'fsdp', [(i, i ^ 2) for i in range(ranks)])  10.7 us
    ppermute x5, waiting for transfers between devices, hop(): return lax.ppermute(values, 'fsdp', moves)  8.82 us
    pallas_call x1, Pallas kernels, prepare_weights(): pl.pallas_call(weight_kernel, grid_spec=pltpu.PrefetchScalarGridSpec(num_...  7.94 us
    pallas_call x3, Pallas kernels, project_part(): pl.pallas_call(project_first_kernel, grid=(blocks,), in_specs=[SMEM, pl.B...  7.74 us
  transfers between devices with their start and end apart: 34, of which 18 were waited for; matrix products, arithmetic and copies ran while one was open for 3% of the time, Pallas kernels for 28%

profile of v8, /device:TPU:0, one launch (start us, length us, event | category | flops | bytes accessed | tf_op | source)
XLA Modules:
  0.0 173.5 jit_solution(16284486161564407567)
XLA Ops:
  2.6 5.4 %pick_rows.2 = bf16[8,32,640]{2,1,0:T(8,128)(2,1)} custom-call(s32[1]{0:T(128)} %constant.156.clone.1.info, f32[8,384]{1,0:T(8,128)S(1)} %get-tuple-element.244.rows, f32[1,5120]{1,0:T(1,128)} %bitcast.60, bf16[600,5120]{1,0:T(8,128)(2,1)} %table.1), custom_call_target="tpu_custom_call" | custom-call | flops 196608000 | bytes 6144000 | tf_op jit(solution)/shard_map/pick_rows/pallas_call | solution.py:281
  8.0 7.0 %all-to-all-start.1 = ((bf16[8,32,640]{2,1,0:T(8,128)(2,1)}), bf16[8,32,640]{2,1,0:T(8,128)(2,1)S(1)}, u32[]{:S(2)}, u32[]{:S(2)}) async-start(bf16[8,32,640]{2,1,0:T(8,128)(2,1)} %pick_rows.2), calls=%async_computation.1 | async-start | bytes 655360 | tf_op jit(solution)/shard_map/all_to_all | solution.py:759
  17.4 2.0 %collective-permute-start.1 = (bf16[2,160,128]{2,1,0:T(8,128)(2,1)}, bf16[2,160,128]{2,1,0:T(8,128)(2,1)}, u32[]{:S(2)}, u32[]{:S(2)}) collective-permute-start(bf16[2,160,128]{2,1,0:T(8,128)(2,1)} %get-tuple-element.180), channel_id=1, source_target_pairs={{0,4},{1,5},{2,6},{3,7},{4,0},{5,1},{6,2},{7,3},{8,12},{9,13},{10,... | collective-permute-start | bytes 245768 | tf_op jit(solution)/shard_map/ppermute | solution.py:753
  19.4 2.4 %collective-permute-start.2 = (bf16[2,160,128]{2,1,0:T(8,128)(2,1)}, bf16[2,160,128]{2,1,0:T(8,128)(2,1)}, u32[]{:S(2)}, u32[]{:S(2)}) collective-permute-start(bf16[2,160,128]{2,1,0:T(8,128)(2,1)} %get-tuple-element.179), channel_id=1, source_target_pairs={{0,8},{1,9},{2,10},{3,11},{4,12},{5,13},{6,14},{7,15},{8,0},{9,1},... | collective-permute-start | bytes 245768 | tf_op jit(solution)/shard_map/ppermute | solution.py:753
  21.9 7.9 %prepare_weights.1 = (bf16[4,320,640]{2,1,0:T(8,128)(2,1)S(1)}, bf16[4,320,640]{2,1,0:T(8,128)(2,1)S(1)}, bf16[4,320,640]{2,1,0:T(8,128)(2,1)}, bf16[4,320,640]{2,1,0:T(8,128)(2,1)}) custom-call(s32[2]{0:T(128)S(1)} %pad_add_fusion.3.info, s32[8]{0:T(128)S(1)} %broadcast_xor_fusion.1.order, f32[40,64]{1,0:T(8,128)S(1)} %copy-done.2, ...), custom_call_target="tpu_custom_call" | custom-call | flops 10485760 | bytes 13107200 | tf_op jit(solution)/shard_map/prepare_weights/pallas_call | solution.py:357
  34.1 2.0 %collective-permute-done.5 = f32[8,128]{1,0:T(8,128)S(1)} collective-permute-done((f32[8,128]{1,0:T(8,128)S(1)}, f32[8,128]{1,0:T(8,128)S(1)}, u32[]{:S(2)}, u32[]{:S(2)}) %collective-permute-start.5) | collective-permute-done | bytes 4128 | tf_op jit(solution)/shard_map/ppermute | solution.py:756
  38.7 3.6 %project_part.3 = bf16[4,192,640]{2,1,0:T(8,128)(2,1)S(1)} custom-call(s32[1]{0:T(128)} %bitcast.5.info, bf16[384,640]{1,0:T(8,128)(2,1)S(1)} %get-tuple-element.112.normed, bf16[4,320,640]{2,1,0:T(8,128)(2,1)S(1)} %get-tuple-element.113.own, bf16[4,320,640]{2,1,0:T(8,128)(2,1)} %collective-permute-done.6.other), custom_call_target="tpu_custom_call" | custom-call | flops 629145600 | bytes 4259840 | tf_op jit(solution)/shard_map/project_part/pallas_call | solution.py:470
  43.8 2.1 %project_part.4 = bf16[2,192,640]{2,1,0:T(8,128)(2,1)S(1)} custom-call(s32[1]{0:T(128)} %bitcast.13.info, bf16[384,640]{1,0:T(8,128)(2,1)S(1)} %get-tuple-element.112.normed, bf16[4,320,640]{2,1,0:T(8,128)(2,1)S(1)} %get-tuple-element.113.own, bf16[4,320,640]{2,1,0:T(8,128)(2,1)} %collective-permute-done.6.other), custom_call_target="tpu_custom_call" | custom-call | flops 314572800 | bytes 2129920 | tf_op jit(solution)/shard_map/project_part/pallas_call | solution.py:470
  45.9 1.6 collective-permute-start.9
  47.5 5.4 %project.1 = (f32[4,192,640]{2,1,0:T(8,128)}, bf16[2,192,640]{2,1,0:T(8,128)(2,1)S(1)}, f32[2,192,640]{2,1,0:T(8,128)S(1)}) custom-call(s32[1]{0:T(128)} %bitcast.14.info, bf16[384,640]{1,0:T(8,128)(2,1)} %copy-done.8, bf16[4,320,640]{2,1,0:T(8,128)(2,1)S(1)} %copy-done.6, bf16[4,320,640]{2,1,0:T(8,128)(2,1)} %collective-permute-done.7.other), custom_call_target="tpu_custom_call" | custom-call | flops 1258291200 | bytes 5242880 | tf_op jit(solution)/shard_map/project/pallas_call | solution.py:428
  53.4 2.0 %project_part.5.away = f32[2,192,640]{2,1,0:T(8,128)S(1)} custom-call(s32[1]{0:T(128)} %bitcast.14.info, bf16[384,640]{1,0:T(8,128)(2,1)S(1)} %copy-done.9, bf16[4,320,640]{2,1,0:T(8,128)(2,1)S(1)} %get-tuple-element.113.own, bf16[4,320,640]{2,1,0:T(8,128)(2,1)} %collective-permute-done.6.other), custom_call_target="tpu_custom_call" | custom-call | flops 314572800 | bytes 2129920 | tf_op jit(solution)/shard_map/project_part/pallas_call | solution.py:470
  55.4 4.7 %collective-permute-done.9.got_away = bf16[2,192,640]{2,1,0:T(8,128)(2,1)S(1)} collective-permute-done((bf16[2,192,640]{2,1,0:T(8,128)(2,1)S(1)}, bf16[2,192,640]{2,1,0:T(8,128)(2,1)S(1)}, u32[]{:S(2)}, u32[]{:S(2)}) %collective-permute-start.9) | collective-permute-done | bytes 491552 | tf_op jit(solution)/shard_map/ppermute | solution.py:753
  60.1 5.8 %collective-permute-done.8.got = bf16[4,192,640]{2,1,0:T(8,128)(2,1)S(1)} collective-permute-done((bf16[4,192,640]{2,1,0:T(8,128)(2,1)S(1)}, bf16[4,192,640]{2,1,0:T(8,128)(2,1)S(1)}, u32[]{:S(2)}, u32[]{:S(2)}) %collective-permute-start.8) | collective-permute-done | bytes 983072 | tf_op jit(solution)/shard_map/ppermute | solution.py:753
  66.7 2.5 %collective-permute-done.10.got_home = bf16[2,192,640]{2,1,0:T(8,128)(2,1)S(1)} collective-permute-done((bf16[2,192,640]{2,1,0:T(8,128)(2,1)S(1)}, bf16[2,192,640]{2,1,0:T(8,128)(2,1)S(1)}, u32[]{:S(2)}, u32[]{:S(2)}) %collective-permute-start.10) | collective-permute-done | bytes 491552 | tf_op jit(solution)/shard_map/ppermute | solution.py:753
  70.0 1.6 collective-permute-start.12
  71.6 1.6 collective-permute-start.13
  75.9 2.5 %collective-permute-done.12.refs_1_ = bf16[192,640]{1,0:T(8,128)(2,1)S(1)} collective-permute-done((bf16[192,640]{1,0:T(8,128)(2,1)}, bf16[192,640]{1,0:T(8,128)(2,1)S(1)}, u32[]{:S(2)}, u32[]{:S(2)}) %collective-permute-start.12) | collective-permute-done | bytes 245792 | tf_op jit(solution)/shard_map/ppermute | solution.py:753
  78.3 2.5 %collective-permute-start.14 = (bf16[192,640]{1,0:T(8,128)(2,1)S(1)}, bf16[192,640]{1,0:T(8,128)(2,1)S(1)}, u32[]{:S(2)}, u32[]{:S(2)}) collective-permute-start(bf16[192,640]{1,0:T(8,128)(2,1)S(1)} %get-tuple-element.126), channel_id=1, source_target_pairs={{0,8},{1,9},{2,10},{3,11},{4,12},{5,13},{6,14},{7,15},{8,0},{9,1},... | collective-permute-start | bytes 737288 | tf_op jit(solution)/shard_map/ppermute | solution.py:753
  80.9 4.8 %collective-permute-done.13.refs_3_ = bf16[192,640]{1,0:T(8,128)(2,1)S(1)} collective-permute-done((bf16[192,640]{1,0:T(8,128)(2,1)S(1)}, bf16[192,640]{1,0:T(8,128)(2,1)S(1)}, u32[]{:S(2)}, u32[]{:S(2)}) %collective-permute-start.13) | collective-permute-done | bytes 245792 | tf_op jit(solution)/shard_map/ppermute | solution.py:753
  85.8 8.5 %collective-permute-start.18 = (bf16[192,640]{1,0:T(8,128)(2,1)S(1)}, bf16[192,640]{1,0:T(8,128)(2,1)S(1)}, u32[]{:S(2)}, u32[]{:S(2)}) collective-permute-start(bf16[192,640]{1,0:T(8,128)(2,1)S(1)} %get-tuple-element.145), channel_id=1, source_target_pairs={{0,8},{1,9},{2,10},{3,11},{4,12},{5,13},{6,14},{7,15},{8,0},{9,1},... | collective-permute-start | bytes 737288 | tf_op jit(solution)/shard_map/ppermute | solution.py:753
  95.2 4.7 %collective-permute-done.14.refs_2_ = bf16[192,640]{1,0:T(8,128)(2,1)S(1)} collective-permute-done((bf16[192,640]{1,0:T(8,128)(2,1)S(1)}, bf16[192,640]{1,0:T(8,128)(2,1)S(1)}, u32[]{:S(2)}, u32[]{:S(2)}) %collective-permute-start.14) | collective-permute-done | bytes 245792 | tf_op jit(solution)/shard_map/ppermute | solution.py:753
  100.9 3.2 %collective-permute-done.18.refs_1_ = bf16[192,640]{1,0:T(8,128)(2,1)S(1)} collective-permute-done((bf16[192,640]{1,0:T(8,128)(2,1)S(1)}, bf16[192,640]{1,0:T(8,128)(2,1)S(1)}, u32[]{:S(2)}, u32[]{:S(2)}) %collective-permute-start.18) | collective-permute-done | bytes 245792 | tf_op jit(solution)/shard_map/ppermute | solution.py:753
  111.4 8.8 %collective-permute-done.21.refs_1_ = bf16[192,1024]{1,0:T(8,128)(2,1)S(1)} collective-permute-done((bf16[192,1024]{1,0:T(8,128)(2,1)S(1)}, bf16[192,1024]{1,0:T(8,128)(2,1)S(1)}, u32[]{:S(2)}, u32[]{:S(2)}) %collective-permute-start.21) | collective-permute-done | bytes 393248 | tf_op jit(solution)/shard_map/ppermute | solution.py:920
  125.8 4.8 %out_project.3.refs_6_ = f32[2,320,192]{2,1,0:T(8,128)S(1)} custom-call(s32[5]{0:T(128)S(1)} %pad_add_fusion.4.info, f32[64,40]{1,0:T(8,128)S(1)} %copy.22.scales, bf16[192,1024]{1,0:T(8,128)(2,1)S(1)} %maximum_maximum_fusion.refs_0_, bf16[192,1024]{1,0:T(8,128)(2,1)S(1)} %collective-permute-done.21.refs_1_, ...), custom_call_target="tpu_custom_call" | custom-call | flops 754974720 | bytes 3932160 | tf_op jit(solution)/shard_map/out_project/pallas_call | solution.py:692
  130.6 1.9 %collective-permute-done.28.far = bf16[8,160,128]{2,1,0:T(8,128)(2,1)S(1)} collective-permute-done((bf16[8,160,128]{2,1,0:T(8,128)(2,1)S(1)}, bf16[8,160,128]{2,1,0:T(8,128)(2,1)S(1)}, u32[]{:S(2)}, u32[]{:S(2)}) %collective-permute-start.28) | collective-permute-done | bytes 327712 | tf_op jit(solution)/shard_map/ppermute | solution.py:756
  132.5 5.5 %collective-permute-done.24 = bf16[192,1024]{1,0:T(8,128)(2,1)S(1)} collective-permute-done((bf16[192,1024]{1,0:T(8,128)(2,1)S(1)}, bf16[192,1024]{1,0:T(8,128)(2,1)S(1)}, u32[]{:S(2)}, u32[]{:S(2)}) %collective-permute-start.24) | collective-permute-done | bytes 393248 | tf_op jit(solution)/shard_map/ppermute | solution.py:906
  143.0 3.3 %collect_keys.1 = bf16[8,2,2,160,128]{4,3,2,1,0:T(8,128)(2,1)} custom-call(s32[3]{0:T(128)S(1)} %pad_add_fusion.5.info, bf16[8,160,128]{2,1,0:T(8,128)(2,1)S(1)} %bitcast.47, bf16[8,160,128]{2,1,0:T(8,128)(2,1)S(1)} %collective-permute-done.28.far, bf16[8,160,128]{2,1,0:T(8,128)(2,1)S(1)} %collective-permute-done.31.other, ...), custom_call_target="tpu_custom_call" | custom-call | bytes 2621440 | tf_op jit(solution)/shard_map/collect_keys/pallas_call | solution.py:888
  146.3 2.1 %collective-permute-done.29 = bf16[192,1024]{1,0:T(8,128)(2,1)S(1)} collective-permute-done((bf16[192,1024]{1,0:T(8,128)(2,1)S(1)}, bf16[192,1024]{1,0:T(8,128)(2,1)S(1)}, u32[]{:S(2)}, u32[]{:S(2)}) %collective-permute-start.29) | collective-permute-done | bytes 393248 | tf_op jit(solution)/shard_map/ppermute | solution.py:906
  150.1 5.6 %out_project.4.refs_3_ = f32[2,320,192]{2,1,0:T(8,128)S(1)} custom-call(s32[6]{0:T(128)S(1)} %pad_add_fusion.6.info, f32[64,40]{1,0:T(8,128)S(1)} %copy.22.scales, bf16[192,1024]{1,0:T(8,128)(2,1)S(1)} %collective-permute-done.26.refs_0_, bf16[192,1024]{1,0:T(8,128)(2,1)S(1)} %broadcast_select_fusion.1.refs_1_, ...), custom_call_target="tpu_custom_call" | custom-call | flops 1006632960 | bytes 5242880 | tf_op jit(solution)/shard_map/out_project/pallas_call | solution.py:692
  155.8 1.8 %collective-permute-done.33.refs_0_ = bf16[192,1024]{1,0:T(8,128)(2,1)S(1)} collective-permute-done((bf16[192,1024]{1,0:T(8,128)(2,1)S(1)}, bf16[192,1024]{1,0:T(8,128)(2,1)S(1)}, u32[]{:S(2)}, u32[]{:S(2)}) %collective-permute-start.33) | collective-permute-done | bytes 393248 | tf_op jit(solution)/shard_map/ppermute | solution.py:920
  157.6 3.3 %out_project.5 = bf16[192,640]{1,0:T(8,128)(2,1)S(1)} custom-call(s32[3]{0:T(128)S(1)} %pad_add_fusion.1.info, f32[64,40]{1,0:T(8,128)S(1)} %copy.22.scales, bf16[192,1024]{1,0:T(8,128)(2,1)S(1)} %collective-permute-done.33.refs_0_, bf16[320,8192]{1,0:T(8,128)(2,1)} %bitcast.57, bf16[320,8192]{1,0:T(8,128)(2,1)} %collective-permute-done.27.refs_4_.refs_5_.refs_2_, ...), custom_call_target="tpu_custom_call" | custom-call | flops 251658240 | bytes 1310720 | tf_op jit(solution)/shard_map/out_project/pallas_call | solution.py:692
  160.9 11.9 %all_to_all.16 = bf16[8,24,640]{2,1,0:T(8,128)(2,1)S(1)} all-to-all(bf16[8,24,640]{2,1,0:T(8,128)(2,1)S(1)} %bitcast.48), channel_id=1, replica_groups={{0,2,4,6,8,10,12,14},{1,3,5,7,9,11,13,15},{16,18,20,22,24,26,28,30},{17..., dimensions={0} | all-to-all | bytes 491520 | tf_op jit(solution)/shard_map/all_to_all | solution.py:759
  (116 shorter events, 39.6 us)
Async XLA Ops:
  0.6 125.2 %collective-permute-start.27 = (bf16[320,8192]{1,0:T(8,128)(2,1)}, bf16[320,8192]{1,0:T(8,128)(2,1)}, u32[]{:S(2)}, u32[]{:S(2)}) collective-permute-start(bf16[320,8192]{1,0:T(8,128)(2,1)} %bitcast.54), channel_id=1, source_target_pairs={{0,1},{1,0},{2,3},{3,2},{4,5},{5,4},{6,7},{7,6},{8,9},{9,8},{10,11... | collective-permute-start | bytes 15728648 | tf_op jit(solution)/shard_map/ppermute | solution.py:753
  8.0 24.0 %all-to-all-start.1 = ((bf16[8,32,640]{2,1,0:T(8,128)(2,1)}), bf16[8,32,640]{2,1,0:T(8,128)(2,1)S(1)}, u32[]{:S(2)}, u32[]{:S(2)}) async-start(bf16[8,32,640]{2,1,0:T(8,128)(2,1)} %pick_rows.2), calls=%async_computation.1 | async-start | bytes 655360 | tf_op jit(solution)/shard_map/all_to_all | solution.py:759
  17.4 13.6 %collective-permute-start.1 = (bf16[2,160,128]{2,1,0:T(8,128)(2,1)}, bf16[2,160,128]{2,1,0:T(8,128)(2,1)}, u32[]{:S(2)}, u32[]{:S(2)}) collective-permute-start(bf16[2,160,128]{2,1,0:T(8,128)(2,1)} %get-tuple-element.180), channel_id=1, source_target_pairs={{0,4},{1,5},{2,6},{3,7},{4,0},{5,1},{6,2},{7,3},{8,12},{9,13},{10,... | collective-permute-start | bytes 245768 | tf_op jit(solution)/shard_map/ppermute | solution.py:753
  19.4 12.6 %collective-permute-start.2 = (bf16[2,160,128]{2,1,0:T(8,128)(2,1)}, bf16[2,160,128]{2,1,0:T(8,128)(2,1)}, u32[]{:S(2)}, u32[]{:S(2)}) collective-permute-start(bf16[2,160,128]{2,1,0:T(8,128)(2,1)} %get-tuple-element.179), channel_id=1, source_target_pairs={{0,8},{1,9},{2,10},{3,11},{4,12},{5,13},{6,14},{7,15},{8,0},{9,1},... | collective-permute-start | bytes 245768 | tf_op jit(solution)/shard_map/ppermute | solution.py:753
  21.8 10.2 %collective-permute-start.3 = (bf16[2,160,128]{2,1,0:T(8,128)(2,1)}, bf16[2,160,128]{2,1,0:T(8,128)(2,1)}, u32[]{:S(2)}, u32[]{:S(2)}) collective-permute-start(bf16[2,160,128]{2,1,0:T(8,128)(2,1)} %get-tuple-element.178), channel_id=1, source_target_pairs={{0,12},{1,13},{2,14},{3,15},{4,8},{5,9},{6,10},{7,11},{8,4},{9,5},... | collective-permute-start | bytes 245768 | tf_op jit(solution)/shard_map/ppermute | solution.py:753
  32.0 6.7 %collective-permute-start.6 = (bf16[4,320,640]{2,1,0:T(8,128)(2,1)}, bf16[4,320,640]{2,1,0:T(8,128)(2,1)}, u32[]{:S(2)}, u32[]{:S(2)}) collective-permute-start(bf16[4,320,640]{2,1,0:T(8,128)(2,1)} %copy-done.7), channel_id=1, source_target_pairs={{0,1},{1,0},{2,3},{3,2},{4,5},{5,4},{6,7},{7,6},{8,9},{9,8},{10,11... | collective-permute-start | bytes 4915208 | tf_op jit(solution)/shard_map/ppermute | solution.py:753
  32.0 15.5 %collective-permute-start.7 = (bf16[4,320,640]{2,1,0:T(8,128)(2,1)}, bf16[4,320,640]{2,1,0:T(8,128)(2,1)}, u32[]{:S(2)}, u32[]{:S(2)}) collective-permute-start(bf16[4,320,640]{2,1,0:T(8,128)(2,1)} %get-tuple-element.118), channel_id=1, source_target_pairs={{0,1},{1,0},{2,3},{3,2},{4,5},{5,4},{6,7},{7,6},{8,9},{9,8},{10,11... | collective-permute-start | bytes 4915208 | tf_op jit(solution)/shard_map/ppermute | solution.py:753
  32.5 4.2 %collective-permute-start.4 = (bf16[8,32,640]{2,1,0:T(8,128)(2,1)S(1)}, bf16[8,32,640]{2,1,0:T(8,128)(2,1)S(1)}, u32[]{:S(2)}, u32[]{:S(2)}) collective-permute-start(bf16[8,32,640]{2,1,0:T(8,128)(2,1)S(1)} %all-to-all-done.1), channel_id=1, source_target_pairs={{0,1},{1,0},{2,3},{3,2},{4,5},{5,4},{6,7},{7,6},{8,9},{9,8},{10,11... | collective-permute-start | bytes 983048 | tf_op jit(solution)/shard_map/ppermute | solution.py:753
  32.6 3.6 %collective-permute-start.5 = (f32[8,128]{1,0:T(8,128)S(1)}, f32[8,128]{1,0:T(8,128)S(1)}, u32[]{:S(2)}, u32[]{:S(2)}) collective-permute-start(f32[8,128]{1,0:T(8,128)S(1)} %get-tuple-element.111), channel_id=1, source_target_pairs={{0,16},{16,0},{1,17},{17,1},{2,18},{18,2},{3,19},{19,3},{4,20},{20... | collective-permute-start | bytes 12296 | tf_op jit(solution)/shard_map/ppermute | solution.py:756
  42.3 23.6 %collective-permute-start.8 = (bf16[4,192,640]{2,1,0:T(8,128)(2,1)S(1)}, bf16[4,192,640]{2,1,0:T(8,128)(2,1)S(1)}, u32[]{:S(2)}, u32[]{:S(2)}) collective-permute-start(bf16[4,192,640]{2,1,0:T(8,128)(2,1)S(1)} %project_part.3), channel_id=1, source_target_pairs={{0,2},{1,3},{2,0},{3,1},{4,6},{5,7},{6,4},{7,5},{8,10},{9,11},{10,... | collective-permute-start | bytes 2949128 | tf_op jit(solution)/shard_map/ppermute | solution.py:753
  45.9 14.2 %collective-permute-start.9 = (bf16[2,192,640]{2,1,0:T(8,128)(2,1)S(1)}, bf16[2,192,640]{2,1,0:T(8,128)(2,1)S(1)}, u32[]{:S(2)}, u32[]{:S(2)}) collective-permute-start(bf16[2,192,640]{2,1,0:T(8,128)(2,1)S(1)} %project_part.4), channel_id=1, source_target_pairs={{0,4},{1,5},{2,6},{3,7},{4,0},{5,1},{6,2},{7,3},{8,12},{9,13},{10,... | collective-permute-start | bytes 1474568 | tf_op jit(solution)/shard_map/ppermute | solution.py:753
  52.9 16.4 %collective-permute-start.10 = (bf16[2,192,640]{2,1,0:T(8,128)(2,1)S(1)}, bf16[2,192,640]{2,1,0:T(8,128)(2,1)S(1)}, u32[]{:S(2)}, u32[]{:S(2)}) collective-permute-start(bf16[2,192,640]{2,1,0:T(8,128)(2,1)S(1)} %get-tuple-element.124), channel_id=1, source_target_pairs={{0,4},{1,5},{2,6},{3,7},{4,0},{5,1},{6,2},{7,3},{8,12},{9,13},{10,... | collective-permute-start | bytes 1474568 | tf_op jit(solution)/shard_map/ppermute | solution.py:753
  69.4 16.3 %collective-permute-start.11 = (bf16[2,192,640]{2,1,0:T(8,128)(2,1)S(1)}, bf16[2,192,640]{2,1,0:T(8,128)(2,1)S(1)}, u32[]{:S(2)}, u32[]{:S(2)}) collective-permute-start(bf16[2,192,640]{2,1,0:T(8,128)(2,1)S(1)} %get-tuple-element.130), channel_id=1, source_target_pairs={{0,2},{1,3},{2,0},{3,1},{4,6},{5,7},{6,4},{7,5},{8,10},{9,11},{10,... | collective-permute-start | bytes 1474568 | tf_op jit(solution)/shard_map/ppermute | solution.py:753
  70.0 8.3 %collective-permute-start.12 = (bf16[192,640]{1,0:T(8,128)(2,1)}, bf16[192,640]{1,0:T(8,128)(2,1)S(1)}, u32[]{:S(2)}, u32[]{:S(2)}) collective-permute-start(bf16[192,640]{1,0:T(8,128)(2,1)} %get-tuple-element.125), channel_id=1, source_target_pairs={{0,4},{1,5},{2,6},{3,7},{4,0},{5,1},{6,2},{7,3},{8,12},{9,13},{10,... | collective-permute-start | bytes 737288 | tf_op jit(solution)/shard_map/ppermute | solution.py:753
  71.6 14.1 %collective-permute-start.13 = (bf16[192,640]{1,0:T(8,128)(2,1)S(1)}, bf16[192,640]{1,0:T(8,128)(2,1)S(1)}, u32[]{:S(2)}, u32[]{:S(2)}) collective-permute-start(bf16[192,640]{1,0:T(8,128)(2,1)S(1)} %get-tuple-element.127), channel_id=1, source_target_pairs={{0,12},{1,13},{2,14},{3,15},{4,8},{5,9},{6,10},{7,11},{8,4},{9,5},... | collective-permute-start | bytes 737288 | tf_op jit(solution)/shard_map/ppermute | solution.py:753
  74.3 26.6 %collective-permute-start.17 = (bf16[4,160,128]{2,1,0:T(8,128)(2,1)S(1)}, bf16[4,160,128]{2,1,0:T(8,128)(2,1)S(1)}, u32[]{:S(2)}, u32[]{:S(2)}) collective-permute-start(bf16[4,160,128]{2,1,0:T(8,128)(2,1)S(1)} %get-tuple-element.183), channel_id=1, source_target_pairs={{0,2},{1,3},{2,0},{3,1},{4,6},{5,7},{6,4},{7,5},{8,10},{9,11},{10,... | collective-permute-start | bytes 491528 | tf_op jit(solution)/shard_map/ppermute | solution.py:753
  78.3 21.6 %collective-permute-start.14 = (bf16[192,640]{1,0:T(8,128)(2,1)S(1)}, bf16[192,640]{1,0:T(8,128)(2,1)S(1)}, u32[]{:S(2)}, u32[]{:S(2)}) collective-permute-start(bf16[192,640]{1,0:T(8,128)(2,1)S(1)} %get-tuple-element.126), channel_id=1, source_target_pairs={{0,8},{1,9},{2,10},{3,11},{4,12},{5,13},{6,14},{7,15},{8,0},{9,1},... | collective-permute-start | bytes 737288 | tf_op jit(solution)/shard_map/ppermute | solution.py:753
  85.8 18.3 %collective-permute-start.18 = (bf16[192,640]{1,0:T(8,128)(2,1)S(1)}, bf16[192,640]{1,0:T(8,128)(2,1)S(1)}, u32[]{:S(2)}, u32[]{:S(2)}) collective-permute-start(bf16[192,640]{1,0:T(8,128)(2,1)S(1)} %get-tuple-element.145), channel_id=1, source_target_pairs={{0,8},{1,9},{2,10},{3,11},{4,12},{5,13},{6,14},{7,15},{8,0},{9,1},... | collective-permute-start | bytes 737288 | tf_op jit(solution)/shard_map/ppermute | solution.py:753
  100.8 4.1 %collective-permute-start.15 = (bf16[192,128]{1,0:T(8,128)(2,1)S(1)}, bf16[192,128]{1,0:T(8,128)(2,1)S(1)}, u32[]{:S(2)}, u32[]{:S(2)}) collective-permute-start(bf16[192,128]{1,0:T(8,128)(2,1)S(1)} %get-tuple-element.134.refs_0_), channel_id=1, source_target_pairs={{0,1},{1,0},{2,3},{3,2},{4,5},{5,4},{6,7},{7,6},{8,9},{9,8},{10,11... | collective-permute-start | bytes 147464 | tf_op jit(solution)/shard_map/ppermute | solution.py:753
  105.8 1.9 %collective-permute-start.16 = (bf16[96,512]{1,0:T(8,128)(2,1)S(1)}, bf16[96,512]{1,0:T(8,128)(2,1)S(1)}, u32[]{:S(2)}, u32[]{:S(2)}) collective-permute-start(bf16[96,512]{1,0:T(8,128)(2,1)S(1)} %get-tuple-element.136), channel_id=1, source_target_pairs={{0,1},{1,0},{2,3},{3,2},{4,5},{5,4},{6,7},{7,6},{8,9},{9,8},{10,11... | collective-permute-start | bytes 294920 | tf_op jit(solution)/shard_map/ppermute | solution.py:753
  109.0 11.2 %collective-permute-start.21 = (bf16[192,1024]{1,0:T(8,128)(2,1)S(1)}, bf16[192,1024]{1,0:T(8,128)(2,1)S(1)}, u32[]{:S(2)}, u32[]{:S(2)}) collective-permute-start(bf16[192,1024]{1,0:T(8,128)(2,1)S(1)} %maximum_maximum_fusion.refs_0_), channel_id=1, source_target_pairs={{0,2},{1,3},{2,0},{3,1},{4,6},{5,7},{6,4},{7,5},{8,10},{9,11},{10,... | collective-permute-start | bytes 1179656 | tf_op jit(solution)/shard_map/ppermute | solution.py:920
  110.5 10.9 %collective-permute-start.22 = (bf16[192,1024]{1,0:T(8,128)(2,1)S(1)}, bf16[192,1024]{1,0:T(8,128)(2,1)S(1)}, u32[]{:S(2)}, u32[]{:S(2)}) collective-permute-start(bf16[192,1024]{1,0:T(8,128)(2,1)S(1)} %maximum_maximum_fusion.refs_0_), channel_id=1, source_target_pairs={{0,4},{1,5},{2,6},{3,7},{4,0},{5,1},{6,2},{7,3},{8,12},{9,13},{10,... | collective-permute-start | bytes 1179656 | tf_op jit(solution)/shard_map/ppermute | solution.py:906
  110.5 10.9 %collective-permute-start.23 = (bf16[192,1024]{1,0:T(8,128)(2,1)S(1)}, bf16[192,1024]{1,0:T(8,128)(2,1)S(1)}, u32[]{:S(2)}, u32[]{:S(2)}) collective-permute-start(bf16[192,1024]{1,0:T(8,128)(2,1)S(1)} %maximum_maximum_fusion.refs_0_), channel_id=1, source_target_pairs={{4,8},{5,9},{6,10},{7,11},{8,4},{9,5},{10,6},{11,7},{20,24},{21,25... | collective-permute-start | bytes 1179656 | tf_op jit(solution)/shard_map/ppermute | solution.py:906
  121.4 16.6 %collective-permute-start.25 = (bf16[192,1024]{1,0:T(8,128)(2,1)S(1)}, bf16[192,1024]{1,0:T(8,128)(2,1)S(1)}, u32[]{:S(2)}, u32[]{:S(2)}) collective-permute-start(bf16[192,1024]{1,0:T(8,128)(2,1)S(1)} %collective-permute-done.22.refs_2_), channel_id=1, source_target_pairs={{4,8},{5,9},{6,10},{7,11},{8,4},{9,5},{10,6},{11,7},{20,24},{21,25... | collective-permute-start | bytes 1179656 | tf_op jit(solution)/shard_map/ppermute | solution.py:906
  122.1 15.9 %collective-permute-start.26 = (bf16[192,1024]{1,0:T(8,128)(2,1)S(1)}, bf16[192,1024]{1,0:T(8,128)(2,1)S(1)}, u32[]{:S(2)}, u32[]{:S(2)}) collective-permute-start(bf16[192,1024]{1,0:T(8,128)(2,1)S(1)} %collective-permute-done.22.refs_2_), channel_id=1, source_target_pairs={{0,2},{1,3},{2,0},{3,1},{4,6},{5,7},{6,4},{7,5},{8,10},{9,11},{10,... | collective-permute-start | bytes 1179656 | tf_op jit(solution)/shard_map/ppermute | solution.py:920
  122.7 15.3 %collective-permute-start.24 = (bf16[192,1024]{1,0:T(8,128)(2,1)S(1)}, bf16[192,1024]{1,0:T(8,128)(2,1)S(1)}, u32[]{:S(2)}, u32[]{:S(2)}) collective-permute-start(bf16[192,1024]{1,0:T(8,128)(2,1)S(1)} %collective-permute-done.23), channel_id=1, source_target_pairs={{4,0},{5,1},{6,2},{7,3},{8,12},{9,13},{10,14},{11,15},{20,16},{21,... | collective-permute-start | bytes 1179656 | tf_op jit(solution)/shard_map/ppermute | solution.py:906
  124.1 8.4 %collective-permute-start.28 = (bf16[8,160,128]{2,1,0:T(8,128)(2,1)S(1)}, bf16[8,160,128]{2,1,0:T(8,128)(2,1)S(1)}, u32[]{:S(2)}, u32[]{:S(2)}) collective-permute-start(bf16[8,160,128]{2,1,0:T(8,128)(2,1)S(1)} %bitcast.45), channel_id=1, source_target_pairs={{0,16},{16,0},{1,17},{17,1},{2,18},{18,2},{3,19},{19,3},{4,20},{20... | collective-permute-start | bytes 983048 | tf_op jit(solution)/shard_map/ppermute | solution.py:756
  138.1 10.4 %collective-permute-start.29 = (bf16[192,1024]{1,0:T(8,128)(2,1)S(1)}, bf16[192,1024]{1,0:T(8,128)(2,1)S(1)}, u32[]{:S(2)}, u32[]{:S(2)}) collective-permute-start(bf16[192,1024]{1,0:T(8,128)(2,1)S(1)} %broadcast_select_fusion.1.refs_1_), channel_id=1, source_target_pairs={{4,0},{5,1},{6,2},{7,3},{8,12},{9,13},{10,14},{11,15},{20,16},{21,... | collective-permute-start | bytes 1179656 | tf_op jit(solution)/shard_map/ppermute | solution.py:906
  139.4 9.1 %collective-permute-start.30 = (bf16[192,1024]{1,0:T(8,128)(2,1)S(1)}, bf16[192,1024]{1,0:T(8,128)(2,1)S(1)}, u32[]{:S(2)}, u32[]{:S(2)}) collective-permute-start(bf16[192,1024]{1,0:T(8,128)(2,1)S(1)} %broadcast_select_fusion.1.refs_1_), channel_id=1, source_target_pairs={{0,2},{1,3},{2,0},{3,1},{4,6},{5,7},{6,4},{7,5},{8,10},{9,11},{10,... | collective-permute-start | bytes 1179656 | tf_op jit(solution)/shard_map/ppermute | solution.py:920
  140.9 1.6 collective-permute-start.31
  140.9 2.1 %collective-permute-start.32 = (bf16[8,160,128]{2,1,0:T(8,128)(2,1)S(1)}, bf16[8,160,128]{2,1,0:T(8,128)(2,1)S(1)}, u32[]{:S(2)}, u32[]{:S(2)}) collective-permute-start(bf16[8,160,128]{2,1,0:T(8,128)(2,1)S(1)} %collective-permute-done.28.far), channel_id=1, source_target_pairs={{0,1},{1,0},{2,3},{3,2},{4,5},{5,4},{6,7},{7,6},{8,9},{9,8},{10,11... | collective-permute-start | bytes 983048 | tf_op jit(solution)/shard_map/ppermute | solution.py:753
  148.5 9.1 %collective-permute-start.33 = (bf16[192,1024]{1,0:T(8,128)(2,1)S(1)}, bf16[192,1024]{1,0:T(8,128)(2,1)S(1)}, u32[]{:S(2)}, u32[]{:S(2)}) collective-permute-start(bf16[192,1024]{1,0:T(8,128)(2,1)S(1)} %broadcast_select_fusion.refs_3_), channel_id=1, source_target_pairs={{0,2},{1,3},{2,0},{3,1},{4,6},{5,7},{6,4},{7,5},{8,10},{9,11},{10,... | collective-permute-start | bytes 1179656 | tf_op jit(solution)/shard_map/ppermute | solution.py:920
  (18 other events, 203.8 us)
